TPU v7x, 256 devices: a whole 4x4x8 slice. The times are simulated.
256 devices in a mesh: row: 32 (over y, z_hi, core), col: 8 (over x, z_lo).
Axes of the slice: x: 4, y: 4, z: 8 (z_hi: 4, z_lo: 2; z = z_hi * 2 + z_lo), core: 2. Of those that a mesh axis runs over, the one named last changes fastest.
Arguments:
- features: bfloat16 [32768, 512], P(('row', 'col')), may hold values from -6 to 6
- degrees: int32 [32768], P(('row', 'col')), may hold values from 768 to 1535
- tile_rows: int32 [32, 8, 32, 3], P('row', 'col'), may hold values from 0 to 7
- tile_masks: int32 [32, 8, 32, 3, 128, 128], P('row', 'col'), may hold values 0 or 1
- w_self: bfloat16 [512, 512], replicated, may hold values from -0.25 to 0.25
- w_neigh: bfloat16 [512, 512], replicated, may hold values from -6 to 6
- bias: float32 [512], replicated, may hold values from -3 to 3
- cotangent: bfloat16 [32768, 512], P(('row', 'col')), may hold values from -6 to 6
Outputs:
- output: bfloat16 [32768, 512], P(('row', 'col'))
- grad_features: bfloat16 [32768, 512], P(('row', 'col'))
All inputs are finite; a program needn't handle non-finite values. No bound on the sum of `tile_masks` on one device may be relied on, other than what follows from the above.
Results may differ from a plain program's by a relative error of at most 0.024.
Values may be sent and summed in bfloat16 or wider, within the bound.
No kernel may reach another device: no remote copies, remote signals or barrier semaphores. Data moves between devices by JAX's collectives and lax.ppermute only.
A program may use at most 128 MiB of HBM per device.

v0:
```python
import jax
import jax.numpy as jnp
from jax import lax
from jax.sharding import PartitionSpec as P


def silu_slope(pre):
    sig = jax.nn.sigmoid(pre)
    return sig * (1.0 + pre * (1.0 - sig))


def body(features, degrees, tile_rows, tile_masks, w_self, w_neigh, bias, cotangent):
    tile = tile_masks.shape[-1]
    slots = tile_masks.shape[3]
    width = features.shape[1]
    local_nodes = features.shape[0]
    row_tiles = lax.axis_size("col") * local_nodes // tile
    masks = tile_masks[0, 0].astype(jnp.bfloat16)
    rows_here = tile_rows[0, 0]
    empty = jnp.zeros((row_tiles, tile, width), jnp.float32)
    piece = lax.all_gather(features, "row", axis=0, tiled=True)
    count = piece.shape[0] // tile
    part = masks
    which = rows_here
    blocks = piece.reshape(count, tile, width)
    prods = jnp.einsum("jkuv,jvf->jkuf", part, blocks, preferred_element_type=jnp.float32)
    summed = empty.at[which.reshape(-1)].add(prods.reshape(count * slots, tile, width))
    mine = lax.psum_scatter(
        summed.reshape(row_tiles * tile, width).astype(jnp.bfloat16),
        "col",
        scatter_dimension=0,
        tiled=True,
    ).astype(jnp.float32)
    degf = degrees.astype(jnp.float32)
    mean_neigh = (mine / degf[:, None]).astype(jnp.bfloat16)
    pre = jnp.dot(features, w_self, preferred_element_type=jnp.float32)
    pre = pre + jnp.dot(mean_neigh, w_neigh, preferred_element_type=jnp.float32) + bias[None, :]
    output = jax.nn.silu(pre).astype(jnp.bfloat16)
    grad_pre = (cotangent.astype(jnp.float32) * silu_slope(pre)).astype(jnp.bfloat16)
    proj = lax.dot_general(
        grad_pre, w_neigh, (((1,), (1,)), ((), ())), preferred_element_type=jnp.float32
    )
    spread = lax.all_gather(
        (proj / degrees.astype(jnp.float32)[:, None]).astype(jnp.bfloat16),
        "col",
        axis=0,
        tiled=True,
    )
    table = spread.reshape(row_tiles, tile, width)
    part = masks
    which = rows_here
    picked = table[which]
    terms = jnp.einsum("jkuv,jkuf->jvf", part, picked, preferred_element_type=jnp.float32)
    back = lax.psum_scatter(
        terms.reshape(local_nodes * lax.axis_size("row"), width).astype(jnp.bfloat16),
        "row",
        scatter_dimension=0,
        tiled=True,
    ).astype(jnp.float32)
    own = lax.dot_general(
        grad_pre, w_self, (((1,), (1,)), ((), ())), preferred_element_type=jnp.float32
    )
    grad_features = (own + back).astype(jnp.bfloat16)
    return (output, grad_features)


def solution(mesh):
    return jax.shard_map(
        body,
        mesh=mesh,
        in_specs=(
            P(("row", "col"), None),
            P(("row", "col")),
            P("row", "col", None, None),
            P("row", "col", None, None, None, None),
            P(),
            P(),
            P(),
            P(("row", "col"), None),
        ),
        out_specs=(P(("row", "col"), None), P(("row", "col"), None)),
        check_vma=False,
    )
```

profile of v0, /device:TPU:32, one launch (start us, length us, event | category | flops | bytes accessed | tf_op | source)
XLA Modules:
  0.0 333.9 jit_solution(10877732764935478335)
XLA Ops:
  7.2 0.0 copy-start
  7.2 0.0 all-gather.3.cloned.1.call-start
  7.2 0.7 all-gather.3.cloned.1.call-update
  7.9 0.0 reduce-scatter.3.cloned.1.call-start
  8.0 0.8 copy.13
  8.7 0.1 reshape_squeeze.3
  8.8 63.7 %all-gather.3.cloned.1.call-done = bf16[4096,512]{1,0:T(8,128)(2,1)} async-done(((bf16[128,512]{1,0:T(8,128)(2,1)}), bf16[4096,512]{1,0:T(8,128)(2,1)}) %all-gather.3.cloned.1.call-update) | async-done | bytes 4194320 | tf_op jit(solution)/shard_map/all_gather | solution.py:21
  72.5 15.7 %fusion.1 = f32[32,3,128,512]{3,2,1,0:T(8,128)} fusion(bf16[32,128,512,1]{2,1,3,0:T(8,128)(2,1)} %bitcast.39, s32[1,1,32,3,128,128]{5,4,3,2,1,0:T(8,128)} %param.11), kind=kOutput, calls=%fused_computation.4 | convolution fusion | flops 1612185600 | bytes 35651584 | tf_op jit(solution)/shard_map/jkuv,jvf->jkuf/dot_general | solution.py:26
  88.3 0.2 broadcast_in_dim.2
  88.5 0.0 copy-start.6
  88.5 0.0 copy-start.1
  88.6 0.0 copy-start.2
  88.6 0.0 copy-start.5
  88.6 34.2 %scatter_fusion = f32[8,128,512]{2,1,0:T(8,128)S(1)} fusion(f32[8,128,512]{2,1,0:T(8,128)S(1)} %broadcast_in_dim.2, s32[96]{0:T(128)S(1)} %fusion.9, f32[96,128,512]{2,1,0:T(8,128)} %bitcast.37), kind=kCustom, calls=%fused_computation.1 | custom fusion | flops 6291456 | bytes 75497856 | tf_op jit(solution)/shard_map/scatter-add | solution.py:27
  122.8 0.0 copy-start.4
  122.8 1.1 convert_element_type.51
  123.9 0.0 reduce-scatter.3.cloned.1.call-update
  123.9 0.0 all-gather.5.cloned.1.call-start
  124.0 0.2 fusion.10
  124.3 39.3 %reduce-scatter.3.cloned.1.call-done = bf16[128,512]{1,0:T(8,128)(2,1)} async-done(((bf16[1024,512]{1,0:T(8,128)(2,1)}), bf16[128,512]{1,0:T(8,128)(2,1)}) %reduce-scatter.3.cloned.1.call-update) | async-done | bytes 131088 | tf_op jit(solution)/shard_map/reduce_scatter | solution.py:28
  163.6 1.9 multiply_convert_fusion.1
  165.5 1.0 fusion.7
  166.4 0.0 all-gather.5.cloned.1.call-update
  166.5 0.0 reduce-scatter.5.cloned.1.call-start
  166.5 0.1 copy.14
  166.6 0.1 reshape.81
  166.7 41.8 %all-gather.5.cloned.1.call-done = bf16[1024,512]{1,0:T(8,128)(2,1)} async-done(((bf16[128,512]{1,0:T(8,128)(2,1)}), bf16[1024,512]{1,0:T(8,128)(2,1)}) %all-gather.5.cloned.1.call-update) | async-done | bytes 1048592 | tf_op jit(solution)/shard_map/all_gather | solution.py:43
  208.6 8.0 %gather_fusion = bf16[96,128,512]{2,1,0:T(8,128)(2,1)} fusion(bf16[8,128,512]{2,1,0:T(8,128)(2,1)} %bitcast.35, s32[1024]{0:T(1024)S(1)} %pad_clamp_fusion), kind=kCustom, calls=%fused_computation | custom fusion | bytes 25166208 | tf_op jit(solution)/shard_map/gather | solution.py:52
  216.6 9.1 %bitcast_convert_fusion = bf16[32,512,128]{1,2,0:T(8,128)(2,1)} fusion(bf16[32,3,128,512]{3,2,1,0:T(8,128)(2,1)} %bitcast.36, s32[1,1,32,3,128,128]{5,4,3,2,1,0:T(8,128)} %param.11), kind=kOutput, calls=%fused_computation.2 | convolution fusion | flops 1614282752 | bytes 23068672 | tf_op jit(solution)/shard_map/jkuv,jkuf->jvf/dot_general | solution.py:53
  225.7 0.0 reduce-scatter.5.cloned.1.call-update
  225.7 99.7 %reduce-scatter.5.cloned.1.call-done = bf16[128,512]{1,0:T(8,128)(2,1)} async-done(((bf16[4096,512]{1,0:T(8,128)(2,1)}), bf16[128,512]{1,0:T(8,128)(2,1)}) %reduce-scatter.5.cloned.1.call-update) | async-done | bytes 131088 | tf_op jit(solution)/shard_map/reduce_scatter | solution.py:54
  325.5 1.9 fusion.6
  (12 shorter events, 0.0 us)
Async XLA Ops:
  7.2 156.4 %copy-start = (bf16[512,512]{1,0:T(8,128)(2,1)S(1)}, bf16[512,512]{1,0:T(8,128)(2,1)}, u32[]{:S(2)}) copy-start(bf16[512,512]{1,0:T(8,128)(2,1)} %param.13) | copy-start | bytes 1572868
  7.2 65.4 %all-gather.3.cloned.1.call-start = ((), (), s32[]{:S(2)}) async-start(), calls=%async_computation.2 | async-start | bytes 4325376 | tf_op jit(solution)/shard_map/all_gather | solution.py:21
  7.9 155.7 %reduce-scatter.3.cloned.1.call-start = ((), (), s32[]{:S(2)}) async-start(), calls=%async_computation.3 | async-start | bytes 1179648 | tf_op jit(solution)/shard_map/reduce_scatter | solution.py:28
  88.5 35.4 %copy-start.6 = (s32[128]{0:T(128)S(1)}, s32[128]{0:T(128)}, u32[]{:S(2)}) copy-start(s32[128]{0:T(128)} %param.9) | copy-start | bytes 1540
  88.5 35.5 %copy-start.1 = (bf16[512,512]{1,0:T(8,128)(2,1)S(1)}, bf16[512,512]{1,0:T(8,128)(2,1)}, u32[]{:S(2)}) copy-start(bf16[512,512]{1,0:T(8,128)(2,1)} %param.12) | copy-start | bytes 1572868
  88.6 35.5 %copy-start.2 = (bf16[128,512]{1,0:T(8,128)(2,1)S(1)}, bf16[128,512]{1,0:T(8,128)(2,1)}, u32[]{:S(2)}) copy-start(bf16[128,512]{1,0:T(8,128)(2,1)} %param.8) | copy-start | bytes 393220
  88.6 75.0 %copy-start.5 = (f32[512]{0:T(512)S(1)}, f32[512]{0:T(512)}, u32[]{:S(2)}) copy-start(f32[512]{0:T(512)} %param.14) | copy-start | bytes 6148
  122.8 42.7 %copy-start.4 = (bf16[128,512]{1,0:T(8,128)(2,1)S(1)}, bf16[128,512]{1,0:T(8,128)(2,1)}, u32[]{:S(2)}) copy-start(bf16[128,512]{1,0:T(8,128)(2,1)} %param.15) | copy-start | bytes 393220
  122.8 43.7 %copy-start.3 = (s32[1,1,32,3]{2,1,3,0:T(1,128)S(1)}, s32[1,1,32,3]{2,1,3,0:T(1,128)}, u32[]{:S(2)}) copy-start(s32[1,1,32,3]{2,1,3,0:T(1,128)} %param.10) | copy-start | bytes 1156
  123.9 84.6 %all-gather.5.cloned.1.call-start = ((), (), s32[]{:S(2)}) async-start(), calls=%async_computation.4 | async-start | bytes 1179648 | tf_op jit(solution)/shard_map/all_gather | solution.py:43
  166.5 159.0 %reduce-scatter.5.cloned.1.call-start = ((), (), s32[]{:S(2)}) async-start(), calls=%async_computation.5 | async-start | bytes 4325376 | tf_op jit(solution)/shard_map/reduce_scatter | solution.py:54
Sparse Core Ops, SparseCore 0:
  10.6 61.9 all-gather.2
  124.0 39.4 reduce-scatter.2
  166.6 41.9 all-gather.4
  225.8 99.5 reduce-scatter.4
where the time goes:
time: 336 us; the launch traced here: 334 us
  waiting for transfers between devices  245 us (73%)
  other arithmetic  35.3 us (11%)
  matrix products  29.8 us (9%)
  between operations  13.9 us (4%)
  local copies, waits for them, and re-layouts  9.36 us (3%)
    reduce_scatter x1, waiting for transfers between devices, body(): lax.psum_scatter(terms.reshape(local_nodes * lax.axis_size('row'), width)...  99.7 us
    all_gather x1, waiting for transfers between devices, body(): piece = lax.all_gather(features, 'row', axis=0, tiled=True)  63.7 us
    all_gather x1, waiting for transfers between devices, body(): lax.all_gather((proj / degrees.astype(jnp.float32)[:, None]).astype(jnp.b...  41.8 us
    reduce_scatter x1, waiting for transfers between devices, body(): lax.psum_scatter(summed.reshape(row_tiles * tile, width).astype(jnp.bfloa...  39.3 us
    scatter-add x1, other arithmetic, body(): empty.at[which.reshape(-1)].add(prods.reshape(count * slots, tile, width))  34.2 us
    dot_general x1, matrix products, body(): jnp.einsum('jkuv,jvf->jkuf', part, blocks, preferred_element_type=jnp.flo...  15.7 us
    dot_general x1, matrix products, body(): jnp.einsum('jkuv,jkuf->jvf', part, picked, preferred_element_type=jnp.flo...  9.13 us
    gather x1, local copies, waits for them, and re-layouts, body(): picked = table[which]  8.01 us
  transfers between devices with their start and end apart: 4, of which 4 were waited for; matrix products, arithmetic and copies ran while one was open for 0% of the time, Pallas kernels for 0%

commit v1 on v0

v1 whole, which is shorter than its diff:
```python
import functools

import jax
import jax.numpy as jnp
from jax import lax
from jax.experimental import pallas as pl
from jax.experimental.pallas import tpu as pltpu
from jax.sharding import PartitionSpec as P

NY, NZH, NCORE, NX, NZL = 4, 4, 2, 4, 2
NCOL = NX * NZL
TILE = 128
SPLIT_AG = 80
SPLIT_RS = 352
BF16 = jnp.bfloat16
F32 = jnp.float32
MB = 1024 * 1024


def pairs_to(dy=0, dzh=0, dc=0, dx=0, dzl=0):
    out = []
    for y in range(NY):
        for zh in range(NZH):
            for c in range(NCORE):
                for x in range(NX):
                    for zl in range(NZL):
                        src = (((y * NZH + zh) * NCORE + c) * NX + x) * NZL + zl
                        y2, zh2, c2 = (y + dy) % NY, (zh + dzh) % NZH, (c + dc) % NCORE
                        x2, zl2 = (x + dx) % NX, (zl + dzl) % NZL
                        out.append((src, (((y2 * NZH + zh2) * NCORE + c2) * NX + x2) * NZL + zl2))
    return out


def push(value, **ahead):
    return lax.ppermute(value, ("row", "col"), pairs_to(**ahead))


def pull(value, **ahead):
    return push(value, **{k: -v for k, v in ahead.items()})


def adjacency_kernel(order, where, *refs):
    del order
    masks, out = refs[:-1], refs[-1]
    step = pl.program_id(0)
    out[...] = jnp.zeros_like(out)
    slots = masks[0].shape[1]
    for i, mask in enumerate(masks):
        for k in range(slots):
            q = where[(step * len(masks) + i) * slots + k]
            at = pl.ds(pl.multiple_of(q * TILE, TILE), TILE)
            cols = slice(i * TILE, (i + 1) * TILE)
            out[at, cols] = out[at, cols] + mask[0, k].astype(F32).astype(BF16)


def adjacency(masks, order, where):
    count, slots = masks.shape[0], masks.shape[1]
    group = 4
    specs = [
        pl.BlockSpec(
            (1, slots, TILE, TILE),
            functools.partial(lambda i, s, order, where: (order[s * group + i], 0, 0, 0), i),
        )
        for i in range(group)
    ]
    return pl.pallas_call(
        adjacency_kernel,
        grid_spec=pltpu.PrefetchScalarGridSpec(
            num_scalar_prefetch=2,
            grid=(count // group,),
            in_specs=specs,
            out_specs=pl.BlockSpec((NCOL * TILE, group * TILE), lambda s, order, where: (0, s)),
        ),
        out_shape=jax.ShapeDtypeStruct((NCOL * TILE, count * TILE), BF16),
        compiler_params=pltpu.CompilerParams(vmem_limit_bytes=32 * MB),
        cost_estimate=pl.CostEstimate(flops=0, bytes_accessed=14 * MB, transcendentals=0),
        name="adjacency",
    )(order, where, *([masks] * group))


def gather_matmul_kernel(adj, *refs):
    nz = NCORE * NY
    zparts, yparts = refs[:nz], refs[nz : nz + NCORE * NZH]
    own_ref, out_refs = refs[nz + NCORE * NZH], refs[nz + NCORE * NZH + 1 : -2]
    whole, acc = refs[-2:]
    step = pl.program_id(0)
    a, b = SPLIT_AG, TILE - SPLIT_AG

    @pl.when(step == 0)
    def _():
        for c in range(NCORE):
            for dy in range(NY):
                for dzh in range(NZH):
                    at = ((c * NY + dy) * NZH + dzh) * TILE
                    whole[at : at + a, :] = zparts[c * NY + dy][dzh * a : (dzh + 1) * a, :]
                    whole[at + a : at + TILE, :] = yparts[c * NZH + dzh][dy * b : (dy + 1) * b, :]
        acc[...] = jnp.zeros_like(acc)

    depth = NZH * TILE
    rhs = whole[pl.ds(pl.multiple_of(step * depth, depth), depth), :]
    acc[...] += jnp.dot(adj[...], rhs, preferred_element_type=F32)

    @pl.when(step == pl.num_programs(0) - 1)
    def _():
        own_ref[...] = acc[0:TILE, :].astype(BF16)
        for i, out in enumerate(out_refs):
            out[...] = acc[(i + 1) * TILE : (i + 2) * TILE, :].astype(BF16)


def gather_matmul(adj, zparts, yparts):
    width = zparts[0].shape[1]
    rows, cols = adj.shape
    full = lambda v: pl.BlockSpec(v.shape, lambda s: (0,) * v.ndim)
    piece = jax.ShapeDtypeStruct((TILE, width), BF16)
    return pl.pallas_call(
        gather_matmul_kernel,
        grid=(NCORE * NY,),
        in_specs=[pl.BlockSpec((rows, NZH * TILE), lambda s: (0, s))] + [full(v) for v in (*zparts, *yparts)],
        out_specs=[full(piece)] * NCOL,
        out_shape=[piece] * NCOL,
        scratch_shapes=[pltpu.VMEM((cols, width), BF16), pltpu.VMEM((rows, width), F32)],
        compiler_params=pltpu.CompilerParams(vmem_limit_bytes=48 * MB),
        cost_estimate=pl.CostEstimate(flops=2 * rows * cols * width, bytes_accessed=14 * MB, transcendentals=0),
        name="gather_matmul",
    )(adj, *zparts, *yparts)


def node_kernel(*refs):
    parts = refs[:NCOL]
    base, degf_col, degf_row, w_neigh, cotangent, out, grad, scaled_t = refs[NCOL:]
    total = parts[0][...].astype(F32)
    for part in parts[1:]:
        total = total + part[...].astype(F32)
    mean = (total / degf_col[...]).astype(BF16)
    pre = base[...] + jnp.dot(mean, w_neigh[...], preferred_element_type=F32)
    sig = jax.nn.sigmoid(pre)
    out[...] = (pre * sig).astype(BF16)
    slope = sig * (1.0 + pre * (1.0 - sig))
    grad_pre = (cotangent[...].astype(F32) * slope).astype(BF16)
    grad[...] = grad_pre
    proj_t = lax.dot_general(w_neigh[...], grad_pre, (((1,), (1,)), ((), ())), preferred_element_type=F32)
    scaled_t[...] = (proj_t / degf_row[...]).astype(BF16)


def node_step(parts, base, degf, w_neigh, cotangent):
    rows, width = cotangent.shape
    return pl.pallas_call(
        node_kernel,
        out_shape=[
            jax.ShapeDtypeStruct((rows, width), BF16),
            jax.ShapeDtypeStruct((rows, width), BF16),
            jax.ShapeDtypeStruct((width, rows), BF16),
        ],
        compiler_params=pltpu.CompilerParams(vmem_limit_bytes=32 * MB),
        cost_estimate=pl.CostEstimate(flops=4 * rows * width * width, bytes_accessed=3 * MB, transcendentals=rows * width),
        name="node_step",
    )(*parts, base, degf[:, None], degf[None, :], w_neigh, cotangent)


def spread_matmul_kernel(*refs):
    parts, adj, out = refs[:NCOL], refs[NCOL], refs[NCOL + 1]
    lhs = jnp.concatenate([part[...] for part in parts], axis=1)
    out[...] = jnp.dot(lhs, adj[...], preferred_element_type=F32).astype(BF16)


def spread_matmul(parts, adj, half):
    width = parts[0].shape[0]
    rows = adj.shape[0]
    steps = NY
    full = lambda v: pl.BlockSpec(v.shape, lambda s: (0,) * v.ndim)
    return pl.pallas_call(
        spread_matmul_kernel,
        grid=(steps,),
        in_specs=[full(v) for v in parts] + [pl.BlockSpec((rows, NZH * TILE), lambda s: (0, half * steps + s))],
        out_specs=pl.BlockSpec((width, NZH * TILE), lambda s: (0, s)),
        out_shape=jax.ShapeDtypeStruct((width, steps * NZH * TILE), BF16),
        compiler_params=pltpu.CompilerParams(vmem_limit_bytes=32 * MB),
        cost_estimate=pl.CostEstimate(flops=2 * rows * width * steps * NZH * TILE, bytes_accessed=7 * MB, transcendentals=0),
        name="spread_matmul",
    )(*parts, adj)


def pair_kernel(mine, theirs, *outs):
    total = (mine[...].astype(F32) + theirs[...].astype(F32)).astype(BF16)
    zouts, youts = outs[:NY], outs[NY:]
    for dy in range(NY):
        zouts[dy][...] = total[:SPLIT_RS, dy * NZH * TILE : (dy + 1) * NZH * TILE]
    for dzh in range(NZH):
        for dy in range(NY):
            at = (dy * NZH + dzh) * TILE
            youts[dzh][:, dy * TILE : (dy + 1) * TILE] = total[SPLIT_RS:, at : at + TILE]


def pair_sum(mine, theirs):
    width = mine.shape[0]
    return pl.pallas_call(
        pair_kernel,
        out_shape=[jax.ShapeDtypeStruct((SPLIT_RS, NZH * TILE), BF16)] * NY
        + [jax.ShapeDtypeStruct((width - SPLIT_RS, NY * TILE), BF16)] * NZH,
        compiler_params=pltpu.CompilerParams(vmem_limit_bytes=32 * MB),
        cost_estimate=pl.CostEstimate(flops=width * 2048, bytes_accessed=6 * MB, transcendentals=0),
        name="pair_sum",
    )(mine, theirs)


def add_kernel(*refs):
    total = refs[0][...].astype(F32)
    for ref in refs[1:-4]:
        total = total + ref[...].astype(F32)
    total = total.astype(BF16)
    for i, out in enumerate(refs[-4:]):
        out[...] = total[:, i * TILE : (i + 1) * TILE]


def add_split(values, name):
    rows = values[0].shape[0]
    return pl.pallas_call(
        add_kernel,
        out_shape=[jax.ShapeDtypeStruct((rows, TILE), BF16)] * 4,
        compiler_params=pltpu.CompilerParams(vmem_limit_bytes=32 * MB),
        cost_estimate=pl.CostEstimate(flops=rows * 2048, bytes_accessed=2 * MB, transcendentals=0),
        name=name,
    )(*values)


def last_kernel(*refs):
    zvals, yvals, own, out = refs[:NZH], refs[NZH : NZH + NY], refs[-2], refs[-1]
    upper = zvals[0][...].astype(F32)
    for ref in zvals[1:]:
        upper = upper + ref[...].astype(F32)
    lower = yvals[0][...].astype(F32)
    for ref in yvals[1:]:
        lower = lower + ref[...].astype(F32)
    back = jnp.concatenate([upper, lower], axis=0)
    out[...] = (own[...] + back.T).astype(BF16)


def last_sum(zvals, yvals, own):
    return pl.pallas_call(
        last_kernel,
        out_shape=jax.ShapeDtypeStruct(own.shape, BF16),
        compiler_params=pltpu.CompilerParams(vmem_limit_bytes=32 * MB),
        name="last_sum",
    )(*zvals, *yvals, own)


def body(features, degrees, tile_rows, tile_masks, w_self, w_neigh, bias, cotangent):
    row, col = lax.axis_index("row"), lax.axis_index("col")
    y, zh, core = row // (NZH * NCORE), (row // NCORE) % NZH, row % NCORE
    x, zl = col // NZL, col % NZL

    m = jnp.arange(NCORE * NY * NZH, dtype=jnp.int32)
    order = (((y + m // NZH) % NY) * NZH + (zh + m) % NZH) * NCORE + (core + m // (NY * NZH)) % NCORE
    order = order.astype(jnp.int32)
    rows_here = tile_rows[0, 0]
    rel = ((rows_here // NZL - x) % NX) * NZL + (rows_here - zl) % NZL
    where = rel[order].reshape(-1).astype(jnp.int32)

    top, rest = features[:SPLIT_AG], features[SPLIT_AG:]
    ztop = [top] + [pull(top, dzh=d) for d in (1, 3, 2)]
    ztop = jnp.concatenate([ztop[0], ztop[1], ztop[3], ztop[2]], axis=0)
    yrest = [rest] + [pull(rest, dy=d) for d in (1, 3, 2)]
    yrest = jnp.concatenate([yrest[0], yrest[1], yrest[3], yrest[2]], axis=0)
    zparts = [ztop] + [pull(ztop, dy=d) for d in (1, 2, 3)]
    yparts = [yrest] + [pull(yrest, dzh=d) for d in (1, 2, 3)]
    zparts = zparts + [push(v, dc=1) for v in zparts]
    yparts = yparts + [push(v, dc=1) for v in yparts]

    adj = adjacency(tile_masks[0, 0], order, where)
    parts = gather_matmul(adj, zparts, yparts)

    arrived = [parts[0]]
    for i in range(1, NCOL):
        arrived.append(push(parts[i], dx=i // NZL, dzl=i % NZL))
    degf = degrees.astype(F32)
    base = jnp.dot(features, w_self, preferred_element_type=F32) + bias[None, :]
    output, grad_pre, scaled_t = node_step(arrived, base, degf, w_neigh, cotangent)

    table = [scaled_t] + [pull(scaled_t, dx=i // NZL, dzl=i % NZL) for i in range(1, NCOL)]
    own = lax.dot_general(grad_pre, w_self, (((1,), (1,)), ((), ())), preferred_element_type=F32)
    theirs = push(spread_matmul(table, adj, 1), dc=1)
    mine = spread_matmul(table, adj, 0)
    sums = pair_sum(mine, theirs)
    zsums, ysums = sums[:NY], sums[NY:]
    zgot = [zsums[0]] + [push(zsums[d], dy=d) for d in (1, 3, 2)]
    ygot = [ysums[0]] + [push(ysums[d], dzh=d) for d in (1, 3, 2)]
    zlast = add_split(zgot, "add_z")
    ylast = add_split(ygot, "add_y")
    zend = [zlast[0]] + [push(zlast[d], dzh=d) for d in (1, 3, 2)]
    yend = [ylast[0]] + [push(ylast[d], dy=d) for d in (1, 3, 2)]
    grad_features = last_sum(zend, yend, own)
    return output, grad_features


def solution(mesh):
    both = P(("row", "col"), None)
    return jax.shard_map(
        body,
        mesh=mesh,
        in_specs=(
            both,
            P(("row", "col")),
            P("row", "col", None, None),
            P("row", "col", None, None, None, None),
            P(),
            P(),
            P(),
            both,
        ),
        out_specs=(both, both),
        check_vma=False,
    )
```

time: 336 us -> 179 us (0.53)
  waiting for transfers between devices: 245 us -> 64.6 us
  starting transfers between devices: 0.16 us -> 71.1 us
  other arithmetic: 35.3 us -> 0.11 us
  matrix products: 29.8 us -> 1.43 us
  Pallas kernels: 0 us -> 22.3 us
  between operations: 13.9 us -> 0.99 us
  local copies, waits for them, and re-layouts: 9.36 us -> 18.3 us
    reduce_scatter x2 -> x0, waiting for transfers between devices: 139 us -> none  [the longest x1 99.7 us: body(): lax.psum_scatter(terms.reshape(local_nodes * lax.axis_size('row'), width)...]
    all_gather x2 -> x0, waiting for transfers between devices: 106 us -> none  [the longest x1 63.7 us: body(): piece = lax.all_gather(features, 'row', axis=0, tiled=True)]
    ppermute x0 -> x47, starting transfers between devices: none -> 71.1 us  [push(): return lax.ppermute(value, ('row', 'col'), pairs_to(**ahead))]
    ppermute x0 -> x47, waiting for transfers between devices: none -> 64.6 us  [push(): return lax.ppermute(value, ('row', 'col'), pairs_to(**ahead))]
    scatter-add x1 -> x0, other arithmetic: 34.2 us -> none  [body(): empty.at[which.reshape(-1)].add(prods.reshape(count * slots, tile, width))]
    dot_general x5 -> x1, matrix products: 27.9 us -> 1.14 us  [body(): base = jnp.dot(features, w_self, preferred_element_type=F32) + bias[None, :]]
    pallas_call x0 -> x9, Pallas kernels: none -> 22.3 us  [the longest x1 10.4 us: gather_matmul(): pl.pallas_call(gather_matmul_kernel, grid=(NCORE * NY,), in_specs=[pl.Blo...]
    unnamed x15 -> x38, local copies, waits for them, and re-layouts: 0.81 us -> 15 us
  transfers between devices with their start and end apart: 4 -> 47, of which waited for: 4 -> 16; matrix products, arithmetic and copies ran while one was open for 0% -> 2% of each run, Pallas kernels for 0% -> 4%
where the time goes in v1:
time: 179 us
  starting transfers between devices  71.1 us (40%)
  waiting for transfers between devices  64.6 us (36%)
  Pallas kernels  22.3 us (12%)
  local copies, waits for them, and re-layouts  18.3 us (10%)
    ppermute x47, starting transfers between devices, push(): return lax.ppermute(value, ('row', 'col'), pairs_to(**ahead))  71.1 us
    ppermute x47, waiting for transfers between devices, push(): return lax.ppermute(value, ('row', 'col'), pairs_to(**ahead))  64.6 us
    unnamed x38, local copies, waits for them, and re-layouts  15 us
    pallas_call x1, Pallas kernels, gather_matmul(): pl.pallas_call(gather_matmul_kernel, grid=(NCORE * NY,), in_specs=[pl.Blo...  10.4 us
    pallas_call x2, Pallas kernels, spread_matmul(): pl.pallas_call(spread_matmul_kernel, grid=(steps,), in_specs=[full(v) for...  6.62 us
  transfers between devices with their start and end apart: 47, of which 16 were waited for; matrix products, arithmetic and copies ran while one was open for 2% of the time, Pallas kernels for 4%

profile of v1, /device:TPU:32, one launch (start us, length us, event | category | flops | bytes accessed | tf_op | source)
XLA Modules:
  0.0 178.9 jit_solution(17247222899321109730)
XLA Ops:
  3.1 2.9 %collective-permute-start.11 = (bf16[48,512]{1,0:T(8,128)(2,1)S(1)}, bf16[48,512]{1,0:T(8,128)(2,1)S(1)}, u32[]{:S(2)}, u32[]{:S(2)}) collective-permute-start(bf16[48,512]{1,0:T(8,128)(2,1)S(1)} %slice.7), channel_id=1, source_target_pairs={{0,128},{1,129},{2,130},{3,131},{4,132},{5,133},{6,134},{7,135},{8... | collective-permute-start | bytes 147464 | tf_op jit(solution)/shard_map/ppermute | solution.py:35
  8.2 3.3 %collective-permute-start.2 = (bf16[80,512]{1,0:T(8,128)(2,1)S(1)}, bf16[80,512]{1,0:T(8,128)(2,1)S(1)}, u32[]{:S(2)}, u32[]{:S(2)}) collective-permute-start(bf16[80,512]{1,0:T(8,128)(2,1)S(1)} %slice.6), channel_id=1, source_target_pairs={{0,16},{1,17},{2,18},{3,19},{4,20},{5,21},{6,22},{7,23},{8,24},{9,... | collective-permute-start | bytes 245768 | tf_op jit(solution)/shard_map/ppermute | solution.py:35
  11.5 4.5 %collective-permute-start.1 = (bf16[80,512]{1,0:T(8,128)(2,1)S(1)}, bf16[80,512]{1,0:T(8,128)(2,1)S(1)}, u32[]{:S(2)}, u32[]{:S(2)}) collective-permute-start(bf16[80,512]{1,0:T(8,128)(2,1)S(1)} %slice.6), channel_id=1, source_target_pairs={{0,32},{1,33},{2,34},{3,35},{4,36},{5,37},{6,38},{7,39},{8,40},{9,... | collective-permute-start | bytes 245768 | tf_op jit(solution)/shard_map/ppermute | solution.py:35
  16.0 2.7 %collective-permute-start = (bf16[80,512]{1,0:T(8,128)(2,1)S(1)}, bf16[80,512]{1,0:T(8,128)(2,1)S(1)}, u32[]{:S(2)}, u32[]{:S(2)}) collective-permute-start(bf16[80,512]{1,0:T(8,128)(2,1)S(1)} %slice.6), channel_id=1, source_target_pairs={{0,48},{1,49},{2,50},{3,51},{4,52},{5,53},{6,54},{7,55},{8,56},{9,... | collective-permute-start | bytes 245768 | tf_op jit(solution)/shard_map/ppermute | solution.py:35
  18.8 3.8 %collective-permute-start.14 = (bf16[192,512]{1,0:T(8,128)(2,1)S(1)}, bf16[192,512]{1,0:T(8,128)(2,1)}, u32[]{:S(2)}, u32[]{:S(2)}) collective-permute-start(bf16[192,512]{1,0:T(8,128)(2,1)S(1)} %pad_maximum_fusion.1.refs_8_), channel_id=1, source_target_pairs={{0,32},{1,33},{2,34},{3,35},{4,36},{5,37},{6,38},{7,39},{8,40},{9,... | collective-permute-start | bytes 589832 | tf_op jit(solution)/shard_map/ppermute | solution.py:35
  23.1 6.1 %collective-permute-done.13.refs_9_ = bf16[192,512]{1,0:T(8,128)(2,1)S(1)} collective-permute-done((bf16[192,512]{1,0:T(8,128)(2,1)S(1)}, bf16[192,512]{1,0:T(8,128)(2,1)S(1)}, u32[]{:S(2)}, u32[]{:S(2)}) %collective-permute-start.13) | collective-permute-done | bytes 196640 | tf_op jit(solution)/shard_map/ppermute | solution.py:35
  29.6 12.4 %collective-permute-done.14.refs_10_ = bf16[192,512]{1,0:T(8,128)(2,1)} collective-permute-done((bf16[192,512]{1,0:T(8,128)(2,1)S(1)}, bf16[192,512]{1,0:T(8,128)(2,1)}, u32[]{:S(2)}, u32[]{:S(2)}) %collective-permute-start.14) | collective-permute-done | bytes 196640 | tf_op jit(solution)/shard_map/ppermute | solution.py:35
  45.4 6.7 %collective-permute-done.5.refs_3_ = bf16[320,512]{1,0:T(8,128)(2,1)S(1)} collective-permute-done((bf16[320,512]{1,0:T(8,128)(2,1)S(1)}, bf16[320,512]{1,0:T(8,128)(2,1)S(1)}, u32[]{:S(2)}, u32[]{:S(2)}) %collective-permute-start.5) | collective-permute-done | bytes 327712 | tf_op jit(solution)/shard_map/ppermute | solution.py:35
  54.3 2.8 %copy-done.1 = s32[1,1,32,3,128,128]{5,4,3,2,1,0:T(8,128)S(1)} copy-done((s32[1,1,32,3,128,128]{5,4,3,2,1,0:T(8,128)S(1)}, s32[1,1,32,3,128,128]{5,4,3,2,1,0:T(8,128)}, u32[]{:S(2)}) %copy-start.1) | copy-done | bytes 6291480
  57.1 2.7 %adjacency.1.adj.refs_8_ = bf16[1024,4096]{1,0:T(8,128)(2,1)S(1)} custom-call(s32[32]{0:T(128)S(1)} %fusion.9.order, s32[96]{0:T(128)S(1)} %reshape.198.where, s32[32,3,128,128]{3,2,1,0:T(8,128)S(1)} %bitcast.34, s32[32,3,128,128]{3,2,1,0:T(8,128)S(1)} %bitcast.35, s32[32,3,128,128]{3,2,1,0:T(8,128)S(1)} %bitcast.36, s32[32,3,128,128]{3,2,1,0:T(8,128)S(1)} %bitcast.37), custom_call_target="tpu_custom_call" | custom-call | bytes 14680064 | tf_op jit(solution)/shard_map/adjacency/pallas_call | solution.py:66
  59.8 3.3 %copy-done.2 = bf16[1024,4096]{1,0:T(8,128)(2,1)} copy-done((bf16[1024,4096]{1,0:T(8,128)(2,1)}, bf16[1024,4096]{1,0:T(8,128)(2,1)S(1)}, u32[]{:S(2)}) %copy-start.2) | copy-done | bytes 8388632
  64.1 10.4 %gather_matmul.1 = (bf16[128,512]{1,0:T(8,128)(2,1)S(1)}, bf16[128,512]{1,0:T(8,128)(2,1)}, bf16[128,512]{1,0:T(8,128)(2,1)}, bf16[128,512]{1,0:T(8,128)(2,1)S(1...) custom-call(bf16[1024,4096]{1,0:T(8,128)(2,1)} %copy-done.2, ...), custom_call_target="tpu_custom_call" | custom-call | flops 4294967296 | bytes 14680064 | tf_op jit(solution)/shard_map/gather_matmul/pallas_call | solution.py:115
  77.8 4.6 %collective-permute-start.20 = (bf16[128,512]{1,0:T(8,128)(2,1)}, bf16[128,512]{1,0:T(8,128)(2,1)S(1)}, u32[]{:S(2)}, u32[]{:S(2)}) collective-permute-start(bf16[128,512]{1,0:T(8,128)(2,1)} %get-tuple-element.30), channel_id=1, source_target_pairs={{0,1},{1,0},{2,3},{3,2},{4,5},{5,4},{6,7},{7,6},{8,9},{9,8},{10,11... | collective-permute-start | bytes 393224 | tf_op jit(solution)/shard_map/ppermute | solution.py:35
  86.9 3.1 %collective-permute-start.24 = (bf16[128,512]{1,0:T(8,128)(2,1)}, bf16[128,512]{1,0:T(8,128)(2,1)S(1)}, u32[]{:S(2)}, u32[]{:S(2)}) collective-permute-start(bf16[128,512]{1,0:T(8,128)(2,1)} %copy-done.14), channel_id=1, source_target_pairs={{0,5},{1,4},{2,7},{3,6},{4,1},{5,0},{6,3},{7,2},{8,13},{9,12},{10,... | collective-permute-start | bytes 393224 | tf_op jit(solution)/shard_map/ppermute | solution.py:35
  91.8 3.2 %collective-permute-done.21.refs_2_ = bf16[128,512]{1,0:T(8,128)(2,1)S(1)} collective-permute-done((bf16[128,512]{1,0:T(8,128)(2,1)}, bf16[128,512]{1,0:T(8,128)(2,1)S(1)}, u32[]{:S(2)}, u32[]{:S(2)}) %collective-permute-start.21) | collective-permute-done | bytes 131104 | tf_op jit(solution)/shard_map/ppermute | solution.py:35
  96.1 2.7 %collective-permute-done.23.refs_4_ = bf16[128,512]{1,0:T(8,128)(2,1)S(1)} collective-permute-done((bf16[128,512]{1,0:T(8,128)(2,1)}, bf16[128,512]{1,0:T(8,128)(2,1)S(1)}, u32[]{:S(2)}, u32[]{:S(2)}) %collective-permute-start.23) | collective-permute-done | bytes 131104 | tf_op jit(solution)/shard_map/ppermute | solution.py:35
  102.6 3.0 %collective-permute-start.28 = (bf16[512,128]{1,0:T(8,128)(2,1)S(1)}, bf16[512,128]{1,0:T(8,128)(2,1)S(1)}, u32[]{:S(2)}, u32[]{:S(2)}) collective-permute-start(bf16[512,128]{1,0:T(8,128)(2,1)S(1)} %get-tuple-element.38.refs_0_), channel_id=1, source_target_pairs={{0,6},{1,7},{2,0},{3,1},{4,2},{5,3},{6,4},{7,5},{8,14},{9,15},{10,... | collective-permute-start | bytes 393224 | tf_op jit(solution)/shard_map/ppermute | solution.py:35
  107.6 3.0 %collective-permute-start.31 = (bf16[512,128]{1,0:T(8,128)(2,1)S(1)}, bf16[512,128]{1,0:T(8,128)(2,1)S(1)}, u32[]{:S(2)}, u32[]{:S(2)}) collective-permute-start(bf16[512,128]{1,0:T(8,128)(2,1)S(1)} %get-tuple-element.38.refs_0_), channel_id=1, source_target_pairs={{0,5},{1,4},{2,7},{3,6},{4,1},{5,0},{6,3},{7,2},{8,13},{9,12},{10,... | collective-permute-start | bytes 393224 | tf_op jit(solution)/shard_map/ppermute | solution.py:35
  112.1 4.0 %collective-permute-done.28.refs_2_ = bf16[512,128]{1,0:T(8,128)(2,1)S(1)} collective-permute-done((bf16[512,128]{1,0:T(8,128)(2,1)S(1)}, bf16[512,128]{1,0:T(8,128)(2,1)S(1)}, u32[]{:S(2)}, u32[]{:S(2)}) %collective-permute-start.28) | collective-permute-done | bytes 131104 | tf_op jit(solution)/shard_map/ppermute | solution.py:35
  117.1 2.5 %collective-permute-done.32.refs_6_ = bf16[512,128]{1,0:T(8,128)(2,1)S(1)} collective-permute-done((bf16[512,128]{1,0:T(8,128)(2,1)S(1)}, bf16[512,128]{1,0:T(8,128)(2,1)S(1)}, u32[]{:S(2)}, u32[]{:S(2)}) %collective-permute-start.32) | collective-permute-done | bytes 131104 | tf_op jit(solution)/shard_map/ppermute | solution.py:35
  119.6 3.5 %collective-permute-done.33.refs_7_ = bf16[512,128]{1,0:T(8,128)(2,1)S(1)} collective-permute-done((bf16[512,128]{1,0:T(8,128)(2,1)S(1)}, bf16[512,128]{1,0:T(8,128)(2,1)S(1)}, u32[]{:S(2)}, u32[]{:S(2)}) %collective-permute-start.33) | collective-permute-done | bytes 131104 | tf_op jit(solution)/shard_map/ppermute | solution.py:35
  123.2 3.4 %copy-done.3 = bf16[1024,4096]{1,0:T(8,128)(2,1)S(1)} copy-done((bf16[1024,4096]{1,0:T(8,128)(2,1)S(1)}, bf16[1024,4096]{1,0:T(8,128)(2,1)}, u32[]{:S(2)}) %copy-start.3) | copy-done | bytes 8388632
  126.5 3.3 %spread_matmul.3 = bf16[512,2048]{1,0:T(8,128)(2,1)S(1)} custom-call(bf16[512,128]{1,0:T(8,128)(2,1)S(1)} %get-tuple-element.38.refs_0_, bf16[512,128]{1,0:T(8,128)(2,1)S(1)} %collective-permute-done.27.refs_1_, bf16[512,128]{1,0:T(8,128)(2,1)S(1)} %collective-permute-done.28.refs_2_, bf16[512,128]{1,0:T(8,128)(2,1)S(1)} %collective-permute-done.29.refs_3_, ...), custom_call_target="tpu_custom_call" | custom-call | flops 2147483648 | bytes 7340032 | tf_op jit(solution)/shard_map/spread_matmul/pallas_call | solution.py:171
  130.0 3.3 %spread_matmul.2.mine = bf16[512,2048]{1,0:T(8,128)(2,1)S(1)} custom-call(bf16[512,128]{1,0:T(8,128)(2,1)S(1)} %get-tuple-element.38.refs_0_, bf16[512,128]{1,0:T(8,128)(2,1)S(1)} %collective-permute-done.27.refs_1_, bf16[512,128]{1,0:T(8,128)(2,1)S(1)} %collective-permute-done.28.refs_2_, bf16[512,128]{1,0:T(8,128)(2,1)S(1)} %collective-permute-done.29.refs_3_, ...), custom_call_target="tpu_custom_call" | custom-call | flops 2147483648 | bytes 7340032 | tf_op jit(solution)/shard_map/spread_matmul/pallas_call | solution.py:171
  134.7 3.1 %collective-permute-start.41 = (bf16[160,512]{1,0:T(8,128)(2,1)S(1)}, bf16[160,512]{1,0:T(8,128)(2,1)S(1)}, u32[]{:S(2)}, u32[]{:S(2)}) collective-permute-start(bf16[160,512]{1,0:T(8,128)(2,1)S(1)} %get-tuple-element.48), channel_id=1, source_target_pairs={{0,16},{1,17},{2,18},{3,19},{4,20},{5,21},{6,22},{7,23},{8,24},{9,... | collective-permute-start | bytes 491528 | tf_op jit(solution)/shard_map/ppermute | solution.py:35
  137.8 3.2 %collective-permute-start.36 = (bf16[352,512]{1,0:T(8,128)(2,1)S(1)}, bf16[352,512]{1,0:T(8,128)(2,1)S(1)}, u32[]{:S(2)}, u32[]{:S(2)}) collective-permute-start(bf16[352,512]{1,0:T(8,128)(2,1)S(1)} %get-tuple-element.41), channel_id=1, source_target_pairs={{0,192},{1,193},{2,194},{3,195},{4,196},{5,197},{6,198},{7,199},{8... | collective-permute-start | bytes 1081352 | tf_op jit(solution)/shard_map/ppermute | solution.py:35
  142.1 4.5 %collective-permute-done.41.refs_1_ = bf16[160,512]{1,0:T(8,128)(2,1)S(1)} collective-permute-done((bf16[160,512]{1,0:T(8,128)(2,1)S(1)}, bf16[160,512]{1,0:T(8,128)(2,1)S(1)}, u32[]{:S(2)}, u32[]{:S(2)}) %collective-permute-start.41) | collective-permute-done | bytes 163872 | tf_op jit(solution)/shard_map/ppermute | solution.py:35
  146.6 3.7 %collective-permute-start.43 = (bf16[160,512]{1,0:T(8,128)(2,1)S(1)}, bf16[160,512]{1,0:T(8,128)(2,1)S(1)}, u32[]{:S(2)}, u32[]{:S(2)}) collective-permute-start(bf16[160,512]{1,0:T(8,128)(2,1)S(1)} %get-tuple-element.50), channel_id=1, source_target_pairs={{0,32},{1,33},{2,34},{3,35},{4,36},{5,37},{6,38},{7,39},{8,40},{9,... | collective-permute-start | bytes 491528 | tf_op jit(solution)/shard_map/ppermute | solution.py:35
  150.3 8.8 %collective-permute-done.43.refs_3_ = bf16[160,512]{1,0:T(8,128)(2,1)S(1)} collective-permute-done((bf16[160,512]{1,0:T(8,128)(2,1)S(1)}, bf16[160,512]{1,0:T(8,128)(2,1)S(1)}, u32[]{:S(2)}, u32[]{:S(2)}) %collective-permute-start.43) | collective-permute-done | bytes 163872 | tf_op jit(solution)/shard_map/ppermute | solution.py:35
  165.3 4.1 %collective-permute-start.39 = (bf16[352,128]{1,0:T(8,128)(2,1)S(1)}, bf16[352,128]{1,0:T(8,128)(2,1)S(1)}, u32[]{:S(2)}, u32[]{:S(2)}) collective-permute-start(bf16[352,128]{1,0:T(8,128)(2,1)S(1)} %get-tuple-element.45), channel_id=1, source_target_pairs={{0,48},{1,49},{2,50},{3,51},{4,52},{5,53},{6,54},{7,55},{8,56},{9,... | collective-permute-start | bytes 270344 | tf_op jit(solution)/shard_map/ppermute | solution.py:35
  169.4 2.7 %collective-permute-start.40 = (bf16[352,128]{1,0:T(8,128)(2,1)S(1)}, bf16[352,128]{1,0:T(8,128)(2,1)S(1)}, u32[]{:S(2)}, u32[]{:S(2)}) collective-permute-start(bf16[352,128]{1,0:T(8,128)(2,1)S(1)} %get-tuple-element.46), channel_id=1, source_target_pairs={{0,32},{1,33},{2,34},{3,35},{4,36},{5,37},{6,38},{7,39},{8,40},{9,... | collective-permute-start | bytes 270344 | tf_op jit(solution)/shard_map/ppermute | solution.py:35
  174.6 3.5 %collective-permute-done.40.refs_3_ = bf16[352,128]{1,0:T(8,128)(2,1)S(1)} collective-permute-done((bf16[352,128]{1,0:T(8,128)(2,1)S(1)}, bf16[352,128]{1,0:T(8,128)(2,1)S(1)}, u32[]{:S(2)}, u32[]{:S(2)}) %collective-permute-start.40) | collective-permute-done | bytes 90144 | tf_op jit(solution)/shard_map/ppermute | solution.py:35
  (124 shorter events, 43.1 us)
Async XLA Ops:
  1.5 14.5 %collective-permute-start.12 = (bf16[48,512]{1,0:T(8,128)(2,1)S(1)}, bf16[48,512]{1,0:T(8,128)(2,1)S(1)}, u32[]{:S(2)}, u32[]{:S(2)}) collective-permute-start(bf16[48,512]{1,0:T(8,128)(2,1)S(1)} %slice.7), channel_id=1, source_target_pairs={{0,64},{1,65},{2,66},{3,67},{4,68},{5,69},{6,70},{7,71},{8,72},{9,... | collective-permute-start | bytes 147464 | tf_op jit(solution)/shard_map/ppermute | solution.py:35
  3.1 15.6 %collective-permute-start.11 = (bf16[48,512]{1,0:T(8,128)(2,1)S(1)}, bf16[48,512]{1,0:T(8,128)(2,1)S(1)}, u32[]{:S(2)}, u32[]{:S(2)}) collective-permute-start(bf16[48,512]{1,0:T(8,128)(2,1)S(1)} %slice.7), channel_id=1, source_target_pairs={{0,128},{1,129},{2,130},{3,131},{4,132},{5,133},{6,134},{7,135},{8... | collective-permute-start | bytes 147464 | tf_op jit(solution)/shard_map/ppermute | solution.py:35
  6.0 12.7 %collective-permute-start.10 = (bf16[48,512]{1,0:T(8,128)(2,1)S(1)}, bf16[48,512]{1,0:T(8,128)(2,1)S(1)}, u32[]{:S(2)}, u32[]{:S(2)}) collective-permute-start(bf16[48,512]{1,0:T(8,128)(2,1)S(1)} %slice.7), channel_id=1, source_target_pairs={{0,192},{1,193},{2,194},{3,195},{4,196},{5,197},{6,198},{7,199},{8... | collective-permute-start | bytes 147464 | tf_op jit(solution)/shard_map/ppermute | solution.py:35
  8.2 14.4 %collective-permute-start.2 = (bf16[80,512]{1,0:T(8,128)(2,1)S(1)}, bf16[80,512]{1,0:T(8,128)(2,1)S(1)}, u32[]{:S(2)}, u32[]{:S(2)}) collective-permute-start(bf16[80,512]{1,0:T(8,128)(2,1)S(1)} %slice.6), channel_id=1, source_target_pairs={{0,16},{1,17},{2,18},{3,19},{4,20},{5,21},{6,22},{7,23},{8,24},{9,... | collective-permute-start | bytes 245768 | tf_op jit(solution)/shard_map/ppermute | solution.py:35
  11.5 11.2 %collective-permute-start.1 = (bf16[80,512]{1,0:T(8,128)(2,1)S(1)}, bf16[80,512]{1,0:T(8,128)(2,1)S(1)}, u32[]{:S(2)}, u32[]{:S(2)}) collective-permute-start(bf16[80,512]{1,0:T(8,128)(2,1)S(1)} %slice.6), channel_id=1, source_target_pairs={{0,32},{1,33},{2,34},{3,35},{4,36},{5,37},{6,38},{7,39},{8,40},{9,... | collective-permute-start | bytes 245768 | tf_op jit(solution)/shard_map/ppermute | solution.py:35
  18.7 10.5 %collective-permute-start.13 = (bf16[192,512]{1,0:T(8,128)(2,1)S(1)}, bf16[192,512]{1,0:T(8,128)(2,1)S(1)}, u32[]{:S(2)}, u32[]{:S(2)}) collective-permute-start(bf16[192,512]{1,0:T(8,128)(2,1)S(1)} %pad_maximum_fusion.1.refs_8_), channel_id=1, source_target_pairs={{0,48},{1,49},{2,50},{3,51},{4,52},{5,53},{6,54},{7,55},{8,56},{9,... | collective-permute-start | bytes 589832 | tf_op jit(solution)/shard_map/ppermute | solution.py:35
  18.8 23.3 %collective-permute-start.14 = (bf16[192,512]{1,0:T(8,128)(2,1)S(1)}, bf16[192,512]{1,0:T(8,128)(2,1)}, u32[]{:S(2)}, u32[]{:S(2)}) collective-permute-start(bf16[192,512]{1,0:T(8,128)(2,1)S(1)} %pad_maximum_fusion.1.refs_8_), channel_id=1, source_target_pairs={{0,32},{1,33},{2,34},{3,35},{4,36},{5,37},{6,38},{7,39},{8,40},{9,... | collective-permute-start | bytes 589832 | tf_op jit(solution)/shard_map/ppermute | solution.py:35
  22.6 20.9 %collective-permute-start.15 = (bf16[192,512]{1,0:T(8,128)(2,1)S(1)}, bf16[192,512]{1,0:T(8,128)(2,1)}, u32[]{:S(2)}, u32[]{:S(2)}) collective-permute-start(bf16[192,512]{1,0:T(8,128)(2,1)S(1)} %pad_maximum_fusion.1.refs_8_), channel_id=1, source_target_pairs={{0,16},{1,17},{2,18},{3,19},{4,20},{5,21},{6,22},{7,23},{8,24},{9,... | collective-permute-start | bytes 589832 | tf_op jit(solution)/shard_map/ppermute | solution.py:35
  22.7 20.8 %collective-permute-start.16 = (bf16[192,512]{1,0:T(8,128)(2,1)S(1)}, bf16[192,512]{1,0:T(8,128)(2,1)S(1)}, u32[]{:S(2)}, u32[]{:S(2)}) collective-permute-start(bf16[192,512]{1,0:T(8,128)(2,1)S(1)} %pad_maximum_fusion.1.refs_8_), channel_id=1, source_target_pairs={{0,8},{1,9},{2,10},{3,11},{4,12},{5,13},{6,14},{7,15},{8,0},{9,1},... | collective-permute-start | bytes 589832 | tf_op jit(solution)/shard_map/ppermute | solution.py:35
  23.0 21.8 %collective-permute-start.3 = (bf16[320,512]{1,0:T(8,128)(2,1)S(1)}, bf16[320,512]{1,0:T(8,128)(2,1)S(1)}, u32[]{:S(2)}, u32[]{:S(2)}) collective-permute-start(bf16[320,512]{1,0:T(8,128)(2,1)S(1)} %pad_maximum_fusion.refs_0_), channel_id=1, source_target_pairs={{0,192},{1,193},{2,194},{3,195},{4,196},{5,197},{6,198},{7,199},{8... | collective-permute-start | bytes 983048 | tf_op jit(solution)/shard_map/ppermute | solution.py:35
  29.2 15.7 %collective-permute-start.4 = (bf16[320,512]{1,0:T(8,128)(2,1)S(1)}, bf16[320,512]{1,0:T(8,128)(2,1)S(1)}, u32[]{:S(2)}, u32[]{:S(2)}) collective-permute-start(bf16[320,512]{1,0:T(8,128)(2,1)S(1)} %pad_maximum_fusion.refs_0_), channel_id=1, source_target_pairs={{0,128},{1,129},{2,130},{3,131},{4,132},{5,133},{6,134},{7,135},{8... | collective-permute-start | bytes 983048 | tf_op jit(solution)/shard_map/ppermute | solution.py:35
  42.0 10.0 %collective-permute-start.5 = (bf16[320,512]{1,0:T(8,128)(2,1)S(1)}, bf16[320,512]{1,0:T(8,128)(2,1)S(1)}, u32[]{:S(2)}, u32[]{:S(2)}) collective-permute-start(bf16[320,512]{1,0:T(8,128)(2,1)S(1)} %pad_maximum_fusion.refs_0_), channel_id=1, source_target_pairs={{0,64},{1,65},{2,66},{3,67},{4,68},{5,69},{6,70},{7,71},{8,72},{9,... | collective-permute-start | bytes 983048 | tf_op jit(solution)/shard_map/ppermute | solution.py:35
  44.8 18.3 %collective-permute-start.7 = (bf16[320,512]{1,0:T(8,128)(2,1)S(1)}, bf16[320,512]{1,0:T(8,128)(2,1)S(1)}, u32[]{:S(2)}, u32[]{:S(2)}) collective-permute-start(bf16[320,512]{1,0:T(8,128)(2,1)S(1)} %collective-permute-done.3.refs_1_), channel_id=1, source_target_pairs={{0,8},{1,9},{2,10},{3,11},{4,12},{5,13},{6,14},{7,15},{8,0},{9,1},... | collective-permute-start | bytes 983048 | tf_op jit(solution)/shard_map/ppermute | solution.py:35
  44.9 18.2 %collective-permute-start.8 = (bf16[320,512]{1,0:T(8,128)(2,1)S(1)}, bf16[320,512]{1,0:T(8,128)(2,1)}, u32[]{:S(2)}, u32[]{:S(2)}) collective-permute-start(bf16[320,512]{1,0:T(8,128)(2,1)S(1)} %collective-permute-done.4.refs_2_), channel_id=1, source_target_pairs={{0,8},{1,9},{2,10},{3,11},{4,12},{5,13},{6,14},{7,15},{8,0},{9,1},... | collective-permute-start | bytes 983048 | tf_op jit(solution)/shard_map/ppermute | solution.py:35
  52.1 11.1 %collective-permute-start.9 = (bf16[320,512]{1,0:T(8,128)(2,1)S(1)}, bf16[320,512]{1,0:T(8,128)(2,1)}, u32[]{:S(2)}, u32[]{:S(2)}) collective-permute-start(bf16[320,512]{1,0:T(8,128)(2,1)S(1)} %collective-permute-done.5.refs_3_), channel_id=1, source_target_pairs={{0,8},{1,9},{2,10},{3,11},{4,12},{5,13},{6,14},{7,15},{8,0},{9,1},... | collective-permute-start | bytes 983048 | tf_op jit(solution)/shard_map/ppermute | solution.py:35
  52.1 11.0 %collective-permute-start.18 = (bf16[192,512]{1,0:T(8,128)(2,1)}, bf16[192,512]{1,0:T(8,128)(2,1)}, u32[]{:S(2)}, u32[]{:S(2)}) collective-permute-start(bf16[192,512]{1,0:T(8,128)(2,1)} %collective-permute-done.14.refs_10_), channel_id=1, source_target_pairs={{0,8},{1,9},{2,10},{3,11},{4,12},{5,13},{6,14},{7,15},{8,0},{9,1},... | collective-permute-start | bytes 589832 | tf_op jit(solution)/shard_map/ppermute | solution.py:35
  77.8 12.2 %collective-permute-start.20 = (bf16[128,512]{1,0:T(8,128)(2,1)}, bf16[128,512]{1,0:T(8,128)(2,1)S(1)}, u32[]{:S(2)}, u32[]{:S(2)}) collective-permute-start(bf16[128,512]{1,0:T(8,128)(2,1)} %get-tuple-element.30), channel_id=1, source_target_pairs={{0,1},{1,0},{2,3},{3,2},{4,5},{5,4},{6,7},{7,6},{8,9},{9,8},{10,11... | collective-permute-start | bytes 393224 | tf_op jit(solution)/shard_map/ppermute | solution.py:35
  82.4 12.6 %collective-permute-start.21 = (bf16[128,512]{1,0:T(8,128)(2,1)}, bf16[128,512]{1,0:T(8,128)(2,1)S(1)}, u32[]{:S(2)}, u32[]{:S(2)}) collective-permute-start(bf16[128,512]{1,0:T(8,128)(2,1)} %get-tuple-element.31), channel_id=1, source_target_pairs={{0,2},{1,3},{2,4},{3,5},{4,6},{5,7},{6,0},{7,1},{8,10},{9,11},{10,... | collective-permute-start | bytes 393224 | tf_op jit(solution)/shard_map/ppermute | solution.py:35
  84.0 12.1 %collective-permute-start.22 = (bf16[128,512]{1,0:T(8,128)(2,1)}, bf16[128,512]{1,0:T(8,128)(2,1)S(1)}, u32[]{:S(2)}, u32[]{:S(2)}) collective-permute-start(bf16[128,512]{1,0:T(8,128)(2,1)} %copy-done.16), channel_id=1, source_target_pairs={{0,3},{1,2},{2,5},{3,4},{4,7},{5,6},{6,1},{7,0},{8,11},{9,10},{10,... | collective-permute-start | bytes 393224 | tf_op jit(solution)/shard_map/ppermute | solution.py:35
  85.0 13.8 %collective-permute-start.23 = (bf16[128,512]{1,0:T(8,128)(2,1)}, bf16[128,512]{1,0:T(8,128)(2,1)S(1)}, u32[]{:S(2)}, u32[]{:S(2)}) collective-permute-start(bf16[128,512]{1,0:T(8,128)(2,1)} %copy-done.15), channel_id=1, source_target_pairs={{0,4},{1,5},{2,6},{3,7},{4,0},{5,1},{6,2},{7,3},{8,12},{9,13},{10,... | collective-permute-start | bytes 393224 | tf_op jit(solution)/shard_map/ppermute | solution.py:35
  86.9 11.9 %collective-permute-start.24 = (bf16[128,512]{1,0:T(8,128)(2,1)}, bf16[128,512]{1,0:T(8,128)(2,1)S(1)}, u32[]{:S(2)}, u32[]{:S(2)}) collective-permute-start(bf16[128,512]{1,0:T(8,128)(2,1)} %copy-done.14), channel_id=1, source_target_pairs={{0,5},{1,4},{2,7},{3,6},{4,1},{5,0},{6,3},{7,2},{8,13},{9,12},{10,... | collective-permute-start | bytes 393224 | tf_op jit(solution)/shard_map/ppermute | solution.py:35
  102.6 13.4 %collective-permute-start.28 = (bf16[512,128]{1,0:T(8,128)(2,1)S(1)}, bf16[512,128]{1,0:T(8,128)(2,1)S(1)}, u32[]{:S(2)}, u32[]{:S(2)}) collective-permute-start(bf16[512,128]{1,0:T(8,128)(2,1)S(1)} %get-tuple-element.38.refs_0_), channel_id=1, source_target_pairs={{0,6},{1,7},{2,0},{3,1},{4,2},{5,3},{6,4},{7,5},{8,14},{9,15},{10,... | collective-permute-start | bytes 393224 | tf_op jit(solution)/shard_map/ppermute | solution.py:35
  105.6 10.5 %collective-permute-start.29 = (bf16[512,128]{1,0:T(8,128)(2,1)S(1)}, bf16[512,128]{1,0:T(8,128)(2,1)S(1)}, u32[]{:S(2)}, u32[]{:S(2)}) collective-permute-start(bf16[512,128]{1,0:T(8,128)(2,1)S(1)} %get-tuple-element.38.refs_0_), channel_id=1, source_target_pairs={{0,7},{1,6},{2,1},{3,0},{4,3},{5,2},{6,5},{7,4},{8,15},{9,14},{10,... | collective-permute-start | bytes 393224 | tf_op jit(solution)/shard_map/ppermute | solution.py:35
  107.1 10.0 %collective-permute-start.30 = (bf16[512,128]{1,0:T(8,128)(2,1)S(1)}, bf16[512,128]{1,0:T(8,128)(2,1)S(1)}, u32[]{:S(2)}, u32[]{:S(2)}) collective-permute-start(bf16[512,128]{1,0:T(8,128)(2,1)S(1)} %get-tuple-element.38.refs_0_), channel_id=1, source_target_pairs={{0,4},{1,5},{2,6},{3,7},{4,0},{5,1},{6,2},{7,3},{8,12},{9,13},{10,... | collective-permute-start | bytes 393224 | tf_op jit(solution)/shard_map/ppermute | solution.py:35
  134.7 11.9 %collective-permute-start.41 = (bf16[160,512]{1,0:T(8,128)(2,1)S(1)}, bf16[160,512]{1,0:T(8,128)(2,1)S(1)}, u32[]{:S(2)}, u32[]{:S(2)}) collective-permute-start(bf16[160,512]{1,0:T(8,128)(2,1)S(1)} %get-tuple-element.48), channel_id=1, source_target_pairs={{0,16},{1,17},{2,18},{3,19},{4,20},{5,21},{6,22},{7,23},{8,24},{9,... | collective-permute-start | bytes 491528 | tf_op jit(solution)/shard_map/ppermute | solution.py:35
  137.8 24.8 %collective-permute-start.35 = (bf16[352,512]{1,0:T(8,128)(2,1)S(1)}, bf16[352,512]{1,0:T(8,128)(2,1)S(1)}, u32[]{:S(2)}, u32[]{:S(2)}) collective-permute-start(bf16[352,512]{1,0:T(8,128)(2,1)S(1)} %get-tuple-element.40), channel_id=1, source_target_pairs={{0,64},{1,65},{2,66},{3,67},{4,68},{5,69},{6,70},{7,71},{8,72},{9,... | collective-permute-start | bytes 1081352 | tf_op jit(solution)/shard_map/ppermute | solution.py:35
  137.8 27.2 %collective-permute-start.36 = (bf16[352,512]{1,0:T(8,128)(2,1)S(1)}, bf16[352,512]{1,0:T(8,128)(2,1)S(1)}, u32[]{:S(2)}, u32[]{:S(2)}) collective-permute-start(bf16[352,512]{1,0:T(8,128)(2,1)S(1)} %get-tuple-element.41), channel_id=1, source_target_pairs={{0,192},{1,193},{2,194},{3,195},{4,196},{5,197},{6,198},{7,199},{8... | collective-permute-start | bytes 1081352 | tf_op jit(solution)/shard_map/ppermute | solution.py:35
  141.0 24.0 %collective-permute-start.37 = (bf16[352,512]{1,0:T(8,128)(2,1)S(1)}, bf16[352,512]{1,0:T(8,128)(2,1)S(1)}, u32[]{:S(2)}, u32[]{:S(2)}) collective-permute-start(bf16[352,512]{1,0:T(8,128)(2,1)S(1)} %get-tuple-element.42), channel_id=1, source_target_pairs={{0,128},{1,129},{2,130},{3,131},{4,132},{5,133},{6,134},{7,135},{8... | collective-permute-start | bytes 1081352 | tf_op jit(solution)/shard_map/ppermute | solution.py:35
  146.6 12.5 %collective-permute-start.43 = (bf16[160,512]{1,0:T(8,128)(2,1)S(1)}, bf16[160,512]{1,0:T(8,128)(2,1)S(1)}, u32[]{:S(2)}, u32[]{:S(2)}) collective-permute-start(bf16[160,512]{1,0:T(8,128)(2,1)S(1)} %get-tuple-element.50), channel_id=1, source_target_pairs={{0,32},{1,33},{2,34},{3,35},{4,36},{5,37},{6,38},{7,39},{8,40},{9,... | collective-permute-start | bytes 491528 | tf_op jit(solution)/shard_map/ppermute | solution.py:35
  159.2 10.2 %collective-permute-start.44 = (bf16[160,128]{1,0:T(8,128)(2,1)S(1)}, bf16[160,128]{1,0:T(8,128)(2,1)S(1)}, u32[]{:S(2)}, u32[]{:S(2)}) collective-permute-start(bf16[160,128]{1,0:T(8,128)(2,1)S(1)} %get-tuple-element.52), channel_id=1, source_target_pairs={{0,64},{1,65},{2,66},{3,67},{4,68},{5,69},{6,70},{7,71},{8,72},{9,... | collective-permute-start | bytes 122888 | tf_op jit(solution)/shard_map/ppermute | solution.py:35
  160.5 11.9 %collective-permute-start.45 = (bf16[160,128]{1,0:T(8,128)(2,1)S(1)}, bf16[160,128]{1,0:T(8,128)(2,1)S(1)}, u32[]{:S(2)}, u32[]{:S(2)}) collective-permute-start(bf16[160,128]{1,0:T(8,128)(2,1)S(1)} %get-tuple-element.53), channel_id=1, source_target_pairs={{0,192},{1,193},{2,194},{3,195},{4,196},{5,197},{6,198},{7,199},{8... | collective-permute-start | bytes 122888 | tf_op jit(solution)/shard_map/ppermute | solution.py:35
  162.5 9.9 %collective-permute-start.46 = (bf16[160,128]{1,0:T(8,128)(2,1)S(1)}, bf16[160,128]{1,0:T(8,128)(2,1)S(1)}, u32[]{:S(2)}, u32[]{:S(2)}) collective-permute-start(bf16[160,128]{1,0:T(8,128)(2,1)S(1)} %get-tuple-element.54), channel_id=1, source_target_pairs={{0,128},{1,129},{2,130},{3,131},{4,132},{5,133},{6,134},{7,135},{8... | collective-permute-start | bytes 122888 | tf_op jit(solution)/shard_map/ppermute | solution.py:35
  (34 other events, 411.0 us)

commit v2 on v0

v2 whole, which is shorter than its diff:
```python
import functools

import jax
import jax.numpy as jnp
from jax import lax
from jax.experimental import pallas as pl
from jax.experimental.pallas import tpu as pltpu
from jax.sharding import PartitionSpec as P

NY, NZH, NCORE, NX, NZL = 4, 4, 2, 4, 2
NROW, NCOL = NY * NZH * NCORE, NX * NZL
CHIPS = NY * NZH
TILE = 128
BF16 = jnp.bfloat16
F32 = jnp.float32
MB = 1024 * 1024


def device(y, zh, c, col):
    return ((y * NZH + zh) * NCORE + c) * NCOL + col


def groups_along(axis):
    out = []
    for c in range(NCORE):
        if axis == "y":
            for zh in range(NZH):
                out.append([(y * NZH + zh) * NCORE + c for y in range(NY)])
        else:
            for y in range(NY):
                out.append([(y * NZH + zh) * NCORE + c for zh in range(NZH)])
    return out


def exchange(value, axis):
    return lax.all_to_all(value, "row", 0, 0, axis_index_groups=groups_along(axis), tiled=True)


def swap(value):
    pairs = [
        (device(y, zh, c, col), device(y, zh, 1 - c, col))
        for y in range(NY)
        for zh in range(NZH)
        for c in range(NCORE)
        for col in range(NCOL)
    ]
    return lax.ppermute(value, ("row", "col"), pairs)


def adjacency_kernel(order, where, *refs):
    masks, out = refs[:-1], refs[-1]
    step = pl.program_id(0)
    out[...] = jnp.zeros_like(out)
    slots = masks[0].shape[1]
    for i, mask in enumerate(masks):
        j = order[step * len(masks) + i]
        for k in range(slots):
            q = where[j * slots + k]
            at = pl.ds(pl.multiple_of(q * TILE, TILE), TILE)
            cols = slice(i * TILE, (i + 1) * TILE)
            out[at, cols] = out[at, cols] + mask[0, k].astype(F32).astype(BF16)


def adjacency(masks, order, where):
    count, slots = masks.shape[0], masks.shape[1]
    group = 4
    specs = [
        pl.BlockSpec(
            (1, slots, TILE, TILE),
            functools.partial(lambda i, s, order, where: (order[s * group + i], 0, 0, 0), i),
        )
        for i in range(group)
    ]
    return pl.pallas_call(
        adjacency_kernel,
        grid_spec=pltpu.PrefetchScalarGridSpec(
            num_scalar_prefetch=2,
            grid=(count // group,),
            in_specs=specs,
            out_specs=pl.BlockSpec((NCOL * TILE, group * TILE), lambda s, order, where: (0, s)),
        ),
        out_shape=jax.ShapeDtypeStruct((NCOL * TILE, count * TILE), BF16),
        compiler_params=pltpu.CompilerParams(vmem_limit_bytes=32 * MB),
        cost_estimate=pl.CostEstimate(flops=0, bytes_accessed=14 * MB, transcendentals=0),
        name="adjacency",
    )(order, where, *([masks] * group))


def first_half_kernel(adj, x, out):
    @pl.when(pl.program_id(0) == 0)
    def _():
        out[...] = jnp.zeros_like(out)

    out[...] += jnp.dot(adj[...], x[...], preferred_element_type=F32)


def first_half(adj, x):
    rows, width = adj.shape[0], x.shape[1]
    depth = NZH * TILE
    return pl.pallas_call(
        first_half_kernel,
        grid=(x.shape[0] // depth,),
        in_specs=[
            pl.BlockSpec((rows, depth), lambda s: (0, s)),
            pl.BlockSpec((depth, width), lambda s: (s, 0)),
        ],
        out_specs=pl.BlockSpec((rows, width), lambda s: (0, 0)),
        out_shape=jax.ShapeDtypeStruct((rows, width), F32),
        compiler_params=pltpu.CompilerParams(vmem_limit_bytes=32 * MB),
        cost_estimate=pl.CostEstimate(flops=2 * rows * x.shape[0] * width, bytes_accessed=8 * MB, transcendentals=0),
        name="first_half",
    )(adj, x)


def second_half_kernel(adj, x, start, out, acc):
    @pl.when(pl.program_id(0) == 0)
    def _():
        acc[...] = start[...]

    acc[...] += jnp.dot(adj[...], x[...], preferred_element_type=F32)

    @pl.when(pl.program_id(0) == pl.num_programs(0) - 1)
    def _():
        out[...] = acc[...].astype(BF16)


def second_half(adj, x, start):
    rows, width = adj.shape[0], x.shape[1]
    depth = NZH * TILE
    return pl.pallas_call(
        second_half_kernel,
        grid=(x.shape[0] // depth,),
        in_specs=[
            pl.BlockSpec((rows, depth), lambda s: (0, NY + s)),
            pl.BlockSpec((depth, width), lambda s: (s, 0)),
            pl.BlockSpec((rows, width), lambda s: (0, 0)),
        ],
        out_specs=pl.BlockSpec((rows, width), lambda s: (0, 0)),
        out_shape=jax.ShapeDtypeStruct((rows, width), BF16),
        scratch_shapes=[pltpu.VMEM((rows, width), F32)],
        compiler_params=pltpu.CompilerParams(vmem_limit_bytes=32 * MB),
        cost_estimate=pl.CostEstimate(flops=2 * rows * x.shape[0] * width, bytes_accessed=9 * MB, transcendentals=0),
        name="second_half",
    )(adj, x, start)


def node_kernel(parts, base, degf_col, degf_row, w_neigh, cotangent, out, grad, scaled_t):
    total = parts[0:TILE, :].astype(F32)
    for i in range(1, NCOL):
        total = total + parts[i * TILE : (i + 1) * TILE, :].astype(F32)
    mean = (total / degf_col[...]).astype(BF16)
    pre = base[...] + jnp.dot(mean, w_neigh[...], preferred_element_type=F32)
    sig = jax.nn.sigmoid(pre)
    out[...] = (pre * sig).astype(BF16)
    slope = sig * (1.0 + pre * (1.0 - sig))
    grad_pre = (cotangent[...].astype(F32) * slope).astype(BF16)
    grad[...] = grad_pre
    proj_t = lax.dot_general(w_neigh[...], grad_pre, (((1,), (1,)), ((), ())), preferred_element_type=F32)
    scaled = (proj_t / degf_row[...]).astype(BF16)
    for i in range(NCOL):
        scaled_t[i, :, :] = scaled


def node_step(parts, base, degf, w_neigh, cotangent):
    rows, width = cotangent.shape
    return pl.pallas_call(
        node_kernel,
        out_shape=[
            jax.ShapeDtypeStruct((rows, width), BF16),
            jax.ShapeDtypeStruct((rows, width), BF16),
            jax.ShapeDtypeStruct((NCOL, width, rows), BF16),
        ],
        compiler_params=pltpu.CompilerParams(vmem_limit_bytes=32 * MB),
        cost_estimate=pl.CostEstimate(flops=4 * rows * width * width, bytes_accessed=4 * MB, transcendentals=rows * width),
        name="node_step",
    )(parts, base, degf[:, None], degf[None, :], w_neigh, cotangent)


def spread_matmul_kernel(parts, adj, out):
    lhs = jnp.concatenate([parts[i] for i in range(NCOL)], axis=1)
    out[0] = jnp.dot(lhs, adj[...], preferred_element_type=F32).astype(BF16)


def spread_matmul(parts, adj, half):
    width = parts.shape[1]
    rows = adj.shape[0]
    return pl.pallas_call(
        spread_matmul_kernel,
        grid=(NY,),
        in_specs=[
            pl.BlockSpec(parts.shape, lambda s: (0, 0, 0)),
            pl.BlockSpec((rows, NZH * TILE), lambda s: (0, half * NY + s)),
        ],
        out_specs=pl.BlockSpec((1, width, NZH * TILE), lambda s: (s, 0, 0)),
        out_shape=jax.ShapeDtypeStruct((NY, width, NZH * TILE), BF16),
        compiler_params=pltpu.CompilerParams(vmem_limit_bytes=32 * MB),
        cost_estimate=pl.CostEstimate(flops=2 * rows * width * CHIPS * TILE, bytes_accessed=7 * MB, transcendentals=0),
        name="spread_matmul",
    )(parts, adj)


def pair_kernel(mine, theirs, out):
    out[...] = (mine[...].astype(F32) + theirs[...].astype(F32)).astype(BF16)


def pair_sum(mine, theirs):
    spec = pl.BlockSpec((1, *mine.shape[1:]), lambda s: (s, 0, 0))
    return pl.pallas_call(
        pair_kernel,
        grid=(mine.shape[0],),
        in_specs=[spec, spec],
        out_specs=spec,
        out_shape=jax.ShapeDtypeStruct(mine.shape, BF16),
        compiler_params=pltpu.CompilerParams(vmem_limit_bytes=32 * MB),
        cost_estimate=pl.CostEstimate(flops=MB, bytes_accessed=6 * MB, transcendentals=0),
        name="pair_sum",
    )(mine, theirs)


def add_kernel(parts, out):
    total = parts[0].astype(F32)
    for i in range(1, parts.shape[0]):
        total = total + parts[i].astype(F32)
    total = total.astype(BF16)
    for i in range(NZH):
        out[i, :, :] = total[:, i * TILE : (i + 1) * TILE]


def add_split(parts):
    width = parts.shape[1]
    return pl.pallas_call(
        add_kernel,
        out_shape=jax.ShapeDtypeStruct((NZH, width, TILE), BF16),
        compiler_params=pltpu.CompilerParams(vmem_limit_bytes=32 * MB),
        cost_estimate=pl.CostEstimate(flops=MB, bytes_accessed=3 * MB, transcendentals=0),
        name="add_split",
    )(parts)


def last_kernel(parts, own, out):
    back = parts[0].astype(F32)
    for i in range(1, parts.shape[0]):
        back = back + parts[i].astype(F32)
    out[...] = (own[...] + back.T).astype(BF16)


def last_sum(parts, own):
    return pl.pallas_call(
        last_kernel,
        out_shape=jax.ShapeDtypeStruct(own.shape, BF16),
        compiler_params=pltpu.CompilerParams(vmem_limit_bytes=32 * MB),
        name="last_sum",
    )(parts, own)


def repeat(value, times):
    return jnp.broadcast_to(value[None], (times, *value.shape))


def body(features, degrees, tile_rows, tile_masks, w_self, w_neigh, bias, cotangent):
    width = features.shape[1]
    core = lax.axis_index("row") % NCORE

    m = jnp.arange(NROW, dtype=jnp.int32)
    order = (m % CHIPS) * NCORE + jnp.where(m < CHIPS, core, 1 - core).astype(jnp.int32)
    adj = adjacency(tile_masks[0, 0], order, tile_rows[0, 0].reshape(-1))

    near = exchange(repeat(features, NZH), "z").reshape(NZH * TILE, width)
    mine = exchange(repeat(near, NY), "y").reshape(CHIPS * TILE, width)
    theirs = swap(mine)
    summed = second_half(adj, theirs, first_half(adj, mine))

    arrived = lax.all_to_all(summed, "col", 0, 0, tiled=True)
    degf = degrees.astype(F32)
    base = jnp.dot(features, w_self, preferred_element_type=F32) + bias[None, :]
    output, grad_pre, scaled_t = node_step(arrived, base, degf, w_neigh, cotangent)

    table = lax.all_to_all(scaled_t, "col", 0, 0, tiled=True)
    own = lax.dot_general(grad_pre, w_self, (((1,), (1,)), ((), ())), preferred_element_type=F32)
    theirs = swap(spread_matmul(table, adj, 1))
    mine = spread_matmul(table, adj, 0)
    sums = add_split(exchange(pair_sum(mine, theirs), "y"))
    grad_features = last_sum(exchange(sums, "z"), own)
    return output, grad_features


def solution(mesh):
    both = P(("row", "col"), None)
    return jax.shard_map(
        body,
        mesh=mesh,
        in_specs=(
            both,
            P(("row", "col")),
            P("row", "col", None, None),
            P("row", "col", None, None, None, None),
            P(),
            P(),
            P(),
            both,
        ),
        out_specs=(both, both),
        check_vma=False,
    )
```

time: 336 us -> 172 us (0.51)
  waiting for transfers between devices: 245 us -> 30.3 us
  blocking collectives: 0 us -> 101 us
  other arithmetic: 35.3 us -> 0.01 us
  matrix products: 29.8 us -> 0.53 us
  Pallas kernels: 0 us -> 21.6 us
  between operations: 13.9 us -> 0.82 us
  starting transfers between devices: 0.16 us -> 9.45 us
    reduce_scatter x2 -> x0, waiting for transfers between devices: 139 us -> none  [the longest x1 99.7 us: body(): lax.psum_scatter(terms.reshape(local_nodes * lax.axis_size('row'), width)...]
    all_gather x2 -> x0, waiting for transfers between devices: 106 us -> none  [the longest x1 63.7 us: body(): piece = lax.all_gather(features, 'row', axis=0, tiled=True)]
    all_to_all x0 -> x4, blocking collectives: none -> 101 us  [the longest x3 82.3 us: exchange(): lax.all_to_all(value, 'row', 0, 0, axis_index_groups=groups_along(axis),...]
    scatter-add x1 -> x0, other arithmetic: 34.2 us -> none  [body(): empty.at[which.reshape(-1)].add(prods.reshape(count * slots, tile, width))]
    all_to_all x0 -> x2, waiting for transfers between devices: none -> 29.4 us  [the longest x1 14.8 us: body(): arrived = lax.all_to_all(summed, 'col', 0, 0, tiled=True)]
    dot_general x5 -> x1, matrix products: 27.9 us -> 0.23 us  [body(): base = jnp.dot(features, w_self, preferred_element_type=F32) + bias[None, :]]
    pallas_call x0 -> x9, Pallas kernels: none -> 21.6 us  [the longest x2 6.41 us: spread_matmul(): pl.pallas_call(spread_matmul_kernel, grid=(NY,), in_specs=[pl.BlockSpec(p...]
    all_to_all x0 -> x2, starting transfers between devices: none -> 9.36 us  [the longest x1 5.89 us: body(): arrived = lax.all_to_all(summed, 'col', 0, 0, tiled=True)]
  transfers between devices with their start and end apart: 4 -> 4, of which waited for: 4 -> 3; matrix products, arithmetic and copies ran while one was open for 0% -> 0% of each run, Pallas kernels for 0% -> 5%
where the time goes in v2:
time: 172 us; the launch traced here: 171 us
  blocking collectives  101 us (59%)
  waiting for transfers between devices  30.3 us (18%)
  Pallas kernels  21.6 us (13%)
  starting transfers between devices  9.45 us (5%)
  local copies, waits for them, and re-layouts  7.67 us (4%)
    all_to_all x3, blocking collectives, exchange(): lax.all_to_all(value, 'row', 0, 0, axis_index_groups=groups_along(axis),...  82.3 us
    all_to_all x1, blocking collectives, body(): table = lax.all_to_all(scaled_t, 'col', 0, 0, tiled=True)  18.4 us
    all_to_all x1, waiting for transfers between devices, body(): arrived = lax.all_to_all(summed, 'col', 0, 0, tiled=True)  14.8 us
    all_to_all x1, waiting for transfers between devices, exchange(): lax.all_to_all(value, 'row', 0, 0, axis_index_groups=groups_along(axis),...  14.6 us
    pallas_call x2, Pallas kernels, spread_matmul(): pl.pallas_call(spread_matmul_kernel, grid=(NY,), in_specs=[pl.BlockSpec(p...  6.41 us
    unnamed x21, local copies, waits for them, and re-layouts  6.29 us
    all_to_all x1, starting transfers between devices, body(): arrived = lax.all_to_all(summed, 'col', 0, 0, tiled=True)  5.89 us
    pallas_call x1, Pallas kernels, second_half(): pl.pallas_call(second_half_kernel, grid=(x.shape[0] // depth,), in_specs=...  5.74 us
  transfers between devices with their start and end apart: 4, of which 3 were waited for; matrix products, arithmetic and copies ran while one was open for 0% of the time, Pallas kernels for 5%

profile of v2, /device:TPU:32, one launch (start us, length us, event | category | flops | bytes accessed | tf_op | source)
XLA Modules:
  0.0 171.1 jit_solution(6223025483024794670)
XLA Ops:
  0.6 0.0 copy-start
  0.6 1.0 broadcast_in_dim.30
  1.7 24.1 %all_to_all.36 = bf16[4,128,512]{2,1,0:T(8,128)(2,1)S(1)} all-to-all(bf16[4,128,512]{2,1,0:T(8,128)(2,1)S(1)} %broadcast_in_dim.30), channel_id=1, replica_groups={{0,16,32,48},{64,80,96,112},{128,144,160,176},{192,208,224,240},{8,24,4..., dimensions={0} | all-to-all | bytes 1048576 | tf_op jit(solution)/shard_map/all_to_all | solution.py:36
  25.7 0.2 broadcast_in_dim.32
  25.9 0.0 copy-start.8
  25.9 28.9 %all_to_all.37 = bf16[4,512,512]{2,1,0:T(8,128)(2,1)S(1)} all-to-all(bf16[4,512,512]{2,1,0:T(8,128)(2,1)S(1)} %broadcast_in_dim.32), channel_id=1, replica_groups={{0,64,128,192},{16,80,144,208},{32,96,160,224},{48,112,176,240},{8,72,1..., dimensions={0} | all-to-all | bytes 4194304 | tf_op jit(solution)/shard_map/all_to_all | solution.py:36
  54.8 0.1 copy.12
  54.9 0.1 reshape_squeeze.3.where
  55.0 0.0 copy-start.3
  55.0 2.8 %copy-done.3 = s32[1,1,32,3,128,128]{5,4,3,2,1,0:T(8,128)S(1)} copy-done((s32[1,1,32,3,128,128]{5,4,3,2,1,0:T(8,128)S(1)}, s32[1,1,32,3,128,128]{5,4,3,2,1,0:T(8,128)}, u32[]{:S(2)}) %copy-start.3) | copy-done | bytes 6291480
  57.8 2.7 %adjacency.1.adj = bf16[1024,4096]{1,0:T(8,128)(2,1)S(1)} custom-call(s32[32]{0:T(128)S(1)} %fusion.1.order, s32[96]{0:T(128)S(1)} %reshape_squeeze.3.where, s32[32,3,128,128]{3,2,1,0:T(8,128)S(1)} %bitcast.15, s32[32,3,128,128]{3,2,1,0:T(8,128)S(1)} %bitcast.16, s32[32,3,128,128]{3,2,1,0:T(8,128)S(1)} %bitcast.17, s32[32,3,128,128]{3,2,1,0:T(8,128)S(1)} %bitcast.18), custom_call_target="tpu_custom_call" | custom-call | bytes 14680064 | tf_op jit(solution)/shard_map/adjacency/pallas_call | solution.py:74
  60.5 3.4 %first_half.1.start = f32[1024,512]{1,0:T(8,128)S(1)} custom-call(bf16[1024,4096]{1,0:T(8,128)(2,1)S(1)} %adjacency.1.adj, bf16[2048,512]{1,0:T(8,128)(2,1)S(1)} %bitcast.20), custom_call_target="tpu_custom_call" | custom-call | flops 2147483648 | bytes 8388608 | tf_op jit(solution)/shard_map/first_half/pallas_call | solution.py:100
  63.8 5.7 %second_half.1 = bf16[1024,512]{1,0:T(8,128)(2,1)} custom-call(bf16[1024,4096]{1,0:T(8,128)(2,1)S(1)} %adjacency.1.adj, bf16[2048,512]{1,0:T(8,128)(2,1)} %collective-permute-done.x, f32[1024,512]{1,0:T(8,128)S(1)} %first_half.1.start), custom_call_target="tpu_custom_call" | custom-call | flops 2147483648 | bytes 9437184 | tf_op jit(solution)/shard_map/second_half/pallas_call | solution.py:130
  69.6 0.0 copy-start.5
  69.6 5.9 %all-to-all-start.2 = ((bf16[8,128,512]{2,1,0:T(8,128)(2,1)}), bf16[8,128,512]{2,1,0:T(8,128)(2,1)S(1)}, u32[]{:S(2)}, u32[]{:S(2)}) async-start(bf16[8,128,512]{2,1,0:T(8,128)(2,1)} %bitcast.3), calls=%async_computation.2 | async-start | bytes 2097152 | tf_op jit(solution)/shard_map/all_to_all | solution.py:273
  75.5 0.1 copy.13.degf_col
  75.6 0.2 convolution_add_fusion.base
  75.9 14.8 %all-to-all-done.2 = bf16[8,128,512]{2,1,0:T(8,128)(2,1)S(1)} async-done(((bf16[8,128,512]{2,1,0:T(8,128)(2,1)}), bf16[8,128,512]{2,1,0:T(8,128)(2,1)S(1)}, u32[]{:S(2)}, u32[]{:S(2)}) %all-to-all-start.2) | async-done | bytes 1048608 | tf_op jit(solution)/shard_map/all_to_all | solution.py:273
  90.7 1.0 node_step.1
  91.7 18.4 %all_to_all.38.parts = bf16[8,512,128]{2,1,0:T(8,128)(2,1)S(1)} all-to-all(bf16[8,512,128]{2,1,0:T(8,128)(2,1)S(1)} %get-tuple-element.6), channel_id=1, replica_groups=mesh['row'=32,'col'=8] {'col'}, dimensions={0} | all-to-all | bytes 2097152 | tf_op jit(solution)/shard_map/all_to_all | solution.py:278
  110.2 3.4 %copy-done.2 = bf16[1024,4096]{1,0:T(8,128)(2,1)S(1)} copy-done((bf16[1024,4096]{1,0:T(8,128)(2,1)S(1)}, bf16[1024,4096]{1,0:T(8,128)(2,1)}, u32[]{:S(2)}) %copy-start.2) | copy-done | bytes 8388632
  113.5 3.2 %spread_matmul.3 = bf16[4,512,512]{2,1,0:T(8,128)(2,1)S(1)} custom-call(bf16[8,512,128]{2,1,0:T(8,128)(2,1)S(1)} %all_to_all.38.parts, bf16[1024,4096]{1,0:T(8,128)(2,1)S(1)} %copy-done.2), custom_call_target="tpu_custom_call" | custom-call | flops 2147483648 | bytes 7340032 | tf_op jit(solution)/shard_map/spread_matmul/pallas_call | solution.py:187
  116.7 0.1 collective-permute-start.1
  116.8 3.2 %spread_matmul.2.mine = bf16[4,512,512]{2,1,0:T(8,128)(2,1)S(1)} custom-call(bf16[8,512,128]{2,1,0:T(8,128)(2,1)S(1)} %all_to_all.38.parts, bf16[1024,4096]{1,0:T(8,128)(2,1)S(1)} %copy-done.2), custom_call_target="tpu_custom_call" | custom-call | flops 2147483648 | bytes 7340032 | tf_op jit(solution)/shard_map/spread_matmul/pallas_call | solution.py:187
  120.1 0.9 collective-permute-done.1.theirs
  121.0 0.5 pair_sum.1
  121.5 29.4 %all_to_all.39.parts = bf16[4,512,512]{2,1,0:T(8,128)(2,1)S(1)} all-to-all(bf16[4,512,512]{2,1,0:T(8,128)(2,1)S(1)} %pair_sum.1), channel_id=1, replica_groups={{0,64,128,192},{16,80,144,208},{32,96,160,224},{48,112,176,240},{8,72,1..., dimensions={0} | all-to-all | bytes 4194304 | tf_op jit(solution)/shard_map/all_to_all | solution.py:36
  150.9 1.1 add_split.1
  152.0 3.5 %all-to-all-start.5 = ((bf16[4,512,128]{2,1,0:T(8,128)(2,1)}), bf16[4,512,128]{2,1,0:T(8,128)(2,1)S(1)}, u32[]{:S(2)}, u32[]{:S(2)}) async-start(bf16[4,512,128]{2,1,0:T(8,128)(2,1)} %add_split.1), calls=%async_computation.5 | async-start | bytes 1048576 | tf_op jit(solution)/shard_map/all_to_all | solution.py:36
  155.4 0.3 fusion.2.own
  155.8 14.6 %all-to-all-done.5.parts = bf16[4,512,128]{2,1,0:T(8,128)(2,1)S(1)} async-done(((bf16[4,512,128]{2,1,0:T(8,128)(2,1)}), bf16[4,512,128]{2,1,0:T(8,128)(2,1)S(1)}, u32[]{:S(2)}, u32[]{:S(2)}) %all-to-all-start.5) | async-done | bytes 524320 | tf_op jit(solution)/shard_map/all_to_all | solution.py:36
  170.3 0.8 last_sum.1
  (18 shorter events, 0.0 us)
Async XLA Ops:
  0.6 75.0 %copy-start = (bf16[512,512]{1,0:T(8,128)(2,1)S(1)}, bf16[512,512]{1,0:T(8,128)(2,1)}, u32[]{:S(2)}) copy-start(bf16[512,512]{1,0:T(8,128)(2,1)} %param.12) | copy-start | bytes 1572868
  25.9 28.9 %copy-start.8 = (s32[1,1,32,3]{2,1,3,0:T(1,128)S(1)}, s32[1,1,32,3]{2,1,3,0:T(1,128)}, u32[]{:S(2)}) copy-start(s32[1,1,32,3]{2,1,3,0:T(1,128)} %param.10) | copy-start | bytes 1156
  54.8 9.1 %collective-permute-start = (bf16[2048,512]{1,0:T(8,128)(2,1)S(1)}, bf16[2048,512]{1,0:T(8,128)(2,1)}, u32[]{:S(2)}, u32[]{:S(2)}) collective-permute-start(bf16[2048,512]{1,0:T(8,128)(2,1)S(1)} %bitcast.19), channel_id=1, source_target_pairs={{0,8},{1,9},{2,10},{3,11},{4,12},{5,13},{6,14},{7,15},{8,0},{9,1},... | collective-permute-start | bytes 6291464 | tf_op jit(solution)/shard_map/ppermute | solution.py:47
  55.0 2.8 %copy-start.3 = (s32[1,1,32,3,128,128]{5,4,3,2,1,0:T(8,128)S(1)}, s32[1,1,32,3,128,128]{5,4,3,2,1,0:T(8,128)}, u32[]{:S(2)}) copy-start(s32[1,1,32,3,128,128]{5,4,3,2,1,0:T(8,128)} %param.11) | copy-start | bytes 18874372
  60.5 3.4 %copy-start.1 = (bf16[1024,4096]{1,0:T(8,128)(2,1)}, bf16[1024,4096]{1,0:T(8,128)(2,1)S(1)}, u32[]{:S(2)}) copy-start(bf16[1024,4096]{1,0:T(8,128)(2,1)S(1)} %adjacency.1.adj) | copy-start | bytes 25165828
  69.6 5.9 %copy-start.9 = (s32[128]{0:T(128)S(1)}, s32[128]{0:T(128)}, u32[]{:S(2)}) copy-start(s32[128]{0:T(128)} %param.9) | copy-start | bytes 1540
  69.6 6.0 %copy-start.6 = (bf16[128,512]{1,0:T(8,128)(2,1)S(1)}, bf16[128,512]{1,0:T(8,128)(2,1)}, u32[]{:S(2)}) copy-start(bf16[128,512]{1,0:T(8,128)(2,1)} %param.8) | copy-start | bytes 393220
  69.6 6.0 %copy-start.7 = (f32[512]{0:T(512)S(1)}, f32[512]{0:T(512)}, u32[]{:S(2)}) copy-start(f32[512]{0:T(512)} %param.14) | copy-start | bytes 6148
  69.6 21.1 %copy-start.4 = (bf16[512,512]{1,0:T(8,128)(2,1)S(1)}, bf16[512,512]{1,0:T(8,128)(2,1)}, u32[]{:S(2)}) copy-start(bf16[512,512]{1,0:T(8,128)(2,1)} %w_neigh.1) | copy-start | bytes 1572868
  69.6 21.1 %copy-start.5 = (bf16[128,512]{1,0:T(8,128)(2,1)S(1)}, bf16[128,512]{1,0:T(8,128)(2,1)}, u32[]{:S(2)}) copy-start(bf16[128,512]{1,0:T(8,128)(2,1)} %cotangent.1) | copy-start | bytes 393220
  69.6 21.1 %all-to-all-start.2 = ((bf16[8,128,512]{2,1,0:T(8,128)(2,1)}), bf16[8,128,512]{2,1,0:T(8,128)(2,1)S(1)}, u32[]{:S(2)}, u32[]{:S(2)}) async-start(bf16[8,128,512]{2,1,0:T(8,128)(2,1)} %bitcast.3), calls=%async_computation.2 | async-start | bytes 2097152 | tf_op jit(solution)/shard_map/all_to_all | solution.py:273
  110.1 3.4 %copy-start.2 = (bf16[1024,4096]{1,0:T(8,128)(2,1)S(1)}, bf16[1024,4096]{1,0:T(8,128)(2,1)}, u32[]{:S(2)}) copy-start(bf16[1024,4096]{1,0:T(8,128)(2,1)} %copy-done.1) | copy-start | bytes 25165828
  116.7 4.2 %collective-permute-start.1 = (bf16[4,512,512]{2,1,0:T(8,128)(2,1)S(1)}, bf16[4,512,512]{2,1,0:T(8,128)(2,1)S(1)}, u32[]{:S(2)}, u32[]{:S(2)}) collective-permute-start(bf16[4,512,512]{2,1,0:T(8,128)(2,1)S(1)} %spread_matmul.3), channel_id=1, source_target_pairs={{0,8},{1,9},{2,10},{3,11},{4,12},{5,13},{6,14},{7,15},{8,0},{9,1},... | collective-permute-start | bytes 6291464 | tf_op jit(solution)/shard_map/ppermute | solution.py:47
  152.0 18.4 %all-to-all-start.5 = ((bf16[4,512,128]{2,1,0:T(8,128)(2,1)}), bf16[4,512,128]{2,1,0:T(8,128)(2,1)S(1)}, u32[]{:S(2)}, u32[]{:S(2)}) async-start(bf16[4,512,128]{2,1,0:T(8,128)(2,1)} %add_split.1), calls=%async_computation.5 | async-start | bytes 1048576 | tf_op jit(solution)/shard_map/all_to_all | solution.py:36

commit v3 on v2

v3 whole, which is shorter than its diff:
```python
import functools

import jax
import jax.numpy as jnp
from jax import lax
from jax.experimental import pallas as pl
from jax.experimental.pallas import tpu as pltpu
from jax.sharding import PartitionSpec as P

NY, NZH, NCORE, NX, NZL = 4, 4, 2, 4, 2
NROW, NCOL = NY * NZH * NCORE, NX * NZL
CHIPS = NY * NZH
STEPS = ((1, 3), (3, 1))
TILE = 128
BF16 = jnp.bfloat16
F32 = jnp.float32
MB = 1024 * 1024


def flip(value, y=0, z=0, core=0):
    pairs = []
    for row in range(NROW):
        there = row ^ ((y * NZH + z) * NCORE + core)
        pairs += [(row * NCOL + col, there * NCOL + col) for col in range(NCOL)]
    return lax.ppermute(value, ("row", "col"), pairs)


def adjacency_kernel(order, where, *refs):
    masks, out = refs[:-1], refs[-1]
    step = pl.program_id(0)
    out[...] = jnp.zeros_like(out)
    slots = masks[0].shape[1]
    for i, mask in enumerate(masks):
        j = order[step * len(masks) + i]
        for k in range(slots):
            q = where[j * slots + k]
            at = pl.ds(pl.multiple_of(q * TILE, TILE), TILE)
            cols = slice(i * TILE, (i + 1) * TILE)
            out[at, cols] = out[at, cols] + mask[0, k].astype(F32).astype(BF16)


def adjacency(masks, order, where):
    count, slots = masks.shape[0], masks.shape[1]
    group = 4
    specs = [
        pl.BlockSpec(
            (1, slots, TILE, TILE),
            functools.partial(lambda i, s, order, where: (order[s * group + i], 0, 0, 0), i),
        )
        for i in range(group)
    ]
    masks = pltpu.with_memory_space_constraint(masks, pltpu.HBM)
    return pl.pallas_call(
        adjacency_kernel,
        grid_spec=pltpu.PrefetchScalarGridSpec(
            num_scalar_prefetch=2,
            grid=(count // group,),
            in_specs=specs,
            out_specs=pl.BlockSpec((NCOL * TILE, group * TILE), lambda s, order, where: (0, s)),
        ),
        out_shape=pltpu.HBM((NCOL * TILE, count * TILE), BF16),
        compiler_params=pltpu.CompilerParams(vmem_limit_bytes=16 * MB),
        cost_estimate=pl.CostEstimate(flops=0, bytes_accessed=14 * MB, transcendentals=0),
        name="adjacency",
    )(order, where, *([masks] * group))


def gather_kernel(plan, blocks, adj, *refs):
    del blocks
    parts, refs = refs[:4], refs[4:]
    start, out, acc = (refs[0], refs[1], refs[2]) if len(refs) == 3 else (None, refs[0], refs[0])
    half = parts[0].shape[1]
    depth = NZH * TILE

    @pl.when(pl.program_id(0) == 0)
    def _():
        acc[...] = jnp.zeros_like(acc) if start is None else start[...]

    for step, (_, places) in enumerate(plan):

        @pl.when(pl.program_id(0) == step)
        def _(places=places):
            for h, array, at in places:
                cols = slice(h * half, (h + 1) * half)
                rhs = parts[array][at * depth : (at + 1) * depth, :]
                acc[:, cols] += jnp.dot(adj[...], rhs, preferred_element_type=F32)

    if start is not None:

        @pl.when(pl.program_id(0) == pl.num_programs(0) - 1)
        def _():
            out[...] = acc[...].astype(BF16)


def gather_matmul(adj, parts, dys, start, name):
    plan = []
    for core in range(NCORE):
        for dy in range(NY):
            places = [(h, core * 2 + h, dys[h].index(dy)) for h in range(2) if dy in dys[h]]
            if places:
                plan.append((core * NY + dy, places))
    rows, width = adj.shape[0], 2 * parts[0].shape[1]
    full = lambda shape: pl.BlockSpec(shape, lambda s, blocks: (0, 0))
    specs = [pl.BlockSpec((rows, NZH * TILE), lambda s, blocks: (0, blocks[s]))] + [full(v.shape) for v in parts]
    operands = [pltpu.with_memory_space_constraint(adj, pltpu.HBM), *parts]
    if start is not None:
        specs.append(full((rows, width)))
        operands.append(start)
    return pl.pallas_call(
        functools.partial(gather_kernel, plan),
        grid_spec=pltpu.PrefetchScalarGridSpec(
            num_scalar_prefetch=1,
            grid=(len(plan),),
            in_specs=specs,
            out_specs=full((rows, width)),
            scratch_shapes=[] if start is None else [pltpu.VMEM((rows, width), F32)],
        ),
        out_shape=jax.ShapeDtypeStruct((rows, width), F32) if start is None else pltpu.HBM((rows, width), BF16),
        compiler_params=pltpu.CompilerParams(vmem_limit_bytes=24 * MB),
        cost_estimate=pl.CostEstimate(flops=2 * rows * width * CHIPS * TILE, bytes_accessed=9 * MB, transcendentals=0),
        name=name,
    )(jnp.array([block for block, _ in plan], jnp.int32), *operands)


def node_kernel(parts, base, degf_col, degf_row, w_neigh, cotangent, out, grad, scaled_t):
    total = parts[0:TILE, :].astype(F32)
    for i in range(1, NCOL):
        total = total + parts[i * TILE : (i + 1) * TILE, :].astype(F32)
    mean = (total / degf_col[...]).astype(BF16)
    pre = base[...] + jnp.dot(mean, w_neigh[...], preferred_element_type=F32)
    sig = jax.nn.sigmoid(pre)
    out[...] = (pre * sig).astype(BF16)
    slope = sig * (1.0 + pre * (1.0 - sig))
    grad_pre = (cotangent[...].astype(F32) * slope).astype(BF16)
    grad[...] = grad_pre
    proj_t = lax.dot_general(w_neigh[...], grad_pre, (((1,), (1,)), ((), ())), preferred_element_type=F32)
    scaled = (proj_t / degf_row[...]).astype(BF16)
    for i in range(NCOL):
        scaled_t[i, :, :] = scaled


def node_step(parts, base, degf, w_neigh, cotangent):
    rows, width = cotangent.shape
    return pl.pallas_call(
        node_kernel,
        out_shape=[
            jax.ShapeDtypeStruct((rows, width), BF16),
            jax.ShapeDtypeStruct((rows, width), BF16),
            jax.ShapeDtypeStruct((NCOL, width, rows), BF16),
        ],
        compiler_params=pltpu.CompilerParams(vmem_limit_bytes=32 * MB),
        cost_estimate=pl.CostEstimate(flops=4 * rows * width * width, bytes_accessed=4 * MB, transcendentals=rows * width),
        name="node_step",
    )(parts, base, degf[:, None], degf[None, :], w_neigh, cotangent)


def spread_kernel(parts, adj, keep, send):
    lhs = jnp.concatenate([parts[i] for i in range(NCOL)], axis=1)
    value = jnp.dot(lhs, adj[...], preferred_element_type=F32).astype(BF16)
    half = value.shape[0] // 2
    depth = NZH * TILE
    for dy in range(NY):

        @pl.when(pl.program_id(0) == dy)
        def _(dy=dy):
            for h, (k1, k2) in enumerate(STEPS):
                out, order = (keep, (0, k1)) if dy in (0, k1) else (send, (k2, k1 ^ k2))
                at = order.index(dy) * depth
                out[h, :, at : at + depth] = value[h * half : (h + 1) * half, :]


def spread_matmul(parts, adj, core, name):
    width = parts.shape[1]
    rows = adj.shape[0]
    shape = (2, width // 2, 2 * NZH * TILE)
    return pl.pallas_call(
        spread_kernel,
        grid=(NY,),
        in_specs=[
            pl.BlockSpec(parts.shape, lambda s: (0, 0, 0)),
            pl.BlockSpec((rows, NZH * TILE), lambda s: (0, core * NY + s)),
        ],
        out_specs=[pl.BlockSpec(shape, lambda s: (0, 0, 0))] * 2,
        out_shape=[jax.ShapeDtypeStruct(shape, BF16)] * 2,
        compiler_params=pltpu.CompilerParams(vmem_limit_bytes=24 * MB),
        cost_estimate=pl.CostEstimate(flops=2 * rows * width * CHIPS * TILE, bytes_accessed=7 * MB, transcendentals=0),
        name=name,
    )(parts, pltpu.with_memory_space_constraint(adj, pltpu.HBM))


def total(refs):
    value = refs[0][...].astype(F32)
    for ref in refs[1:]:
        value = value + ref[...].astype(F32)
    return value


def both_halves_kernel(mine, theirs, *outs):
    for h, out in enumerate(outs):
        out[...] = (mine[h].astype(F32) + theirs[h].astype(F32)).astype(BF16)


def both_halves(mine, theirs):
    shape = mine.shape[1:]
    return pl.pallas_call(
        both_halves_kernel,
        out_shape=[jax.ShapeDtypeStruct(shape, BF16)] * 2,
        compiler_params=pltpu.CompilerParams(vmem_limit_bytes=16 * MB),
        cost_estimate=pl.CostEstimate(flops=MB, bytes_accessed=3 * MB, transcendentals=0),
        name="both_halves",
    )(mine, theirs)


def split_kernel(kept, sent, *refs):
    value = total(refs[:-2])
    for out, tiles in zip(refs[-2:], (kept, sent)):
        for i, tile in enumerate(tiles):
            part = value[:, tile * TILE : (tile + 1) * TILE]
            out[:, i * TILE : (i + 1) * TILE] = part.astype(out.dtype)


def add_split(values, kept, sent, name):
    rows = values[0].shape[0]
    return pl.pallas_call(
        functools.partial(split_kernel, kept, sent),
        out_shape=[
            jax.ShapeDtypeStruct((rows, len(kept) * TILE), F32),
            jax.ShapeDtypeStruct((rows, len(sent) * TILE), BF16),
        ],
        compiler_params=pltpu.CompilerParams(vmem_limit_bytes=16 * MB),
        cost_estimate=pl.CostEstimate(flops=MB, bytes_accessed=2 * MB, transcendentals=0),
        name=name,
    )(*values)


def last_kernel(*refs):
    own, out = refs[-2:]
    back = jnp.concatenate([total(refs[0:2]), total(refs[2:4])], axis=0)
    out[...] = (own[...] + back.T).astype(BF16)


def last_sum(values, own):
    return pl.pallas_call(
        last_kernel,
        out_shape=jax.ShapeDtypeStruct(own.shape, BF16),
        compiler_params=pltpu.CompilerParams(vmem_limit_bytes=16 * MB),
        name="last_sum",
    )(*values, own)


def body(features, degrees, tile_rows, tile_masks, w_self, w_neigh, bias, cotangent):
    half = features.shape[1] // 2
    row = lax.axis_index("row").astype(jnp.int32)

    m = jnp.arange(NROW, dtype=jnp.int32)
    order = row ^ ((m % CHIPS) * NCORE + m // CHIPS)
    adj = adjacency(tile_masks[0, 0], order, tile_rows[0, 0].reshape(-1))

    chunks = [features[:, :half], features[:, half:]]
    firsts = [flip(v, z=k1) for v, (k1, _) in zip(chunks, STEPS)]
    pairs = [jnp.concatenate([v, r], axis=0) for v, r in zip(chunks, firsts)]
    seconds = [flip(v, z=k2) for v, (_, k2) in zip(pairs, STEPS)]
    planes = []
    for v, first, second, (k1, k2) in zip(chunks, firsts, seconds, STEPS):
        tiles = {0: v, k1: first, k2: second[:TILE], k1 ^ k2: second[TILE:]}
        planes.append(jnp.concatenate([tiles[i] for i in range(NZH)], axis=0))
    thirds = [flip(v, y=k1) for v, (k1, _) in zip(planes, STEPS)]
    *thirds, adj = lax.optimization_barrier((*thirds, adj))
    near = [jnp.concatenate([v, r], axis=0) for v, r in zip(planes, thirds)]
    far = [flip(v, y=k2) for v, (_, k2) in zip(near, STEPS)]
    near = near + [flip(v, core=1) for v in near]
    start = gather_matmul(adj, near, [(0, k1) for k1, _ in STEPS], None, "gather_near")
    *far, start = lax.optimization_barrier((*far, start))
    far = far + [flip(v, core=1) for v in far]
    summed = gather_matmul(adj, far, [(k2, k1 ^ k2) for k1, k2 in STEPS], start, "gather_far")

    arrived = lax.all_to_all(summed, "col", 0, 0, tiled=True)
    degf = degrees.astype(F32)
    base = jnp.dot(features, w_self, preferred_element_type=F32) + bias[None, :]
    output, grad_pre, scaled_t = node_step(arrived, base, degf, w_neigh, cotangent)

    table = lax.all_to_all(scaled_t, "col", 0, 0, tiled=True)
    own = lax.dot_general(grad_pre, w_self, (((1,), (1,)), ((), ())), preferred_element_type=F32)
    keep_out, send_out = spread_matmul(table, adj, 1, "spread_other")
    send_in, keep_in = flip(send_out, core=1), flip(keep_out, core=1)
    keep, send = spread_matmul(table, adj, 0, "spread_own")

    ends = []
    for h, (value, (k1, k2)) in enumerate(zip(both_halves(send, send_in), STEPS)):
        got = flip(value, y=k2)
        stay, go = add_split((keep[h], keep_in[h], got), range(NZH), range(NZH, 2 * NZH), "add_y1")
        got = flip(go, y=k1)
        stay, go = add_split((stay, got), (0, k1), (k2, k1 ^ k2), "add_y2")
        got = flip(go, z=k2)
        stay, go = add_split((stay, got), (0,), (1,), "add_z1")
        ends += [stay, flip(go, z=k1)]
    grad_features = last_sum(ends, own)
    return output, grad_features


def solution(mesh):
    both = P(("row", "col"), None)
    return jax.shard_map(
        body,
        mesh=mesh,
        in_specs=(
            both,
            P(("row", "col")),
            P("row", "col", None, None),
            P("row", "col", None, None, None, None),
            P(),
            P(),
            P(),
            both,
        ),
        out_specs=(both, both),
        check_vma=False,
    )
```

time: 172 us -> 151 us (0.88)
  blocking collectives: 101 us -> 18.4 us
  starting transfers between devices: 9.45 us -> 38.9 us
  waiting for transfers between devices: 30.3 us -> 52.2 us
  Pallas kernels: 21.6 us -> 36.3 us
  local copies, waits for them, and re-layouts: 7.67 us -> 2.16 us
    all_to_all x3 -> x0, blocking collectives: 82.3 us -> none  [exchange(): lax.all_to_all(value, 'row', 0, 0, axis_index_groups=groups_along(axis),...]
    ppermute x2 -> x22, waiting for transfers between devices: 0.93 us -> 37.8 us  [flip(): return lax.ppermute(value, ('row', 'col'), pairs)]
    ppermute x2 -> x22, starting transfers between devices: 0.1 us -> 33.2 us  [flip(): return lax.ppermute(value, ('row', 'col'), pairs)]
    all_to_all x1 -> x0, waiting for transfers between devices: 14.6 us -> none  [exchange(): lax.all_to_all(value, 'row', 0, 0, axis_index_groups=groups_along(axis),...]
    pallas_call x6 -> x11, Pallas kernels: 17.1 us -> 25 us  [the longest x2 14.3 us: gather_matmul(): pl.pallas_call(functools.partial(gather_kernel, plan), grid_spec=pltpu.Pr...]
    pallas_call x1, Pallas kernels: 2.67 us -> 9.51 us  [adjacency(): pl.pallas_call(adjacency_kernel, grid_spec=pltpu.PrefetchScalarGridSpec(n...]
    unnamed x21, local copies, waits for them, and re-layouts: 6.29 us -> 1.78 us
    all_to_all x1 -> x0, starting transfers between devices: 3.47 us -> none  [exchange(): lax.all_to_all(value, 'row', 0, 0, axis_index_groups=groups_along(axis),...]
  transfers between devices with their start and end apart: 4 -> 23, of which waited for: 3 -> 12; matrix products, arithmetic and copies ran while one was open for 0% -> 1% of each run, Pallas kernels for 5% -> 15%
where the time goes in v3:
time: 151 us; the launch traced here: 150 us
  waiting for transfers between devices  52.2 us (35%)
  starting transfers between devices  38.9 us (26%)
  Pallas kernels  36.3 us (24%)
  blocking collectives  18.4 us (12%)
  local copies, waits for them, and re-layouts  2.16 us (1%)
    ppermute x22, waiting for transfers between devices, flip(): return lax.ppermute(value, ('row', 'col'), pairs)  37.8 us
    ppermute x22, starting transfers between devices, flip(): return lax.ppermute(value, ('row', 'col'), pairs)  33.2 us
    all_to_all x1, blocking collectives, body(): table = lax.all_to_all(scaled_t, 'col', 0, 0, tiled=True)  18.4 us
    all_to_all x1, waiting for transfers between devices, body(): arrived = lax.all_to_all(summed, 'col', 0, 0, tiled=True)  14.5 us
    pallas_call x2, Pallas kernels, gather_matmul(): pl.pallas_call(functools.partial(gather_kernel, plan), grid_spec=pltpu.Pr...  14.3 us
    pallas_call x2, Pallas kernels, spread_matmul(): pl.pallas_call(spread_kernel, grid=(NY,), in_specs=[pl.BlockSpec(parts.sh...  9.71 us
    pallas_call x1, Pallas kernels, adjacency(): pl.pallas_call(adjacency_kernel, grid_spec=pltpu.PrefetchScalarGridSpec(n...  9.51 us
    all_to_all x1, starting transfers between devices, body(): arrived = lax.all_to_all(summed, 'col', 0, 0, tiled=True)  5.75 us
  transfers between devices with their start and end apart: 23, of which 12 were waited for; matrix products, arithmetic and copies ran while one was open for 1% of the time, Pallas kernels for 15%

profile of v3, /device:TPU:32, one launch (start us, length us, event | category | flops | bytes accessed | tf_op | source)
XLA Modules:
  0.0 149.6 jit_solution(18232661786431743001)
XLA Ops:
  0.6 0.9 constant_dynamic-update-slice_fusion.4
  1.6 3.4 %collective-permute-start = (bf16[128,256]{1,0:T(8,128)(2,1)S(1)}, bf16[128,256]{1,0:T(8,128)(2,1)S(1)}, u32[]{:S(2)}, u32[]{:S(2)}) collective-permute-start(bf16[128,256]{1,0:T(8,128)(2,1)S(1)} %get-tuple-element.64), channel_id=1, source_target_pairs={{0,16},{1,17},{2,18},{3,19},{4,20},{5,21},{6,22},{7,23},{8,24},{9,... | collective-permute-start | bytes 196616 | tf_op jit(solution)/shard_map/ppermute | solution.py:25
  4.9 3.6 %collective-permute-start.3 = (bf16[128,256]{1,0:T(8,128)(2,1)S(1)}, bf16[128,256]{1,0:T(8,128)(2,1)S(1)}, u32[]{:S(2)}, u32[]{:S(2)}) collective-permute-start(bf16[128,256]{1,0:T(8,128)(2,1)S(1)} %get-tuple-element.65), channel_id=1, source_target_pairs={{0,48},{1,49},{2,50},{3,51},{4,52},{5,53},{6,54},{7,55},{8,56},{9,... | collective-permute-start | bytes 196616 | tf_op jit(solution)/shard_map/ppermute | solution.py:25
  8.5 4.8 %collective-permute-start.1 = (bf16[256,256]{1,0:T(8,128)(2,1)S(1)}, bf16[256,256]{1,0:T(8,128)(2,1)S(1)}, u32[]{:S(2)}, u32[]{:S(2)}) collective-permute-start(bf16[256,256]{1,0:T(8,128)(2,1)S(1)} %pad_maximum_fusion.3), channel_id=1, source_target_pairs={{0,48},{1,49},{2,50},{3,51},{4,52},{5,53},{6,54},{7,55},{8,56},{9,... | collective-permute-start | bytes 393224 | tf_op jit(solution)/shard_map/ppermute | solution.py:25
  13.9 4.8 %collective-permute-done.1 = bf16[256,256]{1,0:T(8,128)(2,1)S(1)} collective-permute-done((bf16[256,256]{1,0:T(8,128)(2,1)S(1)}, bf16[256,256]{1,0:T(8,128)(2,1)S(1)}, u32[]{:S(2)}, u32[]{:S(2)}) %collective-permute-start.1) | collective-permute-done | bytes 131104 | tf_op jit(solution)/shard_map/ppermute | solution.py:25
  18.8 1.7 %collective-permute-start.2 = (bf16[512,256]{1,0:T(8,128)(2,1)S(1)}, bf16[512,256]{1,0:T(8,128)(2,1)S(1)}, u32[]{:S(2)}, u32[]{:S(2)}) collective-permute-start(bf16[512,256]{1,0:T(8,128)(2,1)S(1)} %pad_maximum_fusion.1), channel_id=1, source_target_pairs={{0,64},{1,65},{2,66},{3,67},{4,68},{5,69},{6,70},{7,71},{8,72},{9,... | collective-permute-start | bytes 786440 | tf_op jit(solution)/shard_map/ppermute | solution.py:25
  20.5 2.7 %collective-permute-start.5 = (bf16[512,256]{1,0:T(8,128)(2,1)S(1)}, bf16[512,256]{1,0:T(8,128)(2,1)S(1)}, u32[]{:S(2)}, u32[]{:S(2)}) collective-permute-start(bf16[512,256]{1,0:T(8,128)(2,1)S(1)} %pad_maximum_fusion.2), channel_id=1, source_target_pairs={{0,192},{1,193},{2,194},{3,195},{4,196},{5,197},{6,198},{7,199},{8... | collective-permute-start | bytes 786440 | tf_op jit(solution)/shard_map/ppermute | solution.py:25
  23.2 0.8 copy.14
  24.1 9.5 %adjacency.1.adj = bf16[1024,4096]{1,0:T(8,128)(2,1)} custom-call(s32[32]{0:T(128)S(1)} %fusion.2.order, s32[96]{0:T(128)S(1)} %reshape_squeeze.3.where, s32[32,3,128,128]{3,2,1,0:T(8,128)} %bitcast.22, s32[32,3,128,128]{3,2,1,0:T(8,128)} %bitcast.23, s32[32,3,128,128]{3,2,1,0:T(8,128)} %bitcast.24, s32[32,3,128,128]{3,2,1,0:T(8,128)} %bitcast.25), custom_call_target="tpu_custom_call" | custom-call | bytes 14680064 | tf_op jit(solution)/shard_map/adjacency/pallas_call | solution.py:53
  35.6 0.7 collective-permute-done.9.refs_3_
  36.4 6.8 %gather_near.1.refs_4_ = f32[1024,512]{1,0:T(8,128)S(1)} custom-call(s32[6]{0:T(128)S(1)} %copy-done.4, bf16[1024,4096]{1,0:T(8,128)(2,1)} %adjacency.1.adj, bf16[1024,256]{1,0:T(8,128)(2,1)S(1)} %constant_dynamic-update-slice_fusion.refs_0_, bf16[1024,256]{1,0:T(8,128)(2,1)S(1)} %pad_maximum_fusion.refs_1_, ...), custom_call_target="tpu_custom_call" | custom-call | flops 2147483648 | bytes 9437184 | tf_op jit(solution)/shard_map/gather_near/pallas_call | solution.py:109
  43.3 6.3 %collective-permute-done.6.refs_0_ = bf16[1024,256]{1,0:T(8,128)(2,1)S(1)} collective-permute-done((bf16[1024,256]{1,0:T(8,128)(2,1)S(1)}, bf16[1024,256]{1,0:T(8,128)(2,1)S(1)}, u32[]{:S(2)}, u32[]{:S(2)}) %collective-permute-start.6) | collective-permute-done | bytes 524320 | tf_op jit(solution)/shard_map/ppermute | solution.py:25
  50.0 1.4 collective-permute-done.10.refs_2_
  51.4 0.7 collective-permute-done.11.refs_3_
  52.2 7.5 %gather_far.1 = bf16[1024,512]{1,0:T(8,128)(2,1)} custom-call(s32[6]{0:T(128)S(1)} %copy-done.3, bf16[1024,4096]{1,0:T(8,128)(2,1)} %adjacency.1.adj, bf16[1024,256]{1,0:T(8,128)(2,1)S(1)} %collective-permute-done.6.refs_0_, bf16[1024,256]{1,0:T(8,128)(2,1)S(1)} %collective-permute-done.7.refs_1_, bf16[1024,256]{1,0:T(8,128)(2,1)S(1)} %collective-permute-done.10.refs_2_, ...), custom_call_target="tpu_custom_call" | custom-call | flops 2147483648 | bytes 9437184 | tf_op jit(solution)/shard_map/gather_far/pallas_call | solution.py:109
  59.7 5.8 %all-to-all-start = ((bf16[8,128,512]{2,1,0:T(8,128)(2,1)}), bf16[8,128,512]{2,1,0:T(8,128)(2,1)S(1)}, u32[]{:S(2)}, u32[]{:S(2)}) async-start(bf16[8,128,512]{2,1,0:T(8,128)(2,1)} %bitcast.26), calls=%async_computation | async-start | bytes 2097152 | tf_op jit(solution)/shard_map/all_to_all | solution.py:277
  65.9 14.5 %all-to-all-done = bf16[8,128,512]{2,1,0:T(8,128)(2,1)S(1)} async-done(((bf16[8,128,512]{2,1,0:T(8,128)(2,1)}), bf16[8,128,512]{2,1,0:T(8,128)(2,1)S(1)}, u32[]{:S(2)}, u32[]{:S(2)}) %all-to-all-start) | async-done | bytes 1048608 | tf_op jit(solution)/shard_map/all_to_all | solution.py:277
  80.3 1.0 node_step.1
  81.3 18.4 %all_to_all.16.parts = bf16[8,512,128]{2,1,0:T(8,128)(2,1)S(1)} all-to-all(bf16[8,512,128]{2,1,0:T(8,128)(2,1)S(1)} %get-tuple-element.36), channel_id=1, replica_groups=mesh['row'=32,'col'=8] {'col'}, dimensions={0} | all-to-all | bytes 2097152 | tf_op jit(solution)/shard_map/all_to_all | solution.py:282
  99.8 4.9 %spread_other.1 = (bf16[2,256,1024]{2,1,0:T(8,128)(2,1)S(1)}, bf16[2,256,1024]{2,1,0:T(8,128)(2,1)S(1)}) custom-call(bf16[8,512,128]{2,1,0:T(8,128)(2,1)S(1)} %all_to_all.16.parts, bf16[1024,4096]{1,0:T(8,128)(2,1)} %adjacency.1.adj), custom_call_target="tpu_custom_call" | custom-call | flops 2147483648 | bytes 7340032 | tf_op jit(solution)/shard_map/spread_other/pallas_call | solution.py:176
  105.2 4.9 %spread_own.1 = (bf16[2,256,1024]{2,1,0:T(8,128)(2,1)S(1)}, bf16[2,256,1024]{2,1,0:T(8,128)(2,1)S(1)}) custom-call(bf16[8,512,128]{2,1,0:T(8,128)(2,1)S(1)} %all_to_all.16.parts, bf16[1024,4096]{1,0:T(8,128)(2,1)} %adjacency.1.adj), custom_call_target="tpu_custom_call" | custom-call | flops 2147483648 | bytes 7340032 | tf_op jit(solution)/shard_map/spread_own/pallas_call | solution.py:176
  110.4 2.0 %collective-permute-start.14 = (bf16[256,1024]{1,0:T(8,128)(2,1)S(1)}, bf16[256,1024]{1,0:T(8,128)(2,1)S(1)}, u32[]{:S(2)}, u32[]{:S(2)}) collective-permute-start(bf16[256,1024]{1,0:T(8,128)(2,1)S(1)} %get-tuple-element.41), channel_id=1, source_target_pairs={{0,192},{1,193},{2,194},{3,195},{4,196},{5,197},{6,198},{7,199},{8... | collective-permute-start | bytes 1572872 | tf_op jit(solution)/shard_map/ppermute | solution.py:25
  112.6 11.7 %collective-permute-done.18.refs_2_ = bf16[256,1024]{1,0:T(8,128)(2,1)S(1)} collective-permute-done((bf16[256,1024]{1,0:T(8,128)(2,1)S(1)}, bf16[256,1024]{1,0:T(8,128)(2,1)S(1)}, u32[]{:S(2)}, u32[]{:S(2)}) %collective-permute-start.18) | collective-permute-done | bytes 524320 | tf_op jit(solution)/shard_map/ppermute | solution.py:25
  124.6 1.8 %collective-permute-start.19 = (bf16[256,512]{1,0:T(8,128)(2,1)S(1)}, bf16[256,512]{1,0:T(8,128)(2,1)S(1)}, u32[]{:S(2)}, u32[]{:S(2)}) collective-permute-start(bf16[256,512]{1,0:T(8,128)(2,1)S(1)} %get-tuple-element.50), channel_id=1, source_target_pairs={{0,192},{1,193},{2,194},{3,195},{4,196},{5,197},{6,198},{7,199},{8... | collective-permute-start | bytes 786440 | tf_op jit(solution)/shard_map/ppermute | solution.py:25
  126.8 6.6 %collective-permute-done.19.refs_1_ = bf16[256,512]{1,0:T(8,128)(2,1)S(1)} collective-permute-done((bf16[256,512]{1,0:T(8,128)(2,1)S(1)}, bf16[256,512]{1,0:T(8,128)(2,1)S(1)}, u32[]{:S(2)}, u32[]{:S(2)}) %collective-permute-start.19) | collective-permute-done | bytes 262176 | tf_op jit(solution)/shard_map/ppermute | solution.py:25
  133.5 1.8 %collective-permute-start.20 = (bf16[256,256]{1,0:T(8,128)(2,1)S(1)}, bf16[256,256]{1,0:T(8,128)(2,1)S(1)}, u32[]{:S(2)}, u32[]{:S(2)}) collective-permute-start(bf16[256,256]{1,0:T(8,128)(2,1)S(1)} %get-tuple-element.52), channel_id=1, source_target_pairs={{0,16},{1,17},{2,18},{3,19},{4,20},{5,21},{6,22},{7,23},{8,24},{9,... | collective-permute-start | bytes 393224 | tf_op jit(solution)/shard_map/ppermute | solution.py:25
  135.3 2.7 %collective-permute-start.16 = (bf16[256,256]{1,0:T(8,128)(2,1)S(1)}, bf16[256,256]{1,0:T(8,128)(2,1)S(1)}, u32[]{:S(2)}, u32[]{:S(2)}) collective-permute-start(bf16[256,256]{1,0:T(8,128)(2,1)S(1)} %get-tuple-element.45), channel_id=1, source_target_pairs={{0,48},{1,49},{2,50},{3,51},{4,52},{5,53},{6,54},{7,55},{8,56},{9,... | collective-permute-start | bytes 393224 | tf_op jit(solution)/shard_map/ppermute | solution.py:25
  138.0 1.7 %collective-permute-done.20.refs_1_ = bf16[256,256]{1,0:T(8,128)(2,1)S(1)} collective-permute-done((bf16[256,256]{1,0:T(8,128)(2,1)S(1)}, bf16[256,256]{1,0:T(8,128)(2,1)S(1)}, u32[]{:S(2)}, u32[]{:S(2)}) %collective-permute-start.20) | collective-permute-done | bytes 131104 | tf_op jit(solution)/shard_map/ppermute | solution.py:25
  139.7 3.5 %collective-permute-start.21 = (bf16[256,128]{1,0:T(8,128)(2,1)S(1)}, bf16[256,128]{1,0:T(8,128)(2,1)S(1)}, u32[]{:S(2)}, u32[]{:S(2)}) collective-permute-start(bf16[256,128]{1,0:T(8,128)(2,1)S(1)} %get-tuple-element.54), channel_id=1, source_target_pairs={{0,48},{1,49},{2,50},{3,51},{4,52},{5,53},{6,54},{7,55},{8,56},{9,... | collective-permute-start | bytes 196616 | tf_op jit(solution)/shard_map/ppermute | solution.py:25
  143.3 2.1 %collective-permute-start.17 = (bf16[256,128]{1,0:T(8,128)(2,1)S(1)}, bf16[256,128]{1,0:T(8,128)(2,1)S(1)}, u32[]{:S(2)}, u32[]{:S(2)}) collective-permute-start(bf16[256,128]{1,0:T(8,128)(2,1)S(1)} %get-tuple-element.47), channel_id=1, source_target_pairs={{0,16},{1,17},{2,18},{3,19},{4,20},{5,21},{6,22},{7,23},{8,24},{9,... | collective-permute-start | bytes 196616 | tf_op jit(solution)/shard_map/ppermute | solution.py:25
  146.3 2.5 %collective-permute-done.17.refs_1_ = bf16[256,128]{1,0:T(8,128)(2,1)S(1)} collective-permute-done((bf16[256,128]{1,0:T(8,128)(2,1)S(1)}, bf16[256,128]{1,0:T(8,128)(2,1)S(1)}, u32[]{:S(2)}, u32[]{:S(2)}) %collective-permute-start.17) | collective-permute-done | bytes 65568 | tf_op jit(solution)/shard_map/ppermute | solution.py:25
  148.8 0.8 last_sum.1
  (64 shorter events, 6.5 us)
Async XLA Ops:
  0.6 65.0 %copy-start = (bf16[512,512]{1,0:T(8,128)(2,1)S(1)}, bf16[512,512]{1,0:T(8,128)(2,1)}, u32[]{:S(2)}) copy-start(bf16[512,512]{1,0:T(8,128)(2,1)} %param.14) | copy-start | bytes 1572868
  1.6 6.9 %collective-permute-start = (bf16[128,256]{1,0:T(8,128)(2,1)S(1)}, bf16[128,256]{1,0:T(8,128)(2,1)S(1)}, u32[]{:S(2)}, u32[]{:S(2)}) collective-permute-start(bf16[128,256]{1,0:T(8,128)(2,1)S(1)} %get-tuple-element.64), channel_id=1, source_target_pairs={{0,16},{1,17},{2,18},{3,19},{4,20},{5,21},{6,22},{7,23},{8,24},{9,... | collective-permute-start | bytes 196616 | tf_op jit(solution)/shard_map/ppermute | solution.py:25
  4.9 8.4 %collective-permute-start.3 = (bf16[128,256]{1,0:T(8,128)(2,1)S(1)}, bf16[128,256]{1,0:T(8,128)(2,1)S(1)}, u32[]{:S(2)}, u32[]{:S(2)}) collective-permute-start(bf16[128,256]{1,0:T(8,128)(2,1)S(1)} %get-tuple-element.65), channel_id=1, source_target_pairs={{0,48},{1,49},{2,50},{3,51},{4,52},{5,53},{6,54},{7,55},{8,56},{9,... | collective-permute-start | bytes 196616 | tf_op jit(solution)/shard_map/ppermute | solution.py:25
  8.5 10.2 %collective-permute-start.1 = (bf16[256,256]{1,0:T(8,128)(2,1)S(1)}, bf16[256,256]{1,0:T(8,128)(2,1)S(1)}, u32[]{:S(2)}, u32[]{:S(2)}) collective-permute-start(bf16[256,256]{1,0:T(8,128)(2,1)S(1)} %pad_maximum_fusion.3), channel_id=1, source_target_pairs={{0,48},{1,49},{2,50},{3,51},{4,52},{5,53},{6,54},{7,55},{8,56},{9,... | collective-permute-start | bytes 393224 | tf_op jit(solution)/shard_map/ppermute | solution.py:25
  13.3 7.1 %collective-permute-start.4 = (bf16[256,256]{1,0:T(8,128)(2,1)S(1)}, bf16[256,256]{1,0:T(8,128)(2,1)S(1)}, u32[]{:S(2)}, u32[]{:S(2)}) collective-permute-start(bf16[256,256]{1,0:T(8,128)(2,1)S(1)} %pad_maximum_fusion.4), channel_id=1, source_target_pairs={{0,16},{1,17},{2,18},{3,19},{4,20},{5,21},{6,22},{7,23},{8,24},{9,... | collective-permute-start | bytes 393224 | tf_op jit(solution)/shard_map/ppermute | solution.py:25
  18.8 14.8 %collective-permute-start.2 = (bf16[512,256]{1,0:T(8,128)(2,1)S(1)}, bf16[512,256]{1,0:T(8,128)(2,1)S(1)}, u32[]{:S(2)}, u32[]{:S(2)}) collective-permute-start(bf16[512,256]{1,0:T(8,128)(2,1)S(1)} %pad_maximum_fusion.1), channel_id=1, source_target_pairs={{0,64},{1,65},{2,66},{3,67},{4,68},{5,69},{6,70},{7,71},{8,72},{9,... | collective-permute-start | bytes 786440 | tf_op jit(solution)/shard_map/ppermute | solution.py:25
  20.5 13.1 %collective-permute-start.5 = (bf16[512,256]{1,0:T(8,128)(2,1)S(1)}, bf16[512,256]{1,0:T(8,128)(2,1)S(1)}, u32[]{:S(2)}, u32[]{:S(2)}) collective-permute-start(bf16[512,256]{1,0:T(8,128)(2,1)S(1)} %pad_maximum_fusion.2), channel_id=1, source_target_pairs={{0,192},{1,193},{2,194},{3,195},{4,196},{5,197},{6,198},{7,199},{8... | collective-permute-start | bytes 786440 | tf_op jit(solution)/shard_map/ppermute | solution.py:25
  24.1 12.3 %copy-start.4 = (s32[6]{0:T(128)S(1)}, s32[6]{0:T(128)}, u32[]{:S(2)}) copy-start(s32[6]{0:T(128)} %constant.43.clone.blocks) | copy-start | bytes 76
  33.6 2.0 %collective-permute-start.8 = (bf16[1024,256]{1,0:T(8,128)(2,1)S(1)}, bf16[1024,256]{1,0:T(8,128)(2,1)S(1)}, u32[]{:S(2)}, u32[]{:S(2)}) collective-permute-start(bf16[1024,256]{1,0:T(8,128)(2,1)S(1)} %constant_dynamic-update-slice_fusion.refs_0_), channel_id=1, source_target_pairs={{0,8},{1,9},{2,10},{3,11},{4,12},{5,13},{6,14},{7,15},{8,0},{9,1},... | collective-permute-start | bytes 1572872 | tf_op jit(solution)/shard_map/ppermute | solution.py:25
  33.8 18.4 %copy-start.3 = (s32[6]{0:T(128)S(1)}, s32[6]{0:T(128)}, u32[]{:S(2)}) copy-start(s32[6]{0:T(128)} %constant.44.clone.blocks) | copy-start | bytes 76
  33.8 2.6 %collective-permute-start.9 = (bf16[1024,256]{1,0:T(8,128)(2,1)S(1)}, bf16[1024,256]{1,0:T(8,128)(2,1)S(1)}, u32[]{:S(2)}, u32[]{:S(2)}) collective-permute-start(bf16[1024,256]{1,0:T(8,128)(2,1)S(1)} %pad_maximum_fusion.refs_1_), channel_id=1, source_target_pairs={{0,8},{1,9},{2,10},{3,11},{4,12},{5,13},{6,14},{7,15},{8,0},{9,1},... | collective-permute-start | bytes 1572872 | tf_op jit(solution)/shard_map/ppermute | solution.py:25
  34.4 15.1 %collective-permute-start.6 = (bf16[1024,256]{1,0:T(8,128)(2,1)S(1)}, bf16[1024,256]{1,0:T(8,128)(2,1)S(1)}, u32[]{:S(2)}, u32[]{:S(2)}) collective-permute-start(bf16[1024,256]{1,0:T(8,128)(2,1)S(1)} %constant_dynamic-update-slice_fusion.refs_0_), channel_id=1, source_target_pairs={{0,192},{1,193},{2,194},{3,195},{4,196},{5,197},{6,198},{7,199},{8... | collective-permute-start | bytes 1572872 | tf_op jit(solution)/shard_map/ppermute | solution.py:25
  35.0 14.5 %collective-permute-start.7 = (bf16[1024,256]{1,0:T(8,128)(2,1)S(1)}, bf16[1024,256]{1,0:T(8,128)(2,1)S(1)}, u32[]{:S(2)}, u32[]{:S(2)}) collective-permute-start(bf16[1024,256]{1,0:T(8,128)(2,1)S(1)} %pad_maximum_fusion.refs_1_), channel_id=1, source_target_pairs={{0,64},{1,65},{2,66},{3,67},{4,68},{5,69},{6,70},{7,71},{8,72},{9,... | collective-permute-start | bytes 1572872 | tf_op jit(solution)/shard_map/ppermute | solution.py:25
  43.2 22.3 %copy-start.7 = (s32[128]{0:T(128)S(1)}, s32[128]{0:T(128)}, u32[]{:S(2)}) copy-start(s32[128]{0:T(128)} %param.11) | copy-start | bytes 1540
  43.2 22.4 %copy-start.5 = (bf16[128,512]{1,0:T(8,128)(2,1)S(1)}, bf16[128,512]{1,0:T(8,128)(2,1)}, u32[]{:S(2)}) copy-start(bf16[128,512]{1,0:T(8,128)(2,1)} %param.10) | copy-start | bytes 393220
  43.2 22.4 %copy-start.6 = (f32[512]{0:T(512)S(1)}, f32[512]{0:T(512)}, u32[]{:S(2)}) copy-start(f32[512]{0:T(512)} %param.16) | copy-start | bytes 6148
  43.2 37.1 %copy-start.1 = (bf16[512,512]{1,0:T(8,128)(2,1)S(1)}, bf16[512,512]{1,0:T(8,128)(2,1)}, u32[]{:S(2)}) copy-start(bf16[512,512]{1,0:T(8,128)(2,1)} %w_neigh.1) | copy-start | bytes 1572868
  43.2 37.1 %copy-start.2 = (bf16[128,512]{1,0:T(8,128)(2,1)S(1)}, bf16[128,512]{1,0:T(8,128)(2,1)}, u32[]{:S(2)}) copy-start(bf16[128,512]{1,0:T(8,128)(2,1)} %cotangent.1) | copy-start | bytes 393220
  49.5 1.9 %collective-permute-start.10 = (bf16[1024,256]{1,0:T(8,128)(2,1)S(1)}, bf16[1024,256]{1,0:T(8,128)(2,1)S(1)}, u32[]{:S(2)}, u32[]{:S(2)}) collective-permute-start(bf16[1024,256]{1,0:T(8,128)(2,1)S(1)} %collective-permute-done.6.refs_0_), channel_id=1, source_target_pairs={{0,8},{1,9},{2,10},{3,11},{4,12},{5,13},{6,14},{7,15},{8,0},{9,1},... | collective-permute-start | bytes 1572872 | tf_op jit(solution)/shard_map/ppermute | solution.py:25
  49.5 2.7 %collective-permute-start.11 = (bf16[1024,256]{1,0:T(8,128)(2,1)S(1)}, bf16[1024,256]{1,0:T(8,128)(2,1)S(1)}, u32[]{:S(2)}, u32[]{:S(2)}) collective-permute-start(bf16[1024,256]{1,0:T(8,128)(2,1)S(1)} %collective-permute-done.7.refs_1_), channel_id=1, source_target_pairs={{0,8},{1,9},{2,10},{3,11},{4,12},{5,13},{6,14},{7,15},{8,0},{9,1},... | collective-permute-start | bytes 1572872 | tf_op jit(solution)/shard_map/ppermute | solution.py:25
  59.7 20.6 %all-to-all-start = ((bf16[8,128,512]{2,1,0:T(8,128)(2,1)}), bf16[8,128,512]{2,1,0:T(8,128)(2,1)S(1)}, u32[]{:S(2)}, u32[]{:S(2)}) async-start(bf16[8,128,512]{2,1,0:T(8,128)(2,1)} %bitcast.26), calls=%async_computation | async-start | bytes 2097152 | tf_op jit(solution)/shard_map/all_to_all | solution.py:277
  104.6 5.5 %collective-permute-start.13 = (bf16[2,256,1024]{2,1,0:T(8,128)(2,1)S(1)}, bf16[2,256,1024]{2,1,0:T(8,128)(2,1)S(1)}, u32[]{:S(2)}, u32[]{:S(2)}) collective-permute-start(bf16[2,256,1024]{2,1,0:T(8,128)(2,1)S(1)} %get-tuple-element.40), channel_id=1, source_target_pairs={{0,8},{1,9},{2,10},{3,11},{4,12},{5,13},{6,14},{7,15},{8,0},{9,1},... | collective-permute-start | bytes 3145736 | tf_op jit(solution)/shard_map/ppermute | solution.py:25
  104.7 7.8 %collective-permute-start.12 = (bf16[2,256,1024]{2,1,0:T(8,128)(2,1)S(1)}, bf16[2,256,1024]{2,1,0:T(8,128)(2,1)S(1)}, u32[]{:S(2)}, u32[]{:S(2)}) collective-permute-start(bf16[2,256,1024]{2,1,0:T(8,128)(2,1)S(1)} %get-tuple-element.38), channel_id=1, source_target_pairs={{0,8},{1,9},{2,10},{3,11},{4,12},{5,13},{6,14},{7,15},{8,0},{9,1},... | collective-permute-start | bytes 3145736 | tf_op jit(solution)/shard_map/ppermute | solution.py:25
  110.3 14.0 %collective-permute-start.18 = (bf16[256,1024]{1,0:T(8,128)(2,1)S(1)}, bf16[256,1024]{1,0:T(8,128)(2,1)S(1)}, u32[]{:S(2)}, u32[]{:S(2)}) collective-permute-start(bf16[256,1024]{1,0:T(8,128)(2,1)S(1)} %get-tuple-element.48), channel_id=1, source_target_pairs={{0,64},{1,65},{2,66},{3,67},{4,68},{5,69},{6,70},{7,71},{8,72},{9,... | collective-permute-start | bytes 1572872 | tf_op jit(solution)/shard_map/ppermute | solution.py:25
  110.4 16.0 %collective-permute-start.14 = (bf16[256,1024]{1,0:T(8,128)(2,1)S(1)}, bf16[256,1024]{1,0:T(8,128)(2,1)S(1)}, u32[]{:S(2)}, u32[]{:S(2)}) collective-permute-start(bf16[256,1024]{1,0:T(8,128)(2,1)S(1)} %get-tuple-element.41), channel_id=1, source_target_pairs={{0,192},{1,193},{2,194},{3,195},{4,196},{5,197},{6,198},{7,199},{8... | collective-permute-start | bytes 1572872 | tf_op jit(solution)/shard_map/ppermute | solution.py:25
  124.6 8.8 %collective-permute-start.19 = (bf16[256,512]{1,0:T(8,128)(2,1)S(1)}, bf16[256,512]{1,0:T(8,128)(2,1)S(1)}, u32[]{:S(2)}, u32[]{:S(2)}) collective-permute-start(bf16[256,512]{1,0:T(8,128)(2,1)S(1)} %get-tuple-element.50), channel_id=1, source_target_pairs={{0,192},{1,193},{2,194},{3,195},{4,196},{5,197},{6,198},{7,199},{8... | collective-permute-start | bytes 786440 | tf_op jit(solution)/shard_map/ppermute | solution.py:25
  126.7 8.5 %collective-permute-start.15 = (bf16[256,512]{1,0:T(8,128)(2,1)S(1)}, bf16[256,512]{1,0:T(8,128)(2,1)S(1)}, u32[]{:S(2)}, u32[]{:S(2)}) collective-permute-start(bf16[256,512]{1,0:T(8,128)(2,1)S(1)} %get-tuple-element.43), channel_id=1, source_target_pairs={{0,64},{1,65},{2,66},{3,67},{4,68},{5,69},{6,70},{7,71},{8,72},{9,... | collective-permute-start | bytes 786440 | tf_op jit(solution)/shard_map/ppermute | solution.py:25
  133.5 6.2 %collective-permute-start.20 = (bf16[256,256]{1,0:T(8,128)(2,1)S(1)}, bf16[256,256]{1,0:T(8,128)(2,1)S(1)}, u32[]{:S(2)}, u32[]{:S(2)}) collective-permute-start(bf16[256,256]{1,0:T(8,128)(2,1)S(1)} %get-tuple-element.52), channel_id=1, source_target_pairs={{0,16},{1,17},{2,18},{3,19},{4,20},{5,21},{6,22},{7,23},{8,24},{9,... | collective-permute-start | bytes 393224 | tf_op jit(solution)/shard_map/ppermute | solution.py:25
  135.3 7.9 %collective-permute-start.16 = (bf16[256,256]{1,0:T(8,128)(2,1)S(1)}, bf16[256,256]{1,0:T(8,128)(2,1)S(1)}, u32[]{:S(2)}, u32[]{:S(2)}) collective-permute-start(bf16[256,256]{1,0:T(8,128)(2,1)S(1)} %get-tuple-element.45), channel_id=1, source_target_pairs={{0,48},{1,49},{2,50},{3,51},{4,52},{5,53},{6,54},{7,55},{8,56},{9,... | collective-permute-start | bytes 393224 | tf_op jit(solution)/shard_map/ppermute | solution.py:25
  139.7 6.6 %collective-permute-start.21 = (bf16[256,128]{1,0:T(8,128)(2,1)S(1)}, bf16[256,128]{1,0:T(8,128)(2,1)S(1)}, u32[]{:S(2)}, u32[]{:S(2)}) collective-permute-start(bf16[256,128]{1,0:T(8,128)(2,1)S(1)} %get-tuple-element.54), channel_id=1, source_target_pairs={{0,48},{1,49},{2,50},{3,51},{4,52},{5,53},{6,54},{7,55},{8,56},{9,... | collective-permute-start | bytes 196616 | tf_op jit(solution)/shard_map/ppermute | solution.py:25
  143.3 5.5 %collective-permute-start.17 = (bf16[256,128]{1,0:T(8,128)(2,1)S(1)}, bf16[256,128]{1,0:T(8,128)(2,1)S(1)}, u32[]{:S(2)}, u32[]{:S(2)}) collective-permute-start(bf16[256,128]{1,0:T(8,128)(2,1)S(1)} %get-tuple-element.47), channel_id=1, source_target_pairs={{0,16},{1,17},{2,18},{3,19},{4,20},{5,21},{6,22},{7,23},{8,24},{9,... | collective-permute-start | bytes 196616 | tf_op jit(solution)/shard_map/ppermute | solution.py:25

commit v4 on v3

v4 whole, which is shorter than its diff:
```python
import functools

import jax
import jax.numpy as jnp
from jax import lax
from jax.experimental import pallas as pl
from jax.experimental.pallas import tpu as pltpu
from jax.sharding import PartitionSpec as P

NY, NZH, NCORE, NX, NZL = 4, 4, 2, 4, 2
NROW, NCOL = NY * NZH * NCORE, NX * NZL
CHIPS = NY * NZH
STEPS = ((1, 3), (3, 1))
TILE = 128
BF16 = jnp.bfloat16
F32 = jnp.float32
MB = 1024 * 1024


def flip(value, y=0, z=0, core=0):
    pairs = []
    for row in range(NROW):
        there = row ^ ((y * NZH + z) * NCORE + core)
        pairs += [(row * NCOL + col, there * NCOL + col) for col in range(NCOL)]
    return lax.ppermute(value, ("row", "col"), pairs)


def in_vmem(kernel, results, operands, name, flops=MB, grant=16, **extra):
    spec = pl.BlockSpec(memory_space=pltpu.VMEM)
    outs = [shape if plain else pltpu.VMEM(shape.shape, shape.dtype) for shape, plain in results]
    out_specs = [pl.BlockSpec() if plain else spec for _, plain in results]
    return pl.pallas_call(
        kernel,
        in_specs=[spec] * len(operands),
        out_specs=out_specs,
        out_shape=outs,
        compiler_params=pltpu.CompilerParams(vmem_limit_bytes=grant * MB),
        cost_estimate=pl.CostEstimate(flops=flops, bytes_accessed=3 * MB, transcendentals=0),
        name=name,
        **extra,
    )(*[pltpu.with_memory_space_constraint(v, pltpu.VMEM) for v in operands])


def kept(shape, dtype):
    return jax.ShapeDtypeStruct(shape, dtype), False


def plain(shape, dtype):
    return jax.ShapeDtypeStruct(shape, dtype), True


def adjacency_kernel(place, where, masks, out, held, sems):
    count, slots = masks.shape[0], masks.shape[1]
    copies = [pltpu.make_async_copy(masks.at[j], held.at[j], sems.at[j]) for j in range(count)]
    for copy in copies:
        copy.start()
    for j, copy in enumerate(copies):
        cols = pl.ds(pl.multiple_of(place[j] * TILE, TILE), TILE)
        out[:, cols] = jnp.zeros((out.shape[0], TILE), BF16)
        copy.wait()
        for k in range(slots):
            at = pl.ds(pl.multiple_of(where[j * slots + k] * TILE, TILE), TILE)
            out[at, cols] = out[at, cols] + held[j, k].astype(F32).astype(BF16)


def adjacency(masks, place, where):
    count = masks.shape[0]
    return pl.pallas_call(
        adjacency_kernel,
        grid_spec=pltpu.PrefetchScalarGridSpec(
            num_scalar_prefetch=2,
            grid=(1,),
            in_specs=[pl.BlockSpec(memory_space=pl.ANY)],
            out_specs=pl.BlockSpec(memory_space=pltpu.VMEM),
            scratch_shapes=[pltpu.VMEM(masks.shape, masks.dtype), pltpu.SemaphoreType.DMA((count,))],
        ),
        out_shape=pltpu.VMEM((NCOL * TILE, count * TILE), BF16),
        compiler_params=pltpu.CompilerParams(vmem_limit_bytes=16 * MB),
        cost_estimate=pl.CostEstimate(flops=0, bytes_accessed=14 * MB, transcendentals=0),
        name="adjacency",
    )(place, where, pltpu.with_memory_space_constraint(masks, pltpu.HBM))


def gather_kernel(cores, dys, adj, *refs):
    parts, out = refs[: 2 * len(cores)], refs[-1]
    start = refs[-2] if len(refs) > len(parts) + 1 else None
    half = parts[0].shape[1]
    depth = NZH * TILE
    rows = 2 * TILE
    for r in range(0, out.shape[0], rows):
        for h in range(2):
            cols = slice(h * half, (h + 1) * half)
            value = None if start is None else start[r : r + rows, cols]
            for i, core in enumerate(cores):
                at = [(core * NY + dy) * depth for dy in dys[h]]
                lhs = jnp.concatenate([adj[r : r + rows, a : a + depth] for a in at], axis=1)
                term = jnp.dot(lhs, parts[2 * i + h][...], preferred_element_type=F32)
                value = term if value is None else value + term
            out[r : r + rows, cols] = value.astype(out.dtype)


def gather_matmul(adj, parts, cores, dys, start, dtype, name):
    rows, width = adj.shape[0], 2 * parts[0].shape[1]
    operands = [adj, *parts] + ([] if start is None else [start])
    flops = 2 * rows * width * parts[0].shape[0] * len(cores)
    return in_vmem(functools.partial(gather_kernel, cores, dys), [kept((rows, width), dtype)], operands, name, flops)[0]


def node_kernel(parts, base, degf_row, w_neigh, cotangent, grad, scaled_t, out):
    total = parts[0:TILE, :].astype(F32)
    for i in range(1, NCOL):
        total = total + parts[i * TILE : (i + 1) * TILE, :].astype(F32)
    degf_col = jnp.broadcast_to(degf_row[...], (TILE, TILE)).T[:, :1]
    mean = (total / degf_col).astype(BF16)
    pre = base[...] + jnp.dot(mean, w_neigh[...], preferred_element_type=F32)
    sig = jax.nn.sigmoid(pre)
    out[...] = (pre * sig).astype(BF16)
    slope = sig * (1.0 + pre * (1.0 - sig))
    grad_pre = (cotangent[...].astype(F32) * slope).astype(BF16)
    grad[...] = grad_pre
    proj_t = lax.dot_general(w_neigh[...], grad_pre, (((1,), (1,)), ((), ())), preferred_element_type=F32)
    scaled = (proj_t / degf_row[...]).astype(BF16)
    for i in range(NCOL):
        scaled_t[i, :, :] = scaled


def node_step(parts, base, degf_row, w_neigh, cotangent):
    rows, width = cotangent.shape
    results = [kept((rows, width), BF16), kept((NCOL, width, rows), BF16), plain((rows, width), BF16)]
    operands = (parts, base, degf_row, w_neigh, cotangent)
    return in_vmem(node_kernel, results, operands, "node_step", 4 * rows * width * width)


def spread_kernel(core, parts, adj, keep, send):
    lhs = jnp.concatenate([parts[i] for i in range(NCOL)], axis=1)
    half = lhs.shape[0] // 2
    depth = NZH * TILE
    for dy in range(NY):
        at = (core * NY + dy) * depth
        value = jnp.dot(lhs, adj[:, at : at + depth], preferred_element_type=F32).astype(BF16)
        for h, (k1, k2) in enumerate(STEPS):
            out, order = (keep, (0, k1)) if dy in (0, k1) else (send, (k2, k1 ^ k2))
            to = order.index(dy) * depth
            out[h, :, to : to + depth] = value[h * half : (h + 1) * half, :]


def spread_matmul(parts, adj, core, name):
    width = parts.shape[1]
    shape = (2, width // 2, 2 * NZH * TILE)
    flops = 2 * adj.shape[0] * width * CHIPS * TILE
    return in_vmem(functools.partial(spread_kernel, core), [kept(shape, BF16)] * 2, (parts, adj), name, flops)


def total(refs):
    value = refs[0][...].astype(F32)
    for ref in refs[1:]:
        value = value + ref[...].astype(F32)
    return value


def both_halves_kernel(mine, theirs, *outs):
    for h, out in enumerate(outs):
        out[...] = (mine[h].astype(F32) + theirs[h].astype(F32)).astype(BF16)


def both_halves(mine, theirs):
    return in_vmem(both_halves_kernel, [kept(mine.shape[1:], BF16)] * 2, (mine, theirs), "both_halves")


def first_split_kernel(h, mine, theirs, got, stay, go):
    value = mine[h].astype(F32) + theirs[h].astype(F32) + got[...].astype(F32)
    depth = stay.shape[1]
    stay[...] = value[:, :depth]
    go[...] = value[:, depth:].astype(BF16)


def first_split(h, mine, theirs, got, name):
    shape = (got.shape[0], got.shape[1] // 2)
    results = [kept(shape, F32), kept(shape, BF16)]
    return in_vmem(functools.partial(first_split_kernel, h), results, (mine, theirs, got), name)


def split_kernel(stays, goes, *refs):
    value = total(refs[:-2])
    for out, tiles in zip(refs[-2:], (stays, goes)):
        for i, tile in enumerate(tiles):
            part = value[:, tile * TILE : (tile + 1) * TILE]
            out[:, i * TILE : (i + 1) * TILE] = part.astype(out.dtype)


def add_split(values, stays, goes, name):
    rows = values[0].shape[0]
    results = [kept((rows, len(stays) * TILE), F32), kept((rows, len(goes) * TILE), BF16)]
    return in_vmem(functools.partial(split_kernel, stays, goes), results, values, name)


def last_kernel(*refs):
    own, out = refs[-2:]
    back = jnp.concatenate([total(refs[0:2]), total(refs[2:4])], axis=0)
    out[...] = (own[...] + back.T).astype(BF16)


def last_sum(values, own):
    return in_vmem(last_kernel, [plain(own.shape, BF16)], (*values, own), "last_sum")[0]


def body(features, degrees, tile_rows, tile_masks, w_self, w_neigh, bias, cotangent):
    half = features.shape[1] // 2
    row = lax.axis_index("row").astype(jnp.int32)

    differ = jnp.arange(NROW, dtype=jnp.int32) ^ row
    adj = adjacency(tile_masks[0, 0], (differ % NCORE) * CHIPS + differ // NCORE, tile_rows[0, 0].reshape(-1))
    degf_row = degrees.astype(F32)[None, :]
    base = jnp.dot(features, w_self, preferred_element_type=F32) + bias[None, :]

    chunks = [features[:, :half], features[:, half:]]
    firsts = [flip(v, z=k1) for v, (k1, _) in zip(chunks, STEPS)]
    pairs = [jnp.concatenate([v, r], axis=0) for v, r in zip(chunks, firsts)]
    seconds = [flip(v, z=k2) for v, (_, k2) in zip(pairs, STEPS)]
    planes = []
    for v, first, second, (k1, k2) in zip(chunks, firsts, seconds, STEPS):
        tiles = {0: v, k1: first, k2: second[:TILE], k1 ^ k2: second[TILE:]}
        planes.append(jnp.concatenate([tiles[i] for i in range(NZH)], axis=0))
    thirds = [flip(v, y=k1) for v, (k1, _) in zip(planes, STEPS)]
    *thirds, adj, base, degf_row = lax.optimization_barrier((*thirds, adj, base, degf_row))
    near = [jnp.concatenate([v, r], axis=0) for v, r in zip(planes, thirds)]
    far = [flip(v, y=k2) for v, (_, k2) in zip(near, STEPS)]
    first, second = [(0, k1) for k1, _ in STEPS], [(k2, k1 ^ k2) for k1, k2 in STEPS]
    near = near + [flip(v, core=1) for v in near]
    part = gather_matmul(adj, near, (0, 1), first, None, F32, "gather_near")
    *far, part = lax.optimization_barrier((*far, part))
    other = [flip(v, core=1) for v in far]
    part = gather_matmul(adj, far, (0,), second, part, F32, "gather_far")
    *other, part = lax.optimization_barrier((*other, part))
    summed = gather_matmul(adj, other, (1,), second, part, BF16, "gather_far_other")

    arrived = lax.all_to_all(summed, "col", 0, 0, tiled=True)
    grad_pre, scaled_t, output = node_step(arrived, base, degf_row, w_neigh, cotangent)

    table = lax.all_to_all(scaled_t, "col", 0, 0, tiled=True)
    own = lax.dot_general(grad_pre, w_self, (((1,), (1,)), ((), ())), preferred_element_type=F32)
    keep_out, send_out = spread_matmul(table, adj, 1, "spread_other")
    send_in, keep_in = flip(send_out, core=1), flip(keep_out, core=1)
    keep, send = spread_matmul(table, adj, 0, "spread_own")

    ends = []
    for h, (value, (k1, k2)) in enumerate(zip(both_halves(send, send_in), STEPS)):
        got = flip(value, y=k2)
        stay, go = first_split(h, keep, keep_in, got, "add_y1")
        got = flip(go, y=k1)
        stay, go = add_split((stay, got), (0, k1), (k2, k1 ^ k2), "add_y2")
        got = flip(go, z=k2)
        stay, go = add_split((stay, got), (0,), (1,), "add_z1")
        ends += [stay, flip(go, z=k1)]
    grad_features = last_sum(ends, own)
    return output, grad_features


def solution(mesh):
    both = P(("row", "col"), None)
    return jax.shard_map(
        body,
        mesh=mesh,
        in_specs=(
            both,
            P(("row", "col")),
            P("row", "col", None, None),
            P("row", "col", None, None, None, None),
            P(),
            P(),
            P(),
            both,
        ),
        out_specs=(both, both),
        check_vma=False,
    )
```

time: 151 us -> 135 us (0.89)
  blocking collectives: 18.4 us -> 38.1 us
  Pallas kernels: 36.3 us -> 17.7 us
  waiting for transfers between devices: 52.2 us -> 40.7 us
  starting transfers between devices: 38.9 us -> 33 us
    all_to_all x0 -> x1, blocking collectives: none -> 20.4 us  [body(): arrived = lax.all_to_all(summed, 'col', 0, 0, tiled=True)]
    pallas_call x13 -> x14, Pallas kernels: 26.8 us -> 12.2 us  [in_vmem(): pl.pallas_call(kernel, in_specs=[spec] * len(operands), out_specs=out_spe...]
    all_to_all x1 -> x0, waiting for transfers between devices: 14.5 us -> none  [body(): arrived = lax.all_to_all(summed, 'col', 0, 0, tiled=True)]
    all_to_all x1 -> x0, starting transfers between devices: 5.75 us -> none  [body(): arrived = lax.all_to_all(summed, 'col', 0, 0, tiled=True)]
    pallas_call x1, Pallas kernels: 9.51 us -> 5.55 us  [adjacency(): pl.pallas_call(adjacency_kernel, grid_spec=pltpu.PrefetchScalarGridSpec(n...]
    ppermute x22, waiting for transfers between devices: 37.8 us -> 40.7 us  [flip(): return lax.ppermute(value, ('row', 'col'), pairs)]
  transfers between devices with their start and end apart: 23 -> 22, of which waited for: 12 -> 10; matrix products, arithmetic and copies ran while one was open for 1% -> 2% of each run, Pallas kernels for 15% -> 9%
where the time goes in v4:
time: 135 us; the launch traced here: 134 us
  waiting for transfers between devices  40.7 us (30%)
  blocking collectives  38.1 us (28%)
  starting transfers between devices  33 us (24%)
  Pallas kernels  17.7 us (13%)
  local copies, waits for them, and re-layouts  1.89 us (1%)
    ppermute x22, waiting for transfers between devices, flip(): return lax.ppermute(value, ('row', 'col'), pairs)  40.7 us
    ppermute x22, starting transfers between devices, flip(): return lax.ppermute(value, ('row', 'col'), pairs)  33 us
    all_to_all x1, blocking collectives, body(): arrived = lax.all_to_all(summed, 'col', 0, 0, tiled=True)  20.4 us
    all_to_all x1, blocking collectives, body(): table = lax.all_to_all(scaled_t, 'col', 0, 0, tiled=True)  17.7 us
    pallas_call x14, Pallas kernels, in_vmem(): pl.pallas_call(kernel, in_specs=[spec] * len(operands), out_specs=out_spe...  12.2 us
    pallas_call x1, Pallas kernels, adjacency(): pl.pallas_call(adjacency_kernel, grid_spec=pltpu.PrefetchScalarGridSpec(n...  5.55 us
  transfers between devices with their start and end apart: 22, of which 10 were waited for; matrix products, arithmetic and copies ran while one was open for 2% of the time, Pallas kernels for 9%

profile of v4, /device:TPU:32, one launch (start us, length us, event | category | flops | bytes accessed | tf_op | source)
XLA Modules:
  0.0 133.6 jit_solution(18398201914465278826)
XLA Ops:
  0.6 0.9 constant_dynamic-update-slice_fusion.4
  1.6 3.4 %collective-permute-start = (bf16[128,256]{1,0:T(8,128)(2,1)S(1)}, bf16[128,256]{1,0:T(8,128)(2,1)S(1)}, u32[]{:S(2)}, u32[]{:S(2)}) collective-permute-start(bf16[128,256]{1,0:T(8,128)(2,1)S(1)} %get-tuple-element.70), channel_id=1, source_target_pairs={{0,16},{1,17},{2,18},{3,19},{4,20},{5,21},{6,22},{7,23},{8,24},{9,... | collective-permute-start | bytes 196616 | tf_op jit(solution)/shard_map/ppermute | solution.py:25
  4.9 3.6 %collective-permute-start.3 = (bf16[128,256]{1,0:T(8,128)(2,1)S(1)}, bf16[128,256]{1,0:T(8,128)(2,1)S(1)}, u32[]{:S(2)}, u32[]{:S(2)}) collective-permute-start(bf16[128,256]{1,0:T(8,128)(2,1)S(1)} %get-tuple-element.71), channel_id=1, source_target_pairs={{0,48},{1,49},{2,50},{3,51},{4,52},{5,53},{6,54},{7,55},{8,56},{9,... | collective-permute-start | bytes 196616 | tf_op jit(solution)/shard_map/ppermute | solution.py:25
  9.2 4.1 %collective-permute-start.1 = (bf16[256,256]{1,0:T(8,128)(2,1)S(1)}, bf16[256,256]{1,0:T(8,128)(2,1)S(1)}, u32[]{:S(2)}, u32[]{:S(2)}) collective-permute-start(bf16[256,256]{1,0:T(8,128)(2,1)S(1)} %pad_maximum_fusion.3), channel_id=1, source_target_pairs={{0,48},{1,49},{2,50},{3,51},{4,52},{5,53},{6,54},{7,55},{8,56},{9,... | collective-permute-start | bytes 393224 | tf_op jit(solution)/shard_map/ppermute | solution.py:25
  13.9 5.0 %collective-permute-done.1 = bf16[256,256]{1,0:T(8,128)(2,1)S(1)} collective-permute-done((bf16[256,256]{1,0:T(8,128)(2,1)S(1)}, bf16[256,256]{1,0:T(8,128)(2,1)S(1)}, u32[]{:S(2)}, u32[]{:S(2)}) %collective-permute-start.1) | collective-permute-done | bytes 131104 | tf_op jit(solution)/shard_map/ppermute | solution.py:25
  18.9 1.7 %collective-permute-start.2 = (bf16[512,256]{1,0:T(8,128)(2,1)S(1)}, bf16[512,256]{1,0:T(8,128)(2,1)S(1)}, u32[]{:S(2)}, u32[]{:S(2)}) collective-permute-start(bf16[512,256]{1,0:T(8,128)(2,1)S(1)} %pad_maximum_fusion.1), channel_id=1, source_target_pairs={{0,64},{1,65},{2,66},{3,67},{4,68},{5,69},{6,70},{7,71},{8,72},{9,... | collective-permute-start | bytes 786440 | tf_op jit(solution)/shard_map/ppermute | solution.py:25
  20.6 2.9 %collective-permute-start.5 = (bf16[512,256]{1,0:T(8,128)(2,1)S(1)}, bf16[512,256]{1,0:T(8,128)(2,1)S(1)}, u32[]{:S(2)}, u32[]{:S(2)}) collective-permute-start(bf16[512,256]{1,0:T(8,128)(2,1)S(1)} %pad_maximum_fusion.2), channel_id=1, source_target_pairs={{0,192},{1,193},{2,194},{3,195},{4,196},{5,197},{6,198},{7,199},{8... | collective-permute-start | bytes 786440 | tf_op jit(solution)/shard_map/ppermute | solution.py:25
  23.5 0.8 copy.11
  24.4 5.5 %adjacency.1.adj = bf16[1024,4096]{1,0:T(8,128)(2,1)S(1)} custom-call(s32[32]{0:T(128)S(1)} %fusion.1.place, s32[96]{0:T(128)S(1)} %reshape_squeeze.3.where, s32[32,3,128,128]{3,2,1,0:T(8,128)} %bitcast.13), custom_call_target="tpu_custom_call" | custom-call | bytes 14680064 | tf_op jit(solution)/shard_map/adjacency/pallas_call | solution.py:68
  31.0 1.3 collective-permute-start.6
  32.3 0.7 collective-permute-done.9.refs_3_
  33.0 2.3 %gather_near.1.refs_2_ = f32[1024,512]{1,0:T(8,128)S(1)} custom-call(bf16[1024,4096]{1,0:T(8,128)(2,1)S(1)} %adjacency.1.adj, bf16[1024,256]{1,0:T(8,128)(2,1)S(1)} %constant_dynamic-update-slice_fusion.refs_0_, bf16[1024,256]{1,0:T(8,128)(2,1)S(1)} %pad_maximum_fusion.refs_1_, bf16[1024,256]{1,0:T(8,128)(2,1)S(1)} %collective-permute-done.8.refs_2_, ...), custom_call_target="tpu_custom_call" | custom-call | flops 2147483648 | bytes 3145728 | tf_op jit(solution)/shard_map/gather_near/pallas_call | solution.py:32
  35.3 10.8 %collective-permute-done.6.refs_0_ = bf16[1024,256]{1,0:T(8,128)(2,1)S(1)} collective-permute-done((bf16[1024,256]{1,0:T(8,128)(2,1)S(1)}, bf16[1024,256]{1,0:T(8,128)(2,1)S(1)}, u32[]{:S(2)}, u32[]{:S(2)}) %collective-permute-start.6) | collective-permute-done | bytes 524320 | tf_op jit(solution)/shard_map/ppermute | solution.py:25
  46.6 1.2 gather_far.1.refs_2_
  48.0 0.7 collective-permute-done.11.refs_1_
  48.8 1.2 gather_far_other.1
  50.0 20.4 %all_to_all.16 = bf16[8,128,512]{2,1,0:T(8,128)(2,1)S(1)} all-to-all(bf16[8,128,512]{2,1,0:T(8,128)(2,1)S(1)} %bitcast.11), channel_id=1, replica_groups=mesh['row'=32,'col'=8] {'col'}, dimensions={0} | all-to-all | bytes 2097152 | tf_op jit(solution)/shard_map/all_to_all | solution.py:237
  70.4 1.1 node_step.1
  71.5 17.7 %all_to_all.17.parts = bf16[8,512,128]{2,1,0:T(8,128)(2,1)S(1)} all-to-all(bf16[8,512,128]{2,1,0:T(8,128)(2,1)S(1)} %get-tuple-element.46), channel_id=1, replica_groups=mesh['row'=32,'col'=8] {'col'}, dimensions={0} | all-to-all | bytes 2097152 | tf_op jit(solution)/shard_map/all_to_all | solution.py:240
  89.3 2.3 %spread_other.1 = (bf16[2,256,1024]{2,1,0:T(8,128)(2,1)S(1)}, bf16[2,256,1024]{2,1,0:T(8,128)(2,1)S(1)}) custom-call(bf16[8,512,128]{2,1,0:T(8,128)(2,1)S(1)} %all_to_all.17.parts, bf16[1024,4096]{1,0:T(8,128)(2,1)S(1)} %adjacency.1.adj), custom_call_target="tpu_custom_call" | custom-call | flops 2147483648 | bytes 3145728 | tf_op jit(solution)/shard_map/spread_other/pallas_call | solution.py:32
  92.2 2.3 %spread_own.1 = (bf16[2,256,1024]{2,1,0:T(8,128)(2,1)S(1)}, bf16[2,256,1024]{2,1,0:T(8,128)(2,1)S(1)}) custom-call(bf16[8,512,128]{2,1,0:T(8,128)(2,1)S(1)} %all_to_all.17.parts, bf16[1024,4096]{1,0:T(8,128)(2,1)S(1)} %adjacency.1.adj), custom_call_target="tpu_custom_call" | custom-call | flops 2147483648 | bytes 3145728 | tf_op jit(solution)/shard_map/spread_own/pallas_call | solution.py:32
  95.0 1.9 %collective-permute-start.14 = (bf16[256,1024]{1,0:T(8,128)(2,1)S(1)}, bf16[256,1024]{1,0:T(8,128)(2,1)S(1)}, u32[]{:S(2)}, u32[]{:S(2)}) collective-permute-start(bf16[256,1024]{1,0:T(8,128)(2,1)S(1)} %get-tuple-element.51), channel_id=1, source_target_pairs={{0,192},{1,193},{2,194},{3,195},{4,196},{5,197},{6,198},{7,199},{8... | collective-permute-start | bytes 1572872 | tf_op jit(solution)/shard_map/ppermute | solution.py:25
  96.9 11.9 %collective-permute-done.18.got = bf16[256,1024]{1,0:T(8,128)(2,1)S(1)} collective-permute-done((bf16[256,1024]{1,0:T(8,128)(2,1)S(1)}, bf16[256,1024]{1,0:T(8,128)(2,1)S(1)}, u32[]{:S(2)}, u32[]{:S(2)}) %collective-permute-start.18) | collective-permute-done | bytes 524320 | tf_op jit(solution)/shard_map/ppermute | solution.py:25
  109.0 1.8 %collective-permute-start.19 = (bf16[256,512]{1,0:T(8,128)(2,1)S(1)}, bf16[256,512]{1,0:T(8,128)(2,1)S(1)}, u32[]{:S(2)}, u32[]{:S(2)}) collective-permute-start(bf16[256,512]{1,0:T(8,128)(2,1)S(1)} %get-tuple-element.60), channel_id=1, source_target_pairs={{0,192},{1,193},{2,194},{3,195},{4,196},{5,197},{6,198},{7,199},{8... | collective-permute-start | bytes 786440 | tf_op jit(solution)/shard_map/ppermute | solution.py:25
  111.1 6.7 %collective-permute-done.19.refs_1_ = bf16[256,512]{1,0:T(8,128)(2,1)S(1)} collective-permute-done((bf16[256,512]{1,0:T(8,128)(2,1)S(1)}, bf16[256,512]{1,0:T(8,128)(2,1)S(1)}, u32[]{:S(2)}, u32[]{:S(2)}) %collective-permute-start.19) | collective-permute-done | bytes 262176 | tf_op jit(solution)/shard_map/ppermute | solution.py:25
  117.8 1.3 collective-permute-start.20
  119.2 2.9 %collective-permute-start.16 = (bf16[256,256]{1,0:T(8,128)(2,1)S(1)}, bf16[256,256]{1,0:T(8,128)(2,1)S(1)}, u32[]{:S(2)}, u32[]{:S(2)}) collective-permute-start(bf16[256,256]{1,0:T(8,128)(2,1)S(1)} %get-tuple-element.55), channel_id=1, source_target_pairs={{0,48},{1,49},{2,50},{3,51},{4,52},{5,53},{6,54},{7,55},{8,56},{9,... | collective-permute-start | bytes 393224 | tf_op jit(solution)/shard_map/ppermute | solution.py:25
  122.1 2.1 %collective-permute-done.20.refs_1_ = bf16[256,256]{1,0:T(8,128)(2,1)S(1)} collective-permute-done((bf16[256,256]{1,0:T(8,128)(2,1)S(1)}, bf16[256,256]{1,0:T(8,128)(2,1)S(1)}, u32[]{:S(2)}, u32[]{:S(2)}) %collective-permute-start.20) | collective-permute-done | bytes 131104 | tf_op jit(solution)/shard_map/ppermute | solution.py:25
  124.2 3.2 %collective-permute-start.21 = (bf16[256,128]{1,0:T(8,128)(2,1)S(1)}, bf16[256,128]{1,0:T(8,128)(2,1)S(1)}, u32[]{:S(2)}, u32[]{:S(2)}) collective-permute-start(bf16[256,128]{1,0:T(8,128)(2,1)S(1)} %get-tuple-element.64), channel_id=1, source_target_pairs={{0,48},{1,49},{2,50},{3,51},{4,52},{5,53},{6,54},{7,55},{8,56},{9,... | collective-permute-start | bytes 196616 | tf_op jit(solution)/shard_map/ppermute | solution.py:25
  127.5 2.4 %collective-permute-start.17 = (bf16[256,128]{1,0:T(8,128)(2,1)S(1)}, bf16[256,128]{1,0:T(8,128)(2,1)S(1)}, u32[]{:S(2)}, u32[]{:S(2)}) collective-permute-start(bf16[256,128]{1,0:T(8,128)(2,1)S(1)} %get-tuple-element.57), channel_id=1, source_target_pairs={{0,16},{1,17},{2,18},{3,19},{4,20},{5,21},{6,22},{7,23},{8,24},{9,... | collective-permute-start | bytes 196616 | tf_op jit(solution)/shard_map/ppermute | solution.py:25
  130.7 2.1 %collective-permute-done.17.refs_1_ = bf16[256,128]{1,0:T(8,128)(2,1)S(1)} collective-permute-done((bf16[256,128]{1,0:T(8,128)(2,1)S(1)}, bf16[256,128]{1,0:T(8,128)(2,1)S(1)}, u32[]{:S(2)}, u32[]{:S(2)}) %collective-permute-start.17) | collective-permute-done | bytes 65568 | tf_op jit(solution)/shard_map/ppermute | solution.py:25
  132.8 0.8 last_sum.1
  (55 shorter events, 5.5 us)
Async XLA Ops:
  0.6 29.3 %copy-start = (bf16[512,512]{1,0:T(8,128)(2,1)S(1)}, bf16[512,512]{1,0:T(8,128)(2,1)}, u32[]{:S(2)}) copy-start(bf16[512,512]{1,0:T(8,128)(2,1)} %param.12) | copy-start | bytes 1572868
  1.6 7.6 %collective-permute-start = (bf16[128,256]{1,0:T(8,128)(2,1)S(1)}, bf16[128,256]{1,0:T(8,128)(2,1)S(1)}, u32[]{:S(2)}, u32[]{:S(2)}) collective-permute-start(bf16[128,256]{1,0:T(8,128)(2,1)S(1)} %get-tuple-element.70), channel_id=1, source_target_pairs={{0,16},{1,17},{2,18},{3,19},{4,20},{5,21},{6,22},{7,23},{8,24},{9,... | collective-permute-start | bytes 196616 | tf_op jit(solution)/shard_map/ppermute | solution.py:25
  4.9 8.4 %collective-permute-start.3 = (bf16[128,256]{1,0:T(8,128)(2,1)S(1)}, bf16[128,256]{1,0:T(8,128)(2,1)S(1)}, u32[]{:S(2)}, u32[]{:S(2)}) collective-permute-start(bf16[128,256]{1,0:T(8,128)(2,1)S(1)} %get-tuple-element.71), channel_id=1, source_target_pairs={{0,48},{1,49},{2,50},{3,51},{4,52},{5,53},{6,54},{7,55},{8,56},{9,... | collective-permute-start | bytes 196616 | tf_op jit(solution)/shard_map/ppermute | solution.py:25
  9.2 9.7 %collective-permute-start.1 = (bf16[256,256]{1,0:T(8,128)(2,1)S(1)}, bf16[256,256]{1,0:T(8,128)(2,1)S(1)}, u32[]{:S(2)}, u32[]{:S(2)}) collective-permute-start(bf16[256,256]{1,0:T(8,128)(2,1)S(1)} %pad_maximum_fusion.3), channel_id=1, source_target_pairs={{0,48},{1,49},{2,50},{3,51},{4,52},{5,53},{6,54},{7,55},{8,56},{9,... | collective-permute-start | bytes 393224 | tf_op jit(solution)/shard_map/ppermute | solution.py:25
  13.3 7.3 %collective-permute-start.4 = (bf16[256,256]{1,0:T(8,128)(2,1)S(1)}, bf16[256,256]{1,0:T(8,128)(2,1)S(1)}, u32[]{:S(2)}, u32[]{:S(2)}) collective-permute-start(bf16[256,256]{1,0:T(8,128)(2,1)S(1)} %pad_maximum_fusion.4), channel_id=1, source_target_pairs={{0,16},{1,17},{2,18},{3,19},{4,20},{5,21},{6,22},{7,23},{8,24},{9,... | collective-permute-start | bytes 393224 | tf_op jit(solution)/shard_map/ppermute | solution.py:25
  18.9 11.3 %collective-permute-start.2 = (bf16[512,256]{1,0:T(8,128)(2,1)S(1)}, bf16[512,256]{1,0:T(8,128)(2,1)S(1)}, u32[]{:S(2)}, u32[]{:S(2)}) collective-permute-start(bf16[512,256]{1,0:T(8,128)(2,1)S(1)} %pad_maximum_fusion.1), channel_id=1, source_target_pairs={{0,64},{1,65},{2,66},{3,67},{4,68},{5,69},{6,70},{7,71},{8,72},{9,... | collective-permute-start | bytes 786440 | tf_op jit(solution)/shard_map/ppermute | solution.py:25
  20.6 9.6 %collective-permute-start.5 = (bf16[512,256]{1,0:T(8,128)(2,1)S(1)}, bf16[512,256]{1,0:T(8,128)(2,1)S(1)}, u32[]{:S(2)}, u32[]{:S(2)}) collective-permute-start(bf16[512,256]{1,0:T(8,128)(2,1)S(1)} %pad_maximum_fusion.2), channel_id=1, source_target_pairs={{0,192},{1,193},{2,194},{3,195},{4,196},{5,197},{6,198},{7,199},{8... | collective-permute-start | bytes 786440 | tf_op jit(solution)/shard_map/ppermute | solution.py:25
  24.4 5.6 %copy-start.3 = (bf16[128,512]{1,0:T(8,128)(2,1)S(1)}, bf16[128,512]{1,0:T(8,128)(2,1)}, u32[]{:S(2)}) copy-start(bf16[128,512]{1,0:T(8,128)(2,1)} %param.8) | copy-start | bytes 393220
  24.4 5.6 %copy-start.4 = (f32[512]{0:T(512)S(1)}, f32[512]{0:T(512)}, u32[]{:S(2)}) copy-start(f32[512]{0:T(512)} %param.14) | copy-start | bytes 6148
  30.3 2.0 %collective-permute-start.8 = (bf16[1024,256]{1,0:T(8,128)(2,1)S(1)}, bf16[1024,256]{1,0:T(8,128)(2,1)S(1)}, u32[]{:S(2)}, u32[]{:S(2)}) collective-permute-start(bf16[1024,256]{1,0:T(8,128)(2,1)S(1)} %constant_dynamic-update-slice_fusion.refs_0_), channel_id=1, source_target_pairs={{0,8},{1,9},{2,10},{3,11},{4,12},{5,13},{6,14},{7,15},{8,0},{9,1},... | collective-permute-start | bytes 1572872 | tf_op jit(solution)/shard_map/ppermute | solution.py:25
  30.4 2.6 %collective-permute-start.9 = (bf16[1024,256]{1,0:T(8,128)(2,1)S(1)}, bf16[1024,256]{1,0:T(8,128)(2,1)S(1)}, u32[]{:S(2)}, u32[]{:S(2)}) collective-permute-start(bf16[1024,256]{1,0:T(8,128)(2,1)S(1)} %pad_maximum_fusion.refs_1_), channel_id=1, source_target_pairs={{0,8},{1,9},{2,10},{3,11},{4,12},{5,13},{6,14},{7,15},{8,0},{9,1},... | collective-permute-start | bytes 1572872 | tf_op jit(solution)/shard_map/ppermute | solution.py:25
  31.0 15.1 %collective-permute-start.6 = (bf16[1024,256]{1,0:T(8,128)(2,1)S(1)}, bf16[1024,256]{1,0:T(8,128)(2,1)S(1)}, u32[]{:S(2)}, u32[]{:S(2)}) collective-permute-start(bf16[1024,256]{1,0:T(8,128)(2,1)S(1)} %constant_dynamic-update-slice_fusion.refs_0_), channel_id=1, source_target_pairs={{0,192},{1,193},{2,194},{3,195},{4,196},{5,197},{6,198},{7,199},{8... | collective-permute-start | bytes 1572872 | tf_op jit(solution)/shard_map/ppermute | solution.py:25
  32.3 13.8 %collective-permute-start.7 = (bf16[1024,256]{1,0:T(8,128)(2,1)S(1)}, bf16[1024,256]{1,0:T(8,128)(2,1)S(1)}, u32[]{:S(2)}, u32[]{:S(2)}) collective-permute-start(bf16[1024,256]{1,0:T(8,128)(2,1)S(1)} %pad_maximum_fusion.refs_1_), channel_id=1, source_target_pairs={{0,64},{1,65},{2,66},{3,67},{4,68},{5,69},{6,70},{7,71},{8,72},{9,... | collective-permute-start | bytes 1572872 | tf_op jit(solution)/shard_map/ppermute | solution.py:25
  46.1 1.9 %collective-permute-start.10 = (bf16[1024,256]{1,0:T(8,128)(2,1)S(1)}, bf16[1024,256]{1,0:T(8,128)(2,1)S(1)}, u32[]{:S(2)}, u32[]{:S(2)}) collective-permute-start(bf16[1024,256]{1,0:T(8,128)(2,1)S(1)} %collective-permute-done.6.refs_0_), channel_id=1, source_target_pairs={{0,8},{1,9},{2,10},{3,11},{4,12},{5,13},{6,14},{7,15},{8,0},{9,1},... | collective-permute-start | bytes 1572872 | tf_op jit(solution)/shard_map/ppermute | solution.py:25
  46.1 2.7 %collective-permute-start.11 = (bf16[1024,256]{1,0:T(8,128)(2,1)S(1)}, bf16[1024,256]{1,0:T(8,128)(2,1)S(1)}, u32[]{:S(2)}, u32[]{:S(2)}) collective-permute-start(bf16[1024,256]{1,0:T(8,128)(2,1)S(1)} %collective-permute-done.7.refs_1_), channel_id=1, source_target_pairs={{0,8},{1,9},{2,10},{3,11},{4,12},{5,13},{6,14},{7,15},{8,0},{9,1},... | collective-permute-start | bytes 1572872 | tf_op jit(solution)/shard_map/ppermute | solution.py:25
  47.9 22.5 %copy-start.1 = (bf16[512,512]{1,0:T(8,128)(2,1)S(1)}, bf16[512,512]{1,0:T(8,128)(2,1)}, u32[]{:S(2)}) copy-start(bf16[512,512]{1,0:T(8,128)(2,1)} %w_neigh.1) | copy-start | bytes 1572868
  47.9 22.5 %copy-start.2 = (bf16[128,512]{1,0:T(8,128)(2,1)S(1)}, bf16[128,512]{1,0:T(8,128)(2,1)}, u32[]{:S(2)}) copy-start(bf16[128,512]{1,0:T(8,128)(2,1)} %cotangent.1) | copy-start | bytes 393220
  91.6 2.9 %collective-permute-start.13 = (bf16[2,256,1024]{2,1,0:T(8,128)(2,1)S(1)}, bf16[2,256,1024]{2,1,0:T(8,128)(2,1)S(1)}, u32[]{:S(2)}, u32[]{:S(2)}) collective-permute-start(bf16[2,256,1024]{2,1,0:T(8,128)(2,1)S(1)} %get-tuple-element.50), channel_id=1, source_target_pairs={{0,8},{1,9},{2,10},{3,11},{4,12},{5,13},{6,14},{7,15},{8,0},{9,1},... | collective-permute-start | bytes 3145736 | tf_op jit(solution)/shard_map/ppermute | solution.py:25
  91.7 5.2 %collective-permute-start.12 = (bf16[2,256,1024]{2,1,0:T(8,128)(2,1)S(1)}, bf16[2,256,1024]{2,1,0:T(8,128)(2,1)S(1)}, u32[]{:S(2)}, u32[]{:S(2)}) collective-permute-start(bf16[2,256,1024]{2,1,0:T(8,128)(2,1)S(1)} %get-tuple-element.48), channel_id=1, source_target_pairs={{0,8},{1,9},{2,10},{3,11},{4,12},{5,13},{6,14},{7,15},{8,0},{9,1},... | collective-permute-start | bytes 3145736 | tf_op jit(solution)/shard_map/ppermute | solution.py:25
  94.8 14.0 %collective-permute-start.18 = (bf16[256,1024]{1,0:T(8,128)(2,1)S(1)}, bf16[256,1024]{1,0:T(8,128)(2,1)S(1)}, u32[]{:S(2)}, u32[]{:S(2)}) collective-permute-start(bf16[256,1024]{1,0:T(8,128)(2,1)S(1)} %get-tuple-element.58), channel_id=1, source_target_pairs={{0,64},{1,65},{2,66},{3,67},{4,68},{5,69},{6,70},{7,71},{8,72},{9,... | collective-permute-start | bytes 1572872 | tf_op jit(solution)/shard_map/ppermute | solution.py:25
  95.0 15.9 %collective-permute-start.14 = (bf16[256,1024]{1,0:T(8,128)(2,1)S(1)}, bf16[256,1024]{1,0:T(8,128)(2,1)S(1)}, u32[]{:S(2)}, u32[]{:S(2)}) collective-permute-start(bf16[256,1024]{1,0:T(8,128)(2,1)S(1)} %get-tuple-element.51), channel_id=1, source_target_pairs={{0,192},{1,193},{2,194},{3,195},{4,196},{5,197},{6,198},{7,199},{8... | collective-permute-start | bytes 1572872 | tf_op jit(solution)/shard_map/ppermute | solution.py:25
  109.0 8.8 %collective-permute-start.19 = (bf16[256,512]{1,0:T(8,128)(2,1)S(1)}, bf16[256,512]{1,0:T(8,128)(2,1)S(1)}, u32[]{:S(2)}, u32[]{:S(2)}) collective-permute-start(bf16[256,512]{1,0:T(8,128)(2,1)S(1)} %get-tuple-element.60), channel_id=1, source_target_pairs={{0,192},{1,193},{2,194},{3,195},{4,196},{5,197},{6,198},{7,199},{8... | collective-permute-start | bytes 786440 | tf_op jit(solution)/shard_map/ppermute | solution.py:25
  111.0 8.1 %collective-permute-start.15 = (bf16[256,512]{1,0:T(8,128)(2,1)S(1)}, bf16[256,512]{1,0:T(8,128)(2,1)S(1)}, u32[]{:S(2)}, u32[]{:S(2)}) collective-permute-start(bf16[256,512]{1,0:T(8,128)(2,1)S(1)} %get-tuple-element.53), channel_id=1, source_target_pairs={{0,64},{1,65},{2,66},{3,67},{4,68},{5,69},{6,70},{7,71},{8,72},{9,... | collective-permute-start | bytes 786440 | tf_op jit(solution)/shard_map/ppermute | solution.py:25
  117.8 6.4 %collective-permute-start.20 = (bf16[256,256]{1,0:T(8,128)(2,1)S(1)}, bf16[256,256]{1,0:T(8,128)(2,1)S(1)}, u32[]{:S(2)}, u32[]{:S(2)}) collective-permute-start(bf16[256,256]{1,0:T(8,128)(2,1)S(1)} %get-tuple-element.62), channel_id=1, source_target_pairs={{0,16},{1,17},{2,18},{3,19},{4,20},{5,21},{6,22},{7,23},{8,24},{9,... | collective-permute-start | bytes 393224 | tf_op jit(solution)/shard_map/ppermute | solution.py:25
  119.2 8.2 %collective-permute-start.16 = (bf16[256,256]{1,0:T(8,128)(2,1)S(1)}, bf16[256,256]{1,0:T(8,128)(2,1)S(1)}, u32[]{:S(2)}, u32[]{:S(2)}) collective-permute-start(bf16[256,256]{1,0:T(8,128)(2,1)S(1)} %get-tuple-element.55), channel_id=1, source_target_pairs={{0,48},{1,49},{2,50},{3,51},{4,52},{5,53},{6,54},{7,55},{8,56},{9,... | collective-permute-start | bytes 393224 | tf_op jit(solution)/shard_map/ppermute | solution.py:25
  124.2 6.5 %collective-permute-start.21 = (bf16[256,128]{1,0:T(8,128)(2,1)S(1)}, bf16[256,128]{1,0:T(8,128)(2,1)S(1)}, u32[]{:S(2)}, u32[]{:S(2)}) collective-permute-start(bf16[256,128]{1,0:T(8,128)(2,1)S(1)} %get-tuple-element.64), channel_id=1, source_target_pairs={{0,48},{1,49},{2,50},{3,51},{4,52},{5,53},{6,54},{7,55},{8,56},{9,... | collective-permute-start | bytes 196616 | tf_op jit(solution)/shard_map/ppermute | solution.py:25
  127.5 5.4 %collective-permute-start.17 = (bf16[256,128]{1,0:T(8,128)(2,1)S(1)}, bf16[256,128]{1,0:T(8,128)(2,1)S(1)}, u32[]{:S(2)}, u32[]{:S(2)}) collective-permute-start(bf16[256,128]{1,0:T(8,128)(2,1)S(1)} %get-tuple-element.57), channel_id=1, source_target_pairs={{0,16},{1,17},{2,18},{3,19},{4,20},{5,21},{6,22},{7,23},{8,24},{9,... | collective-permute-start | bytes 196616 | tf_op jit(solution)/shard_map/ppermute | solution.py:25

commit v5 on v4

v5 whole, which is shorter than its diff:
```python
import functools

import jax
import jax.numpy as jnp
from jax import lax
from jax.experimental import pallas as pl
from jax.experimental.pallas import tpu as pltpu
from jax.sharding import PartitionSpec as P

NY, NZH, NCORE, NX, NZL = 4, 4, 2, 4, 2
NROW, NCOL = NY * NZH * NCORE, NX * NZL
CHIPS = NY * NZH
RING = (0, 1, 3, 2)
TILE = 128
BF16 = jnp.bfloat16
F32 = jnp.float32
MB = 1024 * 1024


def flip(value, y=0, z=0, core=0):
    pairs = []
    for row in range(NROW):
        there = row ^ ((y * NZH + z) * NCORE + core)
        pairs += [(row * NCOL + col, there * NCOL + col) for col in range(NCOL)]
    return lax.ppermute(value, ("row", "col"), pairs)


def in_vmem(kernel, results, operands, name, flops=MB, grant=16, **extra):
    spec = pl.BlockSpec(memory_space=pltpu.VMEM)
    outs = [shape if plain else pltpu.VMEM(shape.shape, shape.dtype) for shape, plain in results]
    out_specs = [pl.BlockSpec() if plain else spec for _, plain in results]
    return pl.pallas_call(
        kernel,
        in_specs=[spec] * len(operands),
        out_specs=out_specs,
        out_shape=outs,
        compiler_params=pltpu.CompilerParams(vmem_limit_bytes=grant * MB),
        cost_estimate=pl.CostEstimate(flops=0, bytes_accessed=1024, transcendentals=0),
        name=name,
        **extra,
    )(*[pltpu.with_memory_space_constraint(v, pltpu.VMEM) for v in operands])


def kept(shape, dtype):
    return jax.ShapeDtypeStruct(shape, dtype), False


def plain(shape, dtype):
    return jax.ShapeDtypeStruct(shape, dtype), True


def adjacency_kernel(place, where, masks, out, held, sems):
    count, slots = masks.shape[0], masks.shape[1]
    copies = [pltpu.make_async_copy(masks.at[j], held.at[j], sems.at[j]) for j in range(count)]
    for copy in copies:
        copy.start()
    for j, copy in enumerate(copies):
        cols = pl.ds(pl.multiple_of(place[j] * TILE, TILE), TILE)
        out[:, cols] = jnp.zeros((out.shape[0], TILE), BF16)
        copy.wait()
        for k in range(slots):
            at = pl.ds(pl.multiple_of(where[j * slots + k] * TILE, TILE), TILE)
            out[at, cols] = out[at, cols] + held[j, k].astype(F32).astype(BF16)


def adjacency(masks, place, where):
    count = masks.shape[0]
    return pl.pallas_call(
        adjacency_kernel,
        grid_spec=pltpu.PrefetchScalarGridSpec(
            num_scalar_prefetch=2,
            grid=(1,),
            in_specs=[pl.BlockSpec(memory_space=pl.ANY)],
            out_specs=pl.BlockSpec(memory_space=pltpu.VMEM),
            scratch_shapes=[pltpu.VMEM(masks.shape, masks.dtype), pltpu.SemaphoreType.DMA((count,))],
        ),
        out_shape=pltpu.VMEM((NCOL * TILE, count * TILE), BF16),
        compiler_params=pltpu.CompilerParams(vmem_limit_bytes=16 * MB),
        cost_estimate=pl.CostEstimate(flops=0, bytes_accessed=14 * MB, transcendentals=0),
        name="adjacency",
    )(place, where, pltpu.with_memory_space_constraint(masks, pltpu.HBM))


def gather_kernel(starts, adj, *refs):
    parts, out = refs[: len(starts)], refs[-1]
    start = refs[-2] if len(refs) > len(parts) + 1 else None
    rows = 2 * TILE
    rhs = jnp.concatenate([part[...] for part in parts], axis=0)
    for r in range(0, out.shape[0], rows):
        lhs = [adj[r : r + rows, at : at + part.shape[0]] for at, part in zip(starts, parts)]
        value = jnp.dot(jnp.concatenate(lhs, axis=1), rhs, preferred_element_type=F32)
        if start is not None:
            value = value + start[r : r + rows, :]
        out[r : r + rows, :] = value.astype(out.dtype)


def gather_matmul(adj, parts, start, dtype, name):
    starts = [(core * NY + dy) * NZH * TILE + first for core, dy, first, _ in parts]
    parts = [part for *_, part in parts]
    rows, width = adj.shape[0], parts[0].shape[1]
    operands = [adj, *parts] + ([] if start is None else [start])
    return in_vmem(functools.partial(gather_kernel, starts), [kept((rows, width), dtype)], operands, name)[0]


def node_kernel(parts, base, degf_row, w_neigh, cotangent, grad, scaled_t, out):
    total = parts[0:TILE, :].astype(F32)
    for i in range(1, NCOL):
        total = total + parts[i * TILE : (i + 1) * TILE, :].astype(F32)
    degf_col = jnp.broadcast_to(degf_row[...], (TILE, TILE)).T[:, :1]
    mean = (total / degf_col).astype(BF16)
    pre = base[...] + jnp.dot(mean, w_neigh[...], preferred_element_type=F32)
    sig = jax.nn.sigmoid(pre)
    out[...] = (pre * sig).astype(BF16)
    slope = sig * (1.0 + pre * (1.0 - sig))
    grad_pre = (cotangent[...].astype(F32) * slope).astype(BF16)
    grad[...] = grad_pre
    proj_t = lax.dot_general(w_neigh[...], grad_pre, (((1,), (1,)), ((), ())), preferred_element_type=F32)
    scaled = (proj_t / degf_row[...]).astype(BF16)
    for i in range(NCOL):
        scaled_t[i, :, :] = scaled


def node_step(parts, base, degf_row, w_neigh, cotangent):
    rows, width = cotangent.shape
    results = [kept((rows, width), BF16), kept((NCOL, width, rows), BF16), plain((rows, width), BF16)]
    operands = (parts, base, degf_row, w_neigh, cotangent)
    return in_vmem(node_kernel, results, operands, "node_step", 4 * rows * width * width)


def spread_kernel(core, dys, parts, adj, *outs):
    lhs = jnp.concatenate([parts[i] for i in range(NCOL)], axis=1)
    depth = NZH * TILE
    for i, dy in enumerate(dys):
        at = (core * NY + dy) * depth
        value = jnp.dot(lhs, adj[:, at : at + depth], preferred_element_type=F32)
        outs[0][i] = value.astype(BF16)


def spread_matmul(parts, adj, core, dys, name):
    shape = (len(dys), parts.shape[1], NZH * TILE)
    return in_vmem(functools.partial(spread_kernel, core, dys), [kept(shape, BF16)], (parts, adj), name)[0]


def far_sum_kernel(mine, theirs, left, right):
    half = left.shape[0]
    value = mine[0].astype(F32) + theirs[0].astype(F32)
    left[...] = value[:half].astype(BF16)
    right[...] = value[half:].astype(BF16)


def far_sum(mine, theirs):
    shape = (mine.shape[1] // 2, mine.shape[2])
    return in_vmem(far_sum_kernel, [kept(shape, BF16)] * 2, (mine, theirs), "far_sum")


def near_sum_kernel(mine, theirs, left, right, one, three):
    half = left.shape[0]
    first = mine[0].astype(F32) + theirs[0].astype(F32)
    one[:half] = (first[:half] + left[...].astype(F32)).astype(BF16)
    one[half:] = first[half:].astype(BF16)
    second = mine[1].astype(F32) + theirs[1].astype(F32)
    three[:half] = second[:half].astype(BF16)
    three[half:] = (second[half:] + right[...].astype(F32)).astype(BF16)


def near_sum(mine, theirs, left, right):
    return in_vmem(near_sum_kernel, [kept(mine.shape[1:], BF16)] * 2, (mine, theirs, left, right), "near_sum")


def plane_sum_kernel(mine, theirs, one, three, near, left, right):
    value = mine[0].astype(F32) + theirs[0].astype(F32) + one[...].astype(F32) + three[...].astype(F32)
    half = left.shape[0]
    for i, tile in enumerate(RING[:3]):
        near[i] = value[:, tile * TILE : (tile + 1) * TILE]
    far = value[:, RING[3] * TILE : (RING[3] + 1) * TILE].astype(BF16)
    left[...] = far[:half]
    right[...] = far[half:]


def plane_sum(mine, theirs, one, three):
    width = mine.shape[1]
    results = [kept((3, width, TILE), F32)] + [kept((width // 2, TILE), BF16)] * 2
    return in_vmem(plane_sum_kernel, results, (mine, theirs, one, three), "plane_sum")


def tile_sum_kernel(near, left, right, one, three):
    half = left.shape[0]
    one[:half] = (near[1, :half] + left[...].astype(F32)).astype(BF16)
    one[half:] = near[1, half:].astype(BF16)
    three[:half] = near[2, :half].astype(BF16)
    three[half:] = (near[2, half:] + right[...].astype(F32)).astype(BF16)


def tile_sum(near, left, right):
    return in_vmem(tile_sum_kernel, [kept(near.shape[1:], BF16)] * 2, (near, left, right), "tile_sum")


def last_kernel(near, one, three, own, out):
    back = near[0] + one[...].astype(F32) + three[...].astype(F32)
    out[...] = (own[...] + back.T).astype(BF16)


def last_sum(near, one, three, own):
    return in_vmem(last_kernel, [plain(own.shape, BF16)], (near, one, three, own), "last_sum")[0]


def body(features, degrees, tile_rows, tile_masks, w_self, w_neigh, bias, cotangent):
    row = lax.axis_index("row").astype(jnp.int32)

    differ = jnp.arange(NROW, dtype=jnp.int32) ^ row
    adj = adjacency(tile_masks[0, 0], (differ % NCORE) * CHIPS + differ // NCORE, tile_rows[0, 0].reshape(-1))
    degf_row = degrees.astype(F32)[None, :]
    base = jnp.dot(features, w_self, preferred_element_type=F32) + bias[None, :]

    half = TILE // 2
    z1, z3 = flip(features, z=1), flip(features, z=3)
    z2 = [flip(z1[:half], z=3), flip(z3[half:], z=1)]
    plane = jnp.concatenate([features, z1, *z2, z3], axis=0)
    half = plane.shape[0] // 2
    y1, y3 = flip(plane, y=1), flip(plane, y=3)
    plane, adj, base, degf_row = lax.optimization_barrier((plane, adj, base, degf_row))
    other = flip(plane, core=1)
    part = gather_matmul(adj, [(0, 0, 0, plane), (1, 0, 0, other)], None, F32, "gather_plane")
    y1, y3, part = lax.optimization_barrier((y1, y3, part))
    y2 = [flip(y1[:half], y=3), flip(y3[half:], y=1)]
    o1, o3 = flip(y1, core=1), flip(y3, core=1)
    part = gather_matmul(adj, [(0, 1, 0, y1), (0, 3, 0, y3), (1, 1, 0, o1), (1, 3, 0, o3)], part, F32, "gather_near")
    *y2, part = lax.optimization_barrier((*y2, part))
    o2 = [flip(v, core=1) for v in y2]
    part = gather_matmul(adj, [(0, 2, 0, y2[0]), (0, 2, half, y2[1])], part, F32, "gather_far")
    *o2, part = lax.optimization_barrier((*o2, part))
    summed = gather_matmul(adj, [(1, 2, 0, o2[0]), (1, 2, half, o2[1])], part, BF16, "gather_far_other")

    arrived = lax.all_to_all(summed, "col", 0, 0, tiled=True)
    grad_pre, scaled_t, output = node_step(arrived, base, degf_row, w_neigh, cotangent)

    table = lax.all_to_all(scaled_t, "col", 0, 0, tiled=True)
    own = lax.dot_general(grad_pre, w_self, (((1,), (1,)), ((), ())), preferred_element_type=F32)

    theirs = flip(spread_matmul(table, adj, 1, (2,), "spread_far_other"), core=1)
    mine = spread_matmul(table, adj, 0, (2,), "spread_far")
    near_other = spread_matmul(table, adj, 1, (1, 3), "spread_near_other")
    theirs, mine, near_other = lax.optimization_barrier((theirs, mine, near_other))
    left, right = far_sum(mine, theirs)
    left, right, table = lax.optimization_barrier((left, right, table))
    left, right = flip(left, y=3), flip(right, y=1)
    mine = spread_matmul(table, adj, 0, (1, 3), "spread_near")
    theirs = flip(near_other, core=1)
    left, right, mine = lax.optimization_barrier((left, right, mine))
    one, three = near_sum(mine, theirs, left, right)
    one, three, table = lax.optimization_barrier((one, three, table))
    one, three = flip(one, y=1), flip(three, y=3)
    theirs = flip(spread_matmul(table, adj, 1, (0,), "spread_plane_other"), core=1)
    mine = spread_matmul(table, adj, 0, (0,), "spread_plane")
    one, three, mine = lax.optimization_barrier((one, three, mine))
    near, left, right = plane_sum(mine, theirs, one, three)
    left, right = flip(left, z=3), flip(right, z=1)
    one, three = tile_sum(near, left, right)
    grad_features = last_sum(near, flip(one, z=1), flip(three, z=3), own)
    return output, grad_features


def solution(mesh):
    both = P(("row", "col"), None)
    return jax.shard_map(
        body,
        mesh=mesh,
        in_specs=(
            both,
            P(("row", "col")),
            P("row", "col", None, None),
            P("row", "col", None, None, None, None),
            P(),
            P(),
            P(),
            both,
        ),
        out_specs=(both, both),
        check_vma=False,
    )
```

time: 135 us -> 140 us (1.037)
  waiting for transfers between devices: 40.7 us -> 51.2 us
  starting transfers between devices: 33 us -> 27.5 us
    ppermute x22 -> x24, waiting for transfers between devices: 40.7 us -> 51.2 us  [flip(): return lax.ppermute(value, ('row', 'col'), pairs)]
    ppermute x22 -> x24, starting transfers between devices: 33 us -> 27.5 us  [flip(): return lax.ppermute(value, ('row', 'col'), pairs)]
    pallas_call x14 -> x16, Pallas kernels: 12.2 us -> 12.9 us  [in_vmem(): pl.pallas_call(kernel, in_specs=[spec] * len(operands), out_specs=out_spe...]
  transfers between devices with their start and end apart: 22 -> 24, of which waited for: 10 -> 14; matrix products, arithmetic and copies ran while one was open for 2% -> 2% of each run, Pallas kernels for 9% -> 10%
where the time goes in v5:
time: 140 us
  waiting for transfers between devices  51.2 us (37%)
  blocking collectives  38.4 us (27%)
  starting transfers between devices  27.5 us (20%)
  Pallas kernels  18.5 us (13%)
  matrix products  1.44 us (1%)
    ppermute x24, waiting for transfers between devices, flip(): return lax.ppermute(value, ('row', 'col'), pairs)  51.2 us
    ppermute x24, starting transfers between devices, flip(): return lax.ppermute(value, ('row', 'col'), pairs)  27.5 us
    all_to_all x1, blocking collectives, body(): arrived = lax.all_to_all(summed, 'col', 0, 0, tiled=True)  20.6 us
    all_to_all x1, blocking collectives, body(): table = lax.all_to_all(scaled_t, 'col', 0, 0, tiled=True)  17.7 us
    pallas_call x16, Pallas kernels, in_vmem(): pl.pallas_call(kernel, in_specs=[spec] * len(operands), out_specs=out_spe...  12.9 us
    pallas_call x1, Pallas kernels, adjacency(): pl.pallas_call(adjacency_kernel, grid_spec=pltpu.PrefetchScalarGridSpec(n...  5.55 us
  transfers between devices with their start and end apart: 24, of which 14 were waited for; matrix products, arithmetic and copies ran while one was open for 2% of the time, Pallas kernels for 10%

profile of v5, /device:TPU:32, one launch (start us, length us, event | category | flops | bytes accessed | tf_op | source)
XLA Modules:
  0.0 139.5 jit_solution(9814290340833044818)
XLA Ops:
  0.6 3.4 %collective-permute-start = (bf16[128,512]{1,0:T(8,128)(2,1)}, bf16[128,512]{1,0:T(8,128)(2,1)S(1)}, u32[]{:S(2)}, u32[]{:S(2)}) collective-permute-start(bf16[128,512]{1,0:T(8,128)(2,1)} %param.8), channel_id=1, source_target_pairs={{0,16},{1,17},{2,18},{3,19},{4,20},{5,21},{6,22},{7,23},{8,24},{9,... | collective-permute-start | bytes 393224 | tf_op jit(solution)/shard_map/ppermute | solution.py:25
  4.0 3.6 %collective-permute-start.2 = (bf16[128,512]{1,0:T(8,128)(2,1)}, bf16[128,512]{1,0:T(8,128)(2,1)S(1)}, u32[]{:S(2)}, u32[]{:S(2)}) collective-permute-start(bf16[128,512]{1,0:T(8,128)(2,1)} %param.8), channel_id=1, source_target_pairs={{0,48},{1,49},{2,50},{3,51},{4,52},{5,53},{6,54},{7,55},{8,56},{9,... | collective-permute-start | bytes 393224 | tf_op jit(solution)/shard_map/ppermute | solution.py:25
  8.2 1.1 convolution_add_fusion.base
  10.3 5.5 %adjacency.1.adj = bf16[1024,4096]{1,0:T(8,128)(2,1)S(1)} custom-call(s32[32]{0:T(128)S(1)} %fusion.1.place, s32[96]{0:T(128)S(1)} %reshape_squeeze.3.where, s32[32,3,128,128]{3,2,1,0:T(8,128)} %bitcast.13), custom_call_target="tpu_custom_call" | custom-call | bytes 14680064 | tf_op jit(solution)/shard_map/adjacency/pallas_call | solution.py:68
  16.5 1.0 collective-permute-start.3
  17.6 4.9 %collective-permute-done.1 = bf16[64,512]{1,0:T(8,128)(2,1)S(1)} collective-permute-done((bf16[64,512]{1,0:T(8,128)(2,1)S(1)}, bf16[64,512]{1,0:T(8,128)(2,1)S(1)}, u32[]{:S(2)}, u32[]{:S(2)}) %collective-permute-start.1) | collective-permute-done | bytes 65568 | tf_op jit(solution)/shard_map/ppermute | solution.py:25
  22.7 1.7 %collective-permute-start.4 = (bf16[512,512]{1,0:T(8,128)(2,1)S(1)}, bf16[512,512]{1,0:T(8,128)(2,1)S(1)}, u32[]{:S(2)}, u32[]{:S(2)}) collective-permute-start(bf16[512,512]{1,0:T(8,128)(2,1)S(1)} %constant_dynamic-update-slice_fusion.refs_0_), channel_id=1, source_target_pairs={{0,64},{1,65},{2,66},{3,67},{4,68},{5,69},{6,70},{7,71},{8,72},{9,... | collective-permute-start | bytes 1572872 | tf_op jit(solution)/shard_map/ppermute | solution.py:25
  24.3 2.2 %collective-permute-start.5 = (bf16[512,512]{1,0:T(8,128)(2,1)S(1)}, bf16[512,512]{1,0:T(8,128)(2,1)S(1)}, u32[]{:S(2)}, u32[]{:S(2)}) collective-permute-start(bf16[512,512]{1,0:T(8,128)(2,1)S(1)} %constant_dynamic-update-slice_fusion.refs_0_), channel_id=1, source_target_pairs={{0,192},{1,193},{2,194},{3,195},{4,196},{5,197},{6,198},{7,199},{8... | collective-permute-start | bytes 1572872 | tf_op jit(solution)/shard_map/ppermute | solution.py:25
  26.5 1.2 gather_plane.1.refs_4_
  27.7 9.3 %collective-permute-done.4.refs_0_ = bf16[512,512]{1,0:T(8,128)(2,1)S(1)} collective-permute-done((bf16[512,512]{1,0:T(8,128)(2,1)S(1)}, bf16[512,512]{1,0:T(8,128)(2,1)S(1)}, u32[]{:S(2)}, u32[]{:S(2)}) %collective-permute-start.4) | collective-permute-done | bytes 524320 | tf_op jit(solution)/shard_map/ppermute | solution.py:25
  37.0 2.5 %collective-permute-done.5.refs_1_ = bf16[512,512]{1,0:T(8,128)(2,1)S(1)} collective-permute-done((bf16[512,512]{1,0:T(8,128)(2,1)S(1)}, bf16[512,512]{1,0:T(8,128)(2,1)S(1)}, u32[]{:S(2)}, u32[]{:S(2)}) %collective-permute-start.5) | collective-permute-done | bytes 524320 | tf_op jit(solution)/shard_map/ppermute | solution.py:25
  40.1 2.3 %collective-permute-start.7 = (bf16[256,512]{1,0:T(8,128)(2,1)S(1)}, bf16[256,512]{1,0:T(8,128)(2,1)S(1)}, u32[]{:S(2)}, u32[]{:S(2)}) collective-permute-start(bf16[256,512]{1,0:T(8,128)(2,1)S(1)} %slice.14), channel_id=1, source_target_pairs={{0,192},{1,193},{2,194},{3,195},{4,196},{5,197},{6,198},{7,199},{8... | collective-permute-start | bytes 786440 | tf_op jit(solution)/shard_map/ppermute | solution.py:25
  42.3 2.3 %gather_near.1.refs_2_ = f32[1024,512]{1,0:T(8,128)S(1)} custom-call(bf16[1024,4096]{1,0:T(8,128)(2,1)S(1)} %adjacency.1.adj, bf16[512,512]{1,0:T(8,128)(2,1)S(1)} %collective-permute-done.4.refs_0_, bf16[512,512]{1,0:T(8,128)(2,1)S(1)} %collective-permute-done.5.refs_1_, bf16[512,512]{1,0:T(8,128)(2,1)S(1)} %collective-permute-done.9.refs_2_, ...), custom_call_target="tpu_custom_call" | custom-call | bytes 1024 | tf_op jit(solution)/shard_map/gather_near/pallas_call | solution.py:32
  44.7 4.9 %collective-permute-done.7.refs_0_ = bf16[256,512]{1,0:T(8,128)(2,1)S(1)} collective-permute-done((bf16[256,512]{1,0:T(8,128)(2,1)S(1)}, bf16[256,512]{1,0:T(8,128)(2,1)S(1)}, u32[]{:S(2)}, u32[]{:S(2)}) %collective-permute-start.7) | collective-permute-done | bytes 262176 | tf_op jit(solution)/shard_map/ppermute | solution.py:25
  52.9 20.6 %all_to_all.16 = bf16[8,128,512]{2,1,0:T(8,128)(2,1)S(1)} all-to-all(bf16[8,128,512]{2,1,0:T(8,128)(2,1)S(1)} %bitcast.11), channel_id=1, replica_groups=mesh['row'=32,'col'=8] {'col'}, dimensions={0} | all-to-all | bytes 2097152 | tf_op jit(solution)/shard_map/all_to_all | solution.py:234
  73.6 1.1 node_step.1
  74.6 17.7 %all_to_all.17.parts = bf16[8,512,128]{2,1,0:T(8,128)(2,1)S(1)} all-to-all(bf16[8,512,128]{2,1,0:T(8,128)(2,1)S(1)} %get-tuple-element.56), channel_id=1, replica_groups=mesh['row'=32,'col'=8] {'col'}, dimensions={0} | all-to-all | bytes 2097152 | tf_op jit(solution)/shard_map/all_to_all | solution.py:237
  93.2 1.2 spread_near_other.1
  95.9 1.6 %collective-permute-start.14 = (bf16[256,512]{1,0:T(8,128)(2,1)S(1)}, bf16[256,512]{1,0:T(8,128)(2,1)S(1)}, u32[]{:S(2)}, u32[]{:S(2)}) collective-permute-start(bf16[256,512]{1,0:T(8,128)(2,1)S(1)} %get-tuple-element.61), channel_id=1, source_target_pairs={{0,192},{1,193},{2,194},{3,195},{4,196},{5,197},{6,198},{7,199},{8... | collective-permute-start | bytes 786440 | tf_op jit(solution)/shard_map/ppermute | solution.py:25
  97.5 1.2 spread_near.1.mine
  98.7 6.7 %collective-permute-done.14.left = bf16[256,512]{1,0:T(8,128)(2,1)S(1)} collective-permute-done((bf16[256,512]{1,0:T(8,128)(2,1)S(1)}, bf16[256,512]{1,0:T(8,128)(2,1)S(1)}, u32[]{:S(2)}, u32[]{:S(2)}) %collective-permute-start.14) | collective-permute-done | bytes 262176 | tf_op jit(solution)/shard_map/ppermute | solution.py:25
  106.1 1.7 %collective-permute-start.18 = (bf16[512,512]{1,0:T(8,128)(2,1)S(1)}, bf16[512,512]{1,0:T(8,128)(2,1)S(1)}, u32[]{:S(2)}, u32[]{:S(2)}) collective-permute-start(bf16[512,512]{1,0:T(8,128)(2,1)S(1)} %get-tuple-element.71), channel_id=1, source_target_pairs={{0,192},{1,193},{2,194},{3,195},{4,196},{5,197},{6,198},{7,199},{8... | collective-permute-start | bytes 1572872 | tf_op jit(solution)/shard_map/ppermute | solution.py:25
  109.4 9.4 %collective-permute-done.17.one = bf16[512,512]{1,0:T(8,128)(2,1)S(1)} collective-permute-done((bf16[512,512]{1,0:T(8,128)(2,1)S(1)}, bf16[512,512]{1,0:T(8,128)(2,1)S(1)}, u32[]{:S(2)}, u32[]{:S(2)}) %collective-permute-start.17) | collective-permute-done | bytes 524320 | tf_op jit(solution)/shard_map/ppermute | solution.py:25
  118.8 1.3 collective-permute-done.18.three
  120.4 3.5 %collective-permute-start.20 = (bf16[256,128]{1,0:T(8,128)(2,1)S(1)}, bf16[256,128]{1,0:T(8,128)(2,1)S(1)}, u32[]{:S(2)}, u32[]{:S(2)}) collective-permute-start(bf16[256,128]{1,0:T(8,128)(2,1)S(1)} %get-tuple-element.77), channel_id=1, source_target_pairs={{0,48},{1,49},{2,50},{3,51},{4,52},{5,53},{6,54},{7,55},{8,56},{9,... | collective-permute-start | bytes 196616 | tf_op jit(solution)/shard_map/ppermute | solution.py:25
  123.9 1.0 collective-permute-start.21
  124.9 1.9 %collective-permute-done.20.left = bf16[256,128]{1,0:T(8,128)(2,1)S(1)} collective-permute-done((bf16[256,128]{1,0:T(8,128)(2,1)S(1)}, bf16[256,128]{1,0:T(8,128)(2,1)S(1)}, u32[]{:S(2)}, u32[]{:S(2)}) %collective-permute-start.20) | collective-permute-done | bytes 65568 | tf_op jit(solution)/shard_map/ppermute | solution.py:25
  126.9 2.3 %collective-permute-done.21.right = bf16[256,128]{1,0:T(8,128)(2,1)S(1)} collective-permute-done((bf16[256,128]{1,0:T(8,128)(2,1)S(1)}, bf16[256,128]{1,0:T(8,128)(2,1)S(1)}, u32[]{:S(2)}, u32[]{:S(2)}) %collective-permute-start.21) | collective-permute-done | bytes 65568 | tf_op jit(solution)/shard_map/ppermute | solution.py:25
  129.2 1.0 collective-permute-start.22
  130.3 1.6 %collective-permute-start.23 = (bf16[512,128]{1,0:T(8,128)(2,1)S(1)}, bf16[512,128]{1,0:T(8,128)(2,1)S(1)}, u32[]{:S(2)}, u32[]{:S(2)}) collective-permute-start(bf16[512,128]{1,0:T(8,128)(2,1)S(1)} %get-tuple-element.80), channel_id=1, source_target_pairs={{0,48},{1,49},{2,50},{3,51},{4,52},{5,53},{6,54},{7,55},{8,56},{9,... | collective-permute-start | bytes 393224 | tf_op jit(solution)/shard_map/ppermute | solution.py:25
  132.2 3.2 %collective-permute-done.22.one = bf16[512,128]{1,0:T(8,128)(2,1)S(1)} collective-permute-done((bf16[512,128]{1,0:T(8,128)(2,1)S(1)}, bf16[512,128]{1,0:T(8,128)(2,1)S(1)}, u32[]{:S(2)}, u32[]{:S(2)}) %collective-permute-start.22) | collective-permute-done | bytes 131104 | tf_op jit(solution)/shard_map/ppermute | solution.py:25
  135.4 3.3 %collective-permute-done.23.three = bf16[512,128]{1,0:T(8,128)(2,1)S(1)} collective-permute-done((bf16[512,128]{1,0:T(8,128)(2,1)S(1)}, bf16[512,128]{1,0:T(8,128)(2,1)S(1)}, u32[]{:S(2)}, u32[]{:S(2)}) %collective-permute-start.23) | collective-permute-done | bytes 131104 | tf_op jit(solution)/shard_map/ppermute | solution.py:25
  (58 shorter events, 12.0 us)
Async XLA Ops:
  0.6 7.6 %copy-start = (bf16[512,512]{1,0:T(8,128)(2,1)S(1)}, bf16[512,512]{1,0:T(8,128)(2,1)}, u32[]{:S(2)}) copy-start(bf16[512,512]{1,0:T(8,128)(2,1)} %param.12) | copy-start | bytes 1572868
  0.6 15.2 %collective-permute-start = (bf16[128,512]{1,0:T(8,128)(2,1)}, bf16[128,512]{1,0:T(8,128)(2,1)S(1)}, u32[]{:S(2)}, u32[]{:S(2)}) collective-permute-start(bf16[128,512]{1,0:T(8,128)(2,1)} %param.8), channel_id=1, source_target_pairs={{0,16},{1,17},{2,18},{3,19},{4,20},{5,21},{6,22},{7,23},{8,24},{9,... | collective-permute-start | bytes 393224 | tf_op jit(solution)/shard_map/ppermute | solution.py:25
  4.0 12.5 %collective-permute-start.2 = (bf16[128,512]{1,0:T(8,128)(2,1)}, bf16[128,512]{1,0:T(8,128)(2,1)S(1)}, u32[]{:S(2)}, u32[]{:S(2)}) collective-permute-start(bf16[128,512]{1,0:T(8,128)(2,1)} %param.8), channel_id=1, source_target_pairs={{0,48},{1,49},{2,50},{3,51},{4,52},{5,53},{6,54},{7,55},{8,56},{9,... | collective-permute-start | bytes 393224 | tf_op jit(solution)/shard_map/ppermute | solution.py:25
  10.3 5.6 %copy-start.3 = (bf16[128,512]{1,0:T(8,128)(2,1)S(1)}, bf16[128,512]{1,0:T(8,128)(2,1)}, u32[]{:S(2)}) copy-start(bf16[128,512]{1,0:T(8,128)(2,1)} %param.8) | copy-start | bytes 393220
  15.9 6.6 %collective-permute-start.1 = (bf16[64,512]{1,0:T(8,128)(2,1)S(1)}, bf16[64,512]{1,0:T(8,128)(2,1)S(1)}, u32[]{:S(2)}, u32[]{:S(2)}) collective-permute-start(bf16[64,512]{1,0:T(8,128)(2,1)S(1)} %slice.16), channel_id=1, source_target_pairs={{0,48},{1,49},{2,50},{3,51},{4,52},{5,53},{6,54},{7,55},{8,56},{9,... | collective-permute-start | bytes 196616 | tf_op jit(solution)/shard_map/ppermute | solution.py:25
  16.5 6.0 %collective-permute-start.3 = (bf16[64,512]{1,0:T(8,128)(2,1)S(1)}, bf16[64,512]{1,0:T(8,128)(2,1)S(1)}, u32[]{:S(2)}, u32[]{:S(2)}) collective-permute-start(bf16[64,512]{1,0:T(8,128)(2,1)S(1)} %slice.17), channel_id=1, source_target_pairs={{0,16},{1,17},{2,18},{3,19},{4,20},{5,21},{6,22},{7,23},{8,24},{9,... | collective-permute-start | bytes 196616 | tf_op jit(solution)/shard_map/ppermute | solution.py:25
  22.6 3.9 %collective-permute-start.6 = (bf16[512,512]{1,0:T(8,128)(2,1)S(1)}, bf16[512,512]{1,0:T(8,128)(2,1)S(1)}, u32[]{:S(2)}, u32[]{:S(2)}) collective-permute-start(bf16[512,512]{1,0:T(8,128)(2,1)S(1)} %constant_dynamic-update-slice_fusion.refs_0_), channel_id=1, source_target_pairs={{0,8},{1,9},{2,10},{3,11},{4,12},{5,13},{6,14},{7,15},{8,0},{9,1},... | collective-permute-start | bytes 1572872 | tf_op jit(solution)/shard_map/ppermute | solution.py:25
  22.7 14.3 %collective-permute-start.4 = (bf16[512,512]{1,0:T(8,128)(2,1)S(1)}, bf16[512,512]{1,0:T(8,128)(2,1)S(1)}, u32[]{:S(2)}, u32[]{:S(2)}) collective-permute-start(bf16[512,512]{1,0:T(8,128)(2,1)S(1)} %constant_dynamic-update-slice_fusion.refs_0_), channel_id=1, source_target_pairs={{0,64},{1,65},{2,66},{3,67},{4,68},{5,69},{6,70},{7,71},{8,72},{9,... | collective-permute-start | bytes 1572872 | tf_op jit(solution)/shard_map/ppermute | solution.py:25
  24.3 15.2 %collective-permute-start.5 = (bf16[512,512]{1,0:T(8,128)(2,1)S(1)}, bf16[512,512]{1,0:T(8,128)(2,1)S(1)}, u32[]{:S(2)}, u32[]{:S(2)}) collective-permute-start(bf16[512,512]{1,0:T(8,128)(2,1)S(1)} %constant_dynamic-update-slice_fusion.refs_0_), channel_id=1, source_target_pairs={{0,192},{1,193},{2,194},{3,195},{4,196},{5,197},{6,198},{7,199},{8... | collective-permute-start | bytes 1572872 | tf_op jit(solution)/shard_map/ppermute | solution.py:25
  39.5 2.8 %collective-permute-start.10 = (bf16[512,512]{1,0:T(8,128)(2,1)S(1)}, bf16[512,512]{1,0:T(8,128)(2,1)S(1)}, u32[]{:S(2)}, u32[]{:S(2)}) collective-permute-start(bf16[512,512]{1,0:T(8,128)(2,1)S(1)} %collective-permute-done.5.refs_1_), channel_id=1, source_target_pairs={{0,8},{1,9},{2,10},{3,11},{4,12},{5,13},{6,14},{7,15},{8,0},{9,1},... | collective-permute-start | bytes 1572872 | tf_op jit(solution)/shard_map/ppermute | solution.py:25
  39.5 2.8 %collective-permute-start.9 = (bf16[512,512]{1,0:T(8,128)(2,1)S(1)}, bf16[512,512]{1,0:T(8,128)(2,1)S(1)}, u32[]{:S(2)}, u32[]{:S(2)}) collective-permute-start(bf16[512,512]{1,0:T(8,128)(2,1)S(1)} %collective-permute-done.4.refs_0_), channel_id=1, source_target_pairs={{0,8},{1,9},{2,10},{3,11},{4,12},{5,13},{6,14},{7,15},{8,0},{9,1},... | collective-permute-start | bytes 1572872 | tf_op jit(solution)/shard_map/ppermute | solution.py:25
  40.1 9.5 %collective-permute-start.7 = (bf16[256,512]{1,0:T(8,128)(2,1)S(1)}, bf16[256,512]{1,0:T(8,128)(2,1)S(1)}, u32[]{:S(2)}, u32[]{:S(2)}) collective-permute-start(bf16[256,512]{1,0:T(8,128)(2,1)S(1)} %slice.14), channel_id=1, source_target_pairs={{0,192},{1,193},{2,194},{3,195},{4,196},{5,197},{6,198},{7,199},{8... | collective-permute-start | bytes 786440 | tf_op jit(solution)/shard_map/ppermute | solution.py:25
  42.3 7.9 %collective-permute-start.8 = (bf16[256,512]{1,0:T(8,128)(2,1)S(1)}, bf16[256,512]{1,0:T(8,128)(2,1)S(1)}, u32[]{:S(2)}, u32[]{:S(2)}) collective-permute-start(bf16[256,512]{1,0:T(8,128)(2,1)S(1)} %slice.15), channel_id=1, source_target_pairs={{0,64},{1,65},{2,66},{3,67},{4,68},{5,69},{6,70},{7,71},{8,72},{9,... | collective-permute-start | bytes 786440 | tf_op jit(solution)/shard_map/ppermute | solution.py:25
  50.3 1.5 %collective-permute-start.11 = (bf16[256,512]{1,0:T(8,128)(2,1)S(1)}, bf16[256,512]{1,0:T(8,128)(2,1)S(1)}, u32[]{:S(2)}, u32[]{:S(2)}) collective-permute-start(bf16[256,512]{1,0:T(8,128)(2,1)S(1)} %collective-permute-done.7.refs_0_), channel_id=1, source_target_pairs={{0,8},{1,9},{2,10},{3,11},{4,12},{5,13},{6,14},{7,15},{8,0},{9,1},... | collective-permute-start | bytes 786440 | tf_op jit(solution)/shard_map/ppermute | solution.py:25
  50.3 1.9 %collective-permute-start.12 = (bf16[256,512]{1,0:T(8,128)(2,1)S(1)}, bf16[256,512]{1,0:T(8,128)(2,1)S(1)}, u32[]{:S(2)}, u32[]{:S(2)}) collective-permute-start(bf16[256,512]{1,0:T(8,128)(2,1)S(1)} %collective-permute-done.8.refs_1_), channel_id=1, source_target_pairs={{0,8},{1,9},{2,10},{3,11},{4,12},{5,13},{6,14},{7,15},{8,0},{9,1},... | collective-permute-start | bytes 786440 | tf_op jit(solution)/shard_map/ppermute | solution.py:25
  52.9 20.7 %copy-start.1 = (bf16[512,512]{1,0:T(8,128)(2,1)S(1)}, bf16[512,512]{1,0:T(8,128)(2,1)}, u32[]{:S(2)}) copy-start(bf16[512,512]{1,0:T(8,128)(2,1)} %w_neigh.1) | copy-start | bytes 1572868
  52.9 20.7 %copy-start.2 = (bf16[128,512]{1,0:T(8,128)(2,1)S(1)}, bf16[128,512]{1,0:T(8,128)(2,1)}, u32[]{:S(2)}) copy-start(bf16[128,512]{1,0:T(8,128)(2,1)} %cotangent.1) | copy-start | bytes 393220
  93.1 2.1 %collective-permute-start.13 = (bf16[1,512,512]{2,1,0:T(8,128)(2,1)S(1)}, bf16[1,512,512]{2,1,0:T(8,128)(2,1)S(1)}, u32[]{:S(2)}, u32[]{:S(2)}) collective-permute-start(bf16[1,512,512]{2,1,0:T(8,128)(2,1)S(1)} %spread_far_other.1), channel_id=1, source_target_pairs={{0,8},{1,9},{2,10},{3,11},{4,12},{5,13},{6,14},{7,15},{8,0},{9,1},... | collective-permute-start | bytes 1572872 | tf_op jit(solution)/shard_map/ppermute | solution.py:25
  95.2 10.2 %collective-permute-start.16 = (bf16[2,512,512]{2,1,0:T(8,128)(2,1)S(1)}, bf16[2,512,512]{2,1,0:T(8,128)(2,1)S(1)}, u32[]{:S(2)}, u32[]{:S(2)}) collective-permute-start(bf16[2,512,512]{2,1,0:T(8,128)(2,1)S(1)} %spread_near_other.1), channel_id=1, source_target_pairs={{0,8},{1,9},{2,10},{3,11},{4,12},{5,13},{6,14},{7,15},{8,0},{9,1},... | collective-permute-start | bytes 3145736 | tf_op jit(solution)/shard_map/ppermute | solution.py:25
  95.9 9.5 %collective-permute-start.14 = (bf16[256,512]{1,0:T(8,128)(2,1)S(1)}, bf16[256,512]{1,0:T(8,128)(2,1)S(1)}, u32[]{:S(2)}, u32[]{:S(2)}) collective-permute-start(bf16[256,512]{1,0:T(8,128)(2,1)S(1)} %get-tuple-element.61), channel_id=1, source_target_pairs={{0,192},{1,193},{2,194},{3,195},{4,196},{5,197},{6,198},{7,199},{8... | collective-permute-start | bytes 786440 | tf_op jit(solution)/shard_map/ppermute | solution.py:25
  97.4 8.0 %collective-permute-start.15 = (bf16[256,512]{1,0:T(8,128)(2,1)S(1)}, bf16[256,512]{1,0:T(8,128)(2,1)S(1)}, u32[]{:S(2)}, u32[]{:S(2)}) collective-permute-start(bf16[256,512]{1,0:T(8,128)(2,1)S(1)} %get-tuple-element.62), channel_id=1, source_target_pairs={{0,64},{1,65},{2,66},{3,67},{4,68},{5,69},{6,70},{7,71},{8,72},{9,... | collective-permute-start | bytes 786440 | tf_op jit(solution)/shard_map/ppermute | solution.py:25
  105.7 13.1 %collective-permute-start.17 = (bf16[512,512]{1,0:T(8,128)(2,1)S(1)}, bf16[512,512]{1,0:T(8,128)(2,1)S(1)}, u32[]{:S(2)}, u32[]{:S(2)}) collective-permute-start(bf16[512,512]{1,0:T(8,128)(2,1)S(1)} %get-tuple-element.70), channel_id=1, source_target_pairs={{0,64},{1,65},{2,66},{3,67},{4,68},{5,69},{6,70},{7,71},{8,72},{9,... | collective-permute-start | bytes 1572872 | tf_op jit(solution)/shard_map/ppermute | solution.py:25
  106.1 14.0 %collective-permute-start.18 = (bf16[512,512]{1,0:T(8,128)(2,1)S(1)}, bf16[512,512]{1,0:T(8,128)(2,1)S(1)}, u32[]{:S(2)}, u32[]{:S(2)}) collective-permute-start(bf16[512,512]{1,0:T(8,128)(2,1)S(1)} %get-tuple-element.71), channel_id=1, source_target_pairs={{0,192},{1,193},{2,194},{3,195},{4,196},{5,197},{6,198},{7,199},{8... | collective-permute-start | bytes 1572872 | tf_op jit(solution)/shard_map/ppermute | solution.py:25
  108.5 11.6 %collective-permute-start.19 = (bf16[1,512,512]{2,1,0:T(8,128)(2,1)S(1)}, bf16[1,512,512]{2,1,0:T(8,128)(2,1)S(1)}, u32[]{:S(2)}, u32[]{:S(2)}) collective-permute-start(bf16[1,512,512]{2,1,0:T(8,128)(2,1)S(1)} %spread_plane_other.1), channel_id=1, source_target_pairs={{0,8},{1,9},{2,10},{3,11},{4,12},{5,13},{6,14},{7,15},{8,0},{9,1},... | collective-permute-start | bytes 1572872 | tf_op jit(solution)/shard_map/ppermute | solution.py:25
  120.4 6.5 %collective-permute-start.20 = (bf16[256,128]{1,0:T(8,128)(2,1)S(1)}, bf16[256,128]{1,0:T(8,128)(2,1)S(1)}, u32[]{:S(2)}, u32[]{:S(2)}) collective-permute-start(bf16[256,128]{1,0:T(8,128)(2,1)S(1)} %get-tuple-element.77), channel_id=1, source_target_pairs={{0,48},{1,49},{2,50},{3,51},{4,52},{5,53},{6,54},{7,55},{8,56},{9,... | collective-permute-start | bytes 196616 | tf_op jit(solution)/shard_map/ppermute | solution.py:25
  123.9 5.3 %collective-permute-start.21 = (bf16[256,128]{1,0:T(8,128)(2,1)S(1)}, bf16[256,128]{1,0:T(8,128)(2,1)S(1)}, u32[]{:S(2)}, u32[]{:S(2)}) collective-permute-start(bf16[256,128]{1,0:T(8,128)(2,1)S(1)} %get-tuple-element.78), channel_id=1, source_target_pairs={{0,16},{1,17},{2,18},{3,19},{4,20},{5,21},{6,22},{7,23},{8,24},{9,... | collective-permute-start | bytes 196616 | tf_op jit(solution)/shard_map/ppermute | solution.py:25
  129.2 6.2 %collective-permute-start.22 = (bf16[512,128]{1,0:T(8,128)(2,1)S(1)}, bf16[512,128]{1,0:T(8,128)(2,1)S(1)}, u32[]{:S(2)}, u32[]{:S(2)}) collective-permute-start(bf16[512,128]{1,0:T(8,128)(2,1)S(1)} %get-tuple-element.79), channel_id=1, source_target_pairs={{0,16},{1,17},{2,18},{3,19},{4,20},{5,21},{6,22},{7,23},{8,24},{9,... | collective-permute-start | bytes 393224 | tf_op jit(solution)/shard_map/ppermute | solution.py:25
  130.3 8.5 %collective-permute-start.23 = (bf16[512,128]{1,0:T(8,128)(2,1)S(1)}, bf16[512,128]{1,0:T(8,128)(2,1)S(1)}, u32[]{:S(2)}, u32[]{:S(2)}) collective-permute-start(bf16[512,128]{1,0:T(8,128)(2,1)S(1)} %get-tuple-element.80), channel_id=1, source_target_pairs={{0,48},{1,49},{2,50},{3,51},{4,52},{5,53},{6,54},{7,55},{8,56},{9,... | collective-permute-start | bytes 393224 | tf_op jit(solution)/shard_map/ppermute | solution.py:25

commit v6 on v5

v6 whole, which is shorter than its diff:
```python
import functools

import jax
import jax.numpy as jnp
from jax import lax
from jax.experimental import pallas as pl
from jax.experimental.pallas import tpu as pltpu
from jax.sharding import PartitionSpec as P

NY, NZH, NCORE, NX, NZL = 4, 4, 2, 4, 2
NROW, NCOL = NY * NZH * NCORE, NX * NZL
CHIPS = NY * NZH
STEPS = ((1, 3), (3, 1))
TILE = 128
BF16 = jnp.bfloat16
F32 = jnp.float32
MB = 1024 * 1024


def exchange(value, axis, step):
    pairs = []
    for row in range(NROW):
        bits = STEPS[row % NCORE][step]
        there = row ^ ((bits * NZH if axis == "y" else bits) * NCORE)
        pairs += [(row * NCOL + col, there * NCOL + col) for col in range(NCOL)]
    return lax.ppermute(value, ("row", "col"), pairs)


def swap(value):
    pairs = [(row * NCOL + col, (row ^ 1) * NCOL + col) for row in range(NROW) for col in range(NCOL)]
    return lax.ppermute(value, ("row", "col"), pairs)


def in_vmem(kernel, results, operands, name, flops=MB, grant=16, **extra):
    spec = pl.BlockSpec(memory_space=pltpu.VMEM)
    outs = [shape if plain else pltpu.VMEM(shape.shape, shape.dtype) for shape, plain in results]
    out_specs = [pl.BlockSpec() if plain else spec for _, plain in results]
    return pl.pallas_call(
        kernel,
        in_specs=[spec] * len(operands),
        out_specs=out_specs,
        out_shape=outs,
        compiler_params=pltpu.CompilerParams(vmem_limit_bytes=grant * MB),
        cost_estimate=pl.CostEstimate(flops=0, bytes_accessed=1024, transcendentals=0),
        name=name,
        **extra,
    )(*[pltpu.with_memory_space_constraint(v, pltpu.VMEM) for v in operands])


def kept(shape, dtype):
    return jax.ShapeDtypeStruct(shape, dtype), False


def plain(shape, dtype):
    return jax.ShapeDtypeStruct(shape, dtype), True


def adjacency_kernel(place, where, masks, out, held, sems):
    count, slots = masks.shape[0], masks.shape[1]
    copies = [pltpu.make_async_copy(masks.at[j], held.at[j], sems.at[j]) for j in range(count)]
    for copy in copies:
        copy.start()
    for j, copy in enumerate(copies):
        cols = pl.ds(pl.multiple_of(place[j] * TILE, TILE), TILE)
        out[:, cols] = jnp.zeros((out.shape[0], TILE), BF16)
        copy.wait()
        for k in range(slots):
            at = pl.ds(pl.multiple_of(where[j * slots + k] * TILE, TILE), TILE)
            out[at, cols] = out[at, cols] + held[j, k].astype(F32).astype(BF16)


def adjacency(masks, place, where):
    count = masks.shape[0]
    return pl.pallas_call(
        adjacency_kernel,
        grid_spec=pltpu.PrefetchScalarGridSpec(
            num_scalar_prefetch=2,
            grid=(1,),
            in_specs=[pl.BlockSpec(memory_space=pl.ANY)],
            out_specs=pl.BlockSpec(memory_space=pltpu.VMEM),
            scratch_shapes=[pltpu.VMEM(masks.shape, masks.dtype), pltpu.SemaphoreType.DMA((count,))],
        ),
        out_shape=pltpu.VMEM((NCOL * TILE, count * TILE), BF16),
        compiler_params=pltpu.CompilerParams(vmem_limit_bytes=16 * MB),
        cost_estimate=pl.CostEstimate(flops=0, bytes_accessed=14 * MB, transcendentals=0),
        name="adjacency",
    )(place, where, pltpu.with_memory_space_constraint(masks, pltpu.HBM))


def gather_kernel(starts, adj, *refs):
    parts, out = refs[: len(starts)], refs[-1]
    start = refs[-2] if len(refs) > len(parts) + 1 else None
    rows = 2 * TILE
    rhs = jnp.concatenate([part[...] for part in parts], axis=0)
    for r in range(0, out.shape[0], rows):
        lhs = [adj[r : r + rows, at : at + part.shape[0]] for at, part in zip(starts, parts)]
        value = jnp.dot(jnp.concatenate(lhs, axis=1), rhs, preferred_element_type=F32)
        if start is not None:
            value = value + start[r : r + rows, :]
        out[r : r + rows, :] = value.astype(out.dtype)


def gather_matmul(adj, parts, start, dtype, name):
    starts = [(core * 2 + half) * CHIPS // 2 * TILE for core, half, _ in parts]
    parts = [part for *_, part in parts]
    rows, width = adj.shape[0], parts[0].shape[1]
    operands = [adj, *parts] + ([] if start is None else [start])
    return in_vmem(functools.partial(gather_kernel, starts), [kept((rows, width), dtype)], operands, name)[0]


def node_kernel(parts, base, degf_row, w_neigh, cotangent, grad, scaled_t, out):
    total = parts[0:TILE, :].astype(F32)
    for i in range(1, NCOL):
        total = total + parts[i * TILE : (i + 1) * TILE, :].astype(F32)
    degf_col = jnp.broadcast_to(degf_row[...], (TILE, TILE)).T[:, :1]
    mean = (total / degf_col).astype(BF16)
    pre = base[...] + jnp.dot(mean, w_neigh[...], preferred_element_type=F32)
    sig = jax.nn.sigmoid(pre)
    out[...] = (pre * sig).astype(BF16)
    slope = sig * (1.0 + pre * (1.0 - sig))
    grad_pre = (cotangent[...].astype(F32) * slope).astype(BF16)
    grad[...] = grad_pre
    proj_t = lax.dot_general(w_neigh[...], grad_pre, (((1,), (1,)), ((), ())), preferred_element_type=F32)
    scaled = (proj_t / degf_row[...]).astype(BF16)
    for i in range(NCOL):
        scaled_t[i, :, :] = scaled


def node_step(parts, base, degf_row, w_neigh, cotangent):
    rows, width = cotangent.shape
    results = [kept((rows, width), BF16), kept((NCOL, width, rows), BF16), plain((rows, width), BF16)]
    operands = (parts, base, degf_row, w_neigh, cotangent)
    return in_vmem(node_kernel, results, operands, "node_step", 4 * rows * width * width)


def spread_kernel(first, parts, adj, out):
    lhs = jnp.concatenate([parts[i] for i in range(NCOL)], axis=1)
    depth = NZH * TILE
    for at in range(0, out.shape[1], depth):
        value = jnp.dot(lhs, adj[:, first + at : first + at + depth], preferred_element_type=F32)
        out[:, at : at + depth] = value.astype(BF16)


def spread_matmul(parts, adj, core, half, name):
    shape = (parts.shape[1], CHIPS // 2 * TILE)
    first = (core * 2 + half) * shape[1]
    return in_vmem(functools.partial(spread_kernel, first), [kept(shape, BF16)], (parts, adj), name)[0]


def sum_kernel(*refs):
    value = refs[0][...].astype(F32)
    for ref in refs[1:-1]:
        value = value + ref[...].astype(F32)
    refs[-1][...] = value.astype(BF16)


def pair_sum(mine, theirs):
    return in_vmem(sum_kernel, [kept(mine.shape, BF16)], (mine, theirs), "pair_sum")[0]


def split_kernel(*refs):
    value = refs[0][...].astype(F32)
    for ref in refs[1:-2]:
        value = value + ref[...].astype(F32)
    stay, go = refs[-2:]
    half = stay.shape[1]
    stay[...] = value[:, :half]
    go[...] = value[:, half:].astype(BF16)


def split_sum(values, name):
    rows, cols = values[0].shape
    results = [kept((rows, cols // 2), F32), kept((rows, cols // 2), BF16)]
    return in_vmem(split_kernel, results, values, name)


def last_kernel(stay, got, own, out):
    back = stay[...] + got[...].astype(F32)
    out[...] = (own[...] + back.T).astype(BF16)


def last_sum(stay, got, own):
    return in_vmem(last_kernel, [plain(own.shape, BF16)], (stay, got, own), "last_sum")[0]


def body(features, degrees, tile_rows, tile_masks, w_self, w_neigh, bias, cotangent):
    row = lax.axis_index("row").astype(jnp.int32)

    device = jnp.arange(NROW, dtype=jnp.int32)
    differ = device ^ row
    bits = [(differ // (NZH * NCORE)) % NY, (differ // NCORE) % NZH]
    turn = []
    for d in bits:
        by_core = [jnp.where(d == k1, 1, jnp.where(d == k2, 2, jnp.where(d == 0, 0, 3))) for k1, k2 in STEPS]
        turn.append(jnp.where(device % NCORE == 0, *by_core))
    place = (differ % NCORE) * CHIPS + turn[0] * NZH + turn[1]
    adj = adjacency(tile_masks[0, 0], place.astype(jnp.int32), tile_rows[0, 0].reshape(-1))
    degf_row = degrees.astype(F32)[None, :]
    base = jnp.dot(features, w_self, preferred_element_type=F32) + bias[None, :]

    pair = jnp.concatenate([features, exchange(features, "z", 0)], axis=0)
    plane = jnp.concatenate([pair, exchange(pair, "z", 1)], axis=0)
    got = exchange(plane, "y", 0)
    got, adj, base, degf_row = lax.optimization_barrier((got, adj, base, degf_row))
    near = jnp.concatenate([plane, got], axis=0)
    far = exchange(near, "y", 1)
    part = gather_matmul(adj, [(0, 0, near), (1, 0, swap(near))], None, F32, "gather_near")
    far, part = lax.optimization_barrier((far, part))
    other = swap(far)
    part = gather_matmul(adj, [(0, 1, far)], part, F32, "gather_far")
    other, part = lax.optimization_barrier((other, part))
    summed = gather_matmul(adj, [(1, 1, other)], part, BF16, "gather_far_other")

    arrived = lax.all_to_all(summed, "col", 0, 0, tiled=True)
    grad_pre, scaled_t, output = node_step(arrived, base, degf_row, w_neigh, cotangent)

    table = lax.all_to_all(scaled_t, "col", 0, 0, tiled=True)
    own = lax.dot_general(grad_pre, w_self, (((1,), (1,)), ((), ())), preferred_element_type=F32)

    theirs = swap(spread_matmul(table, adj, 1, 1, "spread_far_other"))
    mine = spread_matmul(table, adj, 0, 1, "spread_far")
    near_other = spread_matmul(table, adj, 1, 0, "spread_near_other")
    theirs, mine, near_other = lax.optimization_barrier((theirs, mine, near_other))
    value = pair_sum(mine, theirs)
    value, table = lax.optimization_barrier((value, table))
    got = exchange(value, "y", 1)
    theirs = swap(near_other)
    mine = spread_matmul(table, adj, 0, 0, "spread_near")
    got, mine = lax.optimization_barrier((got, mine))
    stay, go = split_sum((mine, theirs, got), "sum_y1")
    stay, go = split_sum((stay, exchange(go, "y", 0)), "sum_y0")
    stay, go = split_sum((stay, exchange(go, "z", 1)), "sum_z1")
    grad_features = last_sum(stay, exchange(go, "z", 0), own)
    return output, grad_features


def solution(mesh):
    both = P(("row", "col"), None)
    return jax.shard_map(
        body,
        mesh=mesh,
        in_specs=(
            both,
            P(("row", "col")),
            P("row", "col", None, None),
            P("row", "col", None, None, None, None),
            P(),
            P(),
            P(),
            both,
        ),
        out_specs=(both, both),
        check_vma=False,
    )
```

time: 140 us -> 142 us (1.014); the launches traced: 140 us -> 139 us
  starting transfers between devices: 27.5 us -> 21.7 us
  waiting for transfers between devices: 51.2 us -> 56.4 us
  other arithmetic: 0.67 us -> 2.54 us
    ppermute x24 -> x12, starting transfers between devices: 27.5 us -> 21.7 us  [the longest x8 21.3 us: exchange(): return lax.ppermute(value, ('row', 'col'), pairs)]
    ppermute x24 -> x12, waiting for transfers between devices: 51.2 us -> 56.4 us  [the longest x8 54.6 us: exchange(): return lax.ppermute(value, ('row', 'col'), pairs)]
    concatenate x0 -> x2, other arithmetic: none -> 1.86 us  [the longest x1 0.94 us: body(): plane = jnp.concatenate([pair, exchange(pair, 'z', 1)], axis=0)]
    pallas_call x16 -> x13, Pallas kernels: 12.9 us -> 12.4 us  [in_vmem(): pl.pallas_call(kernel, in_specs=[spec] * len(operands), out_specs=out_spe...]
  transfers between devices with their start and end apart: 24 -> 12, of which waited for: 14 -> 11; matrix products, arithmetic and copies ran while one was open for 2% -> 2% of each run, Pallas kernels for 10% -> 9%
where the time goes in v6:
time: 142 us; the launch traced here: 139 us
  waiting for transfers between devices  56.4 us (40%)
  blocking collectives  37.7 us (27%)
  starting transfers between devices  21.7 us (15%)
  Pallas kernels  18 us (13%)
  other arithmetic  2.54 us (2%)
  local copies, waits for them, and re-layouts  1.88 us (1%)
    ppermute x8, waiting for transfers between devices, exchange(): return lax.ppermute(value, ('row', 'col'), pairs)  54.6 us
    ppermute x8, starting transfers between devices, exchange(): return lax.ppermute(value, ('row', 'col'), pairs)  21.3 us
    all_to_all x1, blocking collectives, body(): arrived = lax.all_to_all(summed, 'col', 0, 0, tiled=True)  20 us
    all_to_all x1, blocking collectives, body(): table = lax.all_to_all(scaled_t, 'col', 0, 0, tiled=True)  17.7 us
    pallas_call x13, Pallas kernels, in_vmem(): pl.pallas_call(kernel, in_specs=[spec] * len(operands), out_specs=out_spe...  12.4 us
    pallas_call x1, Pallas kernels, adjacency(): pl.pallas_call(adjacency_kernel, grid_spec=pltpu.PrefetchScalarGridSpec(n...  5.53 us
  transfers between devices with their start and end apart: 12, of which 11 were waited for; matrix products, arithmetic and copies ran while one was open for 2% of the time, Pallas kernels for 9%

profile of v6, /device:TPU:32, one launch (start us, length us, event | category | flops | bytes accessed | tf_op | source)
XLA Modules:
  0.0 139.5 jit_solution(10692050309372615540)
XLA Ops:
  0.6 3.4 %collective-permute-start = (bf16[128,512]{1,0:T(8,128)(2,1)}, bf16[128,512]{1,0:T(8,128)(2,1)S(1)}, u32[]{:S(2)}, u32[]{:S(2)}) collective-permute-start(bf16[128,512]{1,0:T(8,128)(2,1)} %param.8), channel_id=1, source_target_pairs={{0,16},{1,17},{2,18},{3,19},{4,20},{5,21},{6,22},{7,23},{8,56},{9,... | collective-permute-start | bytes 393224 | tf_op jit(solution)/shard_map/ppermute | solution.py:26
  4.0 3.8 %collective-permute-done = bf16[128,512]{1,0:T(8,128)(2,1)S(1)} collective-permute-done((bf16[128,512]{1,0:T(8,128)(2,1)}, bf16[128,512]{1,0:T(8,128)(2,1)S(1)}, u32[]{:S(2)}, u32[]{:S(2)}) %collective-permute-start) | collective-permute-done | bytes 131104 | tf_op jit(solution)/shard_map/ppermute | solution.py:26
  7.8 0.9 pad_maximum_fusion.1
  8.7 5.5 %collective-permute-start.1 = (bf16[256,512]{1,0:T(8,128)(2,1)S(1)}, bf16[256,512]{1,0:T(8,128)(2,1)S(1)}, u32[]{:S(2)}, u32[]{:S(2)}) collective-permute-start(bf16[256,512]{1,0:T(8,128)(2,1)S(1)} %pad_maximum_fusion.1), channel_id=1, source_target_pairs={{0,48},{1,49},{2,50},{3,51},{4,52},{5,53},{6,54},{7,55},{8,24},{9,... | collective-permute-start | bytes 786440 | tf_op jit(solution)/shard_map/ppermute | solution.py:26
  14.2 0.9 constant_dynamic-update-slice_fusion.3
  15.8 5.6 %collective-permute-done.1 = bf16[256,512]{1,0:T(8,128)(2,1)S(1)} collective-permute-done((bf16[256,512]{1,0:T(8,128)(2,1)S(1)}, bf16[256,512]{1,0:T(8,128)(2,1)S(1)}, u32[]{:S(2)}, u32[]{:S(2)}) %collective-permute-start.1) | collective-permute-done | bytes 262176 | tf_op jit(solution)/shard_map/ppermute | solution.py:26
  21.3 0.9 pad_maximum_fusion
  22.3 0.9 collective-permute-start.2
  23.3 0.8 copy.11
  24.2 5.5 %adjacency.1.adj = bf16[1024,4096]{1,0:T(8,128)(2,1)S(1)} custom-call(s32[32]{0:T(128)S(1)} %fusion.2.place, s32[96]{0:T(128)S(1)} %reshape_squeeze.3.where, s32[32,3,128,128]{3,2,1,0:T(8,128)} %bitcast.13), custom_call_target="tpu_custom_call" | custom-call | bytes 14680064 | tf_op jit(solution)/shard_map/adjacency/pallas_call | solution.py:74
  30.0 1.5 %collective-permute-done.2 = bf16[512,512]{1,0:T(8,128)(2,1)S(1)} collective-permute-done((bf16[512,512]{1,0:T(8,128)(2,1)S(1)}, bf16[512,512]{1,0:T(8,128)(2,1)S(1)}, u32[]{:S(2)}, u32[]{:S(2)}) %collective-permute-start.2) | collective-permute-done | bytes 524320 | tf_op jit(solution)/shard_map/ppermute | solution.py:26
  31.7 2.4 %collective-permute-start.3 = (bf16[1024,512]{1,0:T(8,128)(2,1)S(1)}, bf16[1024,512]{1,0:T(8,128)(2,1)S(1)}, u32[]{:S(2)}, u32[]{:S(2)}) collective-permute-start(bf16[1024,512]{1,0:T(8,128)(2,1)S(1)} %constant_dynamic-update-slice_fusion.refs_0_), channel_id=1, source_target_pairs={{0,192},{1,193},{2,194},{3,195},{4,196},{5,197},{6,198},{7,199},{8... | collective-permute-start | bytes 3145736 | tf_op jit(solution)/shard_map/ppermute | solution.py:26
  34.3 2.3 %gather_near.1.refs_1_ = f32[1024,512]{1,0:T(8,128)S(1)} custom-call(bf16[1024,4096]{1,0:T(8,128)(2,1)S(1)} %adjacency.1.adj, bf16[1024,512]{1,0:T(8,128)(2,1)S(1)} %constant_dynamic-update-slice_fusion.refs_0_, bf16[1024,512]{1,0:T(8,128)(2,1)S(1)} %collective-permute-done.4.refs_1_), custom_call_target="tpu_custom_call" | custom-call | bytes 1024 | tf_op jit(solution)/shard_map/gather_near/pallas_call | solution.py:38
  36.7 11.1 %collective-permute-done.3.refs_0_ = bf16[1024,512]{1,0:T(8,128)(2,1)S(1)} collective-permute-done((bf16[1024,512]{1,0:T(8,128)(2,1)S(1)}, bf16[1024,512]{1,0:T(8,128)(2,1)S(1)}, u32[]{:S(2)}, u32[]{:S(2)}) %collective-permute-start.3) | collective-permute-done | bytes 1048608 | tf_op jit(solution)/shard_map/ppermute | solution.py:26
  47.8 1.2 gather_far.1.refs_1_
  49.1 1.4 collective-permute-done.5.refs_0_
  50.5 1.2 gather_far_other.1
  51.7 20.0 %all_to_all.16 = bf16[8,128,512]{2,1,0:T(8,128)(2,1)S(1)} all-to-all(bf16[8,128,512]{2,1,0:T(8,128)(2,1)S(1)} %bitcast.11), channel_id=1, replica_groups=mesh['row'=32,'col'=8] {'col'}, dimensions={0} | all-to-all | bytes 2097152 | tf_op jit(solution)/shard_map/all_to_all | solution.py:214
  71.7 1.1 node_step.1
  72.8 17.7 %all_to_all.17.parts = bf16[8,512,128]{2,1,0:T(8,128)(2,1)S(1)} all-to-all(bf16[8,512,128]{2,1,0:T(8,128)(2,1)S(1)} %get-tuple-element.35), channel_id=1, replica_groups=mesh['row'=32,'col'=8] {'col'}, dimensions={0} | all-to-all | bytes 2097152 | tf_op jit(solution)/shard_map/all_to_all | solution.py:217
  90.5 1.2 spread_far_other.1
  92.0 1.2 spread_near_other.1
  93.3 1.2 spread_far.1.refs_0_
  94.9 3.1 %collective-permute-start.7 = (bf16[512,1024]{1,0:T(8,128)(2,1)S(1)}, bf16[512,1024]{1,0:T(8,128)(2,1)S(1)}, u32[]{:S(2)}, u32[]{:S(2)}) collective-permute-start(bf16[512,1024]{1,0:T(8,128)(2,1)S(1)} %pair_sum.1), channel_id=1, source_target_pairs={{0,192},{1,193},{2,194},{3,195},{4,196},{5,197},{6,198},{7,199},{8... | collective-permute-start | bytes 3145736 | tf_op jit(solution)/shard_map/ppermute | solution.py:26
  98.0 1.2 spread_near.1.refs_0_
  99.3 11.7 %collective-permute-done.7.refs_2_ = bf16[512,1024]{1,0:T(8,128)(2,1)S(1)} collective-permute-done((bf16[512,1024]{1,0:T(8,128)(2,1)S(1)}, bf16[512,1024]{1,0:T(8,128)(2,1)S(1)}, u32[]{:S(2)}, u32[]{:S(2)}) %collective-permute-start.7) | collective-permute-done | bytes 1048608 | tf_op jit(solution)/shard_map/ppermute | solution.py:26
  111.5 9.2 %collective-permute-done.9.refs_1_ = bf16[512,512]{1,0:T(8,128)(2,1)S(1)} collective-permute-done((bf16[512,512]{1,0:T(8,128)(2,1)S(1)}, bf16[512,512]{1,0:T(8,128)(2,1)S(1)}, u32[]{:S(2)}, u32[]{:S(2)}) %collective-permute-start.9) | collective-permute-done | bytes 524320 | tf_op jit(solution)/shard_map/ppermute | solution.py:26
  120.7 4.6 %collective-permute-start.10 = (bf16[512,256]{1,0:T(8,128)(2,1)S(1)}, bf16[512,256]{1,0:T(8,128)(2,1)S(1)}, u32[]{:S(2)}, u32[]{:S(2)}) collective-permute-start(bf16[512,256]{1,0:T(8,128)(2,1)S(1)} %get-tuple-element.46), channel_id=1, source_target_pairs={{0,48},{1,49},{2,50},{3,51},{4,52},{5,53},{6,54},{7,55},{8,24},{9,... | collective-permute-start | bytes 786440 | tf_op jit(solution)/shard_map/ppermute | solution.py:26
  125.4 7.1 %collective-permute-done.10.refs_1_ = bf16[512,256]{1,0:T(8,128)(2,1)S(1)} collective-permute-done((bf16[512,256]{1,0:T(8,128)(2,1)S(1)}, bf16[512,256]{1,0:T(8,128)(2,1)S(1)}, u32[]{:S(2)}, u32[]{:S(2)}) %collective-permute-start.10) | collective-permute-done | bytes 262176 | tf_op jit(solution)/shard_map/ppermute | solution.py:26
  132.6 1.3 collective-permute-start.11
  134.1 4.5 %collective-permute-done.11.got = bf16[512,128]{1,0:T(8,128)(2,1)S(1)} collective-permute-done((bf16[512,128]{1,0:T(8,128)(2,1)S(1)}, bf16[512,128]{1,0:T(8,128)(2,1)S(1)}, u32[]{:S(2)}, u32[]{:S(2)}) %collective-permute-start.11) | collective-permute-done | bytes 131104 | tf_op jit(solution)/shard_map/ppermute | solution.py:26
  138.7 0.8 last_sum.1
  (30 shorter events, 3.0 us)
Async XLA Ops:
  0.6 29.1 %copy-start = (bf16[512,512]{1,0:T(8,128)(2,1)S(1)}, bf16[512,512]{1,0:T(8,128)(2,1)}, u32[]{:S(2)}) copy-start(bf16[512,512]{1,0:T(8,128)(2,1)} %param.12) | copy-start | bytes 1572868
  0.6 7.1 %collective-permute-start = (bf16[128,512]{1,0:T(8,128)(2,1)}, bf16[128,512]{1,0:T(8,128)(2,1)S(1)}, u32[]{:S(2)}, u32[]{:S(2)}) collective-permute-start(bf16[128,512]{1,0:T(8,128)(2,1)} %param.8), channel_id=1, source_target_pairs={{0,16},{1,17},{2,18},{3,19},{4,20},{5,21},{6,22},{7,23},{8,56},{9,... | collective-permute-start | bytes 393224 | tf_op jit(solution)/shard_map/ppermute | solution.py:26
  8.7 12.7 %collective-permute-start.1 = (bf16[256,512]{1,0:T(8,128)(2,1)S(1)}, bf16[256,512]{1,0:T(8,128)(2,1)S(1)}, u32[]{:S(2)}, u32[]{:S(2)}) collective-permute-start(bf16[256,512]{1,0:T(8,128)(2,1)S(1)} %pad_maximum_fusion.1), channel_id=1, source_target_pairs={{0,48},{1,49},{2,50},{3,51},{4,52},{5,53},{6,54},{7,55},{8,24},{9,... | collective-permute-start | bytes 786440 | tf_op jit(solution)/shard_map/ppermute | solution.py:26
  22.3 9.3 %collective-permute-start.2 = (bf16[512,512]{1,0:T(8,128)(2,1)S(1)}, bf16[512,512]{1,0:T(8,128)(2,1)S(1)}, u32[]{:S(2)}, u32[]{:S(2)}) collective-permute-start(bf16[512,512]{1,0:T(8,128)(2,1)S(1)} %pad_maximum_fusion), channel_id=1, source_target_pairs={{0,64},{1,65},{2,66},{3,67},{4,68},{5,69},{6,70},{7,71},{8,200},{9... | collective-permute-start | bytes 1572872 | tf_op jit(solution)/shard_map/ppermute | solution.py:26
  24.1 5.6 %copy-start.3 = (bf16[128,512]{1,0:T(8,128)(2,1)S(1)}, bf16[128,512]{1,0:T(8,128)(2,1)}, u32[]{:S(2)}) copy-start(bf16[128,512]{1,0:T(8,128)(2,1)} %param.8) | copy-start | bytes 393220
  24.1 5.6 %copy-start.4 = (f32[512]{0:T(512)S(1)}, f32[512]{0:T(512)}, u32[]{:S(2)}) copy-start(f32[512]{0:T(512)} %param.14) | copy-start | bytes 6148
  31.6 2.7 %collective-permute-start.4 = (bf16[1024,512]{1,0:T(8,128)(2,1)S(1)}, bf16[1024,512]{1,0:T(8,128)(2,1)S(1)}, u32[]{:S(2)}, u32[]{:S(2)}) collective-permute-start(bf16[1024,512]{1,0:T(8,128)(2,1)S(1)} %constant_dynamic-update-slice_fusion.refs_0_), channel_id=1, source_target_pairs={{0,8},{1,9},{2,10},{3,11},{4,12},{5,13},{6,14},{7,15},{8,0},{9,1},... | collective-permute-start | bytes 3145736 | tf_op jit(solution)/shard_map/ppermute | solution.py:31
  31.7 16.1 %collective-permute-start.3 = (bf16[1024,512]{1,0:T(8,128)(2,1)S(1)}, bf16[1024,512]{1,0:T(8,128)(2,1)S(1)}, u32[]{:S(2)}, u32[]{:S(2)}) collective-permute-start(bf16[1024,512]{1,0:T(8,128)(2,1)S(1)} %constant_dynamic-update-slice_fusion.refs_0_), channel_id=1, source_target_pairs={{0,192},{1,193},{2,194},{3,195},{4,196},{5,197},{6,198},{7,199},{8... | collective-permute-start | bytes 3145736 | tf_op jit(solution)/shard_map/ppermute | solution.py:26
  47.8 2.7 %collective-permute-start.5 = (bf16[1024,512]{1,0:T(8,128)(2,1)S(1)}, bf16[1024,512]{1,0:T(8,128)(2,1)S(1)}, u32[]{:S(2)}, u32[]{:S(2)}) collective-permute-start(bf16[1024,512]{1,0:T(8,128)(2,1)S(1)} %collective-permute-done.3.refs_0_), channel_id=1, source_target_pairs={{0,8},{1,9},{2,10},{3,11},{4,12},{5,13},{6,14},{7,15},{8,0},{9,1},... | collective-permute-start | bytes 3145736 | tf_op jit(solution)/shard_map/ppermute | solution.py:31
  49.0 22.6 %copy-start.1 = (bf16[512,512]{1,0:T(8,128)(2,1)S(1)}, bf16[512,512]{1,0:T(8,128)(2,1)}, u32[]{:S(2)}) copy-start(bf16[512,512]{1,0:T(8,128)(2,1)} %w_neigh.1) | copy-start | bytes 1572868
  49.1 22.6 %copy-start.2 = (bf16[128,512]{1,0:T(8,128)(2,1)S(1)}, bf16[128,512]{1,0:T(8,128)(2,1)}, u32[]{:S(2)}) copy-start(bf16[128,512]{1,0:T(8,128)(2,1)} %cotangent.1) | copy-start | bytes 393220
  91.7 2.9 %collective-permute-start.6 = (bf16[512,1024]{1,0:T(8,128)(2,1)S(1)}, bf16[512,1024]{1,0:T(8,128)(2,1)S(1)}, u32[]{:S(2)}, u32[]{:S(2)}) collective-permute-start(bf16[512,1024]{1,0:T(8,128)(2,1)S(1)} %spread_far_other.1), channel_id=1, source_target_pairs={{0,8},{1,9},{2,10},{3,11},{4,12},{5,13},{6,14},{7,15},{8,0},{9,1},... | collective-permute-start | bytes 3145736 | tf_op jit(solution)/shard_map/ppermute | solution.py:31
  94.9 16.1 %collective-permute-start.7 = (bf16[512,1024]{1,0:T(8,128)(2,1)S(1)}, bf16[512,1024]{1,0:T(8,128)(2,1)S(1)}, u32[]{:S(2)}, u32[]{:S(2)}) collective-permute-start(bf16[512,1024]{1,0:T(8,128)(2,1)S(1)} %pair_sum.1), channel_id=1, source_target_pairs={{0,192},{1,193},{2,194},{3,195},{4,196},{5,197},{6,198},{7,199},{8... | collective-permute-start | bytes 3145736 | tf_op jit(solution)/shard_map/ppermute | solution.py:26
  98.0 13.0 %collective-permute-start.8 = (bf16[512,1024]{1,0:T(8,128)(2,1)S(1)}, bf16[512,1024]{1,0:T(8,128)(2,1)S(1)}, u32[]{:S(2)}, u32[]{:S(2)}) collective-permute-start(bf16[512,1024]{1,0:T(8,128)(2,1)S(1)} %spread_near_other.1), channel_id=1, source_target_pairs={{0,8},{1,9},{2,10},{3,11},{4,12},{5,13},{6,14},{7,15},{8,0},{9,1},... | collective-permute-start | bytes 3145736 | tf_op jit(solution)/shard_map/ppermute | solution.py:31
  111.4 9.3 %collective-permute-start.9 = (bf16[512,512]{1,0:T(8,128)(2,1)S(1)}, bf16[512,512]{1,0:T(8,128)(2,1)S(1)}, u32[]{:S(2)}, u32[]{:S(2)}) collective-permute-start(bf16[512,512]{1,0:T(8,128)(2,1)S(1)} %get-tuple-element.44), channel_id=1, source_target_pairs={{0,64},{1,65},{2,66},{3,67},{4,68},{5,69},{6,70},{7,71},{8,200},{9... | collective-permute-start | bytes 1572872 | tf_op jit(solution)/shard_map/ppermute | solution.py:26
  120.7 11.8 %collective-permute-start.10 = (bf16[512,256]{1,0:T(8,128)(2,1)S(1)}, bf16[512,256]{1,0:T(8,128)(2,1)S(1)}, u32[]{:S(2)}, u32[]{:S(2)}) collective-permute-start(bf16[512,256]{1,0:T(8,128)(2,1)S(1)} %get-tuple-element.46), channel_id=1, source_target_pairs={{0,48},{1,49},{2,50},{3,51},{4,52},{5,53},{6,54},{7,55},{8,24},{9,... | collective-permute-start | bytes 786440 | tf_op jit(solution)/shard_map/ppermute | solution.py:26
  132.6 6.1 %collective-permute-start.11 = (bf16[512,128]{1,0:T(8,128)(2,1)S(1)}, bf16[512,128]{1,0:T(8,128)(2,1)S(1)}, u32[]{:S(2)}, u32[]{:S(2)}) collective-permute-start(bf16[512,128]{1,0:T(8,128)(2,1)S(1)} %get-tuple-element.48), channel_id=1, source_target_pairs={{0,16},{1,17},{2,18},{3,19},{4,20},{5,21},{6,22},{7,23},{8,56},{9,... | collective-permute-start | bytes 393224 | tf_op jit(solution)/shard_map/ppermute | solution.py:26

commit v7 on v6

--- a/solution.py
+++ b/solution.py
@@ -87,13 +87,28 @@
     )(place, where, pltpu.with_memory_space_constraint(masks, pltpu.HBM))
 
 
+def halves_kernel(first, second, *outs):
+    rows = first.shape[0]
+    width = outs[0].shape[1]
+    for w, out in enumerate(outs):
+        out[:rows, :] = first[:, w * width : (w + 1) * width]
+        out[rows:, :] = second[:, w * width : (w + 1) * width]
+
+
+def join(first, second, count, name):
+    shape = (2 * first.shape[0], first.shape[1] // count)
+    return in_vmem(halves_kernel, [kept(shape, BF16)] * count, (first, second), name)
+
+
 def gather_kernel(starts, adj, *refs):
-    parts, out = refs[: len(starts)], refs[-1]
+    parts, out = refs[: 2 * len(starts)], refs[-1]
     start = refs[-2] if len(refs) > len(parts) + 1 else None
     rows = 2 * TILE
-    rhs = jnp.concatenate([part[...] for part in parts], axis=0)
+    rhs = [jnp.concatenate([parts[i][...], parts[i + 1][...]], axis=1) for i in range(0, len(parts), 2)]
+    rhs = jnp.concatenate(rhs, axis=0)
+    depth = parts[0].shape[0]
     for r in range(0, out.shape[0], rows):
-        lhs = [adj[r : r + rows, at : at + part.shape[0]] for at, part in zip(starts, parts)]
+        lhs = [adj[r : r + rows, at : at + depth] for at in starts]
         value = jnp.dot(jnp.concatenate(lhs, axis=1), rhs, preferred_element_type=F32)
         if start is not None:
             value = value + start[r : r + rows, :]
@@ -102,9 +117,9 @@
 
 def gather_matmul(adj, parts, start, dtype, name):
     starts = [(core * 2 + half) * CHIPS // 2 * TILE for core, half, _ in parts]
-    parts = [part for *_, part in parts]
-    rows, width = adj.shape[0], parts[0].shape[1]
-    operands = [adj, *parts] + ([] if start is None else [start])
+    arrays = [wave for *_, waves in parts for wave in waves]
+    rows, width = adj.shape[0], 2 * arrays[0].shape[1]
+    operands = [adj, *arrays] + ([] if start is None else [start])
     return in_vmem(functools.partial(gather_kernel, starts), [kept((rows, width), dtype)], operands, name)[0]
 
 
@@ -133,18 +148,20 @@
     return in_vmem(node_kernel, results, operands, "node_step", 4 * rows * width * width)
 
 
-def spread_kernel(first, parts, adj, out):
+def spread_kernel(first, parts, adj, *outs):
     lhs = jnp.concatenate([parts[i] for i in range(NCOL)], axis=1)
     depth = NZH * TILE
-    for at in range(0, out.shape[1], depth):
-        value = jnp.dot(lhs, adj[:, first + at : first + at + depth], preferred_element_type=F32)
-        out[:, at : at + depth] = value.astype(BF16)
+    rows, cols = outs[0].shape
+    for at in range(0, cols, depth):
+        value = jnp.dot(lhs, adj[:, first + at : first + at + depth], preferred_element_type=F32).astype(BF16)
+        for w, out in enumerate(outs):
+            out[:, at : at + depth] = value[w * rows : (w + 1) * rows, :]
 
 
 def spread_matmul(parts, adj, core, half, name):
-    shape = (parts.shape[1], CHIPS // 2 * TILE)
+    shape = (parts.shape[1] // 2, CHIPS // 2 * TILE)
     first = (core * 2 + half) * shape[1]
-    return in_vmem(functools.partial(spread_kernel, first), [kept(shape, BF16)], (parts, adj), name)[0]
+    return in_vmem(functools.partial(spread_kernel, first), [kept(shape, BF16)] * 2, (parts, adj), name)
 
 
 def sum_kernel(*refs):
@@ -174,13 +191,14 @@
     return in_vmem(split_kernel, results, values, name)
 
 
-def last_kernel(stay, got, own, out):
-    back = stay[...] + got[...].astype(F32)
-    out[...] = (own[...] + back.T).astype(BF16)
-
-
-def last_sum(stay, got, own):
-    return in_vmem(last_kernel, [plain(own.shape, BF16)], (stay, got, own), "last_sum")[0]
+def last_kernel(*refs):
+    waves, own, out = refs[:-2], refs[-2], refs[-1]
+    back = [waves[i][...] + waves[i + 1][...].astype(F32) for i in range(0, len(waves), 2)]
+    out[...] = (own[...] + jnp.concatenate(back, axis=0).T).astype(BF16)
+
+
+def last_sum(waves, own):
+    return in_vmem(last_kernel, [plain(own.shape, BF16)], (*waves, own), "last_sum")[0]
 
 
 def body(features, degrees, tile_rows, tile_masks, w_self, w_neigh, bias, cotangent):
@@ -198,17 +216,20 @@
     degf_row = degrees.astype(F32)[None, :]
     base = jnp.dot(features, w_self, preferred_element_type=F32) + bias[None, :]
 
-    pair = jnp.concatenate([features, exchange(features, "z", 0)], axis=0)
-    plane = jnp.concatenate([pair, exchange(pair, "z", 1)], axis=0)
-    got = exchange(plane, "y", 0)
-    got, adj, base, degf_row = lax.optimization_barrier((got, adj, base, degf_row))
-    near = jnp.concatenate([plane, got], axis=0)
-    far = exchange(near, "y", 1)
-    part = gather_matmul(adj, [(0, 0, near), (1, 0, swap(near))], None, F32, "gather_near")
-    far, part = lax.optimization_barrier((far, part))
-    other = swap(far)
+    got, adj = lax.optimization_barrier((exchange(features, "z", 0), adj))
+    waves = join(features, got, 2, "join_z0")
+    got = [exchange(v, "z", 1) for v in waves]
+    waves = [join(v, g, 1, "join_z1")[0] for v, g in zip(waves, got)]
+    got = [exchange(v, "y", 0) for v in waves]
+    got[1], base, degf_row = lax.optimization_barrier((got[1], base, degf_row))
+    near = [join(v, g, 1, "join_y0")[0] for v, g in zip(waves, got)]
+    far = [exchange(v, "y", 1) for v in near]
+    other = [swap(v) for v in near]
+    part = gather_matmul(adj, [(0, 0, near), (1, 0, other)], None, F32, "gather_near")
+    *far, part = lax.optimization_barrier((*far, part))
+    other = [swap(v) for v in far]
     part = gather_matmul(adj, [(0, 1, far)], part, F32, "gather_far")
-    other, part = lax.optimization_barrier((other, part))
+    *other, part = lax.optimization_barrier((*other, part))
     summed = gather_matmul(adj, [(1, 1, other)], part, BF16, "gather_far_other")
 
     arrived = lax.all_to_all(summed, "col", 0, 0, tiled=True)
@@ -217,20 +238,24 @@
     table = lax.all_to_all(scaled_t, "col", 0, 0, tiled=True)
     own = lax.dot_general(grad_pre, w_self, (((1,), (1,)), ((), ())), preferred_element_type=F32)
 
-    theirs = swap(spread_matmul(table, adj, 1, 1, "spread_far_other"))
+    theirs = [swap(v) for v in spread_matmul(table, adj, 1, 1, "spread_far_other")]
     mine = spread_matmul(table, adj, 0, 1, "spread_far")
     near_other = spread_matmul(table, adj, 1, 0, "spread_near_other")
-    theirs, mine, near_other = lax.optimization_barrier((theirs, mine, near_other))
-    value = pair_sum(mine, theirs)
-    value, table = lax.optimization_barrier((value, table))
-    got = exchange(value, "y", 1)
-    theirs = swap(near_other)
+    *theirs, table = lax.optimization_barrier((*theirs, *mine, *near_other, table))
+    theirs, mine, near_other = theirs[:2], theirs[2:4], theirs[4:]
+    values = [pair_sum(a, b) for a, b in zip(mine, theirs)]
+    values[0], table = lax.optimization_barrier((values[0], table))
+    got = [exchange(v, "y", 1) for v in values]
+    theirs = [swap(v) for v in near_other]
     mine = spread_matmul(table, adj, 0, 0, "spread_near")
-    got, mine = lax.optimization_barrier((got, mine))
-    stay, go = split_sum((mine, theirs, got), "sum_y1")
-    stay, go = split_sum((stay, exchange(go, "y", 0)), "sum_y0")
-    stay, go = split_sum((stay, exchange(go, "z", 1)), "sum_z1")
-    grad_features = last_sum(stay, exchange(go, "z", 0), own)
+    got[0], *mine = lax.optimization_barrier((got[0], *mine))
+    ends = []
+    for w in range(2):
+        stay, go = split_sum((mine[w], theirs[w], got[w]), "sum_y1")
+        stay, go = split_sum((stay, exchange(go, "y", 0)), "sum_y0")
+        stay, go = split_sum((stay, exchange(go, "z", 1)), "sum_z1")
+        ends += [stay, exchange(go, "z", 0)]
+    grad_features = last_sum(ends, own)
     return output, grad_features
 
 

time: 142 us -> 136 us (0.958); the launches traced: 139 us -> 135 us
  waiting for transfers between devices: 56.4 us -> 46.1 us
  starting transfers between devices: 21.7 us -> 30.2 us
  other arithmetic: 2.54 us -> 0.03 us
    ppermute x8 -> x15, waiting for transfers between devices: 54.6 us -> 45.2 us  [exchange(): return lax.ppermute(value, ('row', 'col'), pairs)]
    ppermute x8 -> x15, starting transfers between devices: 21.3 us -> 28.1 us  [exchange(): return lax.ppermute(value, ('row', 'col'), pairs)]
    concatenate x2 -> x0, other arithmetic: 1.86 us -> none  [the longest x1 0.94 us: body(): plane = jnp.concatenate([pair, exchange(pair, 'z', 1)], axis=0)]
    ppermute x4 -> x8, starting transfers between devices: 0.37 us -> 2.08 us  [swap(): return lax.ppermute(value, ('row', 'col'), pairs)]
    pallas_call x13 -> x22, Pallas kernels: 12.4 us -> 12.6 us  [in_vmem(): pl.pallas_call(kernel, in_specs=[spec] * len(operands), out_specs=out_spe...]
  transfers between devices with their start and end apart: 12 -> 23, of which waited for: 11 -> 13; matrix products, arithmetic and copies ran while one was open for 2% -> 1% of each run, Pallas kernels for 9% -> 10%
where the time goes in v7:
time: 136 us; the launch traced here: 135 us
  waiting for transfers between devices  46.1 us (34%)
  blocking collectives  38.3 us (28%)
  starting transfers between devices  30.2 us (22%)
  Pallas kernels  18.1 us (13%)
    ppermute x15, waiting for transfers between devices, exchange(): return lax.ppermute(value, ('row', 'col'), pairs)  45.2 us
    ppermute x15, starting transfers between devices, exchange(): return lax.ppermute(value, ('row', 'col'), pairs)  28.1 us
    all_to_all x1, blocking collectives, body(): arrived = lax.all_to_all(summed, 'col', 0, 0, tiled=True)  20.6 us
    all_to_all x1, blocking collectives, body(): table = lax.all_to_all(scaled_t, 'col', 0, 0, tiled=True)  17.7 us
    pallas_call x22, Pallas kernels, in_vmem(): pl.pallas_call(kernel, in_specs=[spec] * len(operands), out_specs=out_spe...  12.6 us
    pallas_call x1, Pallas kernels, adjacency(): pl.pallas_call(adjacency_kernel, grid_spec=pltpu.PrefetchScalarGridSpec(n...  5.53 us
  transfers between devices with their start and end apart: 23, of which 13 were waited for; matrix products, arithmetic and copies ran while one was open for 1% of the time, Pallas kernels for 10%

profile of v7, /device:TPU:32, one launch (start us, length us, event | category | flops | bytes accessed | tf_op | source)
XLA Modules:
  0.0 135.1 jit_solution(1325346001273503124)
XLA Ops:
  0.6 3.4 %collective-permute-start = (bf16[128,512]{1,0:T(8,128)(2,1)}, bf16[128,512]{1,0:T(8,128)(2,1)S(1)}, u32[]{:S(2)}, u32[]{:S(2)}) collective-permute-start(bf16[128,512]{1,0:T(8,128)(2,1)} %first.1), channel_id=1, source_target_pairs={{0,16},{1,17},{2,18},{3,19},{4,20},{5,21},{6,22},{7,23},{8,56},{9,... | collective-permute-start | bytes 393224 | tf_op jit(solution)/shard_map/ppermute | solution.py:26
  4.9 5.5 %adjacency.1.adj = bf16[1024,4096]{1,0:T(8,128)(2,1)S(1)} custom-call(s32[32]{0:T(128)S(1)} %fusion.2.place, s32[96]{0:T(128)S(1)} %reshape_squeeze.3.where, s32[32,3,128,128]{3,2,1,0:T(8,128)} %bitcast.13), custom_call_target="tpu_custom_call" | custom-call | bytes 14680064 | tf_op jit(solution)/shard_map/adjacency/pallas_call | solution.py:74
  10.5 3.7 %collective-permute-start.4 = (bf16[256,256]{1,0:T(8,128)(2,1)S(1)}, bf16[256,256]{1,0:T(8,128)(2,1)S(1)}, u32[]{:S(2)}, u32[]{:S(2)}) collective-permute-start(bf16[256,256]{1,0:T(8,128)(2,1)S(1)} %get-tuple-element.53.first), channel_id=1, source_target_pairs={{0,48},{1,49},{2,50},{3,51},{4,52},{5,53},{6,54},{7,55},{8,24},{9,... | collective-permute-start | bytes 393224 | tf_op jit(solution)/shard_map/ppermute | solution.py:26
  14.7 4.2 %collective-permute-done.4.second = bf16[256,256]{1,0:T(8,128)(2,1)S(1)} collective-permute-done((bf16[256,256]{1,0:T(8,128)(2,1)S(1)}, bf16[256,256]{1,0:T(8,128)(2,1)S(1)}, u32[]{:S(2)}, u32[]{:S(2)}) %collective-permute-start.4) | collective-permute-done | bytes 131104 | tf_op jit(solution)/shard_map/ppermute | solution.py:26
  19.0 1.9 %collective-permute-start.5 = (bf16[512,256]{1,0:T(8,128)(2,1)S(1)}, bf16[512,256]{1,0:T(8,128)(2,1)S(1)}, u32[]{:S(2)}, u32[]{:S(2)}) collective-permute-start(bf16[512,256]{1,0:T(8,128)(2,1)S(1)} %join_z1.3.first), channel_id=1, source_target_pairs={{0,64},{1,65},{2,66},{3,67},{4,68},{5,69},{6,70},{7,71},{8,200},{9... | collective-permute-start | bytes 786440 | tf_op jit(solution)/shard_map/ppermute | solution.py:26
  21.4 1.7 %collective-permute-start.2 = (bf16[512,256]{1,0:T(8,128)(2,1)S(1)}, bf16[512,256]{1,0:T(8,128)(2,1)S(1)}, u32[]{:S(2)}, u32[]{:S(2)}) collective-permute-start(bf16[512,256]{1,0:T(8,128)(2,1)S(1)} %join_z1.2.first), channel_id=1, source_target_pairs={{0,64},{1,65},{2,66},{3,67},{4,68},{5,69},{6,70},{7,71},{8,200},{9... | collective-permute-start | bytes 786440 | tf_op jit(solution)/shard_map/ppermute | solution.py:26
  23.3 2.2 %collective-permute-done.5.second = bf16[512,256]{1,0:T(8,128)(2,1)S(1)} collective-permute-done((bf16[512,256]{1,0:T(8,128)(2,1)S(1)}, bf16[512,256]{1,0:T(8,128)(2,1)S(1)}, u32[]{:S(2)}, u32[]{:S(2)}) %collective-permute-start.5) | collective-permute-done | bytes 262176 | tf_op jit(solution)/shard_map/ppermute | solution.py:26
  25.5 2.8 %collective-permute-done.2.second = bf16[512,256]{1,0:T(8,128)(2,1)S(1)} collective-permute-done((bf16[512,256]{1,0:T(8,128)(2,1)S(1)}, bf16[512,256]{1,0:T(8,128)(2,1)S(1)}, u32[]{:S(2)}, u32[]{:S(2)}) %collective-permute-start.2) | collective-permute-done | bytes 262176 | tf_op jit(solution)/shard_map/ppermute | solution.py:26
  28.9 3.2 %collective-permute-start.3 = (bf16[1024,256]{1,0:T(8,128)(2,1)S(1)}, bf16[1024,256]{1,0:T(8,128)(2,1)S(1)}, u32[]{:S(2)}, u32[]{:S(2)}) collective-permute-start(bf16[1024,256]{1,0:T(8,128)(2,1)S(1)} %join_y0.2.refs_0_), channel_id=1, source_target_pairs={{0,192},{1,193},{2,194},{3,195},{4,196},{5,197},{6,198},{7,199},{8... | collective-permute-start | bytes 1572872 | tf_op jit(solution)/shard_map/ppermute | solution.py:26
  32.2 2.3 %gather_near.1.refs_2_ = f32[1024,512]{1,0:T(8,128)S(1)} custom-call(bf16[1024,4096]{1,0:T(8,128)(2,1)S(1)} %adjacency.1.adj, bf16[1024,256]{1,0:T(8,128)(2,1)S(1)} %join_y0.2.refs_0_, bf16[1024,256]{1,0:T(8,128)(2,1)S(1)} %join_y0.3.refs_1_, bf16[1024,256]{1,0:T(8,128)(2,1)S(1)} %collective-permute-done.7.refs_2_, ...), custom_call_target="tpu_custom_call" | custom-call | bytes 1024 | tf_op jit(solution)/shard_map/gather_near/pallas_call | solution.py:38
  34.5 4.8 %collective-permute-done.3.refs_0_ = bf16[1024,256]{1,0:T(8,128)(2,1)S(1)} collective-permute-done((bf16[1024,256]{1,0:T(8,128)(2,1)S(1)}, bf16[1024,256]{1,0:T(8,128)(2,1)S(1)}, u32[]{:S(2)}, u32[]{:S(2)}) %collective-permute-start.3) | collective-permute-done | bytes 524320 | tf_op jit(solution)/shard_map/ppermute | solution.py:26
  39.3 5.6 %collective-permute-done.6.refs_1_ = bf16[1024,256]{1,0:T(8,128)(2,1)S(1)} collective-permute-done((bf16[1024,256]{1,0:T(8,128)(2,1)S(1)}, bf16[1024,256]{1,0:T(8,128)(2,1)S(1)}, u32[]{:S(2)}, u32[]{:S(2)}) %collective-permute-start.6) | collective-permute-done | bytes 524320 | tf_op jit(solution)/shard_map/ppermute | solution.py:26
  45.4 1.2 gather_far.1.refs_2_
  47.6 1.2 gather_far_other.1
  48.8 20.6 %all_to_all.16 = bf16[8,128,512]{2,1,0:T(8,128)(2,1)S(1)} all-to-all(bf16[8,128,512]{2,1,0:T(8,128)(2,1)S(1)} %bitcast.11), channel_id=1, replica_groups=mesh['row'=32,'col'=8] {'col'}, dimensions={0} | all-to-all | bytes 2097152 | tf_op jit(solution)/shard_map/all_to_all | solution.py:235
  69.4 1.1 node_step.1
  70.5 17.7 %all_to_all.17.parts = bf16[8,512,128]{2,1,0:T(8,128)(2,1)S(1)} all-to-all(bf16[8,512,128]{2,1,0:T(8,128)(2,1)S(1)} %get-tuple-element.64), channel_id=1, replica_groups=mesh['row'=32,'col'=8] {'col'}, dimensions={0} | all-to-all | bytes 2097152 | tf_op jit(solution)/shard_map/all_to_all | solution.py:238
  88.3 1.2 spread_far_other.1
  90.1 1.2 spread_near_other.1
  91.4 1.2 spread_far.1
  92.8 3.1 %collective-permute-start.13 = (bf16[256,1024]{1,0:T(8,128)(2,1)S(1)}, bf16[256,1024]{1,0:T(8,128)(2,1)S(1)}, u32[]{:S(2)}, u32[]{:S(2)}) collective-permute-start(bf16[256,1024]{1,0:T(8,128)(2,1)S(1)} %pair_sum.2), channel_id=1, source_target_pairs={{0,192},{1,193},{2,194},{3,195},{4,196},{5,197},{6,198},{7,199},{8... | collective-permute-start | bytes 1572872 | tf_op jit(solution)/shard_map/ppermute | solution.py:26
  96.7 1.2 spread_near.1
  97.9 5.3 %collective-permute-done.13.refs_2_ = bf16[256,1024]{1,0:T(8,128)(2,1)S(1)} collective-permute-done((bf16[256,1024]{1,0:T(8,128)(2,1)S(1)}, bf16[256,1024]{1,0:T(8,128)(2,1)S(1)}, u32[]{:S(2)}, u32[]{:S(2)}) %collective-permute-start.13) | collective-permute-done | bytes 524320 | tf_op jit(solution)/shard_map/ppermute | solution.py:26
  103.5 8.7 %collective-permute-done.19.refs_2_ = bf16[256,1024]{1,0:T(8,128)(2,1)S(1)} collective-permute-done((bf16[256,1024]{1,0:T(8,128)(2,1)S(1)}, bf16[256,1024]{1,0:T(8,128)(2,1)S(1)}, u32[]{:S(2)}, u32[]{:S(2)}) %collective-permute-start.19) | collective-permute-done | bytes 524320 | tf_op jit(solution)/shard_map/ppermute | solution.py:26
  112.6 3.3 %collective-permute-start.16 = (bf16[256,256]{1,0:T(8,128)(2,1)S(1)}, bf16[256,256]{1,0:T(8,128)(2,1)S(1)}, u32[]{:S(2)}, u32[]{:S(2)}) collective-permute-start(bf16[256,256]{1,0:T(8,128)(2,1)S(1)} %get-tuple-element.84), channel_id=1, source_target_pairs={{0,48},{1,49},{2,50},{3,51},{4,52},{5,53},{6,54},{7,55},{8,24},{9,... | collective-permute-start | bytes 393224 | tf_op jit(solution)/shard_map/ppermute | solution.py:26
  115.9 3.0 %collective-permute-done.20.refs_1_ = bf16[256,512]{1,0:T(8,128)(2,1)S(1)} collective-permute-done((bf16[256,512]{1,0:T(8,128)(2,1)S(1)}, bf16[256,512]{1,0:T(8,128)(2,1)S(1)}, u32[]{:S(2)}, u32[]{:S(2)}) %collective-permute-start.20) | collective-permute-done | bytes 262176 | tf_op jit(solution)/shard_map/ppermute | solution.py:26
  118.9 3.3 %collective-permute-start.21 = (bf16[256,256]{1,0:T(8,128)(2,1)S(1)}, bf16[256,256]{1,0:T(8,128)(2,1)S(1)}, u32[]{:S(2)}, u32[]{:S(2)}) collective-permute-start(bf16[256,256]{1,0:T(8,128)(2,1)S(1)} %get-tuple-element.94), channel_id=1, source_target_pairs={{0,48},{1,49},{2,50},{3,51},{4,52},{5,53},{6,54},{7,55},{8,24},{9,... | collective-permute-start | bytes 393224 | tf_op jit(solution)/shard_map/ppermute | solution.py:26
  122.2 2.5 %collective-permute-start.17 = (bf16[256,128]{1,0:T(8,128)(2,1)S(1)}, bf16[256,128]{1,0:T(8,128)(2,1)S(1)}, u32[]{:S(2)}, u32[]{:S(2)}) collective-permute-start(bf16[256,128]{1,0:T(8,128)(2,1)S(1)} %get-tuple-element.86), channel_id=1, source_target_pairs={{0,16},{1,17},{2,18},{3,19},{4,20},{5,21},{6,22},{7,23},{8,56},{9,... | collective-permute-start | bytes 196616 | tf_op jit(solution)/shard_map/ppermute | solution.py:26
  124.8 4.2 %collective-permute-done.21.refs_1_ = bf16[256,256]{1,0:T(8,128)(2,1)S(1)} collective-permute-done((bf16[256,256]{1,0:T(8,128)(2,1)S(1)}, bf16[256,256]{1,0:T(8,128)(2,1)S(1)}, u32[]{:S(2)}, u32[]{:S(2)}) %collective-permute-start.21) | collective-permute-done | bytes 131104 | tf_op jit(solution)/shard_map/ppermute | solution.py:26
  129.0 1.1 collective-permute-start.22
  130.4 3.9 %collective-permute-done.22.refs_3_ = bf16[256,128]{1,0:T(8,128)(2,1)S(1)} collective-permute-done((bf16[256,128]{1,0:T(8,128)(2,1)S(1)}, bf16[256,128]{1,0:T(8,128)(2,1)S(1)}, u32[]{:S(2)}, u32[]{:S(2)}) %collective-permute-start.22) | collective-permute-done | bytes 65568 | tf_op jit(solution)/shard_map/ppermute | solution.py:26
  134.3 0.8 last_sum.1
  (57 shorter events, 6.9 us)
Async XLA Ops:
  0.6 22.4 %copy-start = (bf16[512,512]{1,0:T(8,128)(2,1)S(1)}, bf16[512,512]{1,0:T(8,128)(2,1)}, u32[]{:S(2)}) copy-start(bf16[512,512]{1,0:T(8,128)(2,1)} %param.12) | copy-start | bytes 1572868
  0.6 9.8 %collective-permute-start = (bf16[128,512]{1,0:T(8,128)(2,1)}, bf16[128,512]{1,0:T(8,128)(2,1)S(1)}, u32[]{:S(2)}, u32[]{:S(2)}) collective-permute-start(bf16[128,512]{1,0:T(8,128)(2,1)} %first.1), channel_id=1, source_target_pairs={{0,16},{1,17},{2,18},{3,19},{4,20},{5,21},{6,22},{7,23},{8,56},{9,... | collective-permute-start | bytes 393224 | tf_op jit(solution)/shard_map/ppermute | solution.py:26
  4.9 5.6 %copy-start.2 = (bf16[128,512]{1,0:T(8,128)(2,1)S(1)}, bf16[128,512]{1,0:T(8,128)(2,1)}, u32[]{:S(2)}) copy-start(bf16[128,512]{1,0:T(8,128)(2,1)} %first.1) | copy-start | bytes 393220
  4.9 18.1 %copy-start.5 = (s32[128]{0:T(128)S(1)}, s32[128]{0:T(128)}, u32[]{:S(2)}) copy-start(s32[128]{0:T(128)} %param.9) | copy-start | bytes 1540
  4.9 18.1 %copy-start.4 = (f32[512]{0:T(512)S(1)}, f32[512]{0:T(512)}, u32[]{:S(2)}) copy-start(f32[512]{0:T(512)} %param.14) | copy-start | bytes 6148
  10.5 8.5 %collective-permute-start.4 = (bf16[256,256]{1,0:T(8,128)(2,1)S(1)}, bf16[256,256]{1,0:T(8,128)(2,1)S(1)}, u32[]{:S(2)}, u32[]{:S(2)}) collective-permute-start(bf16[256,256]{1,0:T(8,128)(2,1)S(1)} %get-tuple-element.53.first), channel_id=1, source_target_pairs={{0,48},{1,49},{2,50},{3,51},{4,52},{5,53},{6,54},{7,55},{8,24},{9,... | collective-permute-start | bytes 393224 | tf_op jit(solution)/shard_map/ppermute | solution.py:26
  14.2 7.2 %collective-permute-start.1 = (bf16[256,256]{1,0:T(8,128)(2,1)S(1)}, bf16[256,256]{1,0:T(8,128)(2,1)S(1)}, u32[]{:S(2)}, u32[]{:S(2)}) collective-permute-start(bf16[256,256]{1,0:T(8,128)(2,1)S(1)} %get-tuple-element.52.first), channel_id=1, source_target_pairs={{0,48},{1,49},{2,50},{3,51},{4,52},{5,53},{6,54},{7,55},{8,24},{9,... | collective-permute-start | bytes 393224 | tf_op jit(solution)/shard_map/ppermute | solution.py:26
  19.0 6.5 %collective-permute-start.5 = (bf16[512,256]{1,0:T(8,128)(2,1)S(1)}, bf16[512,256]{1,0:T(8,128)(2,1)S(1)}, u32[]{:S(2)}, u32[]{:S(2)}) collective-permute-start(bf16[512,256]{1,0:T(8,128)(2,1)S(1)} %join_z1.3.first), channel_id=1, source_target_pairs={{0,64},{1,65},{2,66},{3,67},{4,68},{5,69},{6,70},{7,71},{8,200},{9... | collective-permute-start | bytes 786440 | tf_op jit(solution)/shard_map/ppermute | solution.py:26
  21.4 6.9 %collective-permute-start.2 = (bf16[512,256]{1,0:T(8,128)(2,1)S(1)}, bf16[512,256]{1,0:T(8,128)(2,1)S(1)}, u32[]{:S(2)}, u32[]{:S(2)}) collective-permute-start(bf16[512,256]{1,0:T(8,128)(2,1)S(1)} %join_z1.2.first), channel_id=1, source_target_pairs={{0,64},{1,65},{2,66},{3,67},{4,68},{5,69},{6,70},{7,71},{8,200},{9... | collective-permute-start | bytes 786440 | tf_op jit(solution)/shard_map/ppermute | solution.py:26
  28.3 3.9 %collective-permute-start.7 = (bf16[1024,256]{1,0:T(8,128)(2,1)S(1)}, bf16[1024,256]{1,0:T(8,128)(2,1)S(1)}, u32[]{:S(2)}, u32[]{:S(2)}) collective-permute-start(bf16[1024,256]{1,0:T(8,128)(2,1)S(1)} %join_y0.2.refs_0_), channel_id=1, source_target_pairs={{0,8},{1,9},{2,10},{3,11},{4,12},{5,13},{6,14},{7,15},{8,0},{9,1},... | collective-permute-start | bytes 1572872 | tf_op jit(solution)/shard_map/ppermute | solution.py:31
  28.4 3.8 %collective-permute-start.8 = (bf16[1024,256]{1,0:T(8,128)(2,1)S(1)}, bf16[1024,256]{1,0:T(8,128)(2,1)S(1)}, u32[]{:S(2)}, u32[]{:S(2)}) collective-permute-start(bf16[1024,256]{1,0:T(8,128)(2,1)S(1)} %join_y0.3.refs_1_), channel_id=1, source_target_pairs={{0,8},{1,9},{2,10},{3,11},{4,12},{5,13},{6,14},{7,15},{8,0},{9,1},... | collective-permute-start | bytes 1572872 | tf_op jit(solution)/shard_map/ppermute | solution.py:31
  28.9 10.4 %collective-permute-start.3 = (bf16[1024,256]{1,0:T(8,128)(2,1)S(1)}, bf16[1024,256]{1,0:T(8,128)(2,1)S(1)}, u32[]{:S(2)}, u32[]{:S(2)}) collective-permute-start(bf16[1024,256]{1,0:T(8,128)(2,1)S(1)} %join_y0.2.refs_0_), channel_id=1, source_target_pairs={{0,192},{1,193},{2,194},{3,195},{4,196},{5,197},{6,198},{7,199},{8... | collective-permute-start | bytes 1572872 | tf_op jit(solution)/shard_map/ppermute | solution.py:26
  32.1 12.8 %collective-permute-start.6 = (bf16[1024,256]{1,0:T(8,128)(2,1)S(1)}, bf16[1024,256]{1,0:T(8,128)(2,1)S(1)}, u32[]{:S(2)}, u32[]{:S(2)}) collective-permute-start(bf16[1024,256]{1,0:T(8,128)(2,1)S(1)} %join_y0.3.refs_1_), channel_id=1, source_target_pairs={{0,192},{1,193},{2,194},{3,195},{4,196},{5,197},{6,198},{7,199},{8... | collective-permute-start | bytes 1572872 | tf_op jit(solution)/shard_map/ppermute | solution.py:26
  44.9 1.9 %collective-permute-start.9 = (bf16[1024,256]{1,0:T(8,128)(2,1)S(1)}, bf16[1024,256]{1,0:T(8,128)(2,1)S(1)}, u32[]{:S(2)}, u32[]{:S(2)}) collective-permute-start(bf16[1024,256]{1,0:T(8,128)(2,1)S(1)} %collective-permute-done.3.refs_0_), channel_id=1, source_target_pairs={{0,8},{1,9},{2,10},{3,11},{4,12},{5,13},{6,14},{7,15},{8,0},{9,1},... | collective-permute-start | bytes 1572872 | tf_op jit(solution)/shard_map/ppermute | solution.py:31
  44.9 2.7 %collective-permute-start.10 = (bf16[1024,256]{1,0:T(8,128)(2,1)S(1)}, bf16[1024,256]{1,0:T(8,128)(2,1)S(1)}, u32[]{:S(2)}, u32[]{:S(2)}) collective-permute-start(bf16[1024,256]{1,0:T(8,128)(2,1)S(1)} %collective-permute-done.6.refs_1_), channel_id=1, source_target_pairs={{0,8},{1,9},{2,10},{3,11},{4,12},{5,13},{6,14},{7,15},{8,0},{9,1},... | collective-permute-start | bytes 1572872 | tf_op jit(solution)/shard_map/ppermute | solution.py:31
  46.7 22.7 %copy-start.1 = (bf16[512,512]{1,0:T(8,128)(2,1)S(1)}, bf16[512,512]{1,0:T(8,128)(2,1)}, u32[]{:S(2)}) copy-start(bf16[512,512]{1,0:T(8,128)(2,1)} %w_neigh.1) | copy-start | bytes 1572868
  46.7 22.7 %copy-start.3 = (bf16[128,512]{1,0:T(8,128)(2,1)S(1)}, bf16[128,512]{1,0:T(8,128)(2,1)}, u32[]{:S(2)}) copy-start(bf16[128,512]{1,0:T(8,128)(2,1)} %cotangent.1) | copy-start | bytes 393220
  89.5 3.1 %collective-permute-start.11 = (bf16[256,1024]{1,0:T(8,128)(2,1)S(1)}, bf16[256,1024]{1,0:T(8,128)(2,1)S(1)}, u32[]{:S(2)}, u32[]{:S(2)}) collective-permute-start(bf16[256,1024]{1,0:T(8,128)(2,1)S(1)} %get-tuple-element.65), channel_id=1, source_target_pairs={{0,8},{1,9},{2,10},{3,11},{4,12},{5,13},{6,14},{7,15},{8,0},{9,1},... | collective-permute-start | bytes 1572872 | tf_op jit(solution)/shard_map/ppermute | solution.py:31
  89.6 3.0 %collective-permute-start.12 = (bf16[256,1024]{1,0:T(8,128)(2,1)S(1)}, bf16[256,1024]{1,0:T(8,128)(2,1)S(1)}, u32[]{:S(2)}, u32[]{:S(2)}) collective-permute-start(bf16[256,1024]{1,0:T(8,128)(2,1)S(1)} %get-tuple-element.66), channel_id=1, source_target_pairs={{0,8},{1,9},{2,10},{3,11},{4,12},{5,13},{6,14},{7,15},{8,0},{9,1},... | collective-permute-start | bytes 1572872 | tf_op jit(solution)/shard_map/ppermute | solution.py:31
  92.8 10.5 %collective-permute-start.13 = (bf16[256,1024]{1,0:T(8,128)(2,1)S(1)}, bf16[256,1024]{1,0:T(8,128)(2,1)S(1)}, u32[]{:S(2)}, u32[]{:S(2)}) collective-permute-start(bf16[256,1024]{1,0:T(8,128)(2,1)S(1)} %pair_sum.2), channel_id=1, source_target_pairs={{0,192},{1,193},{2,194},{3,195},{4,196},{5,197},{6,198},{7,199},{8... | collective-permute-start | bytes 1572872 | tf_op jit(solution)/shard_map/ppermute | solution.py:26
  95.9 7.4 %collective-permute-start.14 = (bf16[256,1024]{1,0:T(8,128)(2,1)S(1)}, bf16[256,1024]{1,0:T(8,128)(2,1)S(1)}, u32[]{:S(2)}, u32[]{:S(2)}) collective-permute-start(bf16[256,1024]{1,0:T(8,128)(2,1)S(1)} %get-tuple-element.79), channel_id=1, source_target_pairs={{0,8},{1,9},{2,10},{3,11},{4,12},{5,13},{6,14},{7,15},{8,0},{9,1},... | collective-permute-start | bytes 1572872 | tf_op jit(solution)/shard_map/ppermute | solution.py:31
  96.0 16.2 %collective-permute-start.19 = (bf16[256,1024]{1,0:T(8,128)(2,1)S(1)}, bf16[256,1024]{1,0:T(8,128)(2,1)S(1)}, u32[]{:S(2)}, u32[]{:S(2)}) collective-permute-start(bf16[256,1024]{1,0:T(8,128)(2,1)S(1)} %pair_sum.3), channel_id=1, source_target_pairs={{0,192},{1,193},{2,194},{3,195},{4,196},{5,197},{6,198},{7,199},{8... | collective-permute-start | bytes 1572872 | tf_op jit(solution)/shard_map/ppermute | solution.py:26
  96.3 15.9 %collective-permute-start.18 = (bf16[256,1024]{1,0:T(8,128)(2,1)S(1)}, bf16[256,1024]{1,0:T(8,128)(2,1)S(1)}, u32[]{:S(2)}, u32[]{:S(2)}) collective-permute-start(bf16[256,1024]{1,0:T(8,128)(2,1)S(1)} %get-tuple-element.88), channel_id=1, source_target_pairs={{0,8},{1,9},{2,10},{3,11},{4,12},{5,13},{6,14},{7,15},{8,0},{9,1},... | collective-permute-start | bytes 1572872 | tf_op jit(solution)/shard_map/ppermute | solution.py:31
  103.4 9.1 %collective-permute-start.15 = (bf16[256,512]{1,0:T(8,128)(2,1)S(1)}, bf16[256,512]{1,0:T(8,128)(2,1)S(1)}, u32[]{:S(2)}, u32[]{:S(2)}) collective-permute-start(bf16[256,512]{1,0:T(8,128)(2,1)S(1)} %get-tuple-element.82), channel_id=1, source_target_pairs={{0,64},{1,65},{2,66},{3,67},{4,68},{5,69},{6,70},{7,71},{8,200},{9... | collective-permute-start | bytes 786440 | tf_op jit(solution)/shard_map/ppermute | solution.py:26
  112.4 6.5 %collective-permute-start.20 = (bf16[256,512]{1,0:T(8,128)(2,1)S(1)}, bf16[256,512]{1,0:T(8,128)(2,1)S(1)}, u32[]{:S(2)}, u32[]{:S(2)}) collective-permute-start(bf16[256,512]{1,0:T(8,128)(2,1)S(1)} %get-tuple-element.92), channel_id=1, source_target_pairs={{0,64},{1,65},{2,66},{3,67},{4,68},{5,69},{6,70},{7,71},{8,200},{9... | collective-permute-start | bytes 786440 | tf_op jit(solution)/shard_map/ppermute | solution.py:26
  112.6 9.6 %collective-permute-start.16 = (bf16[256,256]{1,0:T(8,128)(2,1)S(1)}, bf16[256,256]{1,0:T(8,128)(2,1)S(1)}, u32[]{:S(2)}, u32[]{:S(2)}) collective-permute-start(bf16[256,256]{1,0:T(8,128)(2,1)S(1)} %get-tuple-element.84), channel_id=1, source_target_pairs={{0,48},{1,49},{2,50},{3,51},{4,52},{5,53},{6,54},{7,55},{8,24},{9,... | collective-permute-start | bytes 393224 | tf_op jit(solution)/shard_map/ppermute | solution.py:26
  118.9 10.1 %collective-permute-start.21 = (bf16[256,256]{1,0:T(8,128)(2,1)S(1)}, bf16[256,256]{1,0:T(8,128)(2,1)S(1)}, u32[]{:S(2)}, u32[]{:S(2)}) collective-permute-start(bf16[256,256]{1,0:T(8,128)(2,1)S(1)} %get-tuple-element.94), channel_id=1, source_target_pairs={{0,48},{1,49},{2,50},{3,51},{4,52},{5,53},{6,54},{7,55},{8,24},{9,... | collective-permute-start | bytes 393224 | tf_op jit(solution)/shard_map/ppermute | solution.py:26
  122.2 8.2 %collective-permute-start.17 = (bf16[256,128]{1,0:T(8,128)(2,1)S(1)}, bf16[256,128]{1,0:T(8,128)(2,1)S(1)}, u32[]{:S(2)}, u32[]{:S(2)}) collective-permute-start(bf16[256,128]{1,0:T(8,128)(2,1)S(1)} %get-tuple-element.86), channel_id=1, source_target_pairs={{0,16},{1,17},{2,18},{3,19},{4,20},{5,21},{6,22},{7,23},{8,56},{9,... | collective-permute-start | bytes 196616 | tf_op jit(solution)/shard_map/ppermute | solution.py:26
  129.0 5.3 %collective-permute-start.22 = (bf16[256,128]{1,0:T(8,128)(2,1)S(1)}, bf16[256,128]{1,0:T(8,128)(2,1)S(1)}, u32[]{:S(2)}, u32[]{:S(2)}) collective-permute-start(bf16[256,128]{1,0:T(8,128)(2,1)S(1)} %get-tuple-element.96), channel_id=1, source_target_pairs={{0,16},{1,17},{2,18},{3,19},{4,20},{5,21},{6,22},{7,23},{8,56},{9,... | collective-permute-start | bytes 196616 | tf_op jit(solution)/shard_map/ppermute | solution.py:26

commit v8 on v7

--- a/solution.py
+++ b/solution.py
@@ -12,6 +12,8 @@
 CHIPS = NY * NZH
 STEPS = ((1, 3), (3, 1))
 TILE = 128
+AXES = (("z", "y"), ("y", "z"))
+SPLIT = 320
 BF16 = jnp.bfloat16
 F32 = jnp.float32
 MB = 1024 * 1024
@@ -87,40 +89,59 @@
     )(place, where, pltpu.with_memory_space_constraint(masks, pltpu.HBM))
 
 
-def halves_kernel(first, second, *outs):
-    rows = first.shape[0]
-    width = outs[0].shape[1]
-    for w, out in enumerate(outs):
-        out[:rows, :] = first[:, w * width : (w + 1) * width]
-        out[rows:, :] = second[:, w * width : (w + 1) * width]
-
-
-def join(first, second, count, name):
-    shape = (2 * first.shape[0], first.shape[1] // count)
-    return in_vmem(halves_kernel, [kept(shape, BF16)] * count, (first, second), name)
-
-
-def gather_kernel(starts, adj, *refs):
-    parts, out = refs[: 2 * len(starts)], refs[-1]
-    start = refs[-2] if len(refs) > len(parts) + 1 else None
-    rows = 2 * TILE
-    rhs = [jnp.concatenate([parts[i][...], parts[i + 1][...]], axis=1) for i in range(0, len(parts), 2)]
-    rhs = jnp.concatenate(rhs, axis=0)
-    depth = parts[0].shape[0]
-    for r in range(0, out.shape[0], rows):
-        lhs = [adj[r : r + rows, at : at + depth] for at in starts]
-        value = jnp.dot(jnp.concatenate(lhs, axis=1), rhs, preferred_element_type=F32)
-        if start is not None:
-            value = value + start[r : r + rows, :]
-        out[r : r + rows, :] = value.astype(out.dtype)
+def tiles_of(wave, core, half):
+    out = []
+    for n in range(half * CHIPS // 2, (half + 1) * CHIPS // 2):
+        slow, fast = n // NZH, n % NZH
+        out.append(core * CHIPS + (slow * NZH + fast if wave == 0 else fast * NZH + slow))
+    return out
+
+
+def columns(adj, rows, tiles):
+    pieces = []
+    for tile in tiles:
+        if pieces and pieces[-1][1] == tile:
+            pieces[-1][1] = tile + 1
+        else:
+            pieces.append([tile, tile + 1])
+    parts = [adj[rows, a * TILE : b * TILE] for a, b in pieces]
+    return parts[0] if len(parts) == 1 else jnp.concatenate(parts, axis=1)
+
+
+def join_kernel(at, first, second, out):
+    rows, width = first.shape[0], out.shape[1]
+    out[:rows, :] = first[:, at : at + width]
+    out[rows:, :] = second[:, at : at + width]
+
+
+def join(first, second, at, width, name):
+    shape = (2 * first.shape[0], width)
+    return in_vmem(functools.partial(join_kernel, at), [kept(shape, BF16)], (first, second), name)[0]
+
+
+def gather_kernel(parts, adj, *refs):
+    out = refs[-1]
+    start = refs[-2] if len(refs) > 2 * len(parts) + 1 else None
+    width = out.shape[1] // 2
+    step = 2 * TILE
+    for w in range(2):
+        cols = slice(w * width, (w + 1) * width)
+        rhs = jnp.concatenate([refs[2 * i + w][...] for i in range(len(parts))], axis=0)
+        tiles = [tile for core, half in parts for tile in tiles_of(w, core, half)]
+        for r in range(0, out.shape[0], step):
+            rows = slice(r, r + step)
+            value = jnp.dot(columns(adj, rows, tiles), rhs, preferred_element_type=F32)
+            if start is not None:
+                value = value + start[rows, cols]
+            out[rows, cols] = value.astype(out.dtype)
 
 
 def gather_matmul(adj, parts, start, dtype, name):
-    starts = [(core * 2 + half) * CHIPS // 2 * TILE for core, half, _ in parts]
+    which = [(core, half) for core, half, _ in parts]
     arrays = [wave for *_, waves in parts for wave in waves]
     rows, width = adj.shape[0], 2 * arrays[0].shape[1]
     operands = [adj, *arrays] + ([] if start is None else [start])
-    return in_vmem(functools.partial(gather_kernel, starts), [kept((rows, width), dtype)], operands, name)[0]
+    return in_vmem(functools.partial(gather_kernel, which), [kept((rows, width), dtype)], operands, name)[0]
 
 
 def node_kernel(parts, base, degf_row, w_neigh, cotangent, grad, scaled_t, out):
@@ -148,20 +169,21 @@
     return in_vmem(node_kernel, results, operands, "node_step", 4 * rows * width * width)
 
 
-def spread_kernel(first, parts, adj, *outs):
-    lhs = jnp.concatenate([parts[i] for i in range(NCOL)], axis=1)
-    depth = NZH * TILE
-    rows, cols = outs[0].shape
-    for at in range(0, cols, depth):
-        value = jnp.dot(lhs, adj[:, first + at : first + at + depth], preferred_element_type=F32).astype(BF16)
-        for w, out in enumerate(outs):
-            out[:, at : at + depth] = value[w * rows : (w + 1) * rows, :]
+def spread_kernel(core, half, parts, adj, *outs):
+    for w, out in enumerate(outs):
+        rows = slice(0, SPLIT) if w == 0 else slice(SPLIT, parts.shape[1])
+        lhs = jnp.concatenate([parts[i, rows, :] for i in range(NCOL)], axis=1)
+        tiles = tiles_of(w, core, half)
+        for i in range(0, len(tiles), NZH):
+            rhs = columns(adj, slice(None), tiles[i : i + NZH])
+            value = jnp.dot(lhs, rhs, preferred_element_type=F32)
+            out[:, i * TILE : (i + NZH) * TILE] = value.astype(BF16)
 
 
 def spread_matmul(parts, adj, core, half, name):
-    shape = (parts.shape[1] // 2, CHIPS // 2 * TILE)
-    first = (core * 2 + half) * shape[1]
-    return in_vmem(functools.partial(spread_kernel, first), [kept(shape, BF16)] * 2, (parts, adj), name)
+    cols = CHIPS // 2 * TILE
+    results = [kept((rows, cols), BF16) for rows in (SPLIT, parts.shape[1] - SPLIT)]
+    return in_vmem(functools.partial(spread_kernel, core, half), results, (parts, adj), name)
 
 
 def sum_kernel(*refs):
@@ -216,14 +238,15 @@
     degf_row = degrees.astype(F32)[None, :]
     base = jnp.dot(features, w_self, preferred_element_type=F32) + bias[None, :]
 
-    got, adj = lax.optimization_barrier((exchange(features, "z", 0), adj))
-    waves = join(features, got, 2, "join_z0")
-    got = [exchange(v, "z", 1) for v in waves]
-    waves = [join(v, g, 1, "join_z1")[0] for v, g in zip(waves, got)]
-    got = [exchange(v, "y", 0) for v in waves]
+    width = features.shape[1] // 2
+    *got, adj = lax.optimization_barrier((*[exchange(features, a, 0) for a, _ in AXES], adj))
+    waves = [join(features, g, w * width, width, "join_0") for w, g in enumerate(got)]
+    got = [exchange(v, a, 1) for v, (a, _) in zip(waves, AXES)]
+    waves = [join(v, g, 0, width, "join_1") for v, g in zip(waves, got)]
+    got = [exchange(v, b, 0) for v, (_, b) in zip(waves, AXES)]
     got[1], base, degf_row = lax.optimization_barrier((got[1], base, degf_row))
-    near = [join(v, g, 1, "join_y0")[0] for v, g in zip(waves, got)]
-    far = [exchange(v, "y", 1) for v in near]
+    near = [join(v, g, 0, width, "join_2") for v, g in zip(waves, got)]
+    far = [exchange(v, b, 1) for v, (_, b) in zip(near, AXES)]
     other = [swap(v) for v in near]
     part = gather_matmul(adj, [(0, 0, near), (1, 0, other)], None, F32, "gather_near")
     *far, part = lax.optimization_barrier((*far, part))
@@ -245,16 +268,16 @@
     theirs, mine, near_other = theirs[:2], theirs[2:4], theirs[4:]
     values = [pair_sum(a, b) for a, b in zip(mine, theirs)]
     values[0], table = lax.optimization_barrier((values[0], table))
-    got = [exchange(v, "y", 1) for v in values]
+    got = [exchange(v, b, 1) for v, (_, b) in zip(values, AXES)]
     theirs = [swap(v) for v in near_other]
     mine = spread_matmul(table, adj, 0, 0, "spread_near")
     got[0], *mine = lax.optimization_barrier((got[0], *mine))
     ends = []
-    for w in range(2):
-        stay, go = split_sum((mine[w], theirs[w], got[w]), "sum_y1")
-        stay, go = split_sum((stay, exchange(go, "y", 0)), "sum_y0")
-        stay, go = split_sum((stay, exchange(go, "z", 1)), "sum_z1")
-        ends += [stay, exchange(go, "z", 0)]
+    for w, (a, b) in enumerate(AXES):
+        stay, go = split_sum((mine[w], theirs[w], got[w]), "sum_3")
+        stay, go = split_sum((stay, exchange(go, b, 0)), "sum_2")
+        stay, go = split_sum((stay, exchange(go, a, 1)), "sum_1")
+        ends += [stay, exchange(go, a, 0)]
     grad_features = last_sum(ends, own)
     return output, grad_features
 

time: 136 us -> 139 us (1.022); the launches traced: 135 us -> 136 us
  waiting for transfers between devices: 46.1 us -> 42.2 us
  starting transfers between devices: 30.2 us -> 33.8 us
  blocking collectives: 38.3 us -> 39.9 us
    ppermute x15 -> x16, waiting for transfers between devices: 45.2 us -> 41.3 us  [exchange(): return lax.ppermute(value, ('row', 'col'), pairs)]
    ppermute x15 -> x16, starting transfers between devices: 28.1 us -> 31.5 us  [exchange(): return lax.ppermute(value, ('row', 'col'), pairs)]
    all_to_all x1, blocking collectives: 20.6 us -> 22.2 us  [body(): arrived = lax.all_to_all(summed, 'col', 0, 0, tiled=True)]
    pallas_call x22 -> x23, Pallas kernels: 12.6 us -> 12.6 us  [in_vmem(): pl.pallas_call(kernel, in_specs=[spec] * len(operands), out_specs=out_spe...]
  transfers between devices with their start and end apart: 23 -> 24, of which waited for: 13 -> 13; matrix products, arithmetic and copies ran while one was open for 1% -> 1% of each run, Pallas kernels for 10% -> 10%
where the time goes in v8:
time: 139 us; the launch traced here: 136 us
  waiting for transfers between devices  42.2 us (30%)
  blocking collectives  39.9 us (29%)
  starting transfers between devices  33.8 us (24%)
  Pallas kernels  18.1 us (13%)
    ppermute x16, waiting for transfers between devices, exchange(): return lax.ppermute(value, ('row', 'col'), pairs)  41.3 us
    ppermute x16, starting transfers between devices, exchange(): return lax.ppermute(value, ('row', 'col'), pairs)  31.5 us
    all_to_all x1, blocking collectives, body(): arrived = lax.all_to_all(summed, 'col', 0, 0, tiled=True)  22.2 us
    all_to_all x1, blocking collectives, body(): table = lax.all_to_all(scaled_t, 'col', 0, 0, tiled=True)  17.7 us
    pallas_call x23, Pallas kernels, in_vmem(): pl.pallas_call(kernel, in_specs=[spec] * len(operands), out_specs=out_spe...  12.6 us
    pallas_call x1, Pallas kernels, adjacency(): pl.pallas_call(adjacency_kernel, grid_spec=pltpu.PrefetchScalarGridSpec(n...  5.53 us
  transfers between devices with their start and end apart: 24, of which 13 were waited for; matrix products, arithmetic and copies ran while one was open for 1% of the time, Pallas kernels for 10%

profile of v8, /device:TPU:32, one launch (start us, length us, event | category | flops | bytes accessed | tf_op | source)
XLA Modules:
  0.0 136.3 jit_solution(1729020686484622169)
XLA Ops:
  0.6 1.7 %collective-permute-start.1 = (bf16[128,512]{1,0:T(8,128)(2,1)}, bf16[128,512]{1,0:T(8,128)(2,1)S(1)}, u32[]{:S(2)}, u32[]{:S(2)}) collective-permute-start(bf16[128,512]{1,0:T(8,128)(2,1)} %first.3), channel_id=1, source_target_pairs={{0,64},{1,65},{2,66},{3,67},{4,68},{5,69},{6,70},{7,71},{8,200},{9... | collective-permute-start | bytes 393224 | tf_op jit(solution)/shard_map/ppermute | solution.py:28
  2.3 3.3 %collective-permute-start = (bf16[128,512]{1,0:T(8,128)(2,1)}, bf16[128,512]{1,0:T(8,128)(2,1)S(1)}, u32[]{:S(2)}, u32[]{:S(2)}) collective-permute-start(bf16[128,512]{1,0:T(8,128)(2,1)} %first.3), channel_id=1, source_target_pairs={{0,16},{1,17},{2,18},{3,19},{4,20},{5,21},{6,22},{7,23},{8,56},{9,... | collective-permute-start | bytes 393224 | tf_op jit(solution)/shard_map/ppermute | solution.py:28
  6.5 5.5 %adjacency.1.adj = bf16[1024,4096]{1,0:T(8,128)(2,1)S(1)} custom-call(s32[32]{0:T(128)S(1)} %fusion.2.place, s32[96]{0:T(128)S(1)} %reshape_squeeze.3.where, s32[32,3,128,128]{3,2,1,0:T(8,128)} %bitcast.13), custom_call_target="tpu_custom_call" | custom-call | bytes 14680064 | tf_op jit(solution)/shard_map/adjacency/pallas_call | solution.py:76
  12.1 3.7 %collective-permute-start.2 = (bf16[256,256]{1,0:T(8,128)(2,1)S(1)}, bf16[256,256]{1,0:T(8,128)(2,1)S(1)}, u32[]{:S(2)}, u32[]{:S(2)}) collective-permute-start(bf16[256,256]{1,0:T(8,128)(2,1)S(1)} %join_0.2.first), channel_id=1, source_target_pairs={{0,48},{1,49},{2,50},{3,51},{4,52},{5,53},{6,54},{7,55},{8,24},{9,... | collective-permute-start | bytes 393224 | tf_op jit(solution)/shard_map/ppermute | solution.py:28
  15.8 2.3 %collective-permute-start.5 = (bf16[256,256]{1,0:T(8,128)(2,1)S(1)}, bf16[256,256]{1,0:T(8,128)(2,1)S(1)}, u32[]{:S(2)}, u32[]{:S(2)}) collective-permute-start(bf16[256,256]{1,0:T(8,128)(2,1)S(1)} %join_0.3.first), channel_id=1, source_target_pairs={{0,192},{1,193},{2,194},{3,195},{4,196},{5,197},{6,198},{7,199},{8... | collective-permute-start | bytes 393224 | tf_op jit(solution)/shard_map/ppermute | solution.py:28
  18.1 1.8 %collective-permute-done.2.second = bf16[256,256]{1,0:T(8,128)(2,1)S(1)} collective-permute-done((bf16[256,256]{1,0:T(8,128)(2,1)S(1)}, bf16[256,256]{1,0:T(8,128)(2,1)S(1)}, u32[]{:S(2)}, u32[]{:S(2)}) %collective-permute-start.2) | collective-permute-done | bytes 131104 | tf_op jit(solution)/shard_map/ppermute | solution.py:28
  20.3 1.8 %collective-permute-done.5.second = bf16[256,256]{1,0:T(8,128)(2,1)S(1)} collective-permute-done((bf16[256,256]{1,0:T(8,128)(2,1)S(1)}, bf16[256,256]{1,0:T(8,128)(2,1)S(1)}, u32[]{:S(2)}, u32[]{:S(2)}) %collective-permute-start.5) | collective-permute-done | bytes 131104 | tf_op jit(solution)/shard_map/ppermute | solution.py:28
  22.1 1.6 %collective-permute-start.6 = (bf16[512,256]{1,0:T(8,128)(2,1)S(1)}, bf16[512,256]{1,0:T(8,128)(2,1)S(1)}, u32[]{:S(2)}, u32[]{:S(2)}) collective-permute-start(bf16[512,256]{1,0:T(8,128)(2,1)S(1)} %join_1.3.first), channel_id=1, source_target_pairs={{0,16},{1,17},{2,18},{3,19},{4,20},{5,21},{6,22},{7,23},{8,56},{9,... | collective-permute-start | bytes 786440 | tf_op jit(solution)/shard_map/ppermute | solution.py:28
  23.9 6.4 %collective-permute-done.6.second = bf16[512,256]{1,0:T(8,128)(2,1)S(1)} collective-permute-done((bf16[512,256]{1,0:T(8,128)(2,1)S(1)}, bf16[512,256]{1,0:T(8,128)(2,1)S(1)}, u32[]{:S(2)}, u32[]{:S(2)}) %collective-permute-start.6) | collective-permute-done | bytes 262176 | tf_op jit(solution)/shard_map/ppermute | solution.py:28
  31.6 3.7 %collective-permute-start.7 = (bf16[1024,256]{1,0:T(8,128)(2,1)S(1)}, bf16[1024,256]{1,0:T(8,128)(2,1)S(1)}, u32[]{:S(2)}, u32[]{:S(2)}) collective-permute-start(bf16[1024,256]{1,0:T(8,128)(2,1)S(1)} %join_2.3.refs_1_), channel_id=1, source_target_pairs={{0,48},{1,49},{2,50},{3,51},{4,52},{5,53},{6,54},{7,55},{8,24},{9,... | collective-permute-start | bytes 1572872 | tf_op jit(solution)/shard_map/ppermute | solution.py:28
  35.3 2.9 %collective-permute-start.4 = (bf16[1024,256]{1,0:T(8,128)(2,1)S(1)}, bf16[1024,256]{1,0:T(8,128)(2,1)S(1)}, u32[]{:S(2)}, u32[]{:S(2)}) collective-permute-start(bf16[1024,256]{1,0:T(8,128)(2,1)S(1)} %join_2.2.refs_0_), channel_id=1, source_target_pairs={{0,192},{1,193},{2,194},{3,195},{4,196},{5,197},{6,198},{7,199},{8... | collective-permute-start | bytes 1572872 | tf_op jit(solution)/shard_map/ppermute | solution.py:28
  38.3 2.3 %gather_near.1.refs_2_ = f32[1024,512]{1,0:T(8,128)S(1)} custom-call(bf16[1024,4096]{1,0:T(8,128)(2,1)S(1)} %adjacency.1.adj, bf16[1024,256]{1,0:T(8,128)(2,1)S(1)} %join_2.2.refs_0_, bf16[1024,256]{1,0:T(8,128)(2,1)S(1)} %join_2.3.refs_1_, bf16[1024,256]{1,0:T(8,128)(2,1)S(1)} %collective-permute-done.8.refs_2_, ...), custom_call_target="tpu_custom_call" | custom-call | bytes 1024 | tf_op jit(solution)/shard_map/gather_near/pallas_call | solution.py:40
  40.6 7.1 %collective-permute-done.7.refs_1_ = bf16[1024,256]{1,0:T(8,128)(2,1)S(1)} collective-permute-done((bf16[1024,256]{1,0:T(8,128)(2,1)S(1)}, bf16[1024,256]{1,0:T(8,128)(2,1)S(1)}, u32[]{:S(2)}, u32[]{:S(2)}) %collective-permute-start.7) | collective-permute-done | bytes 524320 | tf_op jit(solution)/shard_map/ppermute | solution.py:28
  48.2 1.3 gather_far.1.refs_2_
  50.3 1.2 gather_far_other.1
  51.6 22.2 %all_to_all.16 = bf16[8,128,512]{2,1,0:T(8,128)(2,1)S(1)} all-to-all(bf16[8,128,512]{2,1,0:T(8,128)(2,1)S(1)} %bitcast.11), channel_id=1, replica_groups=mesh['row'=32,'col'=8] {'col'}, dimensions={0} | all-to-all | bytes 2097152 | tf_op jit(solution)/shard_map/all_to_all | solution.py:258
  74.9 17.7 %all_to_all.17.parts = bf16[8,512,128]{2,1,0:T(8,128)(2,1)S(1)} all-to-all(bf16[8,512,128]{2,1,0:T(8,128)(2,1)S(1)} %get-tuple-element.62), channel_id=1, replica_groups=mesh['row'=32,'col'=8] {'col'}, dimensions={0} | all-to-all | bytes 2097152 | tf_op jit(solution)/shard_map/all_to_all | solution.py:261
  92.6 1.2 spread_far_other.1
  95.7 1.2 spread_far.1
  97.1 2.3 %collective-permute-start.14 = (bf16[320,1024]{1,0:T(8,128)(2,1)S(1)}, bf16[320,1024]{1,0:T(8,128)(2,1)S(1)}, u32[]{:S(2)}, u32[]{:S(2)}) collective-permute-start(bf16[320,1024]{1,0:T(8,128)(2,1)S(1)} %pair_sum.2), channel_id=1, source_target_pairs={{0,192},{1,193},{2,194},{3,195},{4,196},{5,197},{6,198},{7,199},{8... | collective-permute-start | bytes 1966088 | tf_op jit(solution)/shard_map/ppermute | solution.py:28
  99.5 3.4 %collective-permute-start.20 = (bf16[192,1024]{1,0:T(8,128)(2,1)S(1)}, bf16[192,1024]{1,0:T(8,128)(2,1)S(1)}, u32[]{:S(2)}, u32[]{:S(2)}) collective-permute-start(bf16[192,1024]{1,0:T(8,128)(2,1)S(1)} %pair_sum.3), channel_id=1, source_target_pairs={{0,48},{1,49},{2,50},{3,51},{4,52},{5,53},{6,54},{7,55},{8,24},{9,... | collective-permute-start | bytes 1179656 | tf_op jit(solution)/shard_map/ppermute | solution.py:28
  102.9 1.2 spread_near.1
  104.2 4.8 %collective-permute-done.14.refs_2_ = bf16[320,1024]{1,0:T(8,128)(2,1)S(1)} collective-permute-done((bf16[320,1024]{1,0:T(8,128)(2,1)S(1)}, bf16[320,1024]{1,0:T(8,128)(2,1)S(1)}, u32[]{:S(2)}, u32[]{:S(2)}) %collective-permute-start.14) | collective-permute-done | bytes 655392 | tf_op jit(solution)/shard_map/ppermute | solution.py:28
  109.3 4.3 %collective-permute-done.20.refs_2_ = bf16[192,1024]{1,0:T(8,128)(2,1)S(1)} collective-permute-done((bf16[192,1024]{1,0:T(8,128)(2,1)S(1)}, bf16[192,1024]{1,0:T(8,128)(2,1)S(1)}, u32[]{:S(2)}, u32[]{:S(2)}) %collective-permute-start.20) | collective-permute-done | bytes 393248 | tf_op jit(solution)/shard_map/ppermute | solution.py:28
  113.9 2.5 %collective-permute-done.16.refs_1_ = bf16[320,512]{1,0:T(8,128)(2,1)S(1)} collective-permute-done((bf16[320,512]{1,0:T(8,128)(2,1)S(1)}, bf16[320,512]{1,0:T(8,128)(2,1)S(1)}, u32[]{:S(2)}, u32[]{:S(2)}) %collective-permute-start.16) | collective-permute-done | bytes 327712 | tf_op jit(solution)/shard_map/ppermute | solution.py:28
  116.5 2.9 %collective-permute-start.17 = (bf16[320,256]{1,0:T(8,128)(2,1)S(1)}, bf16[320,256]{1,0:T(8,128)(2,1)S(1)}, u32[]{:S(2)}, u32[]{:S(2)}) collective-permute-start(bf16[320,256]{1,0:T(8,128)(2,1)S(1)} %get-tuple-element.82), channel_id=1, source_target_pairs={{0,48},{1,49},{2,50},{3,51},{4,52},{5,53},{6,54},{7,55},{8,24},{9,... | collective-permute-start | bytes 491528 | tf_op jit(solution)/shard_map/ppermute | solution.py:28
  119.4 4.5 %collective-permute-done.21.refs_1_ = bf16[192,512]{1,0:T(8,128)(2,1)S(1)} collective-permute-done((bf16[192,512]{1,0:T(8,128)(2,1)S(1)}, bf16[192,512]{1,0:T(8,128)(2,1)S(1)}, u32[]{:S(2)}, u32[]{:S(2)}) %collective-permute-start.21) | collective-permute-done | bytes 196640 | tf_op jit(solution)/shard_map/ppermute | solution.py:28
  123.9 1.5 %collective-permute-start.22 = (bf16[192,256]{1,0:T(8,128)(2,1)S(1)}, bf16[192,256]{1,0:T(8,128)(2,1)S(1)}, u32[]{:S(2)}, u32[]{:S(2)}) collective-permute-start(bf16[192,256]{1,0:T(8,128)(2,1)S(1)} %get-tuple-element.92), channel_id=1, source_target_pairs={{0,192},{1,193},{2,194},{3,195},{4,196},{5,197},{6,198},{7,199},{8... | collective-permute-start | bytes 294920 | tf_op jit(solution)/shard_map/ppermute | solution.py:28
  125.4 4.5 %collective-permute-done.22.refs_1_ = bf16[192,256]{1,0:T(8,128)(2,1)S(1)} collective-permute-done((bf16[192,256]{1,0:T(8,128)(2,1)S(1)}, bf16[192,256]{1,0:T(8,128)(2,1)S(1)}, u32[]{:S(2)}, u32[]{:S(2)}) %collective-permute-start.22) | collective-permute-done | bytes 98336 | tf_op jit(solution)/shard_map/ppermute | solution.py:28
  130.0 1.7 %collective-permute-start.18 = (bf16[320,128]{1,0:T(8,128)(2,1)S(1)}, bf16[320,128]{1,0:T(8,128)(2,1)S(1)}, u32[]{:S(2)}, u32[]{:S(2)}) collective-permute-start(bf16[320,128]{1,0:T(8,128)(2,1)S(1)} %get-tuple-element.84), channel_id=1, source_target_pairs={{0,16},{1,17},{2,18},{3,19},{4,20},{5,21},{6,22},{7,23},{8,56},{9,... | collective-permute-start | bytes 245768 | tf_op jit(solution)/shard_map/ppermute | solution.py:28
  132.0 2.1 %collective-permute-done.23.refs_3_ = bf16[192,128]{1,0:T(8,128)(2,1)S(1)} collective-permute-done((bf16[192,128]{1,0:T(8,128)(2,1)S(1)}, bf16[192,128]{1,0:T(8,128)(2,1)S(1)}, u32[]{:S(2)}, u32[]{:S(2)}) %collective-permute-start.23) | collective-permute-done | bytes 49184 | tf_op jit(solution)/shard_map/ppermute | solution.py:28
  134.1 1.5 %collective-permute-done.18.refs_1_ = bf16[320,128]{1,0:T(8,128)(2,1)S(1)} collective-permute-done((bf16[320,128]{1,0:T(8,128)(2,1)S(1)}, bf16[320,128]{1,0:T(8,128)(2,1)S(1)}, u32[]{:S(2)}, u32[]{:S(2)}) %collective-permute-start.18) | collective-permute-done | bytes 81952 | tf_op jit(solution)/shard_map/ppermute | solution.py:28
  (60 shorter events, 9.3 us)
Async XLA Ops:
  0.6 23.0 %copy-start = (bf16[512,512]{1,0:T(8,128)(2,1)S(1)}, bf16[512,512]{1,0:T(8,128)(2,1)}, u32[]{:S(2)}) copy-start(bf16[512,512]{1,0:T(8,128)(2,1)} %param.12) | copy-start | bytes 1572868
  0.6 11.4 %collective-permute-start.1 = (bf16[128,512]{1,0:T(8,128)(2,1)}, bf16[128,512]{1,0:T(8,128)(2,1)S(1)}, u32[]{:S(2)}, u32[]{:S(2)}) collective-permute-start(bf16[128,512]{1,0:T(8,128)(2,1)} %first.3), channel_id=1, source_target_pairs={{0,64},{1,65},{2,66},{3,67},{4,68},{5,69},{6,70},{7,71},{8,200},{9... | collective-permute-start | bytes 393224 | tf_op jit(solution)/shard_map/ppermute | solution.py:28
  2.3 9.8 %collective-permute-start = (bf16[128,512]{1,0:T(8,128)(2,1)}, bf16[128,512]{1,0:T(8,128)(2,1)S(1)}, u32[]{:S(2)}, u32[]{:S(2)}) collective-permute-start(bf16[128,512]{1,0:T(8,128)(2,1)} %first.3), channel_id=1, source_target_pairs={{0,16},{1,17},{2,18},{3,19},{4,20},{5,21},{6,22},{7,23},{8,56},{9,... | collective-permute-start | bytes 393224 | tf_op jit(solution)/shard_map/ppermute | solution.py:28
  6.5 5.6 %copy-start.1 = (bf16[128,512]{1,0:T(8,128)(2,1)S(1)}, bf16[128,512]{1,0:T(8,128)(2,1)}, u32[]{:S(2)}) copy-start(bf16[128,512]{1,0:T(8,128)(2,1)} %first.3) | copy-start | bytes 393220
  6.5 17.1 %copy-start.5 = (s32[128]{0:T(128)S(1)}, s32[128]{0:T(128)}, u32[]{:S(2)}) copy-start(s32[128]{0:T(128)} %param.9) | copy-start | bytes 1540
  6.5 17.1 %copy-start.4 = (f32[512]{0:T(512)S(1)}, f32[512]{0:T(512)}, u32[]{:S(2)}) copy-start(f32[512]{0:T(512)} %param.14) | copy-start | bytes 6148
  12.1 7.8 %collective-permute-start.2 = (bf16[256,256]{1,0:T(8,128)(2,1)S(1)}, bf16[256,256]{1,0:T(8,128)(2,1)S(1)}, u32[]{:S(2)}, u32[]{:S(2)}) collective-permute-start(bf16[256,256]{1,0:T(8,128)(2,1)S(1)} %join_0.2.first), channel_id=1, source_target_pairs={{0,48},{1,49},{2,50},{3,51},{4,52},{5,53},{6,54},{7,55},{8,24},{9,... | collective-permute-start | bytes 393224 | tf_op jit(solution)/shard_map/ppermute | solution.py:28
  15.8 6.3 %collective-permute-start.5 = (bf16[256,256]{1,0:T(8,128)(2,1)S(1)}, bf16[256,256]{1,0:T(8,128)(2,1)S(1)}, u32[]{:S(2)}, u32[]{:S(2)}) collective-permute-start(bf16[256,256]{1,0:T(8,128)(2,1)S(1)} %join_0.3.first), channel_id=1, source_target_pairs={{0,192},{1,193},{2,194},{3,195},{4,196},{5,197},{6,198},{7,199},{8... | collective-permute-start | bytes 393224 | tf_op jit(solution)/shard_map/ppermute | solution.py:28
  19.9 11.6 %collective-permute-start.3 = (bf16[512,256]{1,0:T(8,128)(2,1)S(1)}, bf16[512,256]{1,0:T(8,128)(2,1)S(1)}, u32[]{:S(2)}, u32[]{:S(2)}) collective-permute-start(bf16[512,256]{1,0:T(8,128)(2,1)S(1)} %join_1.2.first), channel_id=1, source_target_pairs={{0,64},{1,65},{2,66},{3,67},{4,68},{5,69},{6,70},{7,71},{8,200},{9... | collective-permute-start | bytes 786440 | tf_op jit(solution)/shard_map/ppermute | solution.py:28
  22.1 8.3 %collective-permute-start.6 = (bf16[512,256]{1,0:T(8,128)(2,1)S(1)}, bf16[512,256]{1,0:T(8,128)(2,1)S(1)}, u32[]{:S(2)}, u32[]{:S(2)}) collective-permute-start(bf16[512,256]{1,0:T(8,128)(2,1)S(1)} %join_1.3.first), channel_id=1, source_target_pairs={{0,16},{1,17},{2,18},{3,19},{4,20},{5,21},{6,22},{7,23},{8,56},{9,... | collective-permute-start | bytes 786440 | tf_op jit(solution)/shard_map/ppermute | solution.py:28
  30.4 7.9 %collective-permute-start.9 = (bf16[1024,256]{1,0:T(8,128)(2,1)S(1)}, bf16[1024,256]{1,0:T(8,128)(2,1)S(1)}, u32[]{:S(2)}, u32[]{:S(2)}) collective-permute-start(bf16[1024,256]{1,0:T(8,128)(2,1)S(1)} %join_2.3.refs_1_), channel_id=1, source_target_pairs={{0,8},{1,9},{2,10},{3,11},{4,12},{5,13},{6,14},{7,15},{8,0},{9,1},... | collective-permute-start | bytes 1572872 | tf_op jit(solution)/shard_map/ppermute | solution.py:33
  31.5 6.8 %collective-permute-start.8 = (bf16[1024,256]{1,0:T(8,128)(2,1)S(1)}, bf16[1024,256]{1,0:T(8,128)(2,1)S(1)}, u32[]{:S(2)}, u32[]{:S(2)}) collective-permute-start(bf16[1024,256]{1,0:T(8,128)(2,1)S(1)} %join_2.2.refs_0_), channel_id=1, source_target_pairs={{0,8},{1,9},{2,10},{3,11},{4,12},{5,13},{6,14},{7,15},{8,0},{9,1},... | collective-permute-start | bytes 1572872 | tf_op jit(solution)/shard_map/ppermute | solution.py:33
  31.6 16.1 %collective-permute-start.7 = (bf16[1024,256]{1,0:T(8,128)(2,1)S(1)}, bf16[1024,256]{1,0:T(8,128)(2,1)S(1)}, u32[]{:S(2)}, u32[]{:S(2)}) collective-permute-start(bf16[1024,256]{1,0:T(8,128)(2,1)S(1)} %join_2.3.refs_1_), channel_id=1, source_target_pairs={{0,48},{1,49},{2,50},{3,51},{4,52},{5,53},{6,54},{7,55},{8,24},{9,... | collective-permute-start | bytes 1572872 | tf_op jit(solution)/shard_map/ppermute | solution.py:28
  35.3 12.3 %collective-permute-start.4 = (bf16[1024,256]{1,0:T(8,128)(2,1)S(1)}, bf16[1024,256]{1,0:T(8,128)(2,1)S(1)}, u32[]{:S(2)}, u32[]{:S(2)}) collective-permute-start(bf16[1024,256]{1,0:T(8,128)(2,1)S(1)} %join_2.2.refs_0_), channel_id=1, source_target_pairs={{0,192},{1,193},{2,194},{3,195},{4,196},{5,197},{6,198},{7,199},{8... | collective-permute-start | bytes 1572872 | tf_op jit(solution)/shard_map/ppermute | solution.py:28
  47.7 1.9 %collective-permute-start.10 = (bf16[1024,256]{1,0:T(8,128)(2,1)S(1)}, bf16[1024,256]{1,0:T(8,128)(2,1)S(1)}, u32[]{:S(2)}, u32[]{:S(2)}) collective-permute-start(bf16[1024,256]{1,0:T(8,128)(2,1)S(1)} %collective-permute-done.4.refs_0_), channel_id=1, source_target_pairs={{0,8},{1,9},{2,10},{3,11},{4,12},{5,13},{6,14},{7,15},{8,0},{9,1},... | collective-permute-start | bytes 1572872 | tf_op jit(solution)/shard_map/ppermute | solution.py:33
  47.7 2.7 %collective-permute-start.11 = (bf16[1024,256]{1,0:T(8,128)(2,1)S(1)}, bf16[1024,256]{1,0:T(8,128)(2,1)S(1)}, u32[]{:S(2)}, u32[]{:S(2)}) collective-permute-start(bf16[1024,256]{1,0:T(8,128)(2,1)S(1)} %collective-permute-done.7.refs_1_), channel_id=1, source_target_pairs={{0,8},{1,9},{2,10},{3,11},{4,12},{5,13},{6,14},{7,15},{8,0},{9,1},... | collective-permute-start | bytes 1572872 | tf_op jit(solution)/shard_map/ppermute | solution.py:33
  49.5 24.3 %copy-start.2 = (bf16[512,512]{1,0:T(8,128)(2,1)S(1)}, bf16[512,512]{1,0:T(8,128)(2,1)}, u32[]{:S(2)}) copy-start(bf16[512,512]{1,0:T(8,128)(2,1)} %w_neigh.1) | copy-start | bytes 1572868
  49.5 24.3 %copy-start.3 = (bf16[128,512]{1,0:T(8,128)(2,1)S(1)}, bf16[128,512]{1,0:T(8,128)(2,1)}, u32[]{:S(2)}) copy-start(bf16[128,512]{1,0:T(8,128)(2,1)} %cotangent.1) | copy-start | bytes 393220
  93.8 3.1 %collective-permute-start.12 = (bf16[320,1024]{1,0:T(8,128)(2,1)S(1)}, bf16[320,1024]{1,0:T(8,128)(2,1)S(1)}, u32[]{:S(2)}, u32[]{:S(2)}) collective-permute-start(bf16[320,1024]{1,0:T(8,128)(2,1)S(1)} %get-tuple-element.63), channel_id=1, source_target_pairs={{0,8},{1,9},{2,10},{3,11},{4,12},{5,13},{6,14},{7,15},{8,0},{9,1},... | collective-permute-start | bytes 1966088 | tf_op jit(solution)/shard_map/ppermute | solution.py:33
  93.9 3.0 %collective-permute-start.13 = (bf16[192,1024]{1,0:T(8,128)(2,1)S(1)}, bf16[192,1024]{1,0:T(8,128)(2,1)S(1)}, u32[]{:S(2)}, u32[]{:S(2)}) collective-permute-start(bf16[192,1024]{1,0:T(8,128)(2,1)S(1)} %get-tuple-element.64), channel_id=1, source_target_pairs={{0,8},{1,9},{2,10},{3,11},{4,12},{5,13},{6,14},{7,15},{8,0},{9,1},... | collective-permute-start | bytes 1179656 | tf_op jit(solution)/shard_map/ppermute | solution.py:33
  97.1 11.9 %collective-permute-start.14 = (bf16[320,1024]{1,0:T(8,128)(2,1)S(1)}, bf16[320,1024]{1,0:T(8,128)(2,1)S(1)}, u32[]{:S(2)}, u32[]{:S(2)}) collective-permute-start(bf16[320,1024]{1,0:T(8,128)(2,1)S(1)} %pair_sum.2), channel_id=1, source_target_pairs={{0,192},{1,193},{2,194},{3,195},{4,196},{5,197},{6,198},{7,199},{8... | collective-permute-start | bytes 1966088 | tf_op jit(solution)/shard_map/ppermute | solution.py:28
  99.4 9.6 %collective-permute-start.15 = (bf16[320,1024]{1,0:T(8,128)(2,1)S(1)}, bf16[320,1024]{1,0:T(8,128)(2,1)S(1)}, u32[]{:S(2)}, u32[]{:S(2)}) collective-permute-start(bf16[320,1024]{1,0:T(8,128)(2,1)S(1)} %get-tuple-element.77), channel_id=1, source_target_pairs={{0,8},{1,9},{2,10},{3,11},{4,12},{5,13},{6,14},{7,15},{8,0},{9,1},... | collective-permute-start | bytes 1966088 | tf_op jit(solution)/shard_map/ppermute | solution.py:33
  99.5 14.2 %collective-permute-start.20 = (bf16[192,1024]{1,0:T(8,128)(2,1)S(1)}, bf16[192,1024]{1,0:T(8,128)(2,1)S(1)}, u32[]{:S(2)}, u32[]{:S(2)}) collective-permute-start(bf16[192,1024]{1,0:T(8,128)(2,1)S(1)} %pair_sum.3), channel_id=1, source_target_pairs={{0,48},{1,49},{2,50},{3,51},{4,52},{5,53},{6,54},{7,55},{8,24},{9,... | collective-permute-start | bytes 1179656 | tf_op jit(solution)/shard_map/ppermute | solution.py:28
  102.9 10.8 %collective-permute-start.19 = (bf16[192,1024]{1,0:T(8,128)(2,1)S(1)}, bf16[192,1024]{1,0:T(8,128)(2,1)S(1)}, u32[]{:S(2)}, u32[]{:S(2)}) collective-permute-start(bf16[192,1024]{1,0:T(8,128)(2,1)S(1)} %get-tuple-element.86), channel_id=1, source_target_pairs={{0,8},{1,9},{2,10},{3,11},{4,12},{5,13},{6,14},{7,15},{8,0},{9,1},... | collective-permute-start | bytes 1179656 | tf_op jit(solution)/shard_map/ppermute | solution.py:33
  109.2 7.2 %collective-permute-start.16 = (bf16[320,512]{1,0:T(8,128)(2,1)S(1)}, bf16[320,512]{1,0:T(8,128)(2,1)S(1)}, u32[]{:S(2)}, u32[]{:S(2)}) collective-permute-start(bf16[320,512]{1,0:T(8,128)(2,1)S(1)} %get-tuple-element.80), channel_id=1, source_target_pairs={{0,64},{1,65},{2,66},{3,67},{4,68},{5,69},{6,70},{7,71},{8,200},{9... | collective-permute-start | bytes 983048 | tf_op jit(solution)/shard_map/ppermute | solution.py:28
  113.8 10.1 %collective-permute-start.21 = (bf16[192,512]{1,0:T(8,128)(2,1)S(1)}, bf16[192,512]{1,0:T(8,128)(2,1)S(1)}, u32[]{:S(2)}, u32[]{:S(2)}) collective-permute-start(bf16[192,512]{1,0:T(8,128)(2,1)S(1)} %get-tuple-element.90), channel_id=1, source_target_pairs={{0,16},{1,17},{2,18},{3,19},{4,20},{5,21},{6,22},{7,23},{8,56},{9,... | collective-permute-start | bytes 589832 | tf_op jit(solution)/shard_map/ppermute | solution.py:28
  116.5 13.5 %collective-permute-start.17 = (bf16[320,256]{1,0:T(8,128)(2,1)S(1)}, bf16[320,256]{1,0:T(8,128)(2,1)S(1)}, u32[]{:S(2)}, u32[]{:S(2)}) collective-permute-start(bf16[320,256]{1,0:T(8,128)(2,1)S(1)} %get-tuple-element.82), channel_id=1, source_target_pairs={{0,48},{1,49},{2,50},{3,51},{4,52},{5,53},{6,54},{7,55},{8,24},{9,... | collective-permute-start | bytes 491528 | tf_op jit(solution)/shard_map/ppermute | solution.py:28
  123.9 5.9 %collective-permute-start.22 = (bf16[192,256]{1,0:T(8,128)(2,1)S(1)}, bf16[192,256]{1,0:T(8,128)(2,1)S(1)}, u32[]{:S(2)}, u32[]{:S(2)}) collective-permute-start(bf16[192,256]{1,0:T(8,128)(2,1)S(1)} %get-tuple-element.92), channel_id=1, source_target_pairs={{0,192},{1,193},{2,194},{3,195},{4,196},{5,197},{6,198},{7,199},{8... | collective-permute-start | bytes 294920 | tf_op jit(solution)/shard_map/ppermute | solution.py:28
  129.9 4.2 %collective-permute-start.23 = (bf16[192,128]{1,0:T(8,128)(2,1)S(1)}, bf16[192,128]{1,0:T(8,128)(2,1)S(1)}, u32[]{:S(2)}, u32[]{:S(2)}) collective-permute-start(bf16[192,128]{1,0:T(8,128)(2,1)S(1)} %get-tuple-element.94), channel_id=1, source_target_pairs={{0,64},{1,65},{2,66},{3,67},{4,68},{5,69},{6,70},{7,71},{8,200},{9... | collective-permute-start | bytes 147464 | tf_op jit(solution)/shard_map/ppermute | solution.py:28
  130.0 5.5 %collective-permute-start.18 = (bf16[320,128]{1,0:T(8,128)(2,1)S(1)}, bf16[320,128]{1,0:T(8,128)(2,1)S(1)}, u32[]{:S(2)}, u32[]{:S(2)}) collective-permute-start(bf16[320,128]{1,0:T(8,128)(2,1)S(1)} %get-tuple-element.84), channel_id=1, source_target_pairs={{0,16},{1,17},{2,18},{3,19},{4,20},{5,21},{6,22},{7,23},{8,56},{9,... | collective-permute-start | bytes 245768 | tf_op jit(solution)/shard_map/ppermute | solution.py:28

commit v9 on v8

--- a/solution.py
+++ b/solution.py
@@ -239,12 +239,12 @@
     base = jnp.dot(features, w_self, preferred_element_type=F32) + bias[None, :]
 
     width = features.shape[1] // 2
-    *got, adj = lax.optimization_barrier((*[exchange(features, a, 0) for a, _ in AXES], adj))
+    got = [exchange(features, a, 0) for a, _ in AXES]
     waves = [join(features, g, w * width, width, "join_0") for w, g in enumerate(got)]
     got = [exchange(v, a, 1) for v, (a, _) in zip(waves, AXES)]
+    got[1], base, degf_row = lax.optimization_barrier((got[1], base, degf_row))
     waves = [join(v, g, 0, width, "join_1") for v, g in zip(waves, got)]
     got = [exchange(v, b, 0) for v, (_, b) in zip(waves, AXES)]
-    got[1], base, degf_row = lax.optimization_barrier((got[1], base, degf_row))
     near = [join(v, g, 0, width, "join_2") for v, g in zip(waves, got)]
     far = [exchange(v, b, 1) for v, (_, b) in zip(near, AXES)]
     other = [swap(v) for v in near]
@@ -272,12 +272,15 @@
     theirs = [swap(v) for v in near_other]
     mine = spread_matmul(table, adj, 0, 0, "spread_near")
     got[0], *mine = lax.optimization_barrier((got[0], *mine))
-    ends = []
-    for w, (a, b) in enumerate(AXES):
-        stay, go = split_sum((mine[w], theirs[w], got[w]), "sum_3")
-        stay, go = split_sum((stay, exchange(go, b, 0)), "sum_2")
-        stay, go = split_sum((stay, exchange(go, a, 1)), "sum_1")
-        ends += [stay, exchange(go, a, 0)]
+    stay, go = [None, None], [None, None]
+    for step in range(3):
+        for w, (a, b) in enumerate(AXES):
+            if w == 1 and step == 2:
+                got[1], go[0] = lax.optimization_barrier((got[1], go[0]))
+            terms = (mine[w], theirs[w], got[w]) if step == 0 else (stay[w], got[w])
+            stay[w], go[w] = split_sum(terms, f"sum_{step}")
+        got = [exchange(v, axes[1 - (step + 1) // 2], (step + 1) % 2 ^ 1) for v, axes in zip(go, AXES)]
+    ends = [stay[0], got[0], stay[1], got[1]]
     grad_features = last_sum(ends, own)
     return output, grad_features
 

time: 139 us -> 136 us (0.978); the launches traced: 136 us -> 135 us
  waiting for transfers between devices: 42.2 us -> 35.3 us
  starting transfers between devices: 33.8 us -> 37.9 us
  blocking collectives: 39.9 us -> 38.1 us
    ppermute x16, waiting for transfers between devices: 41.3 us -> 35.2 us  [exchange(): return lax.ppermute(value, ('row', 'col'), pairs)]
    ppermute x16, starting transfers between devices: 31.5 us -> 36.6 us  [exchange(): return lax.ppermute(value, ('row', 'col'), pairs)]
    all_to_all x1, blocking collectives: 22.2 us -> 20.4 us  [body(): arrived = lax.all_to_all(summed, 'col', 0, 0, tiled=True)]
  transfers between devices with their start and end apart: 24 -> 24, of which waited for: 13 -> 11; matrix products, arithmetic and copies ran while one was open for 1% -> 2% of each run, Pallas kernels for 10% -> 11%
where the time goes in v9:
time: 136 us; the launch traced here: 135 us
  blocking collectives  38.1 us (28%)
  starting transfers between devices  37.9 us (28%)
  waiting for transfers between devices  35.3 us (26%)
  Pallas kernels  19.1 us (14%)
  local copies, waits for them, and re-layouts  1.78 us (1%)
  matrix products  1.47 us (1%)
    ppermute x16, starting transfers between devices, exchange(): return lax.ppermute(value, ('row', 'col'), pairs)  36.6 us
    ppermute x16, waiting for transfers between devices, exchange(): return lax.ppermute(value, ('row', 'col'), pairs)  35.2 us
    all_to_all x1, blocking collectives, body(): arrived = lax.all_to_all(summed, 'col', 0, 0, tiled=True)  20.4 us
    all_to_all x1, blocking collectives, body(): table = lax.all_to_all(scaled_t, 'col', 0, 0, tiled=True)  17.7 us
    pallas_call x23, Pallas kernels, in_vmem(): pl.pallas_call(kernel, in_specs=[spec] * len(operands), out_specs=out_spe...  13.6 us
    pallas_call x1, Pallas kernels, adjacency(): pl.pallas_call(adjacency_kernel, grid_spec=pltpu.PrefetchScalarGridSpec(n...  5.53 us
  transfers between devices with their start and end apart: 24, of which 11 were waited for; matrix products, arithmetic and copies ran while one was open for 2% of the time, Pallas kernels for 11%

profile of v9, /device:TPU:32, one launch (start us, length us, event | category | flops | bytes accessed | tf_op | source)
XLA Modules:
  0.0 135.2 jit_solution(6744286269213359739)
XLA Ops:
  0.6 1.7 %collective-permute-start.4 = (bf16[128,512]{1,0:T(8,128)(2,1)}, bf16[128,512]{1,0:T(8,128)(2,1)S(1)}, u32[]{:S(2)}, u32[]{:S(2)}) collective-permute-start(bf16[128,512]{1,0:T(8,128)(2,1)} %first.3), channel_id=1, source_target_pairs={{0,64},{1,65},{2,66},{3,67},{4,68},{5,69},{6,70},{7,71},{8,200},{9... | collective-permute-start | bytes 393224 | tf_op jit(solution)/shard_map/ppermute | solution.py:28
  2.3 3.3 %collective-permute-start = (bf16[128,512]{1,0:T(8,128)(2,1)}, bf16[128,512]{1,0:T(8,128)(2,1)S(1)}, u32[]{:S(2)}, u32[]{:S(2)}) collective-permute-start(bf16[128,512]{1,0:T(8,128)(2,1)} %first.3), channel_id=1, source_target_pairs={{0,16},{1,17},{2,18},{3,19},{4,20},{5,21},{6,22},{7,23},{8,56},{9,... | collective-permute-start | bytes 393224 | tf_op jit(solution)/shard_map/ppermute | solution.py:28
  5.6 1.2 convolution_add_fusion.base
  7.7 2.3 %collective-permute-start.5 = (bf16[256,256]{1,0:T(8,128)(2,1)S(1)}, bf16[256,256]{1,0:T(8,128)(2,1)S(1)}, u32[]{:S(2)}, u32[]{:S(2)}) collective-permute-start(bf16[256,256]{1,0:T(8,128)(2,1)S(1)} %join_0.3.first), channel_id=1, source_target_pairs={{0,192},{1,193},{2,194},{3,195},{4,196},{5,197},{6,198},{7,199},{8... | collective-permute-start | bytes 393224 | tf_op jit(solution)/shard_map/ppermute | solution.py:28
  10.0 5.5 %collective-permute-start.1 = (bf16[256,256]{1,0:T(8,128)(2,1)S(1)}, bf16[256,256]{1,0:T(8,128)(2,1)S(1)}, u32[]{:S(2)}, u32[]{:S(2)}) collective-permute-start(bf16[256,256]{1,0:T(8,128)(2,1)S(1)} %join_0.2.first), channel_id=1, source_target_pairs={{0,48},{1,49},{2,50},{3,51},{4,52},{5,53},{6,54},{7,55},{8,24},{9,... | collective-permute-start | bytes 393224 | tf_op jit(solution)/shard_map/ppermute | solution.py:28
  16.1 3.1 %collective-permute-done.1.second = bf16[256,256]{1,0:T(8,128)(2,1)S(1)} collective-permute-done((bf16[256,256]{1,0:T(8,128)(2,1)S(1)}, bf16[256,256]{1,0:T(8,128)(2,1)S(1)}, u32[]{:S(2)}, u32[]{:S(2)}) %collective-permute-start.1) | collective-permute-done | bytes 131104 | tf_op jit(solution)/shard_map/ppermute | solution.py:28
  19.9 1.9 %collective-permute-start.6 = (bf16[512,256]{1,0:T(8,128)(2,1)S(1)}, bf16[512,256]{1,0:T(8,128)(2,1)S(1)}, u32[]{:S(2)}, u32[]{:S(2)}) collective-permute-start(bf16[512,256]{1,0:T(8,128)(2,1)S(1)} %join_1.3.first), channel_id=1, source_target_pairs={{0,16},{1,17},{2,18},{3,19},{4,20},{5,21},{6,22},{7,23},{8,56},{9,... | collective-permute-start | bytes 786440 | tf_op jit(solution)/shard_map/ppermute | solution.py:28
  21.8 3.9 %collective-permute-done.2.second = bf16[512,256]{1,0:T(8,128)(2,1)S(1)} collective-permute-done((bf16[512,256]{1,0:T(8,128)(2,1)S(1)}, bf16[512,256]{1,0:T(8,128)(2,1)S(1)}, u32[]{:S(2)}, u32[]{:S(2)}) %collective-permute-start.2) | collective-permute-done | bytes 262176 | tf_op jit(solution)/shard_map/ppermute | solution.py:28
  25.8 2.7 %collective-permute-done.6.second = bf16[512,256]{1,0:T(8,128)(2,1)S(1)} collective-permute-done((bf16[512,256]{1,0:T(8,128)(2,1)S(1)}, bf16[512,256]{1,0:T(8,128)(2,1)S(1)}, u32[]{:S(2)}, u32[]{:S(2)}) %collective-permute-start.6) | collective-permute-done | bytes 262176 | tf_op jit(solution)/shard_map/ppermute | solution.py:28
  28.6 2.5 %collective-permute-start.3 = (bf16[1024,256]{1,0:T(8,128)(2,1)S(1)}, bf16[1024,256]{1,0:T(8,128)(2,1)S(1)}, u32[]{:S(2)}, u32[]{:S(2)}) collective-permute-start(bf16[1024,256]{1,0:T(8,128)(2,1)S(1)} %join_2.2.refs_0_), channel_id=1, source_target_pairs={{0,192},{1,193},{2,194},{3,195},{4,196},{5,197},{6,198},{7,199},{8... | collective-permute-start | bytes 1572872 | tf_op jit(solution)/shard_map/ppermute | solution.py:28
  31.1 5.2 %collective-permute-start.7 = (bf16[1024,256]{1,0:T(8,128)(2,1)S(1)}, bf16[1024,256]{1,0:T(8,128)(2,1)}, u32[]{:S(2)}, u32[]{:S(2)}) collective-permute-start(bf16[1024,256]{1,0:T(8,128)(2,1)S(1)} %join_2.3.refs_1_), channel_id=1, source_target_pairs={{0,48},{1,49},{2,50},{3,51},{4,52},{5,53},{6,54},{7,55},{8,24},{9,... | collective-permute-start | bytes 1572872 | tf_op jit(solution)/shard_map/ppermute | solution.py:28
  37.3 5.5 %adjacency.1.adj = bf16[1024,4096]{1,0:T(8,128)(2,1)S(1)} custom-call(s32[32]{0:T(128)S(1)} %fusion.2.place, s32[96]{0:T(128)S(1)} %reshape_squeeze.3.where, s32[32,3,128,128]{3,2,1,0:T(8,128)} %bitcast.13), custom_call_target="tpu_custom_call" | custom-call | bytes 14680064 | tf_op jit(solution)/shard_map/adjacency/pallas_call | solution.py:76
  42.8 2.3 %gather_near.1.refs_2_ = f32[1024,512]{1,0:T(8,128)S(1)} custom-call(bf16[1024,4096]{1,0:T(8,128)(2,1)S(1)} %adjacency.1.adj, bf16[1024,256]{1,0:T(8,128)(2,1)S(1)} %join_2.2.refs_0_, bf16[1024,256]{1,0:T(8,128)(2,1)S(1)} %join_2.3.refs_1_, bf16[1024,256]{1,0:T(8,128)(2,1)S(1)} %collective-permute-done.8.refs_2_, ...), custom_call_target="tpu_custom_call" | custom-call | bytes 1024 | tf_op jit(solution)/shard_map/gather_near/pallas_call | solution.py:40
  45.2 3.9 %collective-permute-done.7.refs_1_ = bf16[1024,256]{1,0:T(8,128)(2,1)} collective-permute-done((bf16[1024,256]{1,0:T(8,128)(2,1)S(1)}, bf16[1024,256]{1,0:T(8,128)(2,1)}, u32[]{:S(2)}, u32[]{:S(2)}) %collective-permute-start.7) | collective-permute-done | bytes 524320 | tf_op jit(solution)/shard_map/ppermute | solution.py:28
  49.6 2.3 %gather_far.1.refs_2_ = f32[1024,512]{1,0:T(8,128)S(1)} custom-call(bf16[1024,4096]{1,0:T(8,128)(2,1)S(1)} %adjacency.1.adj, bf16[1024,256]{1,0:T(8,128)(2,1)S(1)} %collective-permute-done.3.refs_0_, bf16[1024,256]{1,0:T(8,128)(2,1)} %collective-permute-done.7.refs_1_, f32[1024,512]{1,0:T(8,128)S(1)} %gather_near.1.refs_2_), custom_call_target="tpu_custom_call" | custom-call | bytes 1024 | tf_op jit(solution)/shard_map/gather_far/pallas_call | solution.py:40
  51.9 1.3 gather_far_other.1
  53.2 20.4 %all_to_all.16 = bf16[8,128,512]{2,1,0:T(8,128)(2,1)S(1)} all-to-all(bf16[8,128,512]{2,1,0:T(8,128)(2,1)S(1)} %bitcast.11), channel_id=1, replica_groups=mesh['row'=32,'col'=8] {'col'}, dimensions={0} | all-to-all | bytes 2097152 | tf_op jit(solution)/shard_map/all_to_all | solution.py:258
  74.7 17.7 %all_to_all.17.parts = bf16[8,512,128]{2,1,0:T(8,128)(2,1)S(1)} all-to-all(bf16[8,512,128]{2,1,0:T(8,128)(2,1)S(1)} %get-tuple-element.58), channel_id=1, replica_groups=mesh['row'=32,'col'=8] {'col'}, dimensions={0} | all-to-all | bytes 2097152 | tf_op jit(solution)/shard_map/all_to_all | solution.py:261
  92.4 1.2 spread_far_other.1
  94.3 1.2 spread_near_other.1
  95.5 1.2 spread_far.1
  97.0 1.2 collective-permute-start.14
  98.2 3.5 %collective-permute-start.19 = (bf16[192,1024]{1,0:T(8,128)(2,1)S(1)}, bf16[192,1024]{1,0:T(8,128)(2,1)S(1)}, u32[]{:S(2)}, u32[]{:S(2)}) collective-permute-start(bf16[192,1024]{1,0:T(8,128)(2,1)S(1)} %pair_sum.3), channel_id=1, source_target_pairs={{0,48},{1,49},{2,50},{3,51},{4,52},{5,53},{6,54},{7,55},{8,24},{9,... | collective-permute-start | bytes 1179656 | tf_op jit(solution)/shard_map/ppermute | solution.py:28
  101.8 1.2 spread_near.1
  103.0 5.8 %collective-permute-done.14.refs_2_ = bf16[320,1024]{1,0:T(8,128)(2,1)S(1)} collective-permute-done((bf16[320,1024]{1,0:T(8,128)(2,1)S(1)}, bf16[320,1024]{1,0:T(8,128)(2,1)S(1)}, u32[]{:S(2)}, u32[]{:S(2)}) %collective-permute-start.14) | collective-permute-done | bytes 655392 | tf_op jit(solution)/shard_map/ppermute | solution.py:28
  109.2 3.3 %collective-permute-done.19.refs_2_ = bf16[192,1024]{1,0:T(8,128)(2,1)S(1)} collective-permute-done((bf16[192,1024]{1,0:T(8,128)(2,1)S(1)}, bf16[192,1024]{1,0:T(8,128)(2,1)S(1)}, u32[]{:S(2)}, u32[]{:S(2)}) %collective-permute-start.19) | collective-permute-done | bytes 393248 | tf_op jit(solution)/shard_map/ppermute | solution.py:28
  112.7 3.6 %collective-permute-done.16.refs_1_ = bf16[320,512]{1,0:T(8,128)(2,1)S(1)} collective-permute-done((bf16[320,512]{1,0:T(8,128)(2,1)S(1)}, bf16[320,512]{1,0:T(8,128)(2,1)S(1)}, u32[]{:S(2)}, u32[]{:S(2)}) %collective-permute-start.16) | collective-permute-done | bytes 327712 | tf_op jit(solution)/shard_map/ppermute | solution.py:28
  116.3 4.3 %collective-permute-start.17 = (bf16[320,256]{1,0:T(8,128)(2,1)S(1)}, bf16[320,256]{1,0:T(8,128)(2,1)S(1)}, u32[]{:S(2)}, u32[]{:S(2)}) collective-permute-start(bf16[320,256]{1,0:T(8,128)(2,1)S(1)} %get-tuple-element.78), channel_id=1, source_target_pairs={{0,48},{1,49},{2,50},{3,51},{4,52},{5,53},{6,54},{7,55},{8,24},{9,... | collective-permute-start | bytes 491528 | tf_op jit(solution)/shard_map/ppermute | solution.py:28
  121.4 4.2 %collective-permute-start.21 = (bf16[192,256]{1,0:T(8,128)(2,1)S(1)}, bf16[192,256]{1,0:T(8,128)(2,1)S(1)}, u32[]{:S(2)}, u32[]{:S(2)}) collective-permute-start(bf16[192,256]{1,0:T(8,128)(2,1)S(1)} %get-tuple-element.86), channel_id=1, source_target_pairs={{0,192},{1,193},{2,194},{3,195},{4,196},{5,197},{6,198},{7,199},{8... | collective-permute-start | bytes 294920 | tf_op jit(solution)/shard_map/ppermute | solution.py:28
  125.7 3.1 %collective-permute-done.21.refs_1_ = bf16[192,256]{1,0:T(8,128)(2,1)S(1)} collective-permute-done((bf16[192,256]{1,0:T(8,128)(2,1)S(1)}, bf16[192,256]{1,0:T(8,128)(2,1)S(1)}, u32[]{:S(2)}, u32[]{:S(2)}) %collective-permute-start.21) | collective-permute-done | bytes 98336 | tf_op jit(solution)/shard_map/ppermute | solution.py:28
  129.3 3.7 %collective-permute-done.23.refs_3_ = bf16[192,128]{1,0:T(8,128)(2,1)S(1)} collective-permute-done((bf16[192,128]{1,0:T(8,128)(2,1)S(1)}, bf16[192,128]{1,0:T(8,128)(2,1)S(1)}, u32[]{:S(2)}, u32[]{:S(2)}) %collective-permute-start.23) | collective-permute-done | bytes 49184 | tf_op jit(solution)/shard_map/ppermute | solution.py:28
  133.0 1.5 %collective-permute-done.22.refs_1_ = bf16[320,128]{1,0:T(8,128)(2,1)S(1)} collective-permute-done((bf16[320,128]{1,0:T(8,128)(2,1)S(1)}, bf16[320,128]{1,0:T(8,128)(2,1)S(1)}, u32[]{:S(2)}, u32[]{:S(2)}) %collective-permute-start.22) | collective-permute-done | bytes 81952 | tf_op jit(solution)/shard_map/ppermute | solution.py:28
  (56 shorter events, 8.8 us)
Async XLA Ops:
  0.6 5.0 %copy-start = (bf16[512,512]{1,0:T(8,128)(2,1)S(1)}, bf16[512,512]{1,0:T(8,128)(2,1)}, u32[]{:S(2)}) copy-start(bf16[512,512]{1,0:T(8,128)(2,1)} %param.12) | copy-start | bytes 1572868
  0.6 6.1 %collective-permute-start.4 = (bf16[128,512]{1,0:T(8,128)(2,1)}, bf16[128,512]{1,0:T(8,128)(2,1)S(1)}, u32[]{:S(2)}, u32[]{:S(2)}) collective-permute-start(bf16[128,512]{1,0:T(8,128)(2,1)} %first.3), channel_id=1, source_target_pairs={{0,64},{1,65},{2,66},{3,67},{4,68},{5,69},{6,70},{7,71},{8,200},{9... | collective-permute-start | bytes 393224 | tf_op jit(solution)/shard_map/ppermute | solution.py:28
  2.3 7.6 %collective-permute-start = (bf16[128,512]{1,0:T(8,128)(2,1)}, bf16[128,512]{1,0:T(8,128)(2,1)S(1)}, u32[]{:S(2)}, u32[]{:S(2)}) collective-permute-start(bf16[128,512]{1,0:T(8,128)(2,1)} %first.3), channel_id=1, source_target_pairs={{0,16},{1,17},{2,18},{3,19},{4,20},{5,21},{6,22},{7,23},{8,56},{9,... | collective-permute-start | bytes 393224 | tf_op jit(solution)/shard_map/ppermute | solution.py:28
  6.8 0.9 copy-start.1
  7.7 8.4 %collective-permute-start.5 = (bf16[256,256]{1,0:T(8,128)(2,1)S(1)}, bf16[256,256]{1,0:T(8,128)(2,1)S(1)}, u32[]{:S(2)}, u32[]{:S(2)}) collective-permute-start(bf16[256,256]{1,0:T(8,128)(2,1)S(1)} %join_0.3.first), channel_id=1, source_target_pairs={{0,192},{1,193},{2,194},{3,195},{4,196},{5,197},{6,198},{7,199},{8... | collective-permute-start | bytes 393224 | tf_op jit(solution)/shard_map/ppermute | solution.py:28
  10.0 9.2 %collective-permute-start.1 = (bf16[256,256]{1,0:T(8,128)(2,1)S(1)}, bf16[256,256]{1,0:T(8,128)(2,1)S(1)}, u32[]{:S(2)}, u32[]{:S(2)}) collective-permute-start(bf16[256,256]{1,0:T(8,128)(2,1)S(1)} %join_0.2.first), channel_id=1, source_target_pairs={{0,48},{1,49},{2,50},{3,51},{4,52},{5,53},{6,54},{7,55},{8,24},{9,... | collective-permute-start | bytes 393224 | tf_op jit(solution)/shard_map/ppermute | solution.py:28
  19.2 6.5 %collective-permute-start.2 = (bf16[512,256]{1,0:T(8,128)(2,1)S(1)}, bf16[512,256]{1,0:T(8,128)(2,1)S(1)}, u32[]{:S(2)}, u32[]{:S(2)}) collective-permute-start(bf16[512,256]{1,0:T(8,128)(2,1)S(1)} %join_1.2.first), channel_id=1, source_target_pairs={{0,64},{1,65},{2,66},{3,67},{4,68},{5,69},{6,70},{7,71},{8,200},{9... | collective-permute-start | bytes 786440 | tf_op jit(solution)/shard_map/ppermute | solution.py:28
  19.9 8.6 %collective-permute-start.6 = (bf16[512,256]{1,0:T(8,128)(2,1)S(1)}, bf16[512,256]{1,0:T(8,128)(2,1)S(1)}, u32[]{:S(2)}, u32[]{:S(2)}) collective-permute-start(bf16[512,256]{1,0:T(8,128)(2,1)S(1)} %join_1.3.first), channel_id=1, source_target_pairs={{0,16},{1,17},{2,18},{3,19},{4,20},{5,21},{6,22},{7,23},{8,56},{9,... | collective-permute-start | bytes 786440 | tf_op jit(solution)/shard_map/ppermute | solution.py:28
  25.7 17.1 %collective-permute-start.8 = (bf16[1024,256]{1,0:T(8,128)(2,1)S(1)}, bf16[1024,256]{1,0:T(8,128)(2,1)S(1)}, u32[]{:S(2)}, u32[]{:S(2)}) collective-permute-start(bf16[1024,256]{1,0:T(8,128)(2,1)S(1)} %join_2.2.refs_0_), channel_id=1, source_target_pairs={{0,8},{1,9},{2,10},{3,11},{4,12},{5,13},{6,14},{7,15},{8,0},{9,1},... | collective-permute-start | bytes 1572872 | tf_op jit(solution)/shard_map/ppermute | solution.py:33
  28.5 14.3 %collective-permute-start.9 = (bf16[1024,256]{1,0:T(8,128)(2,1)S(1)}, bf16[1024,256]{1,0:T(8,128)(2,1)S(1)}, u32[]{:S(2)}, u32[]{:S(2)}) collective-permute-start(bf16[1024,256]{1,0:T(8,128)(2,1)S(1)} %join_2.3.refs_1_), channel_id=1, source_target_pairs={{0,8},{1,9},{2,10},{3,11},{4,12},{5,13},{6,14},{7,15},{8,0},{9,1},... | collective-permute-start | bytes 1572872 | tf_op jit(solution)/shard_map/ppermute | solution.py:33
  28.6 16.5 %collective-permute-start.3 = (bf16[1024,256]{1,0:T(8,128)(2,1)S(1)}, bf16[1024,256]{1,0:T(8,128)(2,1)S(1)}, u32[]{:S(2)}, u32[]{:S(2)}) collective-permute-start(bf16[1024,256]{1,0:T(8,128)(2,1)S(1)} %join_2.2.refs_0_), channel_id=1, source_target_pairs={{0,192},{1,193},{2,194},{3,195},{4,196},{5,197},{6,198},{7,199},{8... | collective-permute-start | bytes 1572872 | tf_op jit(solution)/shard_map/ppermute | solution.py:28
  31.1 17.9 %collective-permute-start.7 = (bf16[1024,256]{1,0:T(8,128)(2,1)S(1)}, bf16[1024,256]{1,0:T(8,128)(2,1)}, u32[]{:S(2)}, u32[]{:S(2)}) collective-permute-start(bf16[1024,256]{1,0:T(8,128)(2,1)S(1)} %join_2.3.refs_1_), channel_id=1, source_target_pairs={{0,48},{1,49},{2,50},{3,51},{4,52},{5,53},{6,54},{7,55},{8,24},{9,... | collective-permute-start | bytes 1572872 | tf_op jit(solution)/shard_map/ppermute | solution.py:28
  49.1 2.8 %collective-permute-start.10 = (bf16[1024,256]{1,0:T(8,128)(2,1)S(1)}, bf16[1024,256]{1,0:T(8,128)(2,1)S(1)}, u32[]{:S(2)}, u32[]{:S(2)}) collective-permute-start(bf16[1024,256]{1,0:T(8,128)(2,1)S(1)} %collective-permute-done.3.refs_0_), channel_id=1, source_target_pairs={{0,8},{1,9},{2,10},{3,11},{4,12},{5,13},{6,14},{7,15},{8,0},{9,1},... | collective-permute-start | bytes 1572872 | tf_op jit(solution)/shard_map/ppermute | solution.py:33
  49.1 2.9 %collective-permute-start.11 = (bf16[1024,256]{1,0:T(8,128)(2,1)}, bf16[1024,256]{1,0:T(8,128)(2,1)S(1)}, u32[]{:S(2)}, u32[]{:S(2)}) collective-permute-start(bf16[1024,256]{1,0:T(8,128)(2,1)} %collective-permute-done.7.refs_1_), channel_id=1, source_target_pairs={{0,8},{1,9},{2,10},{3,11},{4,12},{5,13},{6,14},{7,15},{8,0},{9,1},... | collective-permute-start | bytes 1572872 | tf_op jit(solution)/shard_map/ppermute | solution.py:33
  51.9 21.7 %copy-start.2 = (bf16[512,512]{1,0:T(8,128)(2,1)S(1)}, bf16[512,512]{1,0:T(8,128)(2,1)}, u32[]{:S(2)}) copy-start(bf16[512,512]{1,0:T(8,128)(2,1)} %w_neigh.1) | copy-start | bytes 1572868
  51.9 21.7 %copy-start.3 = (bf16[128,512]{1,0:T(8,128)(2,1)S(1)}, bf16[128,512]{1,0:T(8,128)(2,1)}, u32[]{:S(2)}) copy-start(bf16[128,512]{1,0:T(8,128)(2,1)} %cotangent.1) | copy-start | bytes 393220
  93.7 3.1 %collective-permute-start.12 = (bf16[320,1024]{1,0:T(8,128)(2,1)S(1)}, bf16[320,1024]{1,0:T(8,128)(2,1)S(1)}, u32[]{:S(2)}, u32[]{:S(2)}) collective-permute-start(bf16[320,1024]{1,0:T(8,128)(2,1)S(1)} %get-tuple-element.59), channel_id=1, source_target_pairs={{0,8},{1,9},{2,10},{3,11},{4,12},{5,13},{6,14},{7,15},{8,0},{9,1},... | collective-permute-start | bytes 1966088 | tf_op jit(solution)/shard_map/ppermute | solution.py:33
  93.8 3.0 %collective-permute-start.13 = (bf16[192,1024]{1,0:T(8,128)(2,1)S(1)}, bf16[192,1024]{1,0:T(8,128)(2,1)S(1)}, u32[]{:S(2)}, u32[]{:S(2)}) collective-permute-start(bf16[192,1024]{1,0:T(8,128)(2,1)S(1)} %get-tuple-element.60), channel_id=1, source_target_pairs={{0,8},{1,9},{2,10},{3,11},{4,12},{5,13},{6,14},{7,15},{8,0},{9,1},... | collective-permute-start | bytes 1179656 | tf_op jit(solution)/shard_map/ppermute | solution.py:33
  97.0 11.9 %collective-permute-start.14 = (bf16[320,1024]{1,0:T(8,128)(2,1)S(1)}, bf16[320,1024]{1,0:T(8,128)(2,1)S(1)}, u32[]{:S(2)}, u32[]{:S(2)}) collective-permute-start(bf16[320,1024]{1,0:T(8,128)(2,1)S(1)} %pair_sum.2), channel_id=1, source_target_pairs={{0,192},{1,193},{2,194},{3,195},{4,196},{5,197},{6,198},{7,199},{8... | collective-permute-start | bytes 1966088 | tf_op jit(solution)/shard_map/ppermute | solution.py:28
  98.1 10.7 %collective-permute-start.15 = (bf16[320,1024]{1,0:T(8,128)(2,1)S(1)}, bf16[320,1024]{1,0:T(8,128)(2,1)S(1)}, u32[]{:S(2)}, u32[]{:S(2)}) collective-permute-start(bf16[320,1024]{1,0:T(8,128)(2,1)S(1)} %get-tuple-element.73), channel_id=1, source_target_pairs={{0,8},{1,9},{2,10},{3,11},{4,12},{5,13},{6,14},{7,15},{8,0},{9,1},... | collective-permute-start | bytes 1966088 | tf_op jit(solution)/shard_map/ppermute | solution.py:33
  98.2 14.2 %collective-permute-start.19 = (bf16[192,1024]{1,0:T(8,128)(2,1)S(1)}, bf16[192,1024]{1,0:T(8,128)(2,1)S(1)}, u32[]{:S(2)}, u32[]{:S(2)}) collective-permute-start(bf16[192,1024]{1,0:T(8,128)(2,1)S(1)} %pair_sum.3), channel_id=1, source_target_pairs={{0,48},{1,49},{2,50},{3,51},{4,52},{5,53},{6,54},{7,55},{8,24},{9,... | collective-permute-start | bytes 1179656 | tf_op jit(solution)/shard_map/ppermute | solution.py:28
  101.8 10.7 %collective-permute-start.18 = (bf16[192,1024]{1,0:T(8,128)(2,1)S(1)}, bf16[192,1024]{1,0:T(8,128)(2,1)S(1)}, u32[]{:S(2)}, u32[]{:S(2)}) collective-permute-start(bf16[192,1024]{1,0:T(8,128)(2,1)S(1)} %get-tuple-element.81), channel_id=1, source_target_pairs={{0,8},{1,9},{2,10},{3,11},{4,12},{5,13},{6,14},{7,15},{8,0},{9,1},... | collective-permute-start | bytes 1179656 | tf_op jit(solution)/shard_map/ppermute | solution.py:33
  109.1 7.2 %collective-permute-start.16 = (bf16[320,512]{1,0:T(8,128)(2,1)S(1)}, bf16[320,512]{1,0:T(8,128)(2,1)S(1)}, u32[]{:S(2)}, u32[]{:S(2)}) collective-permute-start(bf16[320,512]{1,0:T(8,128)(2,1)S(1)} %get-tuple-element.76), channel_id=1, source_target_pairs={{0,64},{1,65},{2,66},{3,67},{4,68},{5,69},{6,70},{7,71},{8,200},{9... | collective-permute-start | bytes 983048 | tf_op jit(solution)/shard_map/ppermute | solution.py:28
  112.6 8.8 %collective-permute-start.20 = (bf16[192,512]{1,0:T(8,128)(2,1)S(1)}, bf16[192,512]{1,0:T(8,128)(2,1)S(1)}, u32[]{:S(2)}, u32[]{:S(2)}) collective-permute-start(bf16[192,512]{1,0:T(8,128)(2,1)S(1)} %get-tuple-element.85), channel_id=1, source_target_pairs={{0,16},{1,17},{2,18},{3,19},{4,20},{5,21},{6,22},{7,23},{8,56},{9,... | collective-permute-start | bytes 589832 | tf_op jit(solution)/shard_map/ppermute | solution.py:28
  116.3 9.4 %collective-permute-start.17 = (bf16[320,256]{1,0:T(8,128)(2,1)S(1)}, bf16[320,256]{1,0:T(8,128)(2,1)S(1)}, u32[]{:S(2)}, u32[]{:S(2)}) collective-permute-start(bf16[320,256]{1,0:T(8,128)(2,1)S(1)} %get-tuple-element.78), channel_id=1, source_target_pairs={{0,48},{1,49},{2,50},{3,51},{4,52},{5,53},{6,54},{7,55},{8,24},{9,... | collective-permute-start | bytes 491528 | tf_op jit(solution)/shard_map/ppermute | solution.py:28
  121.4 7.3 %collective-permute-start.21 = (bf16[192,256]{1,0:T(8,128)(2,1)S(1)}, bf16[192,256]{1,0:T(8,128)(2,1)S(1)}, u32[]{:S(2)}, u32[]{:S(2)}) collective-permute-start(bf16[192,256]{1,0:T(8,128)(2,1)S(1)} %get-tuple-element.86), channel_id=1, source_target_pairs={{0,192},{1,193},{2,194},{3,195},{4,196},{5,197},{6,198},{7,199},{8... | collective-permute-start | bytes 294920 | tf_op jit(solution)/shard_map/ppermute | solution.py:28
  128.8 4.2 %collective-permute-start.23 = (bf16[192,128]{1,0:T(8,128)(2,1)S(1)}, bf16[192,128]{1,0:T(8,128)(2,1)S(1)}, u32[]{:S(2)}, u32[]{:S(2)}) collective-permute-start(bf16[192,128]{1,0:T(8,128)(2,1)S(1)} %get-tuple-element.92), channel_id=1, source_target_pairs={{0,64},{1,65},{2,66},{3,67},{4,68},{5,69},{6,70},{7,71},{8,200},{9... | collective-permute-start | bytes 147464 | tf_op jit(solution)/shard_map/ppermute | solution.py:28
  128.9 5.5 %collective-permute-start.22 = (bf16[320,128]{1,0:T(8,128)(2,1)S(1)}, bf16[320,128]{1,0:T(8,128)(2,1)S(1)}, u32[]{:S(2)}, u32[]{:S(2)}) collective-permute-start(bf16[320,128]{1,0:T(8,128)(2,1)S(1)} %get-tuple-element.88), channel_id=1, source_target_pairs={{0,16},{1,17},{2,18},{3,19},{4,20},{5,21},{6,22},{7,23},{8,56},{9,... | collective-permute-start | bytes 245768 | tf_op jit(solution)/shard_map/ppermute | solution.py:28

commit v10 on v4

--- a/solution.py
+++ b/solution.py
@@ -25,7 +25,7 @@
     return lax.ppermute(value, ("row", "col"), pairs)
 
 
-def in_vmem(kernel, results, operands, name, flops=MB, grant=16, **extra):
+def in_vmem(kernel, results, operands, name, flops=MB, grant=8, **extra):
     spec = pl.BlockSpec(memory_space=pltpu.VMEM)
     outs = [shape if plain else pltpu.VMEM(shape.shape, shape.dtype) for shape, plain in results]
     out_specs = [pl.BlockSpec() if plain else spec for _, plain in results]
@@ -75,7 +75,7 @@
             scratch_shapes=[pltpu.VMEM(masks.shape, masks.dtype), pltpu.SemaphoreType.DMA((count,))],
         ),
         out_shape=pltpu.VMEM((NCOL * TILE, count * TILE), BF16),
-        compiler_params=pltpu.CompilerParams(vmem_limit_bytes=16 * MB),
+        compiler_params=pltpu.CompilerParams(vmem_limit_bytes=8 * MB),
         cost_estimate=pl.CostEstimate(flops=0, bytes_accessed=14 * MB, transcendentals=0),
         name="adjacency",
     )(place, where, pltpu.with_memory_space_constraint(masks, pltpu.HBM))
@@ -131,24 +131,28 @@
     return in_vmem(node_kernel, results, operands, "node_step", 4 * rows * width * width)
 
 
-def spread_kernel(core, parts, adj, keep, send):
-    lhs = jnp.concatenate([parts[i] for i in range(NCOL)], axis=1)
-    half = lhs.shape[0] // 2
+def spread_kernel(core, pick, parts, adj, out):
     depth = NZH * TILE
-    for dy in range(NY):
-        at = (core * NY + dy) * depth
-        value = jnp.dot(lhs, adj[:, at : at + depth], preferred_element_type=F32).astype(BF16)
-        for h, (k1, k2) in enumerate(STEPS):
-            out, order = (keep, (0, k1)) if dy in (0, k1) else (send, (k2, k1 ^ k2))
-            to = order.index(dy) * depth
-            out[h, :, to : to + depth] = value[h * half : (h + 1) * half, :]
-
-
-def spread_matmul(parts, adj, core, name):
-    width = parts.shape[1]
-    shape = (2, width // 2, 2 * NZH * TILE)
-    flops = 2 * adj.shape[0] * width * CHIPS * TILE
-    return in_vmem(functools.partial(spread_kernel, core), [kept(shape, BF16)] * 2, (parts, adj), name, flops)
+    half = out.shape[1]
+    for h, steps in enumerate(STEPS):
+        lhs = jnp.concatenate([parts[i, h * half : (h + 1) * half, :] for i in range(NCOL)], axis=1)
+        for n, dy in enumerate(pick(*steps)):
+            at = (core * NY + dy) * depth
+            value = jnp.dot(lhs, adj[:, at : at + depth], preferred_element_type=F32)
+            out[h, :, n * depth : (n + 1) * depth] = value.astype(BF16)
+
+
+def spread_matmul(parts, adj, core, pick, name):
+    shape = (2, parts.shape[1] // 2, 2 * NZH * TILE)
+    return in_vmem(functools.partial(spread_kernel, core, pick), [kept(shape, BF16)], (parts, adj), name)[0]
+
+
+def goes(k1, k2):
+    return k2, k1 ^ k2
+
+
+def stays(k1, k2):
+    return 0, k1
 
 
 def total(refs):
@@ -228,7 +232,7 @@
     first, second = [(0, k1) for k1, _ in STEPS], [(k2, k1 ^ k2) for k1, k2 in STEPS]
     near = near + [flip(v, core=1) for v in near]
     part = gather_matmul(adj, near, (0, 1), first, None, F32, "gather_near")
-    *far, part = lax.optimization_barrier((*far, part))
+    far[0], part = lax.optimization_barrier((far[0], part))
     other = [flip(v, core=1) for v in far]
     part = gather_matmul(adj, far, (0,), second, part, F32, "gather_far")
     *other, part = lax.optimization_barrier((*other, part))
@@ -239,12 +243,17 @@
 
     table = lax.all_to_all(scaled_t, "col", 0, 0, tiled=True)
     own = lax.dot_general(grad_pre, w_self, (((1,), (1,)), ((), ())), preferred_element_type=F32)
-    keep_out, send_out = spread_matmul(table, adj, 1, "spread_other")
-    send_in, keep_in = flip(send_out, core=1), flip(keep_out, core=1)
-    keep, send = spread_matmul(table, adj, 0, "spread_own")
+    send_in = flip(spread_matmul(table, adj, 1, goes, "spread_go_other"), core=1)
+    send = spread_matmul(table, adj, 0, goes, "spread_go")
+    keep_out = spread_matmul(table, adj, 1, stays, "spread_stay_other")
+    send_in, send, keep_out = lax.optimization_barrier((send_in, send, keep_out))
+    sums = list(both_halves(send, send_in))
+    sums[0], table = lax.optimization_barrier((sums[0], table))
+    keep_in = flip(keep_out, core=1)
+    keep = spread_matmul(table, adj, 0, stays, "spread_stay")
 
     ends = []
-    for h, (value, (k1, k2)) in enumerate(zip(both_halves(send, send_in), STEPS)):
+    for h, (value, (k1, k2)) in enumerate(zip(sums, STEPS)):
         got = flip(value, y=k2)
         stay, go = first_split(h, keep, keep_in, got, "add_y1")
         got = flip(go, y=k1)

time: 135 us -> 134 us (level)
    pallas_call x14 -> x16, Pallas kernels: 12.2 us -> 12.5 us  [in_vmem(): pl.pallas_call(kernel, in_specs=[spec] * len(operands), out_specs=out_spe...]
  transfers between devices with their start and end apart: 22 -> 22, of which waited for: 10 -> 11; matrix products, arithmetic and copies ran while one was open for 2% -> 2% of each run, Pallas kernels for 9% -> 10%
where the time goes in v10:
time: 134 us; the launch traced here: 133 us
  waiting for transfers between devices  40.3 us (30%)
  blocking collectives  38.1 us (28%)
  starting transfers between devices  32 us (24%)
  Pallas kernels  18 us (13%)
  local copies, waits for them, and re-layouts  1.89 us (1%)
    ppermute x22, waiting for transfers between devices, flip(): return lax.ppermute(value, ('row', 'col'), pairs)  40.3 us
    ppermute x22, starting transfers between devices, flip(): return lax.ppermute(value, ('row', 'col'), pairs)  32 us
    all_to_all x1, blocking collectives, body(): arrived = lax.all_to_all(summed, 'col', 0, 0, tiled=True)  20.4 us
    all_to_all x1, blocking collectives, body(): table = lax.all_to_all(scaled_t, 'col', 0, 0, tiled=True)  17.7 us
    pallas_call x16, Pallas kernels, in_vmem(): pl.pallas_call(kernel, in_specs=[spec] * len(operands), out_specs=out_spe...  12.5 us
    pallas_call x1, Pallas kernels, adjacency(): pl.pallas_call(adjacency_kernel, grid_spec=pltpu.PrefetchScalarGridSpec(n...  5.55 us
  transfers between devices with their start and end apart: 22, of which 11 were waited for; matrix products, arithmetic and copies ran while one was open for 2% of the time, Pallas kernels for 10%

profile of v10, /device:TPU:32, one launch (start us, length us, event | category | flops | bytes accessed | tf_op | source)
XLA Modules:
  0.0 132.6 jit_solution(2870621795640364555)
XLA Ops:
  0.6 0.9 constant_dynamic-update-slice_fusion.4
  1.6 3.4 %collective-permute-start = (bf16[128,256]{1,0:T(8,128)(2,1)S(1)}, bf16[128,256]{1,0:T(8,128)(2,1)S(1)}, u32[]{:S(2)}, u32[]{:S(2)}) collective-permute-start(bf16[128,256]{1,0:T(8,128)(2,1)S(1)} %get-tuple-element.70), channel_id=1, source_target_pairs={{0,16},{1,17},{2,18},{3,19},{4,20},{5,21},{6,22},{7,23},{8,24},{9,... | collective-permute-start | bytes 196616 | tf_op jit(solution)/shard_map/ppermute | solution.py:25
  4.9 3.6 %collective-permute-start.3 = (bf16[128,256]{1,0:T(8,128)(2,1)S(1)}, bf16[128,256]{1,0:T(8,128)(2,1)S(1)}, u32[]{:S(2)}, u32[]{:S(2)}) collective-permute-start(bf16[128,256]{1,0:T(8,128)(2,1)S(1)} %get-tuple-element.71), channel_id=1, source_target_pairs={{0,48},{1,49},{2,50},{3,51},{4,52},{5,53},{6,54},{7,55},{8,56},{9,... | collective-permute-start | bytes 196616 | tf_op jit(solution)/shard_map/ppermute | solution.py:25
  9.2 4.1 %collective-permute-start.1 = (bf16[256,256]{1,0:T(8,128)(2,1)S(1)}, bf16[256,256]{1,0:T(8,128)(2,1)S(1)}, u32[]{:S(2)}, u32[]{:S(2)}) collective-permute-start(bf16[256,256]{1,0:T(8,128)(2,1)S(1)} %pad_maximum_fusion.3), channel_id=1, source_target_pairs={{0,48},{1,49},{2,50},{3,51},{4,52},{5,53},{6,54},{7,55},{8,56},{9,... | collective-permute-start | bytes 393224 | tf_op jit(solution)/shard_map/ppermute | solution.py:25
  13.9 5.0 %collective-permute-done.1 = bf16[256,256]{1,0:T(8,128)(2,1)S(1)} collective-permute-done((bf16[256,256]{1,0:T(8,128)(2,1)S(1)}, bf16[256,256]{1,0:T(8,128)(2,1)S(1)}, u32[]{:S(2)}, u32[]{:S(2)}) %collective-permute-start.1) | collective-permute-done | bytes 131104 | tf_op jit(solution)/shard_map/ppermute | solution.py:25
  18.9 1.7 %collective-permute-start.2 = (bf16[512,256]{1,0:T(8,128)(2,1)S(1)}, bf16[512,256]{1,0:T(8,128)(2,1)S(1)}, u32[]{:S(2)}, u32[]{:S(2)}) collective-permute-start(bf16[512,256]{1,0:T(8,128)(2,1)S(1)} %pad_maximum_fusion.1), channel_id=1, source_target_pairs={{0,64},{1,65},{2,66},{3,67},{4,68},{5,69},{6,70},{7,71},{8,72},{9,... | collective-permute-start | bytes 786440 | tf_op jit(solution)/shard_map/ppermute | solution.py:25
  20.6 2.9 %collective-permute-start.5 = (bf16[512,256]{1,0:T(8,128)(2,1)S(1)}, bf16[512,256]{1,0:T(8,128)(2,1)S(1)}, u32[]{:S(2)}, u32[]{:S(2)}) collective-permute-start(bf16[512,256]{1,0:T(8,128)(2,1)S(1)} %pad_maximum_fusion.2), channel_id=1, source_target_pairs={{0,192},{1,193},{2,194},{3,195},{4,196},{5,197},{6,198},{7,199},{8... | collective-permute-start | bytes 786440 | tf_op jit(solution)/shard_map/ppermute | solution.py:25
  23.5 0.8 copy.11
  24.4 5.5 %adjacency.1.adj = bf16[1024,4096]{1,0:T(8,128)(2,1)S(1)} custom-call(s32[32]{0:T(128)S(1)} %fusion.1.place, s32[96]{0:T(128)S(1)} %reshape_squeeze.3.where, s32[32,3,128,128]{3,2,1,0:T(8,128)} %bitcast.13), custom_call_target="tpu_custom_call" | custom-call | bytes 14680064 | tf_op jit(solution)/shard_map/adjacency/pallas_call | solution.py:68
  31.0 1.3 collective-permute-start.6
  33.0 2.3 %gather_near.1.refs_2_ = f32[1024,512]{1,0:T(8,128)S(1)} custom-call(bf16[1024,4096]{1,0:T(8,128)(2,1)S(1)} %adjacency.1.adj, bf16[1024,256]{1,0:T(8,128)(2,1)S(1)} %constant_dynamic-update-slice_fusion.refs_0_, bf16[1024,256]{1,0:T(8,128)(2,1)S(1)} %pad_maximum_fusion.refs_1_, bf16[1024,256]{1,0:T(8,128)(2,1)S(1)} %collective-permute-done.7.refs_2_, ...), custom_call_target="tpu_custom_call" | custom-call | flops 2147483648 | bytes 3145728 | tf_op jit(solution)/shard_map/gather_near/pallas_call | solution.py:32
  35.3 10.8 %collective-permute-done.6.refs_0_ = bf16[1024,256]{1,0:T(8,128)(2,1)S(1)} collective-permute-done((bf16[1024,256]{1,0:T(8,128)(2,1)S(1)}, bf16[1024,256]{1,0:T(8,128)(2,1)S(1)}, u32[]{:S(2)}, u32[]{:S(2)}) %collective-permute-start.6) | collective-permute-done | bytes 524320 | tf_op jit(solution)/shard_map/ppermute | solution.py:25
  46.6 1.2 gather_far.1.refs_2_
  48.8 1.2 gather_far_other.1
  50.0 20.4 %all_to_all.16 = bf16[8,128,512]{2,1,0:T(8,128)(2,1)S(1)} all-to-all(bf16[8,128,512]{2,1,0:T(8,128)(2,1)S(1)} %bitcast.11), channel_id=1, replica_groups=mesh['row'=32,'col'=8] {'col'}, dimensions={0} | all-to-all | bytes 2097152 | tf_op jit(solution)/shard_map/all_to_all | solution.py:241
  70.4 1.1 node_step.1
  71.5 17.7 %all_to_all.17.parts = bf16[8,512,128]{2,1,0:T(8,128)(2,1)S(1)} all-to-all(bf16[8,512,128]{2,1,0:T(8,128)(2,1)S(1)} %get-tuple-element.45), channel_id=1, replica_groups=mesh['row'=32,'col'=8] {'col'}, dimensions={0} | all-to-all | bytes 2097152 | tf_op jit(solution)/shard_map/all_to_all | solution.py:244
  89.3 1.2 spread_go_other.1
  90.6 1.2 spread_stay_other.1
  91.9 1.2 spread_go.1.mine
  94.1 1.4 %collective-permute-start.14 = (bf16[256,1024]{1,0:T(8,128)(2,1)S(1)}, bf16[256,1024]{1,0:T(8,128)(2,1)S(1)}, u32[]{:S(2)}, u32[]{:S(2)}) collective-permute-start(bf16[256,1024]{1,0:T(8,128)(2,1)S(1)} %get-tuple-element.51), channel_id=1, source_target_pairs={{0,192},{1,193},{2,194},{3,195},{4,196},{5,197},{6,198},{7,199},{8... | collective-permute-start | bytes 1572872 | tf_op jit(solution)/shard_map/ppermute | solution.py:25
  95.4 1.2 spread_stay.1.mine
  96.7 11.2 %collective-permute-done.18.got = bf16[256,1024]{1,0:T(8,128)(2,1)S(1)} collective-permute-done((bf16[256,1024]{1,0:T(8,128)(2,1)S(1)}, bf16[256,1024]{1,0:T(8,128)(2,1)S(1)}, u32[]{:S(2)}, u32[]{:S(2)}) %collective-permute-start.18) | collective-permute-done | bytes 524320 | tf_op jit(solution)/shard_map/ppermute | solution.py:25
  108.1 1.4 %collective-permute-start.19 = (bf16[256,512]{1,0:T(8,128)(2,1)S(1)}, bf16[256,512]{1,0:T(8,128)(2,1)S(1)}, u32[]{:S(2)}, u32[]{:S(2)}) collective-permute-start(bf16[256,512]{1,0:T(8,128)(2,1)S(1)} %get-tuple-element.60), channel_id=1, source_target_pairs={{0,192},{1,193},{2,194},{3,195},{4,196},{5,197},{6,198},{7,199},{8... | collective-permute-start | bytes 786440 | tf_op jit(solution)/shard_map/ppermute | solution.py:25
  109.9 6.9 %collective-permute-done.19.refs_1_ = bf16[256,512]{1,0:T(8,128)(2,1)S(1)} collective-permute-done((bf16[256,512]{1,0:T(8,128)(2,1)S(1)}, bf16[256,512]{1,0:T(8,128)(2,1)S(1)}, u32[]{:S(2)}, u32[]{:S(2)}) %collective-permute-start.19) | collective-permute-done | bytes 262176 | tf_op jit(solution)/shard_map/ppermute | solution.py:25
  116.9 1.3 collective-permute-start.20
  118.3 2.9 %collective-permute-start.16 = (bf16[256,256]{1,0:T(8,128)(2,1)S(1)}, bf16[256,256]{1,0:T(8,128)(2,1)S(1)}, u32[]{:S(2)}, u32[]{:S(2)}) collective-permute-start(bf16[256,256]{1,0:T(8,128)(2,1)S(1)} %get-tuple-element.55), channel_id=1, source_target_pairs={{0,48},{1,49},{2,50},{3,51},{4,52},{5,53},{6,54},{7,55},{8,56},{9,... | collective-permute-start | bytes 393224 | tf_op jit(solution)/shard_map/ppermute | solution.py:25
  121.2 2.1 %collective-permute-done.20.refs_1_ = bf16[256,256]{1,0:T(8,128)(2,1)S(1)} collective-permute-done((bf16[256,256]{1,0:T(8,128)(2,1)S(1)}, bf16[256,256]{1,0:T(8,128)(2,1)S(1)}, u32[]{:S(2)}, u32[]{:S(2)}) %collective-permute-start.20) | collective-permute-done | bytes 131104 | tf_op jit(solution)/shard_map/ppermute | solution.py:25
  123.3 3.1 %collective-permute-start.21 = (bf16[256,128]{1,0:T(8,128)(2,1)S(1)}, bf16[256,128]{1,0:T(8,128)(2,1)S(1)}, u32[]{:S(2)}, u32[]{:S(2)}) collective-permute-start(bf16[256,128]{1,0:T(8,128)(2,1)S(1)} %get-tuple-element.64), channel_id=1, source_target_pairs={{0,48},{1,49},{2,50},{3,51},{4,52},{5,53},{6,54},{7,55},{8,56},{9,... | collective-permute-start | bytes 196616 | tf_op jit(solution)/shard_map/ppermute | solution.py:25
  126.4 2.5 %collective-permute-start.17 = (bf16[256,128]{1,0:T(8,128)(2,1)S(1)}, bf16[256,128]{1,0:T(8,128)(2,1)S(1)}, u32[]{:S(2)}, u32[]{:S(2)}) collective-permute-start(bf16[256,128]{1,0:T(8,128)(2,1)S(1)} %get-tuple-element.57), channel_id=1, source_target_pairs={{0,16},{1,17},{2,18},{3,19},{4,20},{5,21},{6,22},{7,23},{8,24},{9,... | collective-permute-start | bytes 196616 | tf_op jit(solution)/shard_map/ppermute | solution.py:25
  129.8 2.0 %collective-permute-done.17.refs_1_ = bf16[256,128]{1,0:T(8,128)(2,1)S(1)} collective-permute-done((bf16[256,128]{1,0:T(8,128)(2,1)S(1)}, bf16[256,128]{1,0:T(8,128)(2,1)S(1)}, u32[]{:S(2)}, u32[]{:S(2)}) %collective-permute-start.17) | collective-permute-done | bytes 65568 | tf_op jit(solution)/shard_map/ppermute | solution.py:25
  131.8 0.8 last_sum.1
  (57 shorter events, 7.2 us)
Async XLA Ops:
  0.6 29.3 %copy-start = (bf16[512,512]{1,0:T(8,128)(2,1)S(1)}, bf16[512,512]{1,0:T(8,128)(2,1)}, u32[]{:S(2)}) copy-start(bf16[512,512]{1,0:T(8,128)(2,1)} %param.12) | copy-start | bytes 1572868
  1.6 7.6 %collective-permute-start = (bf16[128,256]{1,0:T(8,128)(2,1)S(1)}, bf16[128,256]{1,0:T(8,128)(2,1)S(1)}, u32[]{:S(2)}, u32[]{:S(2)}) collective-permute-start(bf16[128,256]{1,0:T(8,128)(2,1)S(1)} %get-tuple-element.70), channel_id=1, source_target_pairs={{0,16},{1,17},{2,18},{3,19},{4,20},{5,21},{6,22},{7,23},{8,24},{9,... | collective-permute-start | bytes 196616 | tf_op jit(solution)/shard_map/ppermute | solution.py:25
  4.9 8.4 %collective-permute-start.3 = (bf16[128,256]{1,0:T(8,128)(2,1)S(1)}, bf16[128,256]{1,0:T(8,128)(2,1)S(1)}, u32[]{:S(2)}, u32[]{:S(2)}) collective-permute-start(bf16[128,256]{1,0:T(8,128)(2,1)S(1)} %get-tuple-element.71), channel_id=1, source_target_pairs={{0,48},{1,49},{2,50},{3,51},{4,52},{5,53},{6,54},{7,55},{8,56},{9,... | collective-permute-start | bytes 196616 | tf_op jit(solution)/shard_map/ppermute | solution.py:25
  9.2 9.7 %collective-permute-start.1 = (bf16[256,256]{1,0:T(8,128)(2,1)S(1)}, bf16[256,256]{1,0:T(8,128)(2,1)S(1)}, u32[]{:S(2)}, u32[]{:S(2)}) collective-permute-start(bf16[256,256]{1,0:T(8,128)(2,1)S(1)} %pad_maximum_fusion.3), channel_id=1, source_target_pairs={{0,48},{1,49},{2,50},{3,51},{4,52},{5,53},{6,54},{7,55},{8,56},{9,... | collective-permute-start | bytes 393224 | tf_op jit(solution)/shard_map/ppermute | solution.py:25
  13.3 7.3 %collective-permute-start.4 = (bf16[256,256]{1,0:T(8,128)(2,1)S(1)}, bf16[256,256]{1,0:T(8,128)(2,1)S(1)}, u32[]{:S(2)}, u32[]{:S(2)}) collective-permute-start(bf16[256,256]{1,0:T(8,128)(2,1)S(1)} %pad_maximum_fusion.4), channel_id=1, source_target_pairs={{0,16},{1,17},{2,18},{3,19},{4,20},{5,21},{6,22},{7,23},{8,24},{9,... | collective-permute-start | bytes 393224 | tf_op jit(solution)/shard_map/ppermute | solution.py:25
  18.9 11.3 %collective-permute-start.2 = (bf16[512,256]{1,0:T(8,128)(2,1)S(1)}, bf16[512,256]{1,0:T(8,128)(2,1)S(1)}, u32[]{:S(2)}, u32[]{:S(2)}) collective-permute-start(bf16[512,256]{1,0:T(8,128)(2,1)S(1)} %pad_maximum_fusion.1), channel_id=1, source_target_pairs={{0,64},{1,65},{2,66},{3,67},{4,68},{5,69},{6,70},{7,71},{8,72},{9,... | collective-permute-start | bytes 786440 | tf_op jit(solution)/shard_map/ppermute | solution.py:25
  20.6 9.6 %collective-permute-start.5 = (bf16[512,256]{1,0:T(8,128)(2,1)S(1)}, bf16[512,256]{1,0:T(8,128)(2,1)S(1)}, u32[]{:S(2)}, u32[]{:S(2)}) collective-permute-start(bf16[512,256]{1,0:T(8,128)(2,1)S(1)} %pad_maximum_fusion.2), channel_id=1, source_target_pairs={{0,192},{1,193},{2,194},{3,195},{4,196},{5,197},{6,198},{7,199},{8... | collective-permute-start | bytes 786440 | tf_op jit(solution)/shard_map/ppermute | solution.py:25
  24.4 5.6 %copy-start.3 = (bf16[128,512]{1,0:T(8,128)(2,1)S(1)}, bf16[128,512]{1,0:T(8,128)(2,1)}, u32[]{:S(2)}) copy-start(bf16[128,512]{1,0:T(8,128)(2,1)} %param.8) | copy-start | bytes 393220
  24.4 5.6 %copy-start.4 = (f32[512]{0:T(512)S(1)}, f32[512]{0:T(512)}, u32[]{:S(2)}) copy-start(f32[512]{0:T(512)} %param.14) | copy-start | bytes 6148
  30.3 2.0 %collective-permute-start.7 = (bf16[1024,256]{1,0:T(8,128)(2,1)S(1)}, bf16[1024,256]{1,0:T(8,128)(2,1)S(1)}, u32[]{:S(2)}, u32[]{:S(2)}) collective-permute-start(bf16[1024,256]{1,0:T(8,128)(2,1)S(1)} %constant_dynamic-update-slice_fusion.refs_0_), channel_id=1, source_target_pairs={{0,8},{1,9},{2,10},{3,11},{4,12},{5,13},{6,14},{7,15},{8,0},{9,1},... | collective-permute-start | bytes 1572872 | tf_op jit(solution)/shard_map/ppermute | solution.py:25
  30.4 2.6 %collective-permute-start.8 = (bf16[1024,256]{1,0:T(8,128)(2,1)S(1)}, bf16[1024,256]{1,0:T(8,128)(2,1)S(1)}, u32[]{:S(2)}, u32[]{:S(2)}) collective-permute-start(bf16[1024,256]{1,0:T(8,128)(2,1)S(1)} %pad_maximum_fusion.refs_1_), channel_id=1, source_target_pairs={{0,8},{1,9},{2,10},{3,11},{4,12},{5,13},{6,14},{7,15},{8,0},{9,1},... | collective-permute-start | bytes 1572872 | tf_op jit(solution)/shard_map/ppermute | solution.py:25
  31.0 15.1 %collective-permute-start.6 = (bf16[1024,256]{1,0:T(8,128)(2,1)S(1)}, bf16[1024,256]{1,0:T(8,128)(2,1)S(1)}, u32[]{:S(2)}, u32[]{:S(2)}) collective-permute-start(bf16[1024,256]{1,0:T(8,128)(2,1)S(1)} %constant_dynamic-update-slice_fusion.refs_0_), channel_id=1, source_target_pairs={{0,192},{1,193},{2,194},{3,195},{4,196},{5,197},{6,198},{7,199},{8... | collective-permute-start | bytes 1572872 | tf_op jit(solution)/shard_map/ppermute | solution.py:25
  32.3 13.8 %collective-permute-start.10 = (bf16[1024,256]{1,0:T(8,128)(2,1)S(1)}, bf16[1024,256]{1,0:T(8,128)(2,1)S(1)}, u32[]{:S(2)}, u32[]{:S(2)}) collective-permute-start(bf16[1024,256]{1,0:T(8,128)(2,1)S(1)} %pad_maximum_fusion.refs_1_), channel_id=1, source_target_pairs={{0,64},{1,65},{2,66},{3,67},{4,68},{5,69},{6,70},{7,71},{8,72},{9,... | collective-permute-start | bytes 1572872 | tf_op jit(solution)/shard_map/ppermute | solution.py:25
  46.1 1.9 %collective-permute-start.9 = (bf16[1024,256]{1,0:T(8,128)(2,1)S(1)}, bf16[1024,256]{1,0:T(8,128)(2,1)S(1)}, u32[]{:S(2)}, u32[]{:S(2)}) collective-permute-start(bf16[1024,256]{1,0:T(8,128)(2,1)S(1)} %collective-permute-done.6.refs_0_), channel_id=1, source_target_pairs={{0,8},{1,9},{2,10},{3,11},{4,12},{5,13},{6,14},{7,15},{8,0},{9,1},... | collective-permute-start | bytes 1572872 | tf_op jit(solution)/shard_map/ppermute | solution.py:25
  46.1 2.7 %collective-permute-start.11 = (bf16[1024,256]{1,0:T(8,128)(2,1)S(1)}, bf16[1024,256]{1,0:T(8,128)(2,1)S(1)}, u32[]{:S(2)}, u32[]{:S(2)}) collective-permute-start(bf16[1024,256]{1,0:T(8,128)(2,1)S(1)} %collective-permute-done.10.refs_1_), channel_id=1, source_target_pairs={{0,8},{1,9},{2,10},{3,11},{4,12},{5,13},{6,14},{7,15},{8,0},{9,1},... | collective-permute-start | bytes 1572872 | tf_op jit(solution)/shard_map/ppermute | solution.py:25
  47.9 22.5 %copy-start.1 = (bf16[512,512]{1,0:T(8,128)(2,1)S(1)}, bf16[512,512]{1,0:T(8,128)(2,1)}, u32[]{:S(2)}) copy-start(bf16[512,512]{1,0:T(8,128)(2,1)} %w_neigh.1) | copy-start | bytes 1572868
  47.9 22.5 %copy-start.2 = (bf16[128,512]{1,0:T(8,128)(2,1)S(1)}, bf16[128,512]{1,0:T(8,128)(2,1)}, u32[]{:S(2)}) copy-start(bf16[128,512]{1,0:T(8,128)(2,1)} %cotangent.1) | copy-start | bytes 393220
  90.5 2.7 %collective-permute-start.12 = (bf16[2,256,1024]{2,1,0:T(8,128)(2,1)S(1)}, bf16[2,256,1024]{2,1,0:T(8,128)(2,1)S(1)}, u32[]{:S(2)}, u32[]{:S(2)}) collective-permute-start(bf16[2,256,1024]{2,1,0:T(8,128)(2,1)S(1)} %spread_go_other.1), channel_id=1, source_target_pairs={{0,8},{1,9},{2,10},{3,11},{4,12},{5,13},{6,14},{7,15},{8,0},{9,1},... | collective-permute-start | bytes 3145736 | tf_op jit(solution)/shard_map/ppermute | solution.py:25
  93.3 14.7 %collective-permute-start.13 = (bf16[2,256,1024]{2,1,0:T(8,128)(2,1)S(1)}, bf16[2,256,1024]{2,1,0:T(8,128)(2,1)S(1)}, u32[]{:S(2)}, u32[]{:S(2)}) collective-permute-start(bf16[2,256,1024]{2,1,0:T(8,128)(2,1)S(1)} %spread_stay_other.1), channel_id=1, source_target_pairs={{0,8},{1,9},{2,10},{3,11},{4,12},{5,13},{6,14},{7,15},{8,0},{9,1},... | collective-permute-start | bytes 3145736 | tf_op jit(solution)/shard_map/ppermute | solution.py:25
  94.0 14.0 %collective-permute-start.18 = (bf16[256,1024]{1,0:T(8,128)(2,1)S(1)}, bf16[256,1024]{1,0:T(8,128)(2,1)S(1)}, u32[]{:S(2)}, u32[]{:S(2)}) collective-permute-start(bf16[256,1024]{1,0:T(8,128)(2,1)S(1)} %get-tuple-element.58), channel_id=1, source_target_pairs={{0,64},{1,65},{2,66},{3,67},{4,68},{5,69},{6,70},{7,71},{8,72},{9,... | collective-permute-start | bytes 1572872 | tf_op jit(solution)/shard_map/ppermute | solution.py:25
  94.1 15.4 %collective-permute-start.14 = (bf16[256,1024]{1,0:T(8,128)(2,1)S(1)}, bf16[256,1024]{1,0:T(8,128)(2,1)S(1)}, u32[]{:S(2)}, u32[]{:S(2)}) collective-permute-start(bf16[256,1024]{1,0:T(8,128)(2,1)S(1)} %get-tuple-element.51), channel_id=1, source_target_pairs={{0,192},{1,193},{2,194},{3,195},{4,196},{5,197},{6,198},{7,199},{8... | collective-permute-start | bytes 1572872 | tf_op jit(solution)/shard_map/ppermute | solution.py:25
  108.1 8.7 %collective-permute-start.19 = (bf16[256,512]{1,0:T(8,128)(2,1)S(1)}, bf16[256,512]{1,0:T(8,128)(2,1)S(1)}, u32[]{:S(2)}, u32[]{:S(2)}) collective-permute-start(bf16[256,512]{1,0:T(8,128)(2,1)S(1)} %get-tuple-element.60), channel_id=1, source_target_pairs={{0,192},{1,193},{2,194},{3,195},{4,196},{5,197},{6,198},{7,199},{8... | collective-permute-start | bytes 786440 | tf_op jit(solution)/shard_map/ppermute | solution.py:25
  109.7 8.5 %collective-permute-start.15 = (bf16[256,512]{1,0:T(8,128)(2,1)S(1)}, bf16[256,512]{1,0:T(8,128)(2,1)S(1)}, u32[]{:S(2)}, u32[]{:S(2)}) collective-permute-start(bf16[256,512]{1,0:T(8,128)(2,1)S(1)} %get-tuple-element.53), channel_id=1, source_target_pairs={{0,64},{1,65},{2,66},{3,67},{4,68},{5,69},{6,70},{7,71},{8,72},{9,... | collective-permute-start | bytes 786440 | tf_op jit(solution)/shard_map/ppermute | solution.py:25
  116.9 6.4 %collective-permute-start.20 = (bf16[256,256]{1,0:T(8,128)(2,1)S(1)}, bf16[256,256]{1,0:T(8,128)(2,1)S(1)}, u32[]{:S(2)}, u32[]{:S(2)}) collective-permute-start(bf16[256,256]{1,0:T(8,128)(2,1)S(1)} %get-tuple-element.62), channel_id=1, source_target_pairs={{0,16},{1,17},{2,18},{3,19},{4,20},{5,21},{6,22},{7,23},{8,24},{9,... | collective-permute-start | bytes 393224 | tf_op jit(solution)/shard_map/ppermute | solution.py:25
  118.3 8.1 %collective-permute-start.16 = (bf16[256,256]{1,0:T(8,128)(2,1)S(1)}, bf16[256,256]{1,0:T(8,128)(2,1)S(1)}, u32[]{:S(2)}, u32[]{:S(2)}) collective-permute-start(bf16[256,256]{1,0:T(8,128)(2,1)S(1)} %get-tuple-element.55), channel_id=1, source_target_pairs={{0,48},{1,49},{2,50},{3,51},{4,52},{5,53},{6,54},{7,55},{8,56},{9,... | collective-permute-start | bytes 393224 | tf_op jit(solution)/shard_map/ppermute | solution.py:25
  123.3 6.5 %collective-permute-start.21 = (bf16[256,128]{1,0:T(8,128)(2,1)S(1)}, bf16[256,128]{1,0:T(8,128)(2,1)S(1)}, u32[]{:S(2)}, u32[]{:S(2)}) collective-permute-start(bf16[256,128]{1,0:T(8,128)(2,1)S(1)} %get-tuple-element.64), channel_id=1, source_target_pairs={{0,48},{1,49},{2,50},{3,51},{4,52},{5,53},{6,54},{7,55},{8,56},{9,... | collective-permute-start | bytes 196616 | tf_op jit(solution)/shard_map/ppermute | solution.py:25
  126.4 5.4 %collective-permute-start.17 = (bf16[256,128]{1,0:T(8,128)(2,1)S(1)}, bf16[256,128]{1,0:T(8,128)(2,1)S(1)}, u32[]{:S(2)}, u32[]{:S(2)}) collective-permute-start(bf16[256,128]{1,0:T(8,128)(2,1)S(1)} %get-tuple-element.57), channel_id=1, source_target_pairs={{0,16},{1,17},{2,18},{3,19},{4,20},{5,21},{6,22},{7,23},{8,24},{9,... | collective-permute-start | bytes 196616 | tf_op jit(solution)/shard_map/ppermute | solution.py:25

commit v11 on v10

--- a/solution.py
+++ b/solution.py
@@ -81,29 +81,33 @@
     )(place, where, pltpu.with_memory_space_constraint(masks, pltpu.HBM))
 
 
-def gather_kernel(cores, dys, adj, *refs):
-    parts, out = refs[: 2 * len(cores)], refs[-1]
-    start = refs[-2] if len(refs) > len(parts) + 1 else None
+def gather_kernel(cores, dys, halves, adj, *refs):
+    parts, start, out = refs[: len(halves) * len(cores)], None, refs[-1]
+    if len(refs) > len(parts) + 1:
+        start = refs[-2]
     half = parts[0].shape[1]
     depth = NZH * TILE
     rows = 2 * TILE
     for r in range(0, out.shape[0], rows):
-        for h in range(2):
+        for n, h in enumerate(halves):
             cols = slice(h * half, (h + 1) * half)
-            value = None if start is None else start[r : r + rows, cols]
+            value = None if start is None else start[r : r + rows, cols].astype(F32)
             for i, core in enumerate(cores):
                 at = [(core * NY + dy) * depth for dy in dys[h]]
                 lhs = jnp.concatenate([adj[r : r + rows, a : a + depth] for a in at], axis=1)
-                term = jnp.dot(lhs, parts[2 * i + h][...], preferred_element_type=F32)
+                term = jnp.dot(lhs, parts[len(halves) * i + n][...], preferred_element_type=F32)
                 value = term if value is None else value + term
             out[r : r + rows, cols] = value.astype(out.dtype)
-
-
-def gather_matmul(adj, parts, cores, dys, start, dtype, name):
+        for h in set(range(2)) - set(halves):
+            cols = slice(h * half, (h + 1) * half)
+            out[r : r + rows, cols] = start[r : r + rows, cols].astype(out.dtype)
+
+
+def gather_matmul(adj, parts, cores, dys, start, dtype, name, halves=(0, 1)):
     rows, width = adj.shape[0], 2 * parts[0].shape[1]
     operands = [adj, *parts] + ([] if start is None else [start])
-    flops = 2 * rows * width * parts[0].shape[0] * len(cores)
-    return in_vmem(functools.partial(gather_kernel, cores, dys), [kept((rows, width), dtype)], operands, name, flops)[0]
+    kernel = functools.partial(gather_kernel, cores, dys, halves)
+    return in_vmem(kernel, [kept((rows, width), dtype)], operands, name)[0]
 
 
 def node_kernel(parts, base, degf_row, w_neigh, cotangent, grad, scaled_t, out):
@@ -213,7 +217,8 @@
     row = lax.axis_index("row").astype(jnp.int32)
 
     differ = jnp.arange(NROW, dtype=jnp.int32) ^ row
-    adj = adjacency(tile_masks[0, 0], (differ % NCORE) * CHIPS + differ // NCORE, tile_rows[0, 0].reshape(-1))
+    place = (differ % NCORE) * CHIPS + differ // NCORE
+    where = tile_rows[0, 0].reshape(-1)
     degf_row = degrees.astype(F32)[None, :]
     base = jnp.dot(features, w_self, preferred_element_type=F32) + bias[None, :]
 
@@ -221,12 +226,14 @@
     firsts = [flip(v, z=k1) for v, (k1, _) in zip(chunks, STEPS)]
     pairs = [jnp.concatenate([v, r], axis=0) for v, r in zip(chunks, firsts)]
     seconds = [flip(v, z=k2) for v, (_, k2) in zip(pairs, STEPS)]
+    seconds[0], place, where, degf_row = lax.optimization_barrier((seconds[0], place, where, degf_row))
+    adj = adjacency(tile_masks[0, 0], place, where)
     planes = []
     for v, first, second, (k1, k2) in zip(chunks, firsts, seconds, STEPS):
         tiles = {0: v, k1: first, k2: second[:TILE], k1 ^ k2: second[TILE:]}
         planes.append(jnp.concatenate([tiles[i] for i in range(NZH)], axis=0))
     thirds = [flip(v, y=k1) for v, (k1, _) in zip(planes, STEPS)]
-    *thirds, adj, base, degf_row = lax.optimization_barrier((*thirds, adj, base, degf_row))
+    *thirds, adj, base = lax.optimization_barrier((*thirds, adj, base))
     near = [jnp.concatenate([v, r], axis=0) for v, r in zip(planes, thirds)]
     far = [flip(v, y=k2) for v, (_, k2) in zip(near, STEPS)]
     first, second = [(0, k1) for k1, _ in STEPS], [(k2, k1 ^ k2) for k1, k2 in STEPS]
@@ -235,8 +242,10 @@
     far[0], part = lax.optimization_barrier((far[0], part))
     other = [flip(v, core=1) for v in far]
     part = gather_matmul(adj, far, (0,), second, part, F32, "gather_far")
-    *other, part = lax.optimization_barrier((*other, part))
-    summed = gather_matmul(adj, other, (1,), second, part, BF16, "gather_far_other")
+    other[0], part = lax.optimization_barrier((other[0], part))
+    part = gather_matmul(adj, other[:1], (1,), second, part, F32, "gather_far_first", (0,))
+    other[1], part = lax.optimization_barrier((other[1], part))
+    summed = gather_matmul(adj, other[1:], (1,), second, part, BF16, "gather_far_second", (1,))
 
     arrived = lax.all_to_all(summed, "col", 0, 0, tiled=True)
     grad_pre, scaled_t, output = node_step(arrived, base, degf_row, w_neigh, cotangent)
@@ -248,7 +257,7 @@
     keep_out = spread_matmul(table, adj, 1, stays, "spread_stay_other")
     send_in, send, keep_out = lax.optimization_barrier((send_in, send, keep_out))
     sums = list(both_halves(send, send_in))
-    sums[0], table = lax.optimization_barrier((sums[0], table))
+    sums[0], keep_out, table = lax.optimization_barrier((sums[0], keep_out, table))
     keep_in = flip(keep_out, core=1)
     keep = spread_matmul(table, adj, 0, stays, "spread_stay")
 

time: 134 us -> 134 us (level); the launches traced: 133 us -> 134 us
  waiting for transfers between devices: 40.3 us -> 47 us
  starting transfers between devices: 32 us -> 26 us
    ppermute x22, waiting for transfers between devices: 40.3 us -> 47 us  [flip(): return lax.ppermute(value, ('row', 'col'), pairs)]
    ppermute x22, starting transfers between devices: 32 us -> 26 us  [flip(): return lax.ppermute(value, ('row', 'col'), pairs)]
    pallas_call x16 -> x17, Pallas kernels: 12.5 us -> 12.7 us  [in_vmem(): pl.pallas_call(kernel, in_specs=[spec] * len(operands), out_specs=out_spe...]
  transfers between devices with their start and end apart: 22 -> 22, of which waited for: 11 -> 11; matrix products, arithmetic and copies ran while one was open for 2% -> 2% of each run, Pallas kernels for 10% -> 11%
where the time goes in v11:
time: 134 us
  waiting for transfers between devices  47 us (35%)
  blocking collectives  38.9 us (29%)
  starting transfers between devices  26 us (19%)
  Pallas kernels  18.2 us (14%)
  local copies, waits for them, and re-layouts  1.88 us (1%)
    ppermute x22, waiting for transfers between devices, flip(): return lax.ppermute(value, ('row', 'col'), pairs)  47 us
    ppermute x22, starting transfers between devices, flip(): return lax.ppermute(value, ('row', 'col'), pairs)  26 us
    all_to_all x1, blocking collectives, body(): arrived = lax.all_to_all(summed, 'col', 0, 0, tiled=True)  20.9 us
    all_to_all x1, blocking collectives, body(): table = lax.all_to_all(scaled_t, 'col', 0, 0, tiled=True)  18 us
    pallas_call x17, Pallas kernels, in_vmem(): pl.pallas_call(kernel, in_specs=[spec] * len(operands), out_specs=out_spe...  12.7 us
    pallas_call x1, Pallas kernels, adjacency(): pl.pallas_call(adjacency_kernel, grid_spec=pltpu.PrefetchScalarGridSpec(n...  5.55 us
  transfers between devices with their start and end apart: 22, of which 11 were waited for; matrix products, arithmetic and copies ran while one was open for 2% of the time, Pallas kernels for 11%

profile of v11, /device:TPU:32, one launch (start us, length us, event | category | flops | bytes accessed | tf_op | source)
XLA Modules:
  0.0 134.2 jit_solution(10636087406442443872)
XLA Ops:
  0.7 0.9 constant_dynamic-update-slice_fusion.4
  1.6 3.4 %collective-permute-start = (bf16[128,256]{1,0:T(8,128)(2,1)S(1)}, bf16[128,256]{1,0:T(8,128)(2,1)S(1)}, u32[]{:S(2)}, u32[]{:S(2)}) collective-permute-start(bf16[128,256]{1,0:T(8,128)(2,1)S(1)} %get-tuple-element.80), channel_id=1, source_target_pairs={{0,16},{1,17},{2,18},{3,19},{4,20},{5,21},{6,22},{7,23},{8,24},{9,... | collective-permute-start | bytes 196616 | tf_op jit(solution)/shard_map/ppermute | solution.py:25
  5.0 3.6 %collective-permute-start.3 = (bf16[128,256]{1,0:T(8,128)(2,1)S(1)}, bf16[128,256]{1,0:T(8,128)(2,1)S(1)}, u32[]{:S(2)}, u32[]{:S(2)}) collective-permute-start(bf16[128,256]{1,0:T(8,128)(2,1)S(1)} %get-tuple-element.81), channel_id=1, source_target_pairs={{0,48},{1,49},{2,50},{3,51},{4,52},{5,53},{6,54},{7,55},{8,56},{9,... | collective-permute-start | bytes 196616 | tf_op jit(solution)/shard_map/ppermute | solution.py:25
  8.6 0.8 copy.11
  10.1 3.2 %collective-permute-start.1 = (bf16[256,256]{1,0:T(8,128)(2,1)S(1)}, bf16[256,256]{1,0:T(8,128)(2,1)S(1)}, u32[]{:S(2)}, u32[]{:S(2)}) collective-permute-start(bf16[256,256]{1,0:T(8,128)(2,1)S(1)} %pad_maximum_fusion.3), channel_id=1, source_target_pairs={{0,48},{1,49},{2,50},{3,51},{4,52},{5,53},{6,54},{7,55},{8,56},{9,... | collective-permute-start | bytes 393224 | tf_op jit(solution)/shard_map/ppermute | solution.py:25
  13.9 5.7 %collective-permute-done.1 = bf16[256,256]{1,0:T(8,128)(2,1)S(1)} collective-permute-done((bf16[256,256]{1,0:T(8,128)(2,1)S(1)}, bf16[256,256]{1,0:T(8,128)(2,1)S(1)}, u32[]{:S(2)}, u32[]{:S(2)}) %collective-permute-start.1) | collective-permute-done | bytes 131104 | tf_op jit(solution)/shard_map/ppermute | solution.py:25
  19.7 1.7 %collective-permute-start.2 = (bf16[512,256]{1,0:T(8,128)(2,1)S(1)}, bf16[512,256]{1,0:T(8,128)(2,1)S(1)}, u32[]{:S(2)}, u32[]{:S(2)}) collective-permute-start(bf16[512,256]{1,0:T(8,128)(2,1)S(1)} %pad_maximum_fusion.1), channel_id=1, source_target_pairs={{0,64},{1,65},{2,66},{3,67},{4,68},{5,69},{6,70},{7,71},{8,72},{9,... | collective-permute-start | bytes 786440 | tf_op jit(solution)/shard_map/ppermute | solution.py:25
  21.4 2.3 %collective-permute-start.5 = (bf16[512,256]{1,0:T(8,128)(2,1)S(1)}, bf16[512,256]{1,0:T(8,128)(2,1)S(1)}, u32[]{:S(2)}, u32[]{:S(2)}) collective-permute-start(bf16[512,256]{1,0:T(8,128)(2,1)S(1)} %pad_maximum_fusion.2), channel_id=1, source_target_pairs={{0,192},{1,193},{2,194},{3,195},{4,196},{5,197},{6,198},{7,199},{8... | collective-permute-start | bytes 786440 | tf_op jit(solution)/shard_map/ppermute | solution.py:25
  23.9 5.5 %adjacency.1.adj = bf16[1024,4096]{1,0:T(8,128)(2,1)S(1)} custom-call(s32[32]{0:T(128)S(1)} %fusion.1.place, s32[96]{0:T(128)S(1)} %reshape_squeeze.3.where, s32[32,3,128,128]{3,2,1,0:T(8,128)} %bitcast.13), custom_call_target="tpu_custom_call" | custom-call | bytes 14680064 | tf_op jit(solution)/shard_map/adjacency/pallas_call | solution.py:68
  30.8 2.2 %collective-permute-start.8 = (bf16[1024,256]{1,0:T(8,128)(2,1)S(1)}, bf16[1024,256]{1,0:T(8,128)(2,1)S(1)}, u32[]{:S(2)}, u32[]{:S(2)}) collective-permute-start(bf16[1024,256]{1,0:T(8,128)(2,1)S(1)} %constant_dynamic-update-slice_fusion.refs_0_), channel_id=1, source_target_pairs={{0,192},{1,193},{2,194},{3,195},{4,196},{5,197},{6,198},{7,199},{8... | collective-permute-start | bytes 1572872 | tf_op jit(solution)/shard_map/ppermute | solution.py:25
  33.0 2.3 %gather_near.1.refs_2_ = f32[1024,512]{1,0:T(8,128)S(1)} custom-call(bf16[1024,4096]{1,0:T(8,128)(2,1)S(1)} %adjacency.1.adj, bf16[1024,256]{1,0:T(8,128)(2,1)S(1)} %constant_dynamic-update-slice_fusion.refs_0_, bf16[1024,256]{1,0:T(8,128)(2,1)S(1)} %pad_maximum_fusion.refs_1_, bf16[1024,256]{1,0:T(8,128)(2,1)S(1)} %collective-permute-done.9.refs_2_, ...), custom_call_target="tpu_custom_call" | custom-call | flops 1048576 | bytes 3145728 | tf_op jit(solution)/shard_map/gather_near/pallas_call | solution.py:32
  35.3 10.6 %collective-permute-done.8.refs_0_ = bf16[1024,256]{1,0:T(8,128)(2,1)S(1)} collective-permute-done((bf16[1024,256]{1,0:T(8,128)(2,1)S(1)}, bf16[1024,256]{1,0:T(8,128)(2,1)S(1)}, u32[]{:S(2)}, u32[]{:S(2)}) %collective-permute-start.8) | collective-permute-done | bytes 524320 | tf_op jit(solution)/shard_map/ppermute | solution.py:25
  46.7 1.2 gather_far.1.refs_1_
  49.4 20.9 %all_to_all.16 = bf16[8,128,512]{2,1,0:T(8,128)(2,1)S(1)} all-to-all(bf16[8,128,512]{2,1,0:T(8,128)(2,1)S(1)} %bitcast.11), channel_id=1, replica_groups=mesh['row'=32,'col'=8] {'col'}, dimensions={0} | all-to-all | bytes 2097152 | tf_op jit(solution)/shard_map/all_to_all | solution.py:250
  70.3 1.1 node_step.1
  71.4 18.0 %all_to_all.17.parts = bf16[8,512,128]{2,1,0:T(8,128)(2,1)S(1)} all-to-all(bf16[8,512,128]{2,1,0:T(8,128)(2,1)S(1)} %get-tuple-element.54), channel_id=1, replica_groups=mesh['row'=32,'col'=8] {'col'}, dimensions={0} | all-to-all | bytes 2097152 | tf_op jit(solution)/shard_map/all_to_all | solution.py:253
  89.3 1.2 spread_go_other.1
  90.7 1.2 spread_stay_other.1
  92.0 1.2 spread_go.1.mine
  94.3 1.3 collective-permute-start.14
  95.6 1.2 spread_stay.1.mine
  96.8 11.2 %collective-permute-done.18.got = bf16[256,1024]{1,0:T(8,128)(2,1)S(1)} collective-permute-done((bf16[256,1024]{1,0:T(8,128)(2,1)S(1)}, bf16[256,1024]{1,0:T(8,128)(2,1)S(1)}, u32[]{:S(2)}, u32[]{:S(2)}) %collective-permute-start.18) | collective-permute-done | bytes 524320 | tf_op jit(solution)/shard_map/ppermute | solution.py:25
  108.2 1.6 %collective-permute-start.19 = (bf16[256,512]{1,0:T(8,128)(2,1)S(1)}, bf16[256,512]{1,0:T(8,128)(2,1)S(1)}, u32[]{:S(2)}, u32[]{:S(2)}) collective-permute-start(bf16[256,512]{1,0:T(8,128)(2,1)S(1)} %get-tuple-element.70), channel_id=1, source_target_pairs={{0,192},{1,193},{2,194},{3,195},{4,196},{5,197},{6,198},{7,199},{8... | collective-permute-start | bytes 786440 | tf_op jit(solution)/shard_map/ppermute | solution.py:25
  110.1 6.9 %collective-permute-done.19.refs_1_ = bf16[256,512]{1,0:T(8,128)(2,1)S(1)} collective-permute-done((bf16[256,512]{1,0:T(8,128)(2,1)S(1)}, bf16[256,512]{1,0:T(8,128)(2,1)S(1)}, u32[]{:S(2)}, u32[]{:S(2)}) %collective-permute-start.19) | collective-permute-done | bytes 262176 | tf_op jit(solution)/shard_map/ppermute | solution.py:25
  117.1 1.1 collective-permute-start.20
  118.3 1.7 %collective-permute-start.16 = (bf16[256,256]{1,0:T(8,128)(2,1)S(1)}, bf16[256,256]{1,0:T(8,128)(2,1)S(1)}, u32[]{:S(2)}, u32[]{:S(2)}) collective-permute-start(bf16[256,256]{1,0:T(8,128)(2,1)S(1)} %get-tuple-element.65), channel_id=1, source_target_pairs={{0,48},{1,49},{2,50},{3,51},{4,52},{5,53},{6,54},{7,55},{8,56},{9,... | collective-permute-start | bytes 393224 | tf_op jit(solution)/shard_map/ppermute | solution.py:25
  120.0 4.3 %collective-permute-done.20.refs_1_ = bf16[256,256]{1,0:T(8,128)(2,1)S(1)} collective-permute-done((bf16[256,256]{1,0:T(8,128)(2,1)S(1)}, bf16[256,256]{1,0:T(8,128)(2,1)S(1)}, u32[]{:S(2)}, u32[]{:S(2)}) %collective-permute-start.20) | collective-permute-done | bytes 131104 | tf_op jit(solution)/shard_map/ppermute | solution.py:25
  124.3 1.8 %collective-permute-start.21 = (bf16[256,128]{1,0:T(8,128)(2,1)S(1)}, bf16[256,128]{1,0:T(8,128)(2,1)S(1)}, u32[]{:S(2)}, u32[]{:S(2)}) collective-permute-start(bf16[256,128]{1,0:T(8,128)(2,1)S(1)} %get-tuple-element.74), channel_id=1, source_target_pairs={{0,48},{1,49},{2,50},{3,51},{4,52},{5,53},{6,54},{7,55},{8,56},{9,... | collective-permute-start | bytes 196616 | tf_op jit(solution)/shard_map/ppermute | solution.py:25
  126.1 2.0 %collective-permute-done.16.refs_1_ = bf16[256,256]{1,0:T(8,128)(2,1)S(1)} collective-permute-done((bf16[256,256]{1,0:T(8,128)(2,1)S(1)}, bf16[256,256]{1,0:T(8,128)(2,1)S(1)}, u32[]{:S(2)}, u32[]{:S(2)}) %collective-permute-start.16) | collective-permute-done | bytes 131104 | tf_op jit(solution)/shard_map/ppermute | solution.py:25
  128.5 2.2 %collective-permute-done.21.refs_3_ = bf16[256,128]{1,0:T(8,128)(2,1)S(1)} collective-permute-done((bf16[256,128]{1,0:T(8,128)(2,1)S(1)}, bf16[256,128]{1,0:T(8,128)(2,1)S(1)}, u32[]{:S(2)}, u32[]{:S(2)}) %collective-permute-start.21) | collective-permute-done | bytes 65568 | tf_op jit(solution)/shard_map/ppermute | solution.py:25
  130.8 2.6 %collective-permute-done.17.refs_1_ = bf16[256,128]{1,0:T(8,128)(2,1)S(1)} collective-permute-done((bf16[256,128]{1,0:T(8,128)(2,1)S(1)}, bf16[256,128]{1,0:T(8,128)(2,1)S(1)}, u32[]{:S(2)}, u32[]{:S(2)}) %collective-permute-start.17) | collective-permute-done | bytes 65568 | tf_op jit(solution)/shard_map/ppermute | solution.py:25
  133.4 0.8 last_sum.1
  (58 shorter events, 7.4 us)
Async XLA Ops:
  0.6 23.1 %copy-start = (bf16[512,512]{1,0:T(8,128)(2,1)S(1)}, bf16[512,512]{1,0:T(8,128)(2,1)}, u32[]{:S(2)}) copy-start(bf16[512,512]{1,0:T(8,128)(2,1)} %param.12) | copy-start | bytes 1572868
  0.6 23.1 %copy-start.3 = (bf16[128,512]{1,0:T(8,128)(2,1)S(1)}, bf16[128,512]{1,0:T(8,128)(2,1)}, u32[]{:S(2)}) copy-start(bf16[128,512]{1,0:T(8,128)(2,1)} %param.8) | copy-start | bytes 393220
  0.7 23.0 %copy-start.4 = (f32[512]{0:T(512)S(1)}, f32[512]{0:T(512)}, u32[]{:S(2)}) copy-start(f32[512]{0:T(512)} %param.14) | copy-start | bytes 6148
  1.6 8.5 %collective-permute-start = (bf16[128,256]{1,0:T(8,128)(2,1)S(1)}, bf16[128,256]{1,0:T(8,128)(2,1)S(1)}, u32[]{:S(2)}, u32[]{:S(2)}) collective-permute-start(bf16[128,256]{1,0:T(8,128)(2,1)S(1)} %get-tuple-element.80), channel_id=1, source_target_pairs={{0,16},{1,17},{2,18},{3,19},{4,20},{5,21},{6,22},{7,23},{8,24},{9,... | collective-permute-start | bytes 196616 | tf_op jit(solution)/shard_map/ppermute | solution.py:25
  5.0 8.4 %collective-permute-start.3 = (bf16[128,256]{1,0:T(8,128)(2,1)S(1)}, bf16[128,256]{1,0:T(8,128)(2,1)S(1)}, u32[]{:S(2)}, u32[]{:S(2)}) collective-permute-start(bf16[128,256]{1,0:T(8,128)(2,1)S(1)} %get-tuple-element.81), channel_id=1, source_target_pairs={{0,48},{1,49},{2,50},{3,51},{4,52},{5,53},{6,54},{7,55},{8,56},{9,... | collective-permute-start | bytes 196616 | tf_op jit(solution)/shard_map/ppermute | solution.py:25
  10.1 9.5 %collective-permute-start.1 = (bf16[256,256]{1,0:T(8,128)(2,1)S(1)}, bf16[256,256]{1,0:T(8,128)(2,1)S(1)}, u32[]{:S(2)}, u32[]{:S(2)}) collective-permute-start(bf16[256,256]{1,0:T(8,128)(2,1)S(1)} %pad_maximum_fusion.3), channel_id=1, source_target_pairs={{0,48},{1,49},{2,50},{3,51},{4,52},{5,53},{6,54},{7,55},{8,56},{9,... | collective-permute-start | bytes 393224 | tf_op jit(solution)/shard_map/ppermute | solution.py:25
  13.4 8.0 %collective-permute-start.4 = (bf16[256,256]{1,0:T(8,128)(2,1)S(1)}, bf16[256,256]{1,0:T(8,128)(2,1)S(1)}, u32[]{:S(2)}, u32[]{:S(2)}) collective-permute-start(bf16[256,256]{1,0:T(8,128)(2,1)S(1)} %pad_maximum_fusion.4), channel_id=1, source_target_pairs={{0,16},{1,17},{2,18},{3,19},{4,20},{5,21},{6,22},{7,23},{8,24},{9,... | collective-permute-start | bytes 393224 | tf_op jit(solution)/shard_map/ppermute | solution.py:25
  19.7 9.8 %collective-permute-start.2 = (bf16[512,256]{1,0:T(8,128)(2,1)S(1)}, bf16[512,256]{1,0:T(8,128)(2,1)S(1)}, u32[]{:S(2)}, u32[]{:S(2)}) collective-permute-start(bf16[512,256]{1,0:T(8,128)(2,1)S(1)} %pad_maximum_fusion.1), channel_id=1, source_target_pairs={{0,64},{1,65},{2,66},{3,67},{4,68},{5,69},{6,70},{7,71},{8,72},{9,... | collective-permute-start | bytes 786440 | tf_op jit(solution)/shard_map/ppermute | solution.py:25
  21.4 8.7 %collective-permute-start.5 = (bf16[512,256]{1,0:T(8,128)(2,1)S(1)}, bf16[512,256]{1,0:T(8,128)(2,1)S(1)}, u32[]{:S(2)}, u32[]{:S(2)}) collective-permute-start(bf16[512,256]{1,0:T(8,128)(2,1)S(1)} %pad_maximum_fusion.2), channel_id=1, source_target_pairs={{0,192},{1,193},{2,194},{3,195},{4,196},{5,197},{6,198},{7,199},{8... | collective-permute-start | bytes 786440 | tf_op jit(solution)/shard_map/ppermute | solution.py:25
  30.1 2.9 %collective-permute-start.9 = (bf16[1024,256]{1,0:T(8,128)(2,1)S(1)}, bf16[1024,256]{1,0:T(8,128)(2,1)S(1)}, u32[]{:S(2)}, u32[]{:S(2)}) collective-permute-start(bf16[1024,256]{1,0:T(8,128)(2,1)S(1)} %constant_dynamic-update-slice_fusion.refs_0_), channel_id=1, source_target_pairs={{0,8},{1,9},{2,10},{3,11},{4,12},{5,13},{6,14},{7,15},{8,0},{9,1},... | collective-permute-start | bytes 1572872 | tf_op jit(solution)/shard_map/ppermute | solution.py:25
  30.2 2.8 %collective-permute-start.10 = (bf16[1024,256]{1,0:T(8,128)(2,1)S(1)}, bf16[1024,256]{1,0:T(8,128)(2,1)S(1)}, u32[]{:S(2)}, u32[]{:S(2)}) collective-permute-start(bf16[1024,256]{1,0:T(8,128)(2,1)S(1)} %pad_maximum_fusion.refs_1_), channel_id=1, source_target_pairs={{0,8},{1,9},{2,10},{3,11},{4,12},{5,13},{6,14},{7,15},{8,0},{9,1},... | collective-permute-start | bytes 1572872 | tf_op jit(solution)/shard_map/ppermute | solution.py:25
  30.8 15.1 %collective-permute-start.8 = (bf16[1024,256]{1,0:T(8,128)(2,1)S(1)}, bf16[1024,256]{1,0:T(8,128)(2,1)S(1)}, u32[]{:S(2)}, u32[]{:S(2)}) collective-permute-start(bf16[1024,256]{1,0:T(8,128)(2,1)S(1)} %constant_dynamic-update-slice_fusion.refs_0_), channel_id=1, source_target_pairs={{0,192},{1,193},{2,194},{3,195},{4,196},{5,197},{6,198},{7,199},{8... | collective-permute-start | bytes 1572872 | tf_op jit(solution)/shard_map/ppermute | solution.py:25
  33.0 13.6 %collective-permute-start.6 = (bf16[1024,256]{1,0:T(8,128)(2,1)S(1)}, bf16[1024,256]{1,0:T(8,128)(2,1)S(1)}, u32[]{:S(2)}, u32[]{:S(2)}) collective-permute-start(bf16[1024,256]{1,0:T(8,128)(2,1)S(1)} %pad_maximum_fusion.refs_1_), channel_id=1, source_target_pairs={{0,64},{1,65},{2,66},{3,67},{4,68},{5,69},{6,70},{7,71},{8,72},{9,... | collective-permute-start | bytes 1572872 | tf_op jit(solution)/shard_map/ppermute | solution.py:25
  46.0 2.0 %collective-permute-start.11 = (bf16[1024,256]{1,0:T(8,128)(2,1)S(1)}, bf16[1024,256]{1,0:T(8,128)(2,1)S(1)}, u32[]{:S(2)}, u32[]{:S(2)}) collective-permute-start(bf16[1024,256]{1,0:T(8,128)(2,1)S(1)} %collective-permute-done.8.refs_0_), channel_id=1, source_target_pairs={{0,8},{1,9},{2,10},{3,11},{4,12},{5,13},{6,14},{7,15},{8,0},{9,1},... | collective-permute-start | bytes 1572872 | tf_op jit(solution)/shard_map/ppermute | solution.py:25
  46.7 2.0 %collective-permute-start.7 = (bf16[1024,256]{1,0:T(8,128)(2,1)S(1)}, bf16[1024,256]{1,0:T(8,128)(2,1)S(1)}, u32[]{:S(2)}, u32[]{:S(2)}) collective-permute-start(bf16[1024,256]{1,0:T(8,128)(2,1)S(1)} %collective-permute-done.6.refs_1_), channel_id=1, source_target_pairs={{0,8},{1,9},{2,10},{3,11},{4,12},{5,13},{6,14},{7,15},{8,0},{9,1},... | collective-permute-start | bytes 1572872 | tf_op jit(solution)/shard_map/ppermute | solution.py:25
  49.4 20.9 %copy-start.1 = (bf16[512,512]{1,0:T(8,128)(2,1)S(1)}, bf16[512,512]{1,0:T(8,128)(2,1)}, u32[]{:S(2)}) copy-start(bf16[512,512]{1,0:T(8,128)(2,1)} %w_neigh.1) | copy-start | bytes 1572868
  49.4 20.9 %copy-start.2 = (bf16[128,512]{1,0:T(8,128)(2,1)S(1)}, bf16[128,512]{1,0:T(8,128)(2,1)}, u32[]{:S(2)}) copy-start(bf16[128,512]{1,0:T(8,128)(2,1)} %cotangent.1) | copy-start | bytes 393220
  90.6 2.7 %collective-permute-start.12 = (bf16[2,256,1024]{2,1,0:T(8,128)(2,1)S(1)}, bf16[2,256,1024]{2,1,0:T(8,128)(2,1)S(1)}, u32[]{:S(2)}, u32[]{:S(2)}) collective-permute-start(bf16[2,256,1024]{2,1,0:T(8,128)(2,1)S(1)} %spread_go_other.1), channel_id=1, source_target_pairs={{0,8},{1,9},{2,10},{3,11},{4,12},{5,13},{6,14},{7,15},{8,0},{9,1},... | collective-permute-start | bytes 3145736 | tf_op jit(solution)/shard_map/ppermute | solution.py:25
  93.6 14.4 %collective-permute-start.13 = (bf16[2,256,1024]{2,1,0:T(8,128)(2,1)S(1)}, bf16[2,256,1024]{2,1,0:T(8,128)(2,1)S(1)}, u32[]{:S(2)}, u32[]{:S(2)}) collective-permute-start(bf16[2,256,1024]{2,1,0:T(8,128)(2,1)S(1)} %spread_stay_other.1), channel_id=1, source_target_pairs={{0,8},{1,9},{2,10},{3,11},{4,12},{5,13},{6,14},{7,15},{8,0},{9,1},... | collective-permute-start | bytes 3145736 | tf_op jit(solution)/shard_map/ppermute | solution.py:25
  94.1 14.0 %collective-permute-start.18 = (bf16[256,1024]{1,0:T(8,128)(2,1)S(1)}, bf16[256,1024]{1,0:T(8,128)(2,1)S(1)}, u32[]{:S(2)}, u32[]{:S(2)}) collective-permute-start(bf16[256,1024]{1,0:T(8,128)(2,1)S(1)} %get-tuple-element.68), channel_id=1, source_target_pairs={{0,64},{1,65},{2,66},{3,67},{4,68},{5,69},{6,70},{7,71},{8,72},{9,... | collective-permute-start | bytes 1572872 | tf_op jit(solution)/shard_map/ppermute | solution.py:25
  94.3 15.5 %collective-permute-start.14 = (bf16[256,1024]{1,0:T(8,128)(2,1)S(1)}, bf16[256,1024]{1,0:T(8,128)(2,1)S(1)}, u32[]{:S(2)}, u32[]{:S(2)}) collective-permute-start(bf16[256,1024]{1,0:T(8,128)(2,1)S(1)} %get-tuple-element.61), channel_id=1, source_target_pairs={{0,192},{1,193},{2,194},{3,195},{4,196},{5,197},{6,198},{7,199},{8... | collective-permute-start | bytes 1572872 | tf_op jit(solution)/shard_map/ppermute | solution.py:25
  108.2 8.8 %collective-permute-start.19 = (bf16[256,512]{1,0:T(8,128)(2,1)S(1)}, bf16[256,512]{1,0:T(8,128)(2,1)S(1)}, u32[]{:S(2)}, u32[]{:S(2)}) collective-permute-start(bf16[256,512]{1,0:T(8,128)(2,1)S(1)} %get-tuple-element.70), channel_id=1, source_target_pairs={{0,192},{1,193},{2,194},{3,195},{4,196},{5,197},{6,198},{7,199},{8... | collective-permute-start | bytes 786440 | tf_op jit(solution)/shard_map/ppermute | solution.py:25
  110.0 8.2 %collective-permute-start.15 = (bf16[256,512]{1,0:T(8,128)(2,1)S(1)}, bf16[256,512]{1,0:T(8,128)(2,1)S(1)}, u32[]{:S(2)}, u32[]{:S(2)}) collective-permute-start(bf16[256,512]{1,0:T(8,128)(2,1)S(1)} %get-tuple-element.63), channel_id=1, source_target_pairs={{0,64},{1,65},{2,66},{3,67},{4,68},{5,69},{6,70},{7,71},{8,72},{9,... | collective-permute-start | bytes 786440 | tf_op jit(solution)/shard_map/ppermute | solution.py:25
  117.1 7.2 %collective-permute-start.20 = (bf16[256,256]{1,0:T(8,128)(2,1)S(1)}, bf16[256,256]{1,0:T(8,128)(2,1)S(1)}, u32[]{:S(2)}, u32[]{:S(2)}) collective-permute-start(bf16[256,256]{1,0:T(8,128)(2,1)S(1)} %get-tuple-element.72), channel_id=1, source_target_pairs={{0,16},{1,17},{2,18},{3,19},{4,20},{5,21},{6,22},{7,23},{8,24},{9,... | collective-permute-start | bytes 393224 | tf_op jit(solution)/shard_map/ppermute | solution.py:25
  118.3 9.8 %collective-permute-start.16 = (bf16[256,256]{1,0:T(8,128)(2,1)S(1)}, bf16[256,256]{1,0:T(8,128)(2,1)S(1)}, u32[]{:S(2)}, u32[]{:S(2)}) collective-permute-start(bf16[256,256]{1,0:T(8,128)(2,1)S(1)} %get-tuple-element.65), channel_id=1, source_target_pairs={{0,48},{1,49},{2,50},{3,51},{4,52},{5,53},{6,54},{7,55},{8,56},{9,... | collective-permute-start | bytes 393224 | tf_op jit(solution)/shard_map/ppermute | solution.py:25
  124.3 6.5 %collective-permute-start.21 = (bf16[256,128]{1,0:T(8,128)(2,1)S(1)}, bf16[256,128]{1,0:T(8,128)(2,1)S(1)}, u32[]{:S(2)}, u32[]{:S(2)}) collective-permute-start(bf16[256,128]{1,0:T(8,128)(2,1)S(1)} %get-tuple-element.74), channel_id=1, source_target_pairs={{0,48},{1,49},{2,50},{3,51},{4,52},{5,53},{6,54},{7,55},{8,56},{9,... | collective-permute-start | bytes 196616 | tf_op jit(solution)/shard_map/ppermute | solution.py:25
  128.1 5.3 %collective-permute-start.17 = (bf16[256,128]{1,0:T(8,128)(2,1)S(1)}, bf16[256,128]{1,0:T(8,128)(2,1)S(1)}, u32[]{:S(2)}, u32[]{:S(2)}) collective-permute-start(bf16[256,128]{1,0:T(8,128)(2,1)S(1)} %get-tuple-element.67), channel_id=1, source_target_pairs={{0,16},{1,17},{2,18},{3,19},{4,20},{5,21},{6,22},{7,23},{8,24},{9,... | collective-permute-start | bytes 196616 | tf_op jit(solution)/shard_map/ppermute | solution.py:25

commit v12 on v11

--- a/solution.py
+++ b/solution.py
@@ -226,14 +226,13 @@
     firsts = [flip(v, z=k1) for v, (k1, _) in zip(chunks, STEPS)]
     pairs = [jnp.concatenate([v, r], axis=0) for v, r in zip(chunks, firsts)]
     seconds = [flip(v, z=k2) for v, (_, k2) in zip(pairs, STEPS)]
-    seconds[0], place, where, degf_row = lax.optimization_barrier((seconds[0], place, where, degf_row))
     adj = adjacency(tile_masks[0, 0], place, where)
     planes = []
     for v, first, second, (k1, k2) in zip(chunks, firsts, seconds, STEPS):
         tiles = {0: v, k1: first, k2: second[:TILE], k1 ^ k2: second[TILE:]}
         planes.append(jnp.concatenate([tiles[i] for i in range(NZH)], axis=0))
     thirds = [flip(v, y=k1) for v, (k1, _) in zip(planes, STEPS)]
-    *thirds, adj, base = lax.optimization_barrier((*thirds, adj, base))
+    *thirds, adj, base, degf_row = lax.optimization_barrier((*thirds, adj, base, degf_row))
     near = [jnp.concatenate([v, r], axis=0) for v, r in zip(planes, thirds)]
     far = [flip(v, y=k2) for v, (_, k2) in zip(near, STEPS)]
     first, second = [(0, k1) for k1, _ in STEPS], [(k2, k1 ^ k2) for k1, k2 in STEPS]

time: 134 us -> 134 us (level); the launches traced: 134 us -> 132 us
  waiting for transfers between devices: 47 us -> 39.5 us
  starting transfers between devices: 26 us -> 32.2 us
    ppermute x22, waiting for transfers between devices: 47 us -> 39.5 us  [flip(): return lax.ppermute(value, ('row', 'col'), pairs)]
    ppermute x22, starting transfers between devices: 26 us -> 32.2 us  [flip(): return lax.ppermute(value, ('row', 'col'), pairs)]
  transfers between devices with their start and end apart: 22 -> 22, of which waited for: 11 -> 11; matrix products, arithmetic and copies ran while one was open for 2% -> 1% of each run, Pallas kernels for 11% -> 11%
where the time goes in v12:
time: 134 us; the launch traced here: 132 us
  waiting for transfers between devices  39.5 us (29%)
  blocking collectives  38.5 us (29%)
  starting transfers between devices  32.2 us (24%)
  Pallas kernels  18.2 us (14%)
    ppermute x22, waiting for transfers between devices, flip(): return lax.ppermute(value, ('row', 'col'), pairs)  39.5 us
    ppermute x22, starting transfers between devices, flip(): return lax.ppermute(value, ('row', 'col'), pairs)  32.2 us
    all_to_all x1, blocking collectives, body(): arrived = lax.all_to_all(summed, 'col', 0, 0, tiled=True)  20.7 us
    all_to_all x1, blocking collectives, body(): table = lax.all_to_all(scaled_t, 'col', 0, 0, tiled=True)  17.8 us
    pallas_call x17, Pallas kernels, in_vmem(): pl.pallas_call(kernel, in_specs=[spec] * len(operands), out_specs=out_spe...  12.7 us
    pallas_call x1, Pallas kernels, adjacency(): pl.pallas_call(adjacency_kernel, grid_spec=pltpu.PrefetchScalarGridSpec(n...  5.55 us
  transfers between devices with their start and end apart: 22, of which 11 were waited for; matrix products, arithmetic and copies ran while one was open for 1% of the time, Pallas kernels for 11%

profile of v12, /device:TPU:32, one launch (start us, length us, event | category | flops | bytes accessed | tf_op | source)
XLA Modules:
  0.0 131.9 jit_solution(1630095696657147099)
XLA Ops:
  0.7 0.9 constant_dynamic-update-slice_fusion.4
  1.6 3.4 %collective-permute-start = (bf16[128,256]{1,0:T(8,128)(2,1)S(1)}, bf16[128,256]{1,0:T(8,128)(2,1)S(1)}, u32[]{:S(2)}, u32[]{:S(2)}) collective-permute-start(bf16[128,256]{1,0:T(8,128)(2,1)S(1)} %get-tuple-element.74), channel_id=1, source_target_pairs={{0,16},{1,17},{2,18},{3,19},{4,20},{5,21},{6,22},{7,23},{8,24},{9,... | collective-permute-start | bytes 196616 | tf_op jit(solution)/shard_map/ppermute | solution.py:25
  5.0 3.6 %collective-permute-start.3 = (bf16[128,256]{1,0:T(8,128)(2,1)S(1)}, bf16[128,256]{1,0:T(8,128)(2,1)S(1)}, u32[]{:S(2)}, u32[]{:S(2)}) collective-permute-start(bf16[128,256]{1,0:T(8,128)(2,1)S(1)} %get-tuple-element.75), channel_id=1, source_target_pairs={{0,48},{1,49},{2,50},{3,51},{4,52},{5,53},{6,54},{7,55},{8,56},{9,... | collective-permute-start | bytes 196616 | tf_op jit(solution)/shard_map/ppermute | solution.py:25
  9.2 4.1 %collective-permute-start.1 = (bf16[256,256]{1,0:T(8,128)(2,1)S(1)}, bf16[256,256]{1,0:T(8,128)(2,1)S(1)}, u32[]{:S(2)}, u32[]{:S(2)}) collective-permute-start(bf16[256,256]{1,0:T(8,128)(2,1)S(1)} %pad_maximum_fusion.3), channel_id=1, source_target_pairs={{0,48},{1,49},{2,50},{3,51},{4,52},{5,53},{6,54},{7,55},{8,56},{9,... | collective-permute-start | bytes 393224 | tf_op jit(solution)/shard_map/ppermute | solution.py:25
  13.9 5.0 %collective-permute-done.1 = bf16[256,256]{1,0:T(8,128)(2,1)S(1)} collective-permute-done((bf16[256,256]{1,0:T(8,128)(2,1)S(1)}, bf16[256,256]{1,0:T(8,128)(2,1)S(1)}, u32[]{:S(2)}, u32[]{:S(2)}) %collective-permute-start.1) | collective-permute-done | bytes 131104 | tf_op jit(solution)/shard_map/ppermute | solution.py:25
  19.0 1.7 %collective-permute-start.2 = (bf16[512,256]{1,0:T(8,128)(2,1)S(1)}, bf16[512,256]{1,0:T(8,128)(2,1)S(1)}, u32[]{:S(2)}, u32[]{:S(2)}) collective-permute-start(bf16[512,256]{1,0:T(8,128)(2,1)S(1)} %pad_maximum_fusion.1), channel_id=1, source_target_pairs={{0,64},{1,65},{2,66},{3,67},{4,68},{5,69},{6,70},{7,71},{8,72},{9,... | collective-permute-start | bytes 786440 | tf_op jit(solution)/shard_map/ppermute | solution.py:25
  20.6 2.9 %collective-permute-start.5 = (bf16[512,256]{1,0:T(8,128)(2,1)S(1)}, bf16[512,256]{1,0:T(8,128)(2,1)S(1)}, u32[]{:S(2)}, u32[]{:S(2)}) collective-permute-start(bf16[512,256]{1,0:T(8,128)(2,1)S(1)} %pad_maximum_fusion.2), channel_id=1, source_target_pairs={{0,192},{1,193},{2,194},{3,195},{4,196},{5,197},{6,198},{7,199},{8... | collective-permute-start | bytes 786440 | tf_op jit(solution)/shard_map/ppermute | solution.py:25
  23.7 5.5 %adjacency.1.adj = bf16[1024,4096]{1,0:T(8,128)(2,1)S(1)} custom-call(s32[32]{0:T(128)S(1)} %fusion.1.place, s32[96]{0:T(128)S(1)} %reshape_squeeze.3.where, s32[32,3,128,128]{3,2,1,0:T(8,128)} %bitcast.13), custom_call_target="tpu_custom_call" | custom-call | bytes 14680064 | tf_op jit(solution)/shard_map/adjacency/pallas_call | solution.py:68
  30.3 2.0 %collective-permute-start.8 = (bf16[1024,256]{1,0:T(8,128)(2,1)S(1)}, bf16[1024,256]{1,0:T(8,128)(2,1)S(1)}, u32[]{:S(2)}, u32[]{:S(2)}) collective-permute-start(bf16[1024,256]{1,0:T(8,128)(2,1)S(1)} %constant_dynamic-update-slice_fusion.refs_0_), channel_id=1, source_target_pairs={{0,192},{1,193},{2,194},{3,195},{4,196},{5,197},{6,198},{7,199},{8... | collective-permute-start | bytes 1572872 | tf_op jit(solution)/shard_map/ppermute | solution.py:25
  32.4 2.3 %gather_near.1.refs_2_ = f32[1024,512]{1,0:T(8,128)S(1)} custom-call(bf16[1024,4096]{1,0:T(8,128)(2,1)S(1)} %adjacency.1.adj, bf16[1024,256]{1,0:T(8,128)(2,1)S(1)} %constant_dynamic-update-slice_fusion.refs_0_, bf16[1024,256]{1,0:T(8,128)(2,1)S(1)} %pad_maximum_fusion.refs_1_, bf16[1024,256]{1,0:T(8,128)(2,1)S(1)} %collective-permute-done.9.refs_2_, ...), custom_call_target="tpu_custom_call" | custom-call | flops 1048576 | bytes 3145728 | tf_op jit(solution)/shard_map/gather_near/pallas_call | solution.py:32
  34.7 10.8 %collective-permute-done.8.refs_0_ = bf16[1024,256]{1,0:T(8,128)(2,1)S(1)} collective-permute-done((bf16[1024,256]{1,0:T(8,128)(2,1)S(1)}, bf16[1024,256]{1,0:T(8,128)(2,1)S(1)}, u32[]{:S(2)}, u32[]{:S(2)}) %collective-permute-start.8) | collective-permute-done | bytes 524320 | tf_op jit(solution)/shard_map/ppermute | solution.py:25
  46.0 1.2 gather_far.1.refs_1_
  47.4 0.7 gather_far_first.1.refs_1_
  48.9 20.7 %all_to_all.16 = bf16[8,128,512]{2,1,0:T(8,128)(2,1)S(1)} all-to-all(bf16[8,128,512]{2,1,0:T(8,128)(2,1)S(1)} %bitcast.11), channel_id=1, replica_groups=mesh['row'=32,'col'=8] {'col'}, dimensions={0} | all-to-all | bytes 2097152 | tf_op jit(solution)/shard_map/all_to_all | solution.py:249
  69.6 1.1 node_step.1
  70.7 17.8 %all_to_all.17.parts = bf16[8,512,128]{2,1,0:T(8,128)(2,1)S(1)} all-to-all(bf16[8,512,128]{2,1,0:T(8,128)(2,1)S(1)} %get-tuple-element.48), channel_id=1, replica_groups=mesh['row'=32,'col'=8] {'col'}, dimensions={0} | all-to-all | bytes 2097152 | tf_op jit(solution)/shard_map/all_to_all | solution.py:252
  88.5 1.2 spread_go_other.1
  89.9 1.2 spread_stay_other.1
  91.1 1.2 spread_go.1.mine
  93.6 1.3 collective-permute-start.14
  94.9 1.2 spread_stay.1.mine
  96.2 11.0 %collective-permute-done.18.got = bf16[256,1024]{1,0:T(8,128)(2,1)S(1)} collective-permute-done((bf16[256,1024]{1,0:T(8,128)(2,1)S(1)}, bf16[256,1024]{1,0:T(8,128)(2,1)S(1)}, u32[]{:S(2)}, u32[]{:S(2)}) %collective-permute-start.18) | collective-permute-done | bytes 524320 | tf_op jit(solution)/shard_map/ppermute | solution.py:25
  107.4 1.8 %collective-permute-start.19 = (bf16[256,512]{1,0:T(8,128)(2,1)S(1)}, bf16[256,512]{1,0:T(8,128)(2,1)S(1)}, u32[]{:S(2)}, u32[]{:S(2)}) collective-permute-start(bf16[256,512]{1,0:T(8,128)(2,1)S(1)} %get-tuple-element.64), channel_id=1, source_target_pairs={{0,192},{1,193},{2,194},{3,195},{4,196},{5,197},{6,198},{7,199},{8... | collective-permute-start | bytes 786440 | tf_op jit(solution)/shard_map/ppermute | solution.py:25
  109.4 6.8 %collective-permute-done.19.refs_1_ = bf16[256,512]{1,0:T(8,128)(2,1)S(1)} collective-permute-done((bf16[256,512]{1,0:T(8,128)(2,1)S(1)}, bf16[256,512]{1,0:T(8,128)(2,1)S(1)}, u32[]{:S(2)}, u32[]{:S(2)}) %collective-permute-start.19) | collective-permute-done | bytes 262176 | tf_op jit(solution)/shard_map/ppermute | solution.py:25
  116.3 1.0 collective-permute-start.20
  117.3 2.9 %collective-permute-start.16 = (bf16[256,256]{1,0:T(8,128)(2,1)S(1)}, bf16[256,256]{1,0:T(8,128)(2,1)S(1)}, u32[]{:S(2)}, u32[]{:S(2)}) collective-permute-start(bf16[256,256]{1,0:T(8,128)(2,1)S(1)} %get-tuple-element.59), channel_id=1, source_target_pairs={{0,48},{1,49},{2,50},{3,51},{4,52},{5,53},{6,54},{7,55},{8,56},{9,... | collective-permute-start | bytes 393224 | tf_op jit(solution)/shard_map/ppermute | solution.py:25
  120.2 2.4 %collective-permute-done.20.refs_1_ = bf16[256,256]{1,0:T(8,128)(2,1)S(1)} collective-permute-done((bf16[256,256]{1,0:T(8,128)(2,1)S(1)}, bf16[256,256]{1,0:T(8,128)(2,1)S(1)}, u32[]{:S(2)}, u32[]{:S(2)}) %collective-permute-start.20) | collective-permute-done | bytes 131104 | tf_op jit(solution)/shard_map/ppermute | solution.py:25
  122.6 3.0 %collective-permute-start.21 = (bf16[256,128]{1,0:T(8,128)(2,1)S(1)}, bf16[256,128]{1,0:T(8,128)(2,1)S(1)}, u32[]{:S(2)}, u32[]{:S(2)}) collective-permute-start(bf16[256,128]{1,0:T(8,128)(2,1)S(1)} %get-tuple-element.68), channel_id=1, source_target_pairs={{0,48},{1,49},{2,50},{3,51},{4,52},{5,53},{6,54},{7,55},{8,56},{9,... | collective-permute-start | bytes 196616 | tf_op jit(solution)/shard_map/ppermute | solution.py:25
  125.7 2.4 %collective-permute-start.17 = (bf16[256,128]{1,0:T(8,128)(2,1)S(1)}, bf16[256,128]{1,0:T(8,128)(2,1)S(1)}, u32[]{:S(2)}, u32[]{:S(2)}) collective-permute-start(bf16[256,128]{1,0:T(8,128)(2,1)S(1)} %get-tuple-element.61), channel_id=1, source_target_pairs={{0,16},{1,17},{2,18},{3,19},{4,20},{5,21},{6,22},{7,23},{8,24},{9,... | collective-permute-start | bytes 196616 | tf_op jit(solution)/shard_map/ppermute | solution.py:25
  128.4 0.7 collective-permute-done.21.refs_3_
  129.1 2.0 %collective-permute-done.17.refs_1_ = bf16[256,128]{1,0:T(8,128)(2,1)S(1)} collective-permute-done((bf16[256,128]{1,0:T(8,128)(2,1)S(1)}, bf16[256,128]{1,0:T(8,128)(2,1)S(1)}, u32[]{:S(2)}, u32[]{:S(2)}) %collective-permute-start.17) | collective-permute-done | bytes 65568 | tf_op jit(solution)/shard_map/ppermute | solution.py:25
  131.1 0.8 last_sum.1
  (60 shorter events, 6.3 us)
Async XLA Ops:
  0.6 28.7 %copy-start = (bf16[512,512]{1,0:T(8,128)(2,1)S(1)}, bf16[512,512]{1,0:T(8,128)(2,1)}, u32[]{:S(2)}) copy-start(bf16[512,512]{1,0:T(8,128)(2,1)} %param.12) | copy-start | bytes 1572868
  0.6 22.9 %copy-start.5 = (s32[1,1,32,3]{2,1,3,0:T(1,128)S(1)}, s32[1,1,32,3]{2,1,3,0:T(1,128)}, u32[]{:S(2)}) copy-start(s32[1,1,32,3]{2,1,3,0:T(1,128)} %param.10) | copy-start | bytes 1156
  1.6 7.6 %collective-permute-start = (bf16[128,256]{1,0:T(8,128)(2,1)S(1)}, bf16[128,256]{1,0:T(8,128)(2,1)S(1)}, u32[]{:S(2)}, u32[]{:S(2)}) collective-permute-start(bf16[128,256]{1,0:T(8,128)(2,1)S(1)} %get-tuple-element.74), channel_id=1, source_target_pairs={{0,16},{1,17},{2,18},{3,19},{4,20},{5,21},{6,22},{7,23},{8,24},{9,... | collective-permute-start | bytes 196616 | tf_op jit(solution)/shard_map/ppermute | solution.py:25
  5.0 8.4 %collective-permute-start.3 = (bf16[128,256]{1,0:T(8,128)(2,1)S(1)}, bf16[128,256]{1,0:T(8,128)(2,1)S(1)}, u32[]{:S(2)}, u32[]{:S(2)}) collective-permute-start(bf16[128,256]{1,0:T(8,128)(2,1)S(1)} %get-tuple-element.75), channel_id=1, source_target_pairs={{0,48},{1,49},{2,50},{3,51},{4,52},{5,53},{6,54},{7,55},{8,56},{9,... | collective-permute-start | bytes 196616 | tf_op jit(solution)/shard_map/ppermute | solution.py:25
  9.2 9.7 %collective-permute-start.1 = (bf16[256,256]{1,0:T(8,128)(2,1)S(1)}, bf16[256,256]{1,0:T(8,128)(2,1)S(1)}, u32[]{:S(2)}, u32[]{:S(2)}) collective-permute-start(bf16[256,256]{1,0:T(8,128)(2,1)S(1)} %pad_maximum_fusion.3), channel_id=1, source_target_pairs={{0,48},{1,49},{2,50},{3,51},{4,52},{5,53},{6,54},{7,55},{8,56},{9,... | collective-permute-start | bytes 393224 | tf_op jit(solution)/shard_map/ppermute | solution.py:25
  13.3 7.3 %collective-permute-start.4 = (bf16[256,256]{1,0:T(8,128)(2,1)S(1)}, bf16[256,256]{1,0:T(8,128)(2,1)S(1)}, u32[]{:S(2)}, u32[]{:S(2)}) collective-permute-start(bf16[256,256]{1,0:T(8,128)(2,1)S(1)} %pad_maximum_fusion.4), channel_id=1, source_target_pairs={{0,16},{1,17},{2,18},{3,19},{4,20},{5,21},{6,22},{7,23},{8,24},{9,... | collective-permute-start | bytes 393224 | tf_op jit(solution)/shard_map/ppermute | solution.py:25
  19.0 10.6 %collective-permute-start.2 = (bf16[512,256]{1,0:T(8,128)(2,1)S(1)}, bf16[512,256]{1,0:T(8,128)(2,1)S(1)}, u32[]{:S(2)}, u32[]{:S(2)}) collective-permute-start(bf16[512,256]{1,0:T(8,128)(2,1)S(1)} %pad_maximum_fusion.1), channel_id=1, source_target_pairs={{0,64},{1,65},{2,66},{3,67},{4,68},{5,69},{6,70},{7,71},{8,72},{9,... | collective-permute-start | bytes 786440 | tf_op jit(solution)/shard_map/ppermute | solution.py:25
  20.6 8.9 %collective-permute-start.5 = (bf16[512,256]{1,0:T(8,128)(2,1)S(1)}, bf16[512,256]{1,0:T(8,128)(2,1)S(1)}, u32[]{:S(2)}, u32[]{:S(2)}) collective-permute-start(bf16[512,256]{1,0:T(8,128)(2,1)S(1)} %pad_maximum_fusion.2), channel_id=1, source_target_pairs={{0,192},{1,193},{2,194},{3,195},{4,196},{5,197},{6,198},{7,199},{8... | collective-permute-start | bytes 786440 | tf_op jit(solution)/shard_map/ppermute | solution.py:25
  23.7 5.6 %copy-start.3 = (bf16[128,512]{1,0:T(8,128)(2,1)S(1)}, bf16[128,512]{1,0:T(8,128)(2,1)}, u32[]{:S(2)}) copy-start(bf16[128,512]{1,0:T(8,128)(2,1)} %param.8) | copy-start | bytes 393220
  23.7 5.6 %copy-start.4 = (f32[512]{0:T(512)S(1)}, f32[512]{0:T(512)}, u32[]{:S(2)}) copy-start(f32[512]{0:T(512)} %param.14) | copy-start | bytes 6148
  29.6 2.7 %collective-permute-start.9 = (bf16[1024,256]{1,0:T(8,128)(2,1)S(1)}, bf16[1024,256]{1,0:T(8,128)(2,1)S(1)}, u32[]{:S(2)}, u32[]{:S(2)}) collective-permute-start(bf16[1024,256]{1,0:T(8,128)(2,1)S(1)} %constant_dynamic-update-slice_fusion.refs_0_), channel_id=1, source_target_pairs={{0,8},{1,9},{2,10},{3,11},{4,12},{5,13},{6,14},{7,15},{8,0},{9,1},... | collective-permute-start | bytes 1572872 | tf_op jit(solution)/shard_map/ppermute | solution.py:25
  29.8 2.6 %collective-permute-start.10 = (bf16[1024,256]{1,0:T(8,128)(2,1)S(1)}, bf16[1024,256]{1,0:T(8,128)(2,1)S(1)}, u32[]{:S(2)}, u32[]{:S(2)}) collective-permute-start(bf16[1024,256]{1,0:T(8,128)(2,1)S(1)} %pad_maximum_fusion.refs_1_), channel_id=1, source_target_pairs={{0,8},{1,9},{2,10},{3,11},{4,12},{5,13},{6,14},{7,15},{8,0},{9,1},... | collective-permute-start | bytes 1572872 | tf_op jit(solution)/shard_map/ppermute | solution.py:25
  30.3 15.1 %collective-permute-start.8 = (bf16[1024,256]{1,0:T(8,128)(2,1)S(1)}, bf16[1024,256]{1,0:T(8,128)(2,1)S(1)}, u32[]{:S(2)}, u32[]{:S(2)}) collective-permute-start(bf16[1024,256]{1,0:T(8,128)(2,1)S(1)} %constant_dynamic-update-slice_fusion.refs_0_), channel_id=1, source_target_pairs={{0,192},{1,193},{2,194},{3,195},{4,196},{5,197},{6,198},{7,199},{8... | collective-permute-start | bytes 1572872 | tf_op jit(solution)/shard_map/ppermute | solution.py:25
  32.3 13.6 %collective-permute-start.6 = (bf16[1024,256]{1,0:T(8,128)(2,1)S(1)}, bf16[1024,256]{1,0:T(8,128)(2,1)S(1)}, u32[]{:S(2)}, u32[]{:S(2)}) collective-permute-start(bf16[1024,256]{1,0:T(8,128)(2,1)S(1)} %pad_maximum_fusion.refs_1_), channel_id=1, source_target_pairs={{0,64},{1,65},{2,66},{3,67},{4,68},{5,69},{6,70},{7,71},{8,72},{9,... | collective-permute-start | bytes 1572872 | tf_op jit(solution)/shard_map/ppermute | solution.py:25
  45.5 1.9 %collective-permute-start.11 = (bf16[1024,256]{1,0:T(8,128)(2,1)S(1)}, bf16[1024,256]{1,0:T(8,128)(2,1)S(1)}, u32[]{:S(2)}, u32[]{:S(2)}) collective-permute-start(bf16[1024,256]{1,0:T(8,128)(2,1)S(1)} %collective-permute-done.8.refs_0_), channel_id=1, source_target_pairs={{0,8},{1,9},{2,10},{3,11},{4,12},{5,13},{6,14},{7,15},{8,0},{9,1},... | collective-permute-start | bytes 1572872 | tf_op jit(solution)/shard_map/ppermute | solution.py:25
  45.9 2.2 %collective-permute-start.7 = (bf16[1024,256]{1,0:T(8,128)(2,1)S(1)}, bf16[1024,256]{1,0:T(8,128)(2,1)S(1)}, u32[]{:S(2)}, u32[]{:S(2)}) collective-permute-start(bf16[1024,256]{1,0:T(8,128)(2,1)S(1)} %collective-permute-done.6.refs_1_), channel_id=1, source_target_pairs={{0,8},{1,9},{2,10},{3,11},{4,12},{5,13},{6,14},{7,15},{8,0},{9,1},... | collective-permute-start | bytes 1572872 | tf_op jit(solution)/shard_map/ppermute | solution.py:25
  48.8 20.7 %copy-start.1 = (bf16[512,512]{1,0:T(8,128)(2,1)S(1)}, bf16[512,512]{1,0:T(8,128)(2,1)}, u32[]{:S(2)}) copy-start(bf16[512,512]{1,0:T(8,128)(2,1)} %w_neigh.1) | copy-start | bytes 1572868
  48.9 20.7 %copy-start.2 = (bf16[128,512]{1,0:T(8,128)(2,1)S(1)}, bf16[128,512]{1,0:T(8,128)(2,1)}, u32[]{:S(2)}) copy-start(bf16[128,512]{1,0:T(8,128)(2,1)} %cotangent.1) | copy-start | bytes 393220
  89.8 2.7 %collective-permute-start.12 = (bf16[2,256,1024]{2,1,0:T(8,128)(2,1)S(1)}, bf16[2,256,1024]{2,1,0:T(8,128)(2,1)S(1)}, u32[]{:S(2)}, u32[]{:S(2)}) collective-permute-start(bf16[2,256,1024]{2,1,0:T(8,128)(2,1)S(1)} %spread_go_other.1), channel_id=1, source_target_pairs={{0,8},{1,9},{2,10},{3,11},{4,12},{5,13},{6,14},{7,15},{8,0},{9,1},... | collective-permute-start | bytes 3145736 | tf_op jit(solution)/shard_map/ppermute | solution.py:25
  92.8 14.4 %collective-permute-start.13 = (bf16[2,256,1024]{2,1,0:T(8,128)(2,1)S(1)}, bf16[2,256,1024]{2,1,0:T(8,128)(2,1)S(1)}, u32[]{:S(2)}, u32[]{:S(2)}) collective-permute-start(bf16[2,256,1024]{2,1,0:T(8,128)(2,1)S(1)} %spread_stay_other.1), channel_id=1, source_target_pairs={{0,8},{1,9},{2,10},{3,11},{4,12},{5,13},{6,14},{7,15},{8,0},{9,1},... | collective-permute-start | bytes 3145736 | tf_op jit(solution)/shard_map/ppermute | solution.py:25
  93.2 14.0 %collective-permute-start.18 = (bf16[256,1024]{1,0:T(8,128)(2,1)S(1)}, bf16[256,1024]{1,0:T(8,128)(2,1)S(1)}, u32[]{:S(2)}, u32[]{:S(2)}) collective-permute-start(bf16[256,1024]{1,0:T(8,128)(2,1)S(1)} %get-tuple-element.62), channel_id=1, source_target_pairs={{0,64},{1,65},{2,66},{3,67},{4,68},{5,69},{6,70},{7,71},{8,72},{9,... | collective-permute-start | bytes 1572872 | tf_op jit(solution)/shard_map/ppermute | solution.py:25
  93.6 15.5 %collective-permute-start.14 = (bf16[256,1024]{1,0:T(8,128)(2,1)S(1)}, bf16[256,1024]{1,0:T(8,128)(2,1)S(1)}, u32[]{:S(2)}, u32[]{:S(2)}) collective-permute-start(bf16[256,1024]{1,0:T(8,128)(2,1)S(1)} %get-tuple-element.55), channel_id=1, source_target_pairs={{0,192},{1,193},{2,194},{3,195},{4,196},{5,197},{6,198},{7,199},{8... | collective-permute-start | bytes 1572872 | tf_op jit(solution)/shard_map/ppermute | solution.py:25
  107.4 8.8 %collective-permute-start.19 = (bf16[256,512]{1,0:T(8,128)(2,1)S(1)}, bf16[256,512]{1,0:T(8,128)(2,1)S(1)}, u32[]{:S(2)}, u32[]{:S(2)}) collective-permute-start(bf16[256,512]{1,0:T(8,128)(2,1)S(1)} %get-tuple-element.64), channel_id=1, source_target_pairs={{0,192},{1,193},{2,194},{3,195},{4,196},{5,197},{6,198},{7,199},{8... | collective-permute-start | bytes 786440 | tf_op jit(solution)/shard_map/ppermute | solution.py:25
  109.3 7.9 %collective-permute-start.15 = (bf16[256,512]{1,0:T(8,128)(2,1)S(1)}, bf16[256,512]{1,0:T(8,128)(2,1)S(1)}, u32[]{:S(2)}, u32[]{:S(2)}) collective-permute-start(bf16[256,512]{1,0:T(8,128)(2,1)S(1)} %get-tuple-element.57), channel_id=1, source_target_pairs={{0,64},{1,65},{2,66},{3,67},{4,68},{5,69},{6,70},{7,71},{8,72},{9,... | collective-permute-start | bytes 786440 | tf_op jit(solution)/shard_map/ppermute | solution.py:25
  116.3 6.4 %collective-permute-start.20 = (bf16[256,256]{1,0:T(8,128)(2,1)S(1)}, bf16[256,256]{1,0:T(8,128)(2,1)S(1)}, u32[]{:S(2)}, u32[]{:S(2)}) collective-permute-start(bf16[256,256]{1,0:T(8,128)(2,1)S(1)} %get-tuple-element.66), channel_id=1, source_target_pairs={{0,16},{1,17},{2,18},{3,19},{4,20},{5,21},{6,22},{7,23},{8,24},{9,... | collective-permute-start | bytes 393224 | tf_op jit(solution)/shard_map/ppermute | solution.py:25
  117.3 8.3 %collective-permute-start.16 = (bf16[256,256]{1,0:T(8,128)(2,1)S(1)}, bf16[256,256]{1,0:T(8,128)(2,1)S(1)}, u32[]{:S(2)}, u32[]{:S(2)}) collective-permute-start(bf16[256,256]{1,0:T(8,128)(2,1)S(1)} %get-tuple-element.59), channel_id=1, source_target_pairs={{0,48},{1,49},{2,50},{3,51},{4,52},{5,53},{6,54},{7,55},{8,56},{9,... | collective-permute-start | bytes 393224 | tf_op jit(solution)/shard_map/ppermute | solution.py:25
  122.6 6.5 %collective-permute-start.21 = (bf16[256,128]{1,0:T(8,128)(2,1)S(1)}, bf16[256,128]{1,0:T(8,128)(2,1)S(1)}, u32[]{:S(2)}, u32[]{:S(2)}) collective-permute-start(bf16[256,128]{1,0:T(8,128)(2,1)S(1)} %get-tuple-element.68), channel_id=1, source_target_pairs={{0,48},{1,49},{2,50},{3,51},{4,52},{5,53},{6,54},{7,55},{8,56},{9,... | collective-permute-start | bytes 196616 | tf_op jit(solution)/shard_map/ppermute | solution.py:25
  125.7 5.4 %collective-permute-start.17 = (bf16[256,128]{1,0:T(8,128)(2,1)S(1)}, bf16[256,128]{1,0:T(8,128)(2,1)S(1)}, u32[]{:S(2)}, u32[]{:S(2)}) collective-permute-start(bf16[256,128]{1,0:T(8,128)(2,1)S(1)} %get-tuple-element.61), channel_id=1, source_target_pairs={{0,16},{1,17},{2,18},{3,19},{4,20},{5,21},{6,22},{7,23},{8,24},{9,... | collective-permute-start | bytes 196616 | tf_op jit(solution)/shard_map/ppermute | solution.py:25

commit v13 on v12

--- a/solution.py
+++ b/solution.py
@@ -110,7 +110,7 @@
     return in_vmem(kernel, [kept((rows, width), dtype)], operands, name)[0]
 
 
-def node_kernel(parts, base, degf_row, w_neigh, cotangent, grad, scaled_t, out):
+def node_kernel(parts, base, degf_row, w_neigh, cotangent, grad, scaled_t, before):
     total = parts[0:TILE, :].astype(F32)
     for i in range(1, NCOL):
         total = total + parts[i * TILE : (i + 1) * TILE, :].astype(F32)
@@ -118,7 +118,7 @@
     mean = (total / degf_col).astype(BF16)
     pre = base[...] + jnp.dot(mean, w_neigh[...], preferred_element_type=F32)
     sig = jax.nn.sigmoid(pre)
-    out[...] = (pre * sig).astype(BF16)
+    before[...] = pre
     slope = sig * (1.0 + pre * (1.0 - sig))
     grad_pre = (cotangent[...].astype(F32) * slope).astype(BF16)
     grad[...] = grad_pre
@@ -130,9 +130,17 @@
 
 def node_step(parts, base, degf_row, w_neigh, cotangent):
     rows, width = cotangent.shape
-    results = [kept((rows, width), BF16), kept((NCOL, width, rows), BF16), plain((rows, width), BF16)]
+    results = [kept((rows, width), BF16), kept((NCOL, width, rows), BF16), kept((rows, width), F32)]
     operands = (parts, base, degf_row, w_neigh, cotangent)
     return in_vmem(node_kernel, results, operands, "node_step", 4 * rows * width * width)
+
+
+def silu_kernel(pre, out):
+    out[...] = (pre[...] * jax.nn.sigmoid(pre[...])).astype(BF16)
+
+
+def silu(pre):
+    return in_vmem(silu_kernel, [plain(pre.shape, BF16)], (pre,), "silu")[0]
 
 
 def spread_kernel(core, pick, parts, adj, out):
@@ -247,7 +255,7 @@
     summed = gather_matmul(adj, other[1:], (1,), second, part, BF16, "gather_far_second", (1,))
 
     arrived = lax.all_to_all(summed, "col", 0, 0, tiled=True)
-    grad_pre, scaled_t, output = node_step(arrived, base, degf_row, w_neigh, cotangent)
+    grad_pre, scaled_t, pre = node_step(arrived, base, degf_row, w_neigh, cotangent)
 
     table = lax.all_to_all(scaled_t, "col", 0, 0, tiled=True)
     own = lax.dot_general(grad_pre, w_self, (((1,), (1,)), ((), ())), preferred_element_type=F32)
@@ -256,7 +264,8 @@
     keep_out = spread_matmul(table, adj, 1, stays, "spread_stay_other")
     send_in, send, keep_out = lax.optimization_barrier((send_in, send, keep_out))
     sums = list(both_halves(send, send_in))
-    sums[0], keep_out, table = lax.optimization_barrier((sums[0], keep_out, table))
+    sums[0], keep_out, table, pre = lax.optimization_barrier((sums[0], keep_out, table, pre))
+    output = silu(pre)
     keep_in = flip(keep_out, core=1)
     keep = spread_matmul(table, adj, 0, stays, "spread_stay")
 

time: 134 us -> 133 us (level)
    pallas_call x17 -> x18, Pallas kernels: 12.7 us -> 13 us  [in_vmem(): pl.pallas_call(kernel, in_specs=[spec] * len(operands), out_specs=out_spe...]
  transfers between devices with their start and end apart: 22 -> 22, of which waited for: 11 -> 10; matrix products, arithmetic and copies ran while one was open for 1% -> 1% of each run, Pallas kernels for 11% -> 11%
where the time goes in v13:
time: 133 us; the launch traced here: 131 us
  waiting for transfers between devices  38.8 us (29%)
  blocking collectives  38.5 us (29%)
  starting transfers between devices  32.2 us (24%)
  Pallas kernels  18.5 us (14%)
    ppermute x22, waiting for transfers between devices, flip(): return lax.ppermute(value, ('row', 'col'), pairs)  38.8 us
    ppermute x22, starting transfers between devices, flip(): return lax.ppermute(value, ('row', 'col'), pairs)  32.2 us
    all_to_all x1, blocking collectives, body(): arrived = lax.all_to_all(summed, 'col', 0, 0, tiled=True)  20.7 us
    all_to_all x1, blocking collectives, body(): table = lax.all_to_all(scaled_t, 'col', 0, 0, tiled=True)  17.8 us
    pallas_call x18, Pallas kernels, in_vmem(): pl.pallas_call(kernel, in_specs=[spec] * len(operands), out_specs=out_spe...  13 us
    pallas_call x1, Pallas kernels, adjacency(): pl.pallas_call(adjacency_kernel, grid_spec=pltpu.PrefetchScalarGridSpec(n...  5.55 us
  transfers between devices with their start and end apart: 22, of which 10 were waited for; matrix products, arithmetic and copies ran while one was open for 1% of the time, Pallas kernels for 11%

profile of v13, /device:TPU:32, one launch (start us, length us, event | category | flops | bytes accessed | tf_op | source)
XLA Modules:
  0.0 131.5 jit_solution(6475029405891750086)
XLA Ops:
  0.7 0.9 constant_dynamic-update-slice_fusion.4
  1.6 3.4 %collective-permute-start = (bf16[128,256]{1,0:T(8,128)(2,1)S(1)}, bf16[128,256]{1,0:T(8,128)(2,1)S(1)}, u32[]{:S(2)}, u32[]{:S(2)}) collective-permute-start(bf16[128,256]{1,0:T(8,128)(2,1)S(1)} %get-tuple-element.76), channel_id=1, source_target_pairs={{0,16},{1,17},{2,18},{3,19},{4,20},{5,21},{6,22},{7,23},{8,24},{9,... | collective-permute-start | bytes 196616 | tf_op jit(solution)/shard_map/ppermute | solution.py:25
  5.0 3.6 %collective-permute-start.3 = (bf16[128,256]{1,0:T(8,128)(2,1)S(1)}, bf16[128,256]{1,0:T(8,128)(2,1)S(1)}, u32[]{:S(2)}, u32[]{:S(2)}) collective-permute-start(bf16[128,256]{1,0:T(8,128)(2,1)S(1)} %get-tuple-element.77), channel_id=1, source_target_pairs={{0,48},{1,49},{2,50},{3,51},{4,52},{5,53},{6,54},{7,55},{8,56},{9,... | collective-permute-start | bytes 196616 | tf_op jit(solution)/shard_map/ppermute | solution.py:25
  9.2 4.1 %collective-permute-start.1 = (bf16[256,256]{1,0:T(8,128)(2,1)S(1)}, bf16[256,256]{1,0:T(8,128)(2,1)S(1)}, u32[]{:S(2)}, u32[]{:S(2)}) collective-permute-start(bf16[256,256]{1,0:T(8,128)(2,1)S(1)} %pad_maximum_fusion.3), channel_id=1, source_target_pairs={{0,48},{1,49},{2,50},{3,51},{4,52},{5,53},{6,54},{7,55},{8,56},{9,... | collective-permute-start | bytes 393224 | tf_op jit(solution)/shard_map/ppermute | solution.py:25
  13.9 5.0 %collective-permute-done.1 = bf16[256,256]{1,0:T(8,128)(2,1)S(1)} collective-permute-done((bf16[256,256]{1,0:T(8,128)(2,1)S(1)}, bf16[256,256]{1,0:T(8,128)(2,1)S(1)}, u32[]{:S(2)}, u32[]{:S(2)}) %collective-permute-start.1) | collective-permute-done | bytes 131104 | tf_op jit(solution)/shard_map/ppermute | solution.py:25
  19.0 1.7 %collective-permute-start.2 = (bf16[512,256]{1,0:T(8,128)(2,1)S(1)}, bf16[512,256]{1,0:T(8,128)(2,1)S(1)}, u32[]{:S(2)}, u32[]{:S(2)}) collective-permute-start(bf16[512,256]{1,0:T(8,128)(2,1)S(1)} %pad_maximum_fusion.1), channel_id=1, source_target_pairs={{0,64},{1,65},{2,66},{3,67},{4,68},{5,69},{6,70},{7,71},{8,72},{9,... | collective-permute-start | bytes 786440 | tf_op jit(solution)/shard_map/ppermute | solution.py:25
  20.6 2.9 %collective-permute-start.5 = (bf16[512,256]{1,0:T(8,128)(2,1)S(1)}, bf16[512,256]{1,0:T(8,128)(2,1)S(1)}, u32[]{:S(2)}, u32[]{:S(2)}) collective-permute-start(bf16[512,256]{1,0:T(8,128)(2,1)S(1)} %pad_maximum_fusion.2), channel_id=1, source_target_pairs={{0,192},{1,193},{2,194},{3,195},{4,196},{5,197},{6,198},{7,199},{8... | collective-permute-start | bytes 786440 | tf_op jit(solution)/shard_map/ppermute | solution.py:25
  23.7 5.5 %adjacency.1.adj = bf16[1024,4096]{1,0:T(8,128)(2,1)S(1)} custom-call(s32[32]{0:T(128)S(1)} %fusion.1.place, s32[96]{0:T(128)S(1)} %reshape_squeeze.3.where, s32[32,3,128,128]{3,2,1,0:T(8,128)} %bitcast.13), custom_call_target="tpu_custom_call" | custom-call | bytes 14680064 | tf_op jit(solution)/shard_map/adjacency/pallas_call | solution.py:68
  30.3 2.0 %collective-permute-start.8 = (bf16[1024,256]{1,0:T(8,128)(2,1)S(1)}, bf16[1024,256]{1,0:T(8,128)(2,1)S(1)}, u32[]{:S(2)}, u32[]{:S(2)}) collective-permute-start(bf16[1024,256]{1,0:T(8,128)(2,1)S(1)} %constant_dynamic-update-slice_fusion.refs_0_), channel_id=1, source_target_pairs={{0,192},{1,193},{2,194},{3,195},{4,196},{5,197},{6,198},{7,199},{8... | collective-permute-start | bytes 1572872 | tf_op jit(solution)/shard_map/ppermute | solution.py:25
  32.4 2.3 %gather_near.1.refs_2_ = f32[1024,512]{1,0:T(8,128)S(1)} custom-call(bf16[1024,4096]{1,0:T(8,128)(2,1)S(1)} %adjacency.1.adj, bf16[1024,256]{1,0:T(8,128)(2,1)S(1)} %constant_dynamic-update-slice_fusion.refs_0_, bf16[1024,256]{1,0:T(8,128)(2,1)S(1)} %pad_maximum_fusion.refs_1_, bf16[1024,256]{1,0:T(8,128)(2,1)S(1)} %collective-permute-done.9.refs_2_, ...), custom_call_target="tpu_custom_call" | custom-call | flops 1048576 | bytes 3145728 | tf_op jit(solution)/shard_map/gather_near/pallas_call | solution.py:32
  34.7 10.8 %collective-permute-done.8.refs_0_ = bf16[1024,256]{1,0:T(8,128)(2,1)S(1)} collective-permute-done((bf16[1024,256]{1,0:T(8,128)(2,1)S(1)}, bf16[1024,256]{1,0:T(8,128)(2,1)S(1)}, u32[]{:S(2)}, u32[]{:S(2)}) %collective-permute-start.8) | collective-permute-done | bytes 524320 | tf_op jit(solution)/shard_map/ppermute | solution.py:25
  46.0 1.2 gather_far.1.refs_1_
  47.4 0.7 gather_far_first.1.refs_1_
  48.1 0.7 gather_far_second.1
  48.9 20.7 %all_to_all.16 = bf16[8,128,512]{2,1,0:T(8,128)(2,1)S(1)} all-to-all(bf16[8,128,512]{2,1,0:T(8,128)(2,1)S(1)} %bitcast.11), channel_id=1, replica_groups=mesh['row'=32,'col'=8] {'col'}, dimensions={0} | all-to-all | bytes 2097152 | tf_op jit(solution)/shard_map/all_to_all | solution.py:257
  70.3 17.8 %all_to_all.17.parts = bf16[8,512,128]{2,1,0:T(8,128)(2,1)S(1)} all-to-all(bf16[8,512,128]{2,1,0:T(8,128)(2,1)S(1)} %get-tuple-element.48), channel_id=1, replica_groups=mesh['row'=32,'col'=8] {'col'}, dimensions={0} | all-to-all | bytes 2097152 | tf_op jit(solution)/shard_map/all_to_all | solution.py:260
  88.1 1.2 spread_go_other.1
  89.5 1.2 spread_stay_other.1
  90.7 1.2 spread_go.1.mine
  93.2 1.3 collective-permute-start.14
  94.5 1.2 spread_stay.1.mine
  95.8 11.0 %collective-permute-done.18.got = bf16[256,1024]{1,0:T(8,128)(2,1)S(1)} collective-permute-done((bf16[256,1024]{1,0:T(8,128)(2,1)S(1)}, bf16[256,1024]{1,0:T(8,128)(2,1)S(1)}, u32[]{:S(2)}, u32[]{:S(2)}) %collective-permute-start.18) | collective-permute-done | bytes 524320 | tf_op jit(solution)/shard_map/ppermute | solution.py:25
  107.0 1.8 %collective-permute-start.19 = (bf16[256,512]{1,0:T(8,128)(2,1)S(1)}, bf16[256,512]{1,0:T(8,128)(2,1)S(1)}, u32[]{:S(2)}, u32[]{:S(2)}) collective-permute-start(bf16[256,512]{1,0:T(8,128)(2,1)S(1)} %get-tuple-element.66), channel_id=1, source_target_pairs={{0,192},{1,193},{2,194},{3,195},{4,196},{5,197},{6,198},{7,199},{8... | collective-permute-start | bytes 786440 | tf_op jit(solution)/shard_map/ppermute | solution.py:25
  109.0 6.8 %collective-permute-done.19.refs_1_ = bf16[256,512]{1,0:T(8,128)(2,1)S(1)} collective-permute-done((bf16[256,512]{1,0:T(8,128)(2,1)S(1)}, bf16[256,512]{1,0:T(8,128)(2,1)S(1)}, u32[]{:S(2)}, u32[]{:S(2)}) %collective-permute-start.19) | collective-permute-done | bytes 262176 | tf_op jit(solution)/shard_map/ppermute | solution.py:25
  115.9 1.0 collective-permute-start.20
  116.9 2.9 %collective-permute-start.16 = (bf16[256,256]{1,0:T(8,128)(2,1)S(1)}, bf16[256,256]{1,0:T(8,128)(2,1)S(1)}, u32[]{:S(2)}, u32[]{:S(2)}) collective-permute-start(bf16[256,256]{1,0:T(8,128)(2,1)S(1)} %get-tuple-element.61), channel_id=1, source_target_pairs={{0,48},{1,49},{2,50},{3,51},{4,52},{5,53},{6,54},{7,55},{8,56},{9,... | collective-permute-start | bytes 393224 | tf_op jit(solution)/shard_map/ppermute | solution.py:25
  119.8 2.4 %collective-permute-done.20.refs_1_ = bf16[256,256]{1,0:T(8,128)(2,1)S(1)} collective-permute-done((bf16[256,256]{1,0:T(8,128)(2,1)S(1)}, bf16[256,256]{1,0:T(8,128)(2,1)S(1)}, u32[]{:S(2)}, u32[]{:S(2)}) %collective-permute-start.20) | collective-permute-done | bytes 131104 | tf_op jit(solution)/shard_map/ppermute | solution.py:25
  122.3 3.0 %collective-permute-start.21 = (bf16[256,128]{1,0:T(8,128)(2,1)S(1)}, bf16[256,128]{1,0:T(8,128)(2,1)S(1)}, u32[]{:S(2)}, u32[]{:S(2)}) collective-permute-start(bf16[256,128]{1,0:T(8,128)(2,1)S(1)} %get-tuple-element.70), channel_id=1, source_target_pairs={{0,48},{1,49},{2,50},{3,51},{4,52},{5,53},{6,54},{7,55},{8,56},{9,... | collective-permute-start | bytes 196616 | tf_op jit(solution)/shard_map/ppermute | solution.py:25
  125.3 2.4 %collective-permute-start.17 = (bf16[256,128]{1,0:T(8,128)(2,1)S(1)}, bf16[256,128]{1,0:T(8,128)(2,1)S(1)}, u32[]{:S(2)}, u32[]{:S(2)}) collective-permute-start(bf16[256,128]{1,0:T(8,128)(2,1)S(1)} %get-tuple-element.63), channel_id=1, source_target_pairs={{0,16},{1,17},{2,18},{3,19},{4,20},{5,21},{6,22},{7,23},{8,24},{9,... | collective-permute-start | bytes 196616 | tf_op jit(solution)/shard_map/ppermute | solution.py:25
  128.0 0.7 silu.1
  128.7 1.9 %collective-permute-done.17.refs_1_ = bf16[256,128]{1,0:T(8,128)(2,1)S(1)} collective-permute-done((bf16[256,128]{1,0:T(8,128)(2,1)S(1)}, bf16[256,128]{1,0:T(8,128)(2,1)S(1)}, u32[]{:S(2)}, u32[]{:S(2)}) %collective-permute-start.17) | collective-permute-done | bytes 65568 | tf_op jit(solution)/shard_map/ppermute | solution.py:25
  130.7 0.8 last_sum.1
  (61 shorter events, 6.3 us)
Async XLA Ops:
  0.6 28.7 %copy-start = (bf16[512,512]{1,0:T(8,128)(2,1)S(1)}, bf16[512,512]{1,0:T(8,128)(2,1)}, u32[]{:S(2)}) copy-start(bf16[512,512]{1,0:T(8,128)(2,1)} %param.12) | copy-start | bytes 1572868
  0.6 22.9 %copy-start.5 = (s32[1,1,32,3]{2,1,3,0:T(1,128)S(1)}, s32[1,1,32,3]{2,1,3,0:T(1,128)}, u32[]{:S(2)}) copy-start(s32[1,1,32,3]{2,1,3,0:T(1,128)} %param.10) | copy-start | bytes 1156
  1.6 7.6 %collective-permute-start = (bf16[128,256]{1,0:T(8,128)(2,1)S(1)}, bf16[128,256]{1,0:T(8,128)(2,1)S(1)}, u32[]{:S(2)}, u32[]{:S(2)}) collective-permute-start(bf16[128,256]{1,0:T(8,128)(2,1)S(1)} %get-tuple-element.76), channel_id=1, source_target_pairs={{0,16},{1,17},{2,18},{3,19},{4,20},{5,21},{6,22},{7,23},{8,24},{9,... | collective-permute-start | bytes 196616 | tf_op jit(solution)/shard_map/ppermute | solution.py:25
  5.0 8.4 %collective-permute-start.3 = (bf16[128,256]{1,0:T(8,128)(2,1)S(1)}, bf16[128,256]{1,0:T(8,128)(2,1)S(1)}, u32[]{:S(2)}, u32[]{:S(2)}) collective-permute-start(bf16[128,256]{1,0:T(8,128)(2,1)S(1)} %get-tuple-element.77), channel_id=1, source_target_pairs={{0,48},{1,49},{2,50},{3,51},{4,52},{5,53},{6,54},{7,55},{8,56},{9,... | collective-permute-start | bytes 196616 | tf_op jit(solution)/shard_map/ppermute | solution.py:25
  9.2 9.7 %collective-permute-start.1 = (bf16[256,256]{1,0:T(8,128)(2,1)S(1)}, bf16[256,256]{1,0:T(8,128)(2,1)S(1)}, u32[]{:S(2)}, u32[]{:S(2)}) collective-permute-start(bf16[256,256]{1,0:T(8,128)(2,1)S(1)} %pad_maximum_fusion.3), channel_id=1, source_target_pairs={{0,48},{1,49},{2,50},{3,51},{4,52},{5,53},{6,54},{7,55},{8,56},{9,... | collective-permute-start | bytes 393224 | tf_op jit(solution)/shard_map/ppermute | solution.py:25
  13.3 7.3 %collective-permute-start.4 = (bf16[256,256]{1,0:T(8,128)(2,1)S(1)}, bf16[256,256]{1,0:T(8,128)(2,1)S(1)}, u32[]{:S(2)}, u32[]{:S(2)}) collective-permute-start(bf16[256,256]{1,0:T(8,128)(2,1)S(1)} %pad_maximum_fusion.4), channel_id=1, source_target_pairs={{0,16},{1,17},{2,18},{3,19},{4,20},{5,21},{6,22},{7,23},{8,24},{9,... | collective-permute-start | bytes 393224 | tf_op jit(solution)/shard_map/ppermute | solution.py:25
  19.0 10.6 %collective-permute-start.2 = (bf16[512,256]{1,0:T(8,128)(2,1)S(1)}, bf16[512,256]{1,0:T(8,128)(2,1)S(1)}, u32[]{:S(2)}, u32[]{:S(2)}) collective-permute-start(bf16[512,256]{1,0:T(8,128)(2,1)S(1)} %pad_maximum_fusion.1), channel_id=1, source_target_pairs={{0,64},{1,65},{2,66},{3,67},{4,68},{5,69},{6,70},{7,71},{8,72},{9,... | collective-permute-start | bytes 786440 | tf_op jit(solution)/shard_map/ppermute | solution.py:25
  20.6 8.9 %collective-permute-start.5 = (bf16[512,256]{1,0:T(8,128)(2,1)S(1)}, bf16[512,256]{1,0:T(8,128)(2,1)S(1)}, u32[]{:S(2)}, u32[]{:S(2)}) collective-permute-start(bf16[512,256]{1,0:T(8,128)(2,1)S(1)} %pad_maximum_fusion.2), channel_id=1, source_target_pairs={{0,192},{1,193},{2,194},{3,195},{4,196},{5,197},{6,198},{7,199},{8... | collective-permute-start | bytes 786440 | tf_op jit(solution)/shard_map/ppermute | solution.py:25
  23.7 5.6 %copy-start.3 = (bf16[128,512]{1,0:T(8,128)(2,1)S(1)}, bf16[128,512]{1,0:T(8,128)(2,1)}, u32[]{:S(2)}) copy-start(bf16[128,512]{1,0:T(8,128)(2,1)} %param.8) | copy-start | bytes 393220
  23.7 5.6 %copy-start.4 = (f32[512]{0:T(512)S(1)}, f32[512]{0:T(512)}, u32[]{:S(2)}) copy-start(f32[512]{0:T(512)} %param.14) | copy-start | bytes 6148
  29.6 2.7 %collective-permute-start.9 = (bf16[1024,256]{1,0:T(8,128)(2,1)S(1)}, bf16[1024,256]{1,0:T(8,128)(2,1)S(1)}, u32[]{:S(2)}, u32[]{:S(2)}) collective-permute-start(bf16[1024,256]{1,0:T(8,128)(2,1)S(1)} %constant_dynamic-update-slice_fusion.refs_0_), channel_id=1, source_target_pairs={{0,8},{1,9},{2,10},{3,11},{4,12},{5,13},{6,14},{7,15},{8,0},{9,1},... | collective-permute-start | bytes 1572872 | tf_op jit(solution)/shard_map/ppermute | solution.py:25
  29.8 2.6 %collective-permute-start.10 = (bf16[1024,256]{1,0:T(8,128)(2,1)S(1)}, bf16[1024,256]{1,0:T(8,128)(2,1)S(1)}, u32[]{:S(2)}, u32[]{:S(2)}) collective-permute-start(bf16[1024,256]{1,0:T(8,128)(2,1)S(1)} %pad_maximum_fusion.refs_1_), channel_id=1, source_target_pairs={{0,8},{1,9},{2,10},{3,11},{4,12},{5,13},{6,14},{7,15},{8,0},{9,1},... | collective-permute-start | bytes 1572872 | tf_op jit(solution)/shard_map/ppermute | solution.py:25
  30.3 15.1 %collective-permute-start.8 = (bf16[1024,256]{1,0:T(8,128)(2,1)S(1)}, bf16[1024,256]{1,0:T(8,128)(2,1)S(1)}, u32[]{:S(2)}, u32[]{:S(2)}) collective-permute-start(bf16[1024,256]{1,0:T(8,128)(2,1)S(1)} %constant_dynamic-update-slice_fusion.refs_0_), channel_id=1, source_target_pairs={{0,192},{1,193},{2,194},{3,195},{4,196},{5,197},{6,198},{7,199},{8... | collective-permute-start | bytes 1572872 | tf_op jit(solution)/shard_map/ppermute | solution.py:25
  32.3 13.6 %collective-permute-start.6 = (bf16[1024,256]{1,0:T(8,128)(2,1)S(1)}, bf16[1024,256]{1,0:T(8,128)(2,1)S(1)}, u32[]{:S(2)}, u32[]{:S(2)}) collective-permute-start(bf16[1024,256]{1,0:T(8,128)(2,1)S(1)} %pad_maximum_fusion.refs_1_), channel_id=1, source_target_pairs={{0,64},{1,65},{2,66},{3,67},{4,68},{5,69},{6,70},{7,71},{8,72},{9,... | collective-permute-start | bytes 1572872 | tf_op jit(solution)/shard_map/ppermute | solution.py:25
  45.5 1.9 %collective-permute-start.11 = (bf16[1024,256]{1,0:T(8,128)(2,1)S(1)}, bf16[1024,256]{1,0:T(8,128)(2,1)S(1)}, u32[]{:S(2)}, u32[]{:S(2)}) collective-permute-start(bf16[1024,256]{1,0:T(8,128)(2,1)S(1)} %collective-permute-done.8.refs_0_), channel_id=1, source_target_pairs={{0,8},{1,9},{2,10},{3,11},{4,12},{5,13},{6,14},{7,15},{8,0},{9,1},... | collective-permute-start | bytes 1572872 | tf_op jit(solution)/shard_map/ppermute | solution.py:25
  45.9 2.2 %collective-permute-start.7 = (bf16[1024,256]{1,0:T(8,128)(2,1)S(1)}, bf16[1024,256]{1,0:T(8,128)(2,1)S(1)}, u32[]{:S(2)}, u32[]{:S(2)}) collective-permute-start(bf16[1024,256]{1,0:T(8,128)(2,1)S(1)} %collective-permute-done.6.refs_1_), channel_id=1, source_target_pairs={{0,8},{1,9},{2,10},{3,11},{4,12},{5,13},{6,14},{7,15},{8,0},{9,1},... | collective-permute-start | bytes 1572872 | tf_op jit(solution)/shard_map/ppermute | solution.py:25
  48.8 20.7 %copy-start.1 = (bf16[512,512]{1,0:T(8,128)(2,1)S(1)}, bf16[512,512]{1,0:T(8,128)(2,1)}, u32[]{:S(2)}) copy-start(bf16[512,512]{1,0:T(8,128)(2,1)} %w_neigh.1) | copy-start | bytes 1572868
  48.9 20.7 %copy-start.2 = (bf16[128,512]{1,0:T(8,128)(2,1)S(1)}, bf16[128,512]{1,0:T(8,128)(2,1)}, u32[]{:S(2)}) copy-start(bf16[128,512]{1,0:T(8,128)(2,1)} %cotangent.1) | copy-start | bytes 393220
  89.4 2.7 %collective-permute-start.12 = (bf16[2,256,1024]{2,1,0:T(8,128)(2,1)S(1)}, bf16[2,256,1024]{2,1,0:T(8,128)(2,1)S(1)}, u32[]{:S(2)}, u32[]{:S(2)}) collective-permute-start(bf16[2,256,1024]{2,1,0:T(8,128)(2,1)S(1)} %spread_go_other.1), channel_id=1, source_target_pairs={{0,8},{1,9},{2,10},{3,11},{4,12},{5,13},{6,14},{7,15},{8,0},{9,1},... | collective-permute-start | bytes 3145736 | tf_op jit(solution)/shard_map/ppermute | solution.py:25
  92.4 14.4 %collective-permute-start.13 = (bf16[2,256,1024]{2,1,0:T(8,128)(2,1)S(1)}, bf16[2,256,1024]{2,1,0:T(8,128)(2,1)S(1)}, u32[]{:S(2)}, u32[]{:S(2)}) collective-permute-start(bf16[2,256,1024]{2,1,0:T(8,128)(2,1)S(1)} %spread_stay_other.1), channel_id=1, source_target_pairs={{0,8},{1,9},{2,10},{3,11},{4,12},{5,13},{6,14},{7,15},{8,0},{9,1},... | collective-permute-start | bytes 3145736 | tf_op jit(solution)/shard_map/ppermute | solution.py:25
  92.8 14.0 %collective-permute-start.18 = (bf16[256,1024]{1,0:T(8,128)(2,1)S(1)}, bf16[256,1024]{1,0:T(8,128)(2,1)S(1)}, u32[]{:S(2)}, u32[]{:S(2)}) collective-permute-start(bf16[256,1024]{1,0:T(8,128)(2,1)S(1)} %get-tuple-element.64), channel_id=1, source_target_pairs={{0,64},{1,65},{2,66},{3,67},{4,68},{5,69},{6,70},{7,71},{8,72},{9,... | collective-permute-start | bytes 1572872 | tf_op jit(solution)/shard_map/ppermute | solution.py:25
  93.2 15.5 %collective-permute-start.14 = (bf16[256,1024]{1,0:T(8,128)(2,1)S(1)}, bf16[256,1024]{1,0:T(8,128)(2,1)S(1)}, u32[]{:S(2)}, u32[]{:S(2)}) collective-permute-start(bf16[256,1024]{1,0:T(8,128)(2,1)S(1)} %get-tuple-element.57), channel_id=1, source_target_pairs={{0,192},{1,193},{2,194},{3,195},{4,196},{5,197},{6,198},{7,199},{8... | collective-permute-start | bytes 1572872 | tf_op jit(solution)/shard_map/ppermute | solution.py:25
  107.0 8.8 %collective-permute-start.19 = (bf16[256,512]{1,0:T(8,128)(2,1)S(1)}, bf16[256,512]{1,0:T(8,128)(2,1)S(1)}, u32[]{:S(2)}, u32[]{:S(2)}) collective-permute-start(bf16[256,512]{1,0:T(8,128)(2,1)S(1)} %get-tuple-element.66), channel_id=1, source_target_pairs={{0,192},{1,193},{2,194},{3,195},{4,196},{5,197},{6,198},{7,199},{8... | collective-permute-start | bytes 786440 | tf_op jit(solution)/shard_map/ppermute | solution.py:25
  108.9 7.9 %collective-permute-start.15 = (bf16[256,512]{1,0:T(8,128)(2,1)S(1)}, bf16[256,512]{1,0:T(8,128)(2,1)S(1)}, u32[]{:S(2)}, u32[]{:S(2)}) collective-permute-start(bf16[256,512]{1,0:T(8,128)(2,1)S(1)} %get-tuple-element.59), channel_id=1, source_target_pairs={{0,64},{1,65},{2,66},{3,67},{4,68},{5,69},{6,70},{7,71},{8,72},{9,... | collective-permute-start | bytes 786440 | tf_op jit(solution)/shard_map/ppermute | solution.py:25
  115.9 6.4 %collective-permute-start.20 = (bf16[256,256]{1,0:T(8,128)(2,1)S(1)}, bf16[256,256]{1,0:T(8,128)(2,1)S(1)}, u32[]{:S(2)}, u32[]{:S(2)}) collective-permute-start(bf16[256,256]{1,0:T(8,128)(2,1)S(1)} %get-tuple-element.68), channel_id=1, source_target_pairs={{0,16},{1,17},{2,18},{3,19},{4,20},{5,21},{6,22},{7,23},{8,24},{9,... | collective-permute-start | bytes 393224 | tf_op jit(solution)/shard_map/ppermute | solution.py:25
  116.9 8.3 %collective-permute-start.16 = (bf16[256,256]{1,0:T(8,128)(2,1)S(1)}, bf16[256,256]{1,0:T(8,128)(2,1)S(1)}, u32[]{:S(2)}, u32[]{:S(2)}) collective-permute-start(bf16[256,256]{1,0:T(8,128)(2,1)S(1)} %get-tuple-element.61), channel_id=1, source_target_pairs={{0,48},{1,49},{2,50},{3,51},{4,52},{5,53},{6,54},{7,55},{8,56},{9,... | collective-permute-start | bytes 393224 | tf_op jit(solution)/shard_map/ppermute | solution.py:25
  122.3 6.5 %collective-permute-start.21 = (bf16[256,128]{1,0:T(8,128)(2,1)S(1)}, bf16[256,128]{1,0:T(8,128)(2,1)S(1)}, u32[]{:S(2)}, u32[]{:S(2)}) collective-permute-start(bf16[256,128]{1,0:T(8,128)(2,1)S(1)} %get-tuple-element.70), channel_id=1, source_target_pairs={{0,48},{1,49},{2,50},{3,51},{4,52},{5,53},{6,54},{7,55},{8,56},{9,... | collective-permute-start | bytes 196616 | tf_op jit(solution)/shard_map/ppermute | solution.py:25
  125.3 5.4 %collective-permute-start.17 = (bf16[256,128]{1,0:T(8,128)(2,1)S(1)}, bf16[256,128]{1,0:T(8,128)(2,1)S(1)}, u32[]{:S(2)}, u32[]{:S(2)}) collective-permute-start(bf16[256,128]{1,0:T(8,128)(2,1)S(1)} %get-tuple-element.63), channel_id=1, source_target_pairs={{0,16},{1,17},{2,18},{3,19},{4,20},{5,21},{6,22},{7,23},{8,24},{9,... | collective-permute-start | bytes 196616 | tf_op jit(solution)/shard_map/ppermute | solution.py:25
